TPU v7x, 32 devices: a whole 2x2x4 slice. The times are simulated.
32 devices in a mesh: shard: 16 (over z, y, x), rep: 2 (over core).
Axes of the slice: x: 2, y: 2, z: 4, core: 2. Of those that a mesh axis runs over, the one named last changes fastest.
Arguments:
- momentum: bfloat16 [16, 512, 2048], P(None, 'shard'), may hold values from -6 to 6
- gradient: bfloat16 [16, 512, 2048], P(None, 'shard'), may hold values from -6 to 6
Outputs:
- new_momentum: bfloat16 [16, 512, 2048], P(None, 'shard')
- update: bfloat16 [16, 512, 2048], P(None, 'shard')
All inputs are finite; a program needn't handle non-finite values.
Results may differ from a plain program's by a relative error of at most 0.00065.
The roundings to bfloat16 on the way count: a program that leaves them out, or rounds other values in their place, can miss the bound.
Values may be sent and summed in bfloat16 or wider, within the bound.
No kernel may reach another device: no remote copies, remote signals or barrier semaphores. Data moves between devices by JAX's collectives and lax.ppermute only.
A program may use at most 64 MiB of HBM per device.

v0:
```python
import functools

import jax
import jax.numpy as jnp
from jax import lax
from jax.experimental import pallas as pl
from jax.experimental.pallas import tpu as pltpu
from jax.sharding import PartitionSpec as P

ITERS = 5

coef_a = 3.4445
coef_b = -4.775
coef_c = 2.0315

BF = jnp.bfloat16
F32 = jnp.float32


def blend_kernel(rep_ref, m_ref, g_ref, new_ref, part_ref):
    width = part_ref.shape[-1]
    new_ref[...] = (0.95 * m_ref[...].astype(F32) + g_ref[...].astype(F32)).astype(BF)
    cols = pl.ds(pl.multiple_of(rep_ref[0] * width, width), width)
    part_ref[...] = (
        g_ref[:, :, cols].astype(F32) + 0.95 * new_ref[:, :, cols].astype(F32)
    ).astype(BF)


def blend(rep, momentum, gradient, n_rep):
    experts, rows, cols = momentum.shape
    step = 2
    whole = pl.BlockSpec((step, rows, cols), lambda i, r: (i, 0, 0))
    part = pl.BlockSpec((step, rows, cols // n_rep), lambda i, r: (i, 0, 0))
    return pl.pallas_call(
        blend_kernel,
        grid_spec=pltpu.PrefetchScalarGridSpec(
            num_scalar_prefetch=1,
            grid=(experts // step,),
            in_specs=[whole, whole],
            out_specs=[whole, part],
        ),
        out_shape=[
            jax.ShapeDtypeStruct(momentum.shape, BF),
            jax.ShapeDtypeStruct((experts, rows, cols // n_rep), BF),
        ],
        name="blend",
    )(rep, momentum, gradient)


def halves(x):
    high = x.astype(BF)
    return high, (x - high.astype(F32)).astype(BF)


def put_left(ref, x):
    n = x.shape[0]
    high, low = halves(x)
    ref[:, :n] = high
    ref[:, n : 2 * n] = high
    ref[:, 2 * n :] = low


def put_right(ref, x, at):
    n = x.shape[0]
    high, low = halves(x)
    ref[:n, at : at + n] = high
    ref[n : 2 * n, at : at + n] = low
    ref[2 * n :, at : at + n] = high


def dot(x, y):
    return jnp.dot(x, y, preferred_element_type=F32)


def orthogonal_kernel(scale, *refs):
    *parts, out_ref, a_ref, q_ref, s_ref, left, right = refs
    n = a_ref.shape[0]

    def gram(x):
        return lax.dot_general(
            x, x, (((1,), (1,)), ((), ())), preferred_element_type=F32
        )

    total = gram(parts[0][...])
    for part in parts[1:]:
        total = total + gram(part[...])
    eye = lax.broadcasted_iota(jnp.int32, (n, n), 0) == lax.broadcasted_iota(
        jnp.int32, (n, n), 1
    )
    square = jnp.sum(jnp.where(eye, total, 0.0), keepdims=True)
    inverse = 1.0 / (jnp.sqrt(square) + 1e-07)
    first = total * (inverse * inverse)
    a_ref[...] = first

    def middle():
        a = a_ref[...]
        put_left(left, a)
        put_right(right, a, 0)
        m = coef_b * a + coef_c * dot(left[...], right[:, :n])
        put_left(left, m)
        return m

    def advance():
        s_ref[...] = coef_a * a_ref[...] + dot(left[...], right[:, :n])
        put_right(right, s_ref[...], 0)
        a_ref[...] = coef_a * s_ref[...] + dot(left[...], right[:, :n])

    q_ref[...] = jnp.where(eye, coef_a, 0.0) + middle()
    advance()

    def step(_, carry):
        middle()
        put_right(right, q_ref[...], n)
        q_ref[...] = coef_a * q_ref[...] + dot(left[...], right[:, n:])
        advance()
        return carry

    lax.fori_loop(1, ITERS - 1, step, 0)
    middle()
    put_right(right, q_ref[...], n)
    q = coef_a * q_ref[...] + dot(left[...], right[:, n:])
    high, low = halves(q * (inverse * scale))
    left[:, :n] = high
    left[:, n : 2 * n] = low
    width = out_ref.shape[1]
    block = min(width, 256)
    for at in range(0, width, block):
        x = parts[0][:, at : at + block]
        out_ref[:, at : at + block] = (
            dot(left[:, :n], x) + dot(left[:, n : 2 * n], x)
        ).astype(BF)


def orthogonal(parts, scale):
    rows, width = parts[0].shape
    vmem = pl.BlockSpec(memory_space=pltpu.VMEM)
    return pl.pallas_call(
        functools.partial(orthogonal_kernel, scale),
        in_specs=[vmem] * len(parts),
        out_specs=vmem,
        out_shape=jax.ShapeDtypeStruct((rows, width), BF),
        scratch_shapes=[
            pltpu.VMEM((rows, rows), F32),
            pltpu.VMEM((rows, rows), F32),
            pltpu.VMEM((rows, rows), F32),
            pltpu.VMEM((rows, 3 * rows), BF),
            pltpu.VMEM((3 * rows, 2 * rows), BF),
        ],
        compiler_params=pltpu.CompilerParams(vmem_limit_bytes=40 * 2**20),
        name="orthogonal",
    )(*parts)


def solution(mesh):
    n_rep = mesh.shape["rep"]

    def swap(x):
        return [
            lax.ppermute(x, "rep", [((i + j) % n_rep, i) for i in range(n_rep)])
            for j in range(1, n_rep)
        ]

    def shards(momentum, gradient):
        experts, rows, cols = momentum.shape
        rep = lax.axis_index("rep")
        new_momentum, part = blend(rep[None], momentum, gradient, n_rep)
        width = part.shape[2]
        mine = lax.all_to_all(part, "shard", split_axis=0, concat_axis=0, tiled=True)
        mine = mine.reshape(experts * rows, width)
        scale = float(max(experts * rows, cols)) ** 0.5
        update = orthogonal([mine, *swap(mine)], scale)
        update = lax.all_to_all(
            update.reshape(experts, rows, width), "shard", split_axis=0, concat_axis=0, tiled=True
        )
        whole = jnp.zeros((experts, rows, cols), BF)
        for j, piece in enumerate([update, *swap(update)]):
            at = lax.rem(rep + j, n_rep) * width
            whole = lax.dynamic_update_slice(whole, piece, (0, 0, at))
        return new_momentum, whole

    return jax.shard_map(
        shards,
        mesh=mesh,
        in_specs=(P(None, "shard", None), P(None, "shard", None)),
        out_specs=(P(None, "shard", None), P(None, "shard", None)),
        check_vma=False,
    )
```

profile of v0, /device:TPU:0, one launch (start us, length us, event | category | flops | bytes accessed | tf_op | source)
XLA Modules:
  0.0 97.9 jit_solution(4050131668692170917)
XLA Ops:
  0.6 6.6 %blend.1 = (bf16[16,32,2048]{2,1,0:T(8,128)(2,1)}, bf16[16,32,1024]{2,1,0:T(8,128)(2,1)}) custom-call(s32[1]{0:T(128)} %bitcast.rep_ref, bf16[16,32,2048]{2,1,0:T(8,128)(2,1)} %m_ref.1, bf16[16,32,2048]{2,1,0:T(8,128)(2,1)} %g_ref.1), custom_call_target="tpu_custom_call" | custom-call | tf_op jit(solution)/shard_map/blend/pallas_call | solution.py:34
  7.3 34.7 %all_to_all.10 = bf16[16,32,1024]{2,1,0:T(8,128)(2,1)S(1)} all-to-all(bf16[16,32,1024]{2,1,0:T(8,128)(2,1)} %get-tuple-element.5), channel_id=1, replica_groups=mesh['shard'=16,'rep'=2] {'shard'}, dimensions={0} | all-to-all | bytes 2097152 | tf_op jit(solution)/shard_map/all_to_all | solution.py:168
  41.9 0.0 collective-permute-start
  41.9 2.7 %collective-permute-done.refs_1_ = bf16[512,1024]{1,0:T(8,128)(2,1)S(1)} collective-permute-done((bf16[512,1024]{1,0:T(8,128)(2,1)S(1)}, bf16[512,1024]{1,0:T(8,128)(2,1)S(1)}, u32[]{:S(2)}, u32[]{:S(2)}) %collective-permute-start) | collective-permute-done | bytes 1048608 | tf_op jit(solution)/shard_map/ppermute | solution.py:159
  44.6 18.8 %orthogonal.1 = bf16[512,1024]{1,0:T(8,128)(2,1)S(1)} custom-call(bf16[512,1024]{1,0:T(8,128)(2,1)S(1)} %bitcast.4, bf16[512,1024]{1,0:T(8,128)(2,1)S(1)} %collective-permute-done.refs_1_), custom_call_target="tpu_custom_call" | custom-call | tf_op jit(solution)/shard_map/orthogonal/pallas_call | solution.py:137
  63.4 30.3 %all_to_all.11 = bf16[16,32,1024]{2,1,0:T(8,128)(2,1)S(1)} all-to-all(bf16[16,32,1024]{2,1,0:T(8,128)(2,1)S(1)} %bitcast.5), channel_id=1, replica_groups=mesh['shard'=16,'rep'=2] {'shard'}, dimensions={0} | all-to-all | bytes 2097152 | tf_op jit(solution)/shard_map/all_to_all | solution.py:172
  93.8 0.0 collective-permute-start.1
  93.8 0.2 broadcast_in_dim.7
  94.0 0.1 constant_dynamic-update-slice_fusion.1
  94.1 2.3 %collective-permute-done.1 = bf16[16,32,1024]{2,1,0:T(8,128)(2,1)S(1)} collective-permute-done((bf16[16,32,1024]{2,1,0:T(8,128)(2,1)S(1)}, bf16[16,32,1024]{2,1,0:T(8,128)(2,1)S(1)}, u32[]{:S(2)}, u32[]{:S(2)}) %collective-permute-start.1) | collective-permute-done | bytes 1048608 | tf_op jit(solution)/shard_map/ppermute | solution.py:159
  96.4 0.1 constant_dynamic-update-slice_fusion
  96.5 0.0 copy-start
  96.6 1.3 %copy-done = bf16[16,32,2048]{2,1,0:T(8,128)(2,1)} copy-done((bf16[16,32,2048]{2,1,0:T(8,128)(2,1)}, bf16[16,32,2048]{2,1,0:T(8,128)(2,1)S(1)}, u32[]{:S(2)}) %copy-start) | copy-done | bytes 2097176
Async XLA Ops:
  41.9 2.7 %collective-permute-start = (bf16[512,1024]{1,0:T(8,128)(2,1)S(1)}, bf16[512,1024]{1,0:T(8,128)(2,1)S(1)}, u32[]{:S(2)}, u32[]{:S(2)}) collective-permute-start(bf16[512,1024]{1,0:T(8,128)(2,1)S(1)} %bitcast.3), channel_id=1, source_target_pairs={{1,0},{0,1},{3,2},{2,3},{5,4},{4,5},{7,6},{6,7},{9,8},{8,9},{11,10... | collective-permute-start | bytes 3145736 | tf_op jit(solution)/shard_map/ppermute | solution.py:159
  93.8 2.7 %collective-permute-start.1 = (bf16[16,32,1024]{2,1,0:T(8,128)(2,1)S(1)}, bf16[16,32,1024]{2,1,0:T(8,128)(2,1)S(1)}, u32[]{:S(2)}, u32[]{:S(2)}) collective-permute-start(bf16[16,32,1024]{2,1,0:T(8,128)(2,1)S(1)} %all_to_all.11), channel_id=1, source_target_pairs={{1,0},{0,1},{3,2},{2,3},{5,4},{4,5},{7,6},{6,7},{9,8},{8,9},{11,10... | collective-permute-start | bytes 3145736 | tf_op jit(solution)/shard_map/ppermute | solution.py:159
  96.5 1.3 %copy-start = (bf16[16,32,2048]{2,1,0:T(8,128)(2,1)}, bf16[16,32,2048]{2,1,0:T(8,128)(2,1)S(1)}, u32[]{:S(2)}) copy-start(bf16[16,32,2048]{2,1,0:T(8,128)(2,1)S(1)} %constant_dynamic-update-slice_fusion) | copy-start | bytes 6291460
where the time goes:
time: 98.2 us; the launch traced here: 97.9 us
  blocking collectives  65 us (66%)
  Pallas kernels  25.4 us (26%)
  waiting for transfers between devices  4.94 us (5%)
  local copies, waits for them, and re-layouts  1.78 us (2%)
    all_to_all x1, blocking collectives, shards(): lax.all_to_all(part, 'shard', split_axis=0, concat_axis=0, tiled=True)  34.7 us
    all_to_all x1, blocking collectives, shards(): lax.all_to_all(update.reshape(experts, rows, width), 'shard', split_axis=...  30.3 us
    pallas_call x1, Pallas kernels, orthogonal(): pl.pallas_call(functools.partial(orthogonal_kernel, scale), in_specs=[vme...  18.8 us
    pallas_call x1, Pallas kernels, blend(): pl.pallas_call(blend_kernel, grid_spec=pltpu.PrefetchScalarGridSpec(num_s...  6.63 us
    ppermute x2, waiting for transfers between devices, swap(): lax.ppermute(x, 'rep', [((i + j) % n_rep, i) for i in range(n_rep)])  4.94 us
  transfers between devices with their start and end apart: 2, of which 2 were waited for; matrix products, arithmetic and copies ran while one was open for 0% of the time, Pallas kernels for 0%

commit v1 on v0

v1 whole, which is shorter than its diff:
```python
import functools

import jax
import jax.numpy as jnp
from jax import lax
from jax.experimental import pallas as pl
from jax.experimental.pallas import tpu as pltpu
from jax.sharding import PartitionSpec as P

ITERS = 5

coef_a = 3.4445
coef_b = -4.775
coef_c = 2.0315

BF = jnp.bfloat16
F32 = jnp.float32


def pieces_kernel(at_ref, m_ref, g_ref, *part_refs):
    experts = len(part_refs)
    for k, part_ref in enumerate(part_refs):
        e = lax.rem(at_ref[0] + k, experts)
        g = g_ref[e].astype(F32)
        new = (0.95 * m_ref[e].astype(F32) + g).astype(BF)
        part_ref[...] = (g + 0.95 * new.astype(F32)).astype(BF)


def blended_pieces(at, momentum, gradient, n_rep):
    experts, rows, cols = momentum.shape
    width = cols // n_rep
    block = pl.BlockSpec((experts, rows, width), lambda i, at: (0, 0, at[1]))
    piece = pl.BlockSpec((rows, width), lambda i, at: (0, 0))
    return pl.pallas_call(
        pieces_kernel,
        grid_spec=pltpu.PrefetchScalarGridSpec(
            num_scalar_prefetch=1,
            grid=(1,),
            in_specs=[block, block],
            out_specs=[piece] * experts,
        ),
        out_shape=[jax.ShapeDtypeStruct((rows, width), BF)] * experts,
        compiler_params=pltpu.CompilerParams(vmem_limit_bytes=24 * 2**20),
        name="blended",
    )(at, momentum, gradient)


def momentum_kernel(m_ref, g_ref, new_ref):
    new_ref[...] = (0.95 * m_ref[...].astype(F32) + g_ref[...].astype(F32)).astype(BF)


def next_momentum(momentum, gradient):
    experts, rows, cols = momentum.shape
    step = 2
    block = pl.BlockSpec((step, rows, cols), lambda i: (i, 0, 0))
    return pl.pallas_call(
        momentum_kernel,
        grid=(experts // step,),
        in_specs=[block, block],
        out_specs=block,
        out_shape=jax.ShapeDtypeStruct(momentum.shape, BF),
        cost_estimate=pl.CostEstimate(
            flops=2 * momentum.size, bytes_accessed=6 * momentum.size, transcendentals=0
        ),
        name="new_momentum",
    )(momentum, gradient)


def halves(x):
    high = x.astype(BF)
    return high, (x - high.astype(F32)).astype(BF)


def put_left(ref, x):
    n = x.shape[0]
    high, low = halves(x)
    ref[:, :n] = high
    ref[:, n : 2 * n] = high
    ref[:, 2 * n :] = low


def put_right(ref, x, at):
    n = x.shape[0]
    high, low = halves(x)
    ref[:n, at : at + n] = high
    ref[n : 2 * n, at : at + n] = low
    ref[2 * n :, at : at + n] = high


def dot(x, y):
    return jnp.dot(x, y, preferred_element_type=F32)


def orthogonal_kernel(scale, count, n_in, *refs):
    ins, refs = refs[:n_in], refs[n_in:]
    out_refs, (a_ref, q_ref, s_ref, left, right, *parts) = refs[:count], refs[count:]
    n = a_ref.shape[0]
    rows, width = ins[0].shape
    for i, ref in enumerate(ins):
        at = i % count * rows
        parts[i // count][at : at + rows, :] = ref[...]

    def gram(x):
        return lax.dot_general(
            x, x, (((1,), (1,)), ((), ())), preferred_element_type=F32
        )

    total = gram(parts[0][...])
    for part in parts[1:]:
        total = total + gram(part[...])
    eye = lax.broadcasted_iota(jnp.int32, (n, n), 0) == lax.broadcasted_iota(
        jnp.int32, (n, n), 1
    )
    square = jnp.sum(jnp.where(eye, total, 0.0), keepdims=True)
    inverse = 1.0 / (jnp.sqrt(square) + 1e-07)
    first = total * (inverse * inverse)
    a_ref[...] = first

    def middle():
        a = a_ref[...]
        put_left(left, a)
        put_right(right, a, 0)
        m = coef_b * a + coef_c * dot(left[...], right[:, :n])
        put_left(left, m)
        return m

    def advance():
        s_ref[...] = coef_a * a_ref[...] + dot(left[...], right[:, :n])
        put_right(right, s_ref[...], 0)
        a_ref[...] = coef_a * s_ref[...] + dot(left[...], right[:, :n])

    q_ref[...] = jnp.where(eye, coef_a, 0.0) + middle()
    advance()

    def step(_, carry):
        middle()
        put_right(right, q_ref[...], n)
        q_ref[...] = coef_a * q_ref[...] + dot(left[...], right[:, n:])
        advance()
        return carry

    lax.fori_loop(1, ITERS - 1, step, 0)
    middle()
    put_right(right, q_ref[...], n)
    q = coef_a * q_ref[...] + dot(left[...], right[:, n:])
    high, low = halves(q * (inverse * scale))
    left[:, :n] = high
    left[:, n : 2 * n] = low
    block = min(width, 256)
    for at in range(0, width, block):
        x = parts[0][:, at : at + block]
        y = (dot(left[:, :n], x) + dot(left[:, n : 2 * n], x)).astype(BF)
        for i, out_ref in enumerate(out_refs):
            out_ref[:, at : at + block] = y[i * rows : (i + 1) * rows]


def orthogonal(parts, scale):
    count = len(parts[0])
    rows, width = parts[0][0].shape
    n = rows * count
    flat = [piece for part in parts for piece in part]
    vmem = pl.BlockSpec(memory_space=pltpu.VMEM)
    return pl.pallas_call(
        functools.partial(orthogonal_kernel, scale, count, len(flat)),
        in_specs=[vmem] * len(flat),
        out_specs=[vmem] * count,
        out_shape=[jax.ShapeDtypeStruct((rows, width), BF)] * count,
        scratch_shapes=[
            pltpu.VMEM((n, n), F32),
            pltpu.VMEM((n, n), F32),
            pltpu.VMEM((n, n), F32),
            pltpu.VMEM((n, 3 * n), BF),
            pltpu.VMEM((3 * n, 2 * n), BF),
        ]
        + [pltpu.VMEM((n, width), BF)] * len(parts),
        compiler_params=pltpu.CompilerParams(vmem_limit_bytes=40 * 2**20),
        name="orthogonal",
    )(*flat)


def collect_kernel(count, at_ref, *refs):
    *ins, out_ref = refs
    width = ins[0].shape[1]
    n_rep = len(ins) // count
    for i, ref in enumerate(ins):
        e = lax.rem(at_ref[0] + i % count, count)
        c = lax.rem(at_ref[1] + i // count, n_rep)
        out_ref[e, :, pl.ds(pl.multiple_of(c * width, width), width)] = ref[...]


def collect(at, parts):
    count = len(parts[0])
    rows, width = parts[0][0].shape
    flat = [piece for part in parts for piece in part]
    shape = (count, rows, width * len(parts))
    piece = pl.BlockSpec((rows, width), lambda i, at: (0, 0))
    return pl.pallas_call(
        functools.partial(collect_kernel, count),
        grid_spec=pltpu.PrefetchScalarGridSpec(
            num_scalar_prefetch=1,
            grid=(1,),
            in_specs=[piece] * len(flat),
            out_specs=pl.BlockSpec(shape, lambda i, at: (0, 0, 0)),
        ),
        out_shape=jax.ShapeDtypeStruct(shape, BF),
        compiler_params=pltpu.CompilerParams(vmem_limit_bytes=24 * 2**20),
        name="collect",
    )(at, *flat)


def solution(mesh):
    n_rep = mesh.shape["rep"]
    n_shard = mesh.shape["shard"]

    def turn(x, axis, size, j):
        return lax.ppermute(x, axis, [(i, (i + j) % size) for i in range(size)])

    def others(pieces):
        if n_rep == 2:
            return [[turn(x, "rep", n_rep, 1) for x in pieces]]
        whole = jnp.concatenate(pieces)
        return [
            jnp.split(turn(whole, "rep", n_rep, -j), len(pieces)) for j in range(1, n_rep)
        ]

    def shards(momentum, gradient):
        experts, rows, cols = momentum.shape
        at = jnp.stack([lax.axis_index("shard"), lax.axis_index("rep")])
        sent = blended_pieces(at, momentum, gradient, n_rep)
        mine = [turn(x, "shard", n_shard, k) if k else x for k, x in enumerate(sent)]
        new_momentum = next_momentum(momentum, gradient)
        scale = float(max(experts * rows, cols)) ** 0.5
        update = orthogonal([mine, *others(mine)], scale)
        update = [turn(x, "shard", n_shard, -k) if k else x for k, x in enumerate(update)]
        return new_momentum, collect(at, [update, *others(update)])

    return jax.shard_map(
        shards,
        mesh=mesh,
        in_specs=(P(None, "shard", None), P(None, "shard", None)),
        out_specs=(P(None, "shard", None), P(None, "shard", None)),
        check_vma=False,
    )
```

time: 98.2 us -> 116 us (1.18)
  blocking collectives: 65 us -> 0 us
  starting transfers between devices: 0.01 us -> 62.2 us
  waiting for transfers between devices: 4.94 us -> 21.1 us
  Pallas kernels: 25.4 us -> 28.4 us
  local copies, waits for them, and re-layouts: 1.78 us -> 3.18 us
    all_to_all x2 -> x0, blocking collectives: 65 us -> none  [the longest x1 34.7 us: shards(): lax.all_to_all(part, 'shard', split_axis=0, concat_axis=0, tiled=True)]
    ppermute x2 -> x62, starting transfers between devices: 0.01 us -> 62.2 us  [turn(): return lax.ppermute(x, axis, [(i, (i + j) % size) for i in range(size)])]
    ppermute x2 -> x62, waiting for transfers between devices: 4.94 us -> 21.1 us  [turn(): return lax.ppermute(x, axis, [(i, (i + j) % size) for i in range(size)])]
    pallas_call x2 -> x4, Pallas kernels: 25.4 us -> 28.4 us  [the longest x1 18.8 us: orthogonal(): pl.pallas_call(functools.partial(orthogonal_kernel, scale, count, len(fla...]
    unnamed x2 -> x4, local copies, waits for them, and re-layouts: 1.32 us -> 3.18 us
  transfers between devices with their start and end apart: 2 -> 62, of which waited for: 2 -> 15; matrix products, arithmetic and copies ran while one was open for 0% -> 0% of each run, Pallas kernels for 0% -> 5%
where the time goes in v1:
time: 116 us
  starting transfers between devices  62.2 us (54%)
  Pallas kernels  28.4 us (24%)
  waiting for transfers between devices  21.1 us (18%)
  local copies, waits for them, and re-layouts  3.18 us (3%)
    ppermute x62, starting transfers between devices, turn(): return lax.ppermute(x, axis, [(i, (i + j) % size) for i in range(size)])  62.2 us
    ppermute x62, waiting for transfers between devices, turn(): return lax.ppermute(x, axis, [(i, (i + j) % size) for i in range(size)])  21.1 us
    pallas_call x1, Pallas kernels, orthogonal(): pl.pallas_call(functools.partial(orthogonal_kernel, scale, count, len(fla...  18.8 us
    pallas_call x1, Pallas kernels, next_momentum(): pl.pallas_call(momentum_kernel, grid=(experts // step,), in_specs=[block,...  6.23 us
    unnamed x4, local copies, waits for them, and re-layouts  3.18 us
  transfers between devices with their start and end apart: 62, of which 15 were waited for; matrix products, arithmetic and copies ran while one was open for 0% of the time, Pallas kernels for 5%

profile of v1, /device:TPU:0, one launch (start us, length us, event | category | flops | bytes accessed | tf_op | source)
XLA Modules:
  0.0 115.8 jit_solution(17947391240134532071)
XLA Ops:
  0.7 1.6 %copy-done = bf16[16,32,2048]{2,1,0:T(8,128)(2,1)S(1)} copy-done((bf16[16,32,2048]{2,1,0:T(8,128)(2,1)S(1)}, bf16[16,32,2048]{2,1,0:T(8,128)(2,1)}, u32[]{:S(2)}) %copy-start) | copy-done | bytes 2097176
  2.3 1.6 %copy-done.1 = bf16[16,32,2048]{2,1,0:T(8,128)(2,1)S(1)} copy-done((bf16[16,32,2048]{2,1,0:T(8,128)(2,1)S(1)}, bf16[16,32,2048]{2,1,0:T(8,128)(2,1)}, u32[]{:S(2)}) %copy-start.1) | copy-done | bytes 2097176
  3.9 1.3 %blended.1 = (bf16[32,1024]{1,0:T(8,128)(2,1)S(1)}, bf16[32,1024]{1,0:T(8,128)(2,1)S(1)}, bf16[32,1024]{1,0:T(8,128)(2,1)S(1)}, bf16[32,1024]{1,0:T(8,128)(2,1)S...) custom-call(s32[2]{0:T(128)S(1)} %pad_add_fusion.at_ref, ...), custom_call_target="tpu_custom_call" | custom-call | tf_op jit(solution)/shard_map/blended/pallas_call | solution.py:34
  5.2 3.0 %collective-permute-start = (bf16[32,1024]{1,0:T(8,128)(2,1)S(1)}, bf16[32,1024]{1,0:T(8,128)(2,1)S(1)}, u32[]{:S(2)}, u32[]{:S(2)}) collective-permute-start(bf16[32,1024]{1,0:T(8,128)(2,1)S(1)} %get-tuple-element.35), channel_id=1, source_target_pairs={{0,2},{2,4},{4,6},{6,8},{8,10},{10,12},{12,14},{14,16},{16,18},{18... | collective-permute-start | bytes 196616 | tf_op jit(solution)/shard_map/ppermute | solution.py:216
  8.2 1.5 %collective-permute-start.1 = (bf16[32,1024]{1,0:T(8,128)(2,1)S(1)}, bf16[32,1024]{1,0:T(8,128)(2,1)S(1)}, u32[]{:S(2)}, u32[]{:S(2)}) collective-permute-start(bf16[32,1024]{1,0:T(8,128)(2,1)S(1)} %get-tuple-element.36), channel_id=1, source_target_pairs={{0,4},{2,6},{4,8},{6,10},{8,12},{10,14},{12,16},{14,18},{16,20},{1... | collective-permute-start | bytes 196616 | tf_op jit(solution)/shard_map/ppermute | solution.py:216
  9.8 2.4 %collective-permute-start.2 = (bf16[32,1024]{1,0:T(8,128)(2,1)S(1)}, bf16[32,1024]{1,0:T(8,128)(2,1)S(1)}, u32[]{:S(2)}, u32[]{:S(2)}) collective-permute-start(bf16[32,1024]{1,0:T(8,128)(2,1)S(1)} %get-tuple-element.37), channel_id=1, source_target_pairs={{0,6},{2,8},{4,10},{6,12},{8,14},{10,16},{12,18},{14,20},{16,22},{... | collective-permute-start | bytes 196616 | tf_op jit(solution)/shard_map/ppermute | solution.py:216
  12.2 1.6 %collective-permute-start.3 = (bf16[32,1024]{1,0:T(8,128)(2,1)S(1)}, bf16[32,1024]{1,0:T(8,128)(2,1)S(1)}, u32[]{:S(2)}, u32[]{:S(2)}) collective-permute-start(bf16[32,1024]{1,0:T(8,128)(2,1)S(1)} %get-tuple-element.38), channel_id=1, source_target_pairs={{0,8},{2,10},{4,12},{6,14},{8,16},{10,18},{12,20},{14,22},{16,24},... | collective-permute-start | bytes 196616 | tf_op jit(solution)/shard_map/ppermute | solution.py:216
  13.8 1.6 %collective-permute-start.4 = (bf16[32,1024]{1,0:T(8,128)(2,1)S(1)}, bf16[32,1024]{1,0:T(8,128)(2,1)S(1)}, u32[]{:S(2)}, u32[]{:S(2)}) collective-permute-start(bf16[32,1024]{1,0:T(8,128)(2,1)S(1)} %get-tuple-element.39), channel_id=1, source_target_pairs={{0,10},{2,12},{4,14},{6,16},{8,18},{10,20},{12,22},{14,24},{16,26}... | collective-permute-start | bytes 196616 | tf_op jit(solution)/shard_map/ppermute | solution.py:216
  15.5 1.1 collective-permute-start.5
  16.6 4.4 %collective-permute-start.6 = (bf16[32,1024]{1,0:T(8,128)(2,1)S(1)}, bf16[32,1024]{1,0:T(8,128)(2,1)S(1)}, u32[]{:S(2)}, u32[]{:S(2)}) collective-permute-start(bf16[32,1024]{1,0:T(8,128)(2,1)S(1)} %get-tuple-element.41), channel_id=1, source_target_pairs={{0,14},{2,16},{4,18},{6,20},{8,22},{10,24},{12,26},{14,28},{16,30}... | collective-permute-start | bytes 196616 | tf_op jit(solution)/shard_map/ppermute | solution.py:216
  20.9 0.3 collective-permute-start.7
  21.3 1.7 %collective-permute-start.8 = (bf16[32,1024]{1,0:T(8,128)(2,1)S(1)}, bf16[32,1024]{1,0:T(8,128)(2,1)S(1)}, u32[]{:S(2)}, u32[]{:S(2)}) collective-permute-start(bf16[32,1024]{1,0:T(8,128)(2,1)S(1)} %get-tuple-element.43), channel_id=1, source_target_pairs={{0,18},{2,20},{4,22},{6,24},{8,26},{10,28},{12,30},{14,0},{16,2},{... | collective-permute-start | bytes 196616 | tf_op jit(solution)/shard_map/ppermute | solution.py:216
  23.0 3.4 %collective-permute-done.4.refs_5_ = bf16[32,1024]{1,0:T(8,128)(2,1)S(1)} collective-permute-done((bf16[32,1024]{1,0:T(8,128)(2,1)S(1)}, bf16[32,1024]{1,0:T(8,128)(2,1)S(1)}, u32[]{:S(2)}, u32[]{:S(2)}) %collective-permute-start.4) | collective-permute-done | bytes 65568 | tf_op jit(solution)/shard_map/ppermute | solution.py:216
  26.4 1.9 %collective-permute-start.10 = (bf16[32,1024]{1,0:T(8,128)(2,1)S(1)}, bf16[32,1024]{1,0:T(8,128)(2,1)S(1)}, u32[]{:S(2)}, u32[]{:S(2)}) collective-permute-start(bf16[32,1024]{1,0:T(8,128)(2,1)S(1)} %get-tuple-element.45), channel_id=1, source_target_pairs={{0,22},{2,24},{4,26},{6,28},{8,30},{10,0},{12,2},{14,4},{16,6},{18... | collective-permute-start | bytes 196616 | tf_op jit(solution)/shard_map/ppermute | solution.py:216
  28.3 6.7 %collective-permute-start.11 = (bf16[32,1024]{1,0:T(8,128)(2,1)S(1)}, bf16[32,1024]{1,0:T(8,128)(2,1)S(1)}, u32[]{:S(2)}, u32[]{:S(2)}) collective-permute-start(bf16[32,1024]{1,0:T(8,128)(2,1)S(1)} %get-tuple-element.46), channel_id=1, source_target_pairs={{0,24},{2,26},{4,28},{6,30},{8,0},{10,2},{12,4},{14,6},{16,8},{18,... | collective-permute-start | bytes 196616 | tf_op jit(solution)/shard_map/ppermute | solution.py:216
  35.1 0.5 collective-permute-start.12
  35.6 2.5 %collective-permute-start.13 = (bf16[32,1024]{1,0:T(8,128)(2,1)S(1)}, bf16[32,1024]{1,0:T(8,128)(2,1)S(1)}, u32[]{:S(2)}, u32[]{:S(2)}) collective-permute-start(bf16[32,1024]{1,0:T(8,128)(2,1)S(1)} %get-tuple-element.48), channel_id=1, source_target_pairs={{0,28},{2,30},{4,0},{6,2},{8,4},{10,6},{12,8},{14,10},{16,12},{18,... | collective-permute-start | bytes 196616 | tf_op jit(solution)/shard_map/ppermute | solution.py:216
  38.2 0.5 collective-permute-start.16
  38.7 2.2 %collective-permute-done.12.refs_13_ = bf16[32,1024]{1,0:T(8,128)(2,1)S(1)} collective-permute-done((bf16[32,1024]{1,0:T(8,128)(2,1)S(1)}, bf16[32,1024]{1,0:T(8,128)(2,1)S(1)}, u32[]{:S(2)}, u32[]{:S(2)}) %collective-permute-start.12) | collective-permute-done | bytes 65568 | tf_op jit(solution)/shard_map/ppermute | solution.py:216
  41.3 1.5 %collective-permute-done.14.refs_15_ = bf16[32,1024]{1,0:T(8,128)(2,1)S(1)} collective-permute-done((bf16[32,1024]{1,0:T(8,128)(2,1)S(1)}, bf16[32,1024]{1,0:T(8,128)(2,1)S(1)}, u32[]{:S(2)}, u32[]{:S(2)}) %collective-permute-start.14) | collective-permute-done | bytes 65568 | tf_op jit(solution)/shard_map/ppermute | solution.py:216
  42.8 0.5 collective-permute-start.20
  43.4 0.4 collective-permute-start.22
  44.0 0.3 collective-permute-start.24
  44.6 0.3 collective-permute-start.26
  45.1 0.3 collective-permute-start.28
  45.6 0.3 collective-permute-start.30
  46.3 0.3 collective-permute-done.29.refs_30_
  46.9 18.8 %orthogonal.1 = (bf16[32,1024]{1,0:T(8,128)(2,1)S(1)}, bf16[32,1024]{1,0:T(8,128)(2,1)S(1)}, bf16[32,1024]{1,0:T(8,128)(2,1)S(1)}, bf16[32,1024]{1,0:T(8,128)(2,...) custom-call(bf16[32,1024]{1,0:T(8,128)(2,1)S(1)} %get-tuple-element., ...), custom_call_target="tpu_custom_call" | custom-call | tf_op jit(solution)/shard_map/orthogonal/pallas_call | solution.py:163
  65.7 3.9 %collective-permute-start.31 = (bf16[32,1024]{1,0:T(8,128)(2,1)S(1)}, bf16[32,1024]{1,0:T(8,128)(2,1)S(1)}, u32[]{:S(2)}, u32[]{:S(2)}) collective-permute-start(bf16[32,1024]{1,0:T(8,128)(2,1)S(1)} %get-tuple-element.51), channel_id=1, source_target_pairs={{0,30},{2,0},{4,2},{6,4},{8,6},{10,8},{12,10},{14,12},{16,14},{18,... | collective-permute-start | bytes 196616 | tf_op jit(solution)/shard_map/ppermute | solution.py:216
  69.6 3.2 %collective-permute-start.33 = (bf16[32,1024]{1,0:T(8,128)(2,1)S(1)}, bf16[32,1024]{1,0:T(8,128)(2,1)S(1)}, u32[]{:S(2)}, u32[]{:S(2)}) collective-permute-start(bf16[32,1024]{1,0:T(8,128)(2,1)S(1)} %get-tuple-element.53), channel_id=1, source_target_pairs={{0,26},{2,28},{4,30},{6,0},{8,2},{10,4},{12,6},{14,8},{16,10},{18,... | collective-permute-start | bytes 196616 | tf_op jit(solution)/shard_map/ppermute | solution.py:216
  72.8 0.5 collective-permute-start.34
  73.3 0.8 collective-permute-start.35
  74.2 5.3 %collective-permute-start.36 = (bf16[32,1024]{1,0:T(8,128)(2,1)S(1)}, bf16[32,1024]{1,0:T(8,128)(2,1)S(1)}, u32[]{:S(2)}, u32[]{:S(2)}) collective-permute-start(bf16[32,1024]{1,0:T(8,128)(2,1)S(1)} %get-tuple-element.56), channel_id=1, source_target_pairs={{0,20},{2,22},{4,24},{6,26},{8,28},{10,30},{12,0},{14,2},{16,4},{1... | collective-permute-start | bytes 196616 | tf_op jit(solution)/shard_map/ppermute | solution.py:216
  79.5 1.4 %collective-permute-start.38 = (bf16[32,1024]{1,0:T(8,128)(2,1)S(1)}, bf16[32,1024]{1,0:T(8,128)(2,1)S(1)}, u32[]{:S(2)}, u32[]{:S(2)}) collective-permute-start(bf16[32,1024]{1,0:T(8,128)(2,1)S(1)} %get-tuple-element.58), channel_id=1, source_target_pairs={{0,16},{2,18},{4,20},{6,22},{8,24},{10,26},{12,28},{14,30},{16,0},... | collective-permute-start | bytes 196616 | tf_op jit(solution)/shard_map/ppermute | solution.py:216
  80.9 2.5 %collective-permute-start.39 = (bf16[32,1024]{1,0:T(8,128)(2,1)S(1)}, bf16[32,1024]{1,0:T(8,128)(2,1)S(1)}, u32[]{:S(2)}, u32[]{:S(2)}) collective-permute-start(bf16[32,1024]{1,0:T(8,128)(2,1)S(1)} %get-tuple-element.59), channel_id=1, source_target_pairs={{0,14},{2,16},{4,18},{6,20},{8,22},{10,24},{12,26},{14,28},{16,30}... | collective-permute-start | bytes 196616 | tf_op jit(solution)/shard_map/ppermute | solution.py:216
  83.4 2.3 %collective-permute-start.40 = (bf16[32,1024]{1,0:T(8,128)(2,1)S(1)}, bf16[32,1024]{1,0:T(8,128)(2,1)S(1)}, u32[]{:S(2)}, u32[]{:S(2)}) collective-permute-start(bf16[32,1024]{1,0:T(8,128)(2,1)S(1)} %get-tuple-element.60), channel_id=1, source_target_pairs={{0,12},{2,14},{4,16},{6,18},{8,20},{10,22},{12,24},{14,26},{16,28}... | collective-permute-start | bytes 196616 | tf_op jit(solution)/shard_map/ppermute | solution.py:216
  85.7 2.0 %collective-permute-start.41 = (bf16[32,1024]{1,0:T(8,128)(2,1)S(1)}, bf16[32,1024]{1,0:T(8,128)(2,1)S(1)}, u32[]{:S(2)}, u32[]{:S(2)}) collective-permute-start(bf16[32,1024]{1,0:T(8,128)(2,1)S(1)} %get-tuple-element.61), channel_id=1, source_target_pairs={{0,10},{2,12},{4,14},{6,16},{8,18},{10,20},{12,22},{14,24},{16,26}... | collective-permute-start | bytes 196616 | tf_op jit(solution)/shard_map/ppermute | solution.py:216
  87.8 1.6 %collective-permute-start.42 = (bf16[32,1024]{1,0:T(8,128)(2,1)S(1)}, bf16[32,1024]{1,0:T(8,128)(2,1)S(1)}, u32[]{:S(2)}, u32[]{:S(2)}) collective-permute-start(bf16[32,1024]{1,0:T(8,128)(2,1)S(1)} %get-tuple-element.62), channel_id=1, source_target_pairs={{0,8},{2,10},{4,12},{6,14},{8,16},{10,18},{12,20},{14,22},{16,24},... | collective-permute-start | bytes 196616 | tf_op jit(solution)/shard_map/ppermute | solution.py:216
  89.3 5.8 %collective-permute-done.38.refs_8_ = bf16[32,1024]{1,0:T(8,128)(2,1)S(1)} collective-permute-done((bf16[32,1024]{1,0:T(8,128)(2,1)S(1)}, bf16[32,1024]{1,0:T(8,128)(2,1)S(1)}, u32[]{:S(2)}, u32[]{:S(2)}) %collective-permute-start.38) | collective-permute-done | bytes 65568 | tf_op jit(solution)/shard_map/ppermute | solution.py:216
  95.2 2.1 %collective-permute-start.45 = (bf16[32,1024]{1,0:T(8,128)(2,1)S(1)}, bf16[32,1024]{1,0:T(8,128)(2,1)S(1)}, u32[]{:S(2)}, u32[]{:S(2)}) collective-permute-start(bf16[32,1024]{1,0:T(8,128)(2,1)S(1)} %get-tuple-element.65), channel_id=1, source_target_pairs={{0,2},{2,4},{4,6},{6,8},{8,10},{10,12},{12,14},{14,16},{16,18},{18... | collective-permute-start | bytes 196616 | tf_op jit(solution)/shard_map/ppermute | solution.py:216
  97.3 0.5 collective-permute-start.47
  97.8 4.6 %collective-permute-done.43.refs_13_ = bf16[32,1024]{1,0:T(8,128)(2,1)S(1)} collective-permute-done((bf16[32,1024]{1,0:T(8,128)(2,1)S(1)}, bf16[32,1024]{1,0:T(8,128)(2,1)S(1)}, u32[]{:S(2)}, u32[]{:S(2)}) %collective-permute-start.43) | collective-permute-done | bytes 65568 | tf_op jit(solution)/shard_map/ppermute | solution.py:216
  102.4 0.5 collective-permute-done.44.refs_14_
  103.0 1.3 %collective-permute-done.45.refs_15_ = bf16[32,1024]{1,0:T(8,128)(2,1)S(1)} collective-permute-done((bf16[32,1024]{1,0:T(8,128)(2,1)S(1)}, bf16[32,1024]{1,0:T(8,128)(2,1)S(1)}, u32[]{:S(2)}, u32[]{:S(2)}) %collective-permute-start.45) | collective-permute-done | bytes 65568 | tf_op jit(solution)/shard_map/ppermute | solution.py:216
  104.3 0.5 collective-permute-start.51
  104.9 0.4 collective-permute-start.53
  107.4 6.2 %new_momentum.1 = bf16[16,32,2048]{2,1,0:T(8,128)(2,1)} custom-call(bf16[16,32,2048]{2,1,0:T(8,128)(2,1)} %m_ref.3, bf16[16,32,2048]{2,1,0:T(8,128)(2,1)} %g_ref.3), custom_call_target="tpu_custom_call" | custom-call | flops 2097152 | bytes 6291456 | tf_op jit(solution)/shard_map/new_momentum/pallas_call | solution.py:56
  113.7 2.0 %collect.1 = bf16[16,32,2048]{2,1,0:T(8,128)(2,1)} custom-call(s32[2]{0:T(128)S(1)} %pad_add_fusion.at_ref, bf16[32,1024]{1,0:T(8,128)(2,1)S(1)} %get-tuple-element.50.refs_0_, bf16[32,1024]{1,0:T(8,128)(2,1)S(1)} %collective-permute-done.31.refs_1_, bf16[32,1024]{1,0:T(8,128)(2,1)S(1)} %collective-permute-done.32.refs_2_, ...), custom_call_target="tpu_custom_call" | custom-call | tf_op jit(solution)/shard_map/collect/pallas_call | solution.py:197
  (85 shorter events, 4.6 us)
Async XLA Ops:
  5.2 10.2 %collective-permute-start = (bf16[32,1024]{1,0:T(8,128)(2,1)S(1)}, bf16[32,1024]{1,0:T(8,128)(2,1)S(1)}, u32[]{:S(2)}, u32[]{:S(2)}) collective-permute-start(bf16[32,1024]{1,0:T(8,128)(2,1)S(1)} %get-tuple-element.35), channel_id=1, source_target_pairs={{0,2},{2,4},{4,6},{6,8},{8,10},{10,12},{12,14},{14,16},{16,18},{18... | collective-permute-start | bytes 196616 | tf_op jit(solution)/shard_map/ppermute | solution.py:216
  8.2 8.3 %collective-permute-start.1 = (bf16[32,1024]{1,0:T(8,128)(2,1)S(1)}, bf16[32,1024]{1,0:T(8,128)(2,1)S(1)}, u32[]{:S(2)}, u32[]{:S(2)}) collective-permute-start(bf16[32,1024]{1,0:T(8,128)(2,1)S(1)} %get-tuple-element.36), channel_id=1, source_target_pairs={{0,4},{2,6},{4,8},{6,10},{8,12},{10,14},{12,16},{14,18},{16,20},{1... | collective-permute-start | bytes 196616 | tf_op jit(solution)/shard_map/ppermute | solution.py:216
  9.8 11.2 %collective-permute-start.2 = (bf16[32,1024]{1,0:T(8,128)(2,1)S(1)}, bf16[32,1024]{1,0:T(8,128)(2,1)S(1)}, u32[]{:S(2)}, u32[]{:S(2)}) collective-permute-start(bf16[32,1024]{1,0:T(8,128)(2,1)S(1)} %get-tuple-element.37), channel_id=1, source_target_pairs={{0,6},{2,8},{4,10},{6,12},{8,14},{10,16},{12,18},{14,20},{16,22},{... | collective-permute-start | bytes 196616 | tf_op jit(solution)/shard_map/ppermute | solution.py:216
  12.2 9.1 %collective-permute-start.3 = (bf16[32,1024]{1,0:T(8,128)(2,1)S(1)}, bf16[32,1024]{1,0:T(8,128)(2,1)S(1)}, u32[]{:S(2)}, u32[]{:S(2)}) collective-permute-start(bf16[32,1024]{1,0:T(8,128)(2,1)S(1)} %get-tuple-element.38), channel_id=1, source_target_pairs={{0,8},{2,10},{4,12},{6,14},{8,16},{10,18},{12,20},{14,22},{16,24},... | collective-permute-start | bytes 196616 | tf_op jit(solution)/shard_map/ppermute | solution.py:216
  13.8 12.7 %collective-permute-start.4 = (bf16[32,1024]{1,0:T(8,128)(2,1)S(1)}, bf16[32,1024]{1,0:T(8,128)(2,1)S(1)}, u32[]{:S(2)}, u32[]{:S(2)}) collective-permute-start(bf16[32,1024]{1,0:T(8,128)(2,1)S(1)} %get-tuple-element.39), channel_id=1, source_target_pairs={{0,10},{2,12},{4,14},{6,16},{8,18},{10,20},{12,22},{14,24},{16,26}... | collective-permute-start | bytes 196616 | tf_op jit(solution)/shard_map/ppermute | solution.py:216
  15.5 11.0 %collective-permute-start.5 = (bf16[32,1024]{1,0:T(8,128)(2,1)S(1)}, bf16[32,1024]{1,0:T(8,128)(2,1)S(1)}, u32[]{:S(2)}, u32[]{:S(2)}) collective-permute-start(bf16[32,1024]{1,0:T(8,128)(2,1)S(1)} %get-tuple-element.40), channel_id=1, source_target_pairs={{0,12},{2,14},{4,16},{6,18},{8,20},{10,22},{12,24},{14,26},{16,28}... | collective-permute-start | bytes 196616 | tf_op jit(solution)/shard_map/ppermute | solution.py:216
  16.6 11.7 %collective-permute-start.6 = (bf16[32,1024]{1,0:T(8,128)(2,1)S(1)}, bf16[32,1024]{1,0:T(8,128)(2,1)S(1)}, u32[]{:S(2)}, u32[]{:S(2)}) collective-permute-start(bf16[32,1024]{1,0:T(8,128)(2,1)S(1)} %get-tuple-element.41), channel_id=1, source_target_pairs={{0,14},{2,16},{4,18},{6,20},{8,22},{10,24},{12,26},{14,28},{16,30}... | collective-permute-start | bytes 196616 | tf_op jit(solution)/shard_map/ppermute | solution.py:216
  20.9 14.1 %collective-permute-start.7 = (bf16[32,1024]{1,0:T(8,128)(2,1)S(1)}, bf16[32,1024]{1,0:T(8,128)(2,1)S(1)}, u32[]{:S(2)}, u32[]{:S(2)}) collective-permute-start(bf16[32,1024]{1,0:T(8,128)(2,1)S(1)} %get-tuple-element.42), channel_id=1, source_target_pairs={{0,16},{2,18},{4,20},{6,22},{8,24},{10,26},{12,28},{14,30},{16,0},... | collective-permute-start | bytes 196616 | tf_op jit(solution)/shard_map/ppermute | solution.py:216
  21.3 14.3 %collective-permute-start.8 = (bf16[32,1024]{1,0:T(8,128)(2,1)S(1)}, bf16[32,1024]{1,0:T(8,128)(2,1)S(1)}, u32[]{:S(2)}, u32[]{:S(2)}) collective-permute-start(bf16[32,1024]{1,0:T(8,128)(2,1)S(1)} %get-tuple-element.43), channel_id=1, source_target_pairs={{0,18},{2,20},{4,22},{6,24},{8,26},{10,28},{12,30},{14,0},{16,2},{... | collective-permute-start | bytes 196616 | tf_op jit(solution)/shard_map/ppermute | solution.py:216
  26.4 11.6 %collective-permute-start.9 = (bf16[32,1024]{1,0:T(8,128)(2,1)S(1)}, bf16[32,1024]{1,0:T(8,128)(2,1)S(1)}, u32[]{:S(2)}, u32[]{:S(2)}) collective-permute-start(bf16[32,1024]{1,0:T(8,128)(2,1)S(1)} %get-tuple-element.44), channel_id=1, source_target_pairs={{0,20},{2,22},{4,24},{6,26},{8,28},{10,30},{12,0},{14,2},{16,4},{1... | collective-permute-start | bytes 196616 | tf_op jit(solution)/shard_map/ppermute | solution.py:216
  26.4 11.6 %collective-permute-start.10 = (bf16[32,1024]{1,0:T(8,128)(2,1)S(1)}, bf16[32,1024]{1,0:T(8,128)(2,1)S(1)}, u32[]{:S(2)}, u32[]{:S(2)}) collective-permute-start(bf16[32,1024]{1,0:T(8,128)(2,1)S(1)} %get-tuple-element.45), channel_id=1, source_target_pairs={{0,22},{2,24},{4,26},{6,28},{8,30},{10,0},{12,2},{14,4},{16,6},{18... | collective-permute-start | bytes 196616 | tf_op jit(solution)/shard_map/ppermute | solution.py:216
  28.3 9.8 %collective-permute-start.11 = (bf16[32,1024]{1,0:T(8,128)(2,1)S(1)}, bf16[32,1024]{1,0:T(8,128)(2,1)S(1)}, u32[]{:S(2)}, u32[]{:S(2)}) collective-permute-start(bf16[32,1024]{1,0:T(8,128)(2,1)S(1)} %get-tuple-element.46), channel_id=1, source_target_pairs={{0,24},{2,26},{4,28},{6,30},{8,0},{10,2},{12,4},{14,6},{16,8},{18,... | collective-permute-start | bytes 196616 | tf_op jit(solution)/shard_map/ppermute | solution.py:216
  35.1 5.7 %collective-permute-start.12 = (bf16[32,1024]{1,0:T(8,128)(2,1)S(1)}, bf16[32,1024]{1,0:T(8,128)(2,1)S(1)}, u32[]{:S(2)}, u32[]{:S(2)}) collective-permute-start(bf16[32,1024]{1,0:T(8,128)(2,1)S(1)} %get-tuple-element.47), channel_id=1, source_target_pairs={{0,26},{2,28},{4,30},{6,0},{8,2},{10,4},{12,6},{14,8},{16,10},{18,... | collective-permute-start | bytes 196616 | tf_op jit(solution)/shard_map/ppermute | solution.py:216
  35.6 5.4 %collective-permute-start.13 = (bf16[32,1024]{1,0:T(8,128)(2,1)S(1)}, bf16[32,1024]{1,0:T(8,128)(2,1)S(1)}, u32[]{:S(2)}, u32[]{:S(2)}) collective-permute-start(bf16[32,1024]{1,0:T(8,128)(2,1)S(1)} %get-tuple-element.48), channel_id=1, source_target_pairs={{0,28},{2,30},{4,0},{6,2},{8,4},{10,6},{12,8},{14,10},{16,12},{18,... | collective-permute-start | bytes 196616 | tf_op jit(solution)/shard_map/ppermute | solution.py:216
  38.1 4.7 %collective-permute-start.14 = (bf16[32,1024]{1,0:T(8,128)(2,1)S(1)}, bf16[32,1024]{1,0:T(8,128)(2,1)S(1)}, u32[]{:S(2)}, u32[]{:S(2)}) collective-permute-start(bf16[32,1024]{1,0:T(8,128)(2,1)S(1)} %get-tuple-element.49), channel_id=1, source_target_pairs={{0,30},{2,0},{4,2},{6,4},{8,6},{10,8},{12,10},{14,12},{16,14},{18,... | collective-permute-start | bytes 196616 | tf_op jit(solution)/shard_map/ppermute | solution.py:216
  38.1 4.7 %collective-permute-start.15 = (bf16[32,1024]{1,0:T(8,128)(2,1)S(1)}, bf16[32,1024]{1,0:T(8,128)(2,1)S(1)}, u32[]{:S(2)}, u32[]{:S(2)}) collective-permute-start(bf16[32,1024]{1,0:T(8,128)(2,1)S(1)} %get-tuple-element.34.refs_0_), channel_id=1, source_target_pairs={{0,1},{1,0},{2,3},{3,2},{4,5},{5,4},{6,7},{7,6},{8,9},{9,8},{10,11... | collective-permute-start | bytes 196616 | tf_op jit(solution)/shard_map/ppermute | solution.py:216
  38.2 5.1 %collective-permute-start.16 = (bf16[32,1024]{1,0:T(8,128)(2,1)S(1)}, bf16[32,1024]{1,0:T(8,128)(2,1)S(1)}, u32[]{:S(2)}, u32[]{:S(2)}) collective-permute-start(bf16[32,1024]{1,0:T(8,128)(2,1)S(1)} %collective-permute-done.refs_1_), channel_id=1, source_target_pairs={{0,1},{1,0},{2,3},{3,2},{4,5},{5,4},{6,7},{7,6},{8,9},{9,8},{10,11... | collective-permute-start | bytes 196616 | tf_op jit(solution)/shard_map/ppermute | solution.py:216
  40.8 2.6 %collective-permute-start.17 = (bf16[32,1024]{1,0:T(8,128)(2,1)S(1)}, bf16[32,1024]{1,0:T(8,128)(2,1)S(1)}, u32[]{:S(2)}, u32[]{:S(2)}) collective-permute-start(bf16[32,1024]{1,0:T(8,128)(2,1)S(1)} %collective-permute-done.1.refs_2_), channel_id=1, source_target_pairs={{0,1},{1,0},{2,3},{3,2},{4,5},{5,4},{6,7},{7,6},{8,9},{9,8},{10,11... | collective-permute-start | bytes 196616 | tf_op jit(solution)/shard_map/ppermute | solution.py:216
  41.0 2.8 %collective-permute-start.18 = (bf16[32,1024]{1,0:T(8,128)(2,1)S(1)}, bf16[32,1024]{1,0:T(8,128)(2,1)S(1)}, u32[]{:S(2)}, u32[]{:S(2)}) collective-permute-start(bf16[32,1024]{1,0:T(8,128)(2,1)S(1)} %collective-permute-done.2.refs_3_), channel_id=1, source_target_pairs={{0,1},{1,0},{2,3},{3,2},{4,5},{5,4},{6,7},{7,6},{8,9},{9,8},{10,11... | collective-permute-start | bytes 196616 | tf_op jit(solution)/shard_map/ppermute | solution.py:216
  42.8 1.5 %collective-permute-start.20 = (bf16[32,1024]{1,0:T(8,128)(2,1)S(1)}, bf16[32,1024]{1,0:T(8,128)(2,1)S(1)}, u32[]{:S(2)}, u32[]{:S(2)}) collective-permute-start(bf16[32,1024]{1,0:T(8,128)(2,1)S(1)} %collective-permute-done.4.refs_5_), channel_id=1, source_target_pairs={{0,1},{1,0},{2,3},{3,2},{4,5},{5,4},{6,7},{7,6},{8,9},{9,8},{10,11... | collective-permute-start | bytes 196616 | tf_op jit(solution)/shard_map/ppermute | solution.py:216
  43.4 1.5 %collective-permute-start.22 = (bf16[32,1024]{1,0:T(8,128)(2,1)S(1)}, bf16[32,1024]{1,0:T(8,128)(2,1)S(1)}, u32[]{:S(2)}, u32[]{:S(2)}) collective-permute-start(bf16[32,1024]{1,0:T(8,128)(2,1)S(1)} %collective-permute-done.6.refs_7_), channel_id=1, source_target_pairs={{0,1},{1,0},{2,3},{3,2},{4,5},{5,4},{6,7},{7,6},{8,9},{9,8},{10,11... | collective-permute-start | bytes 196616 | tf_op jit(solution)/shard_map/ppermute | solution.py:216
  44.0 1.3 %collective-permute-start.24 = (bf16[32,1024]{1,0:T(8,128)(2,1)S(1)}, bf16[32,1024]{1,0:T(8,128)(2,1)S(1)}, u32[]{:S(2)}, u32[]{:S(2)}) collective-permute-start(bf16[32,1024]{1,0:T(8,128)(2,1)S(1)} %collective-permute-done.8.refs_9_), channel_id=1, source_target_pairs={{0,1},{1,0},{2,3},{3,2},{4,5},{5,4},{6,7},{7,6},{8,9},{9,8},{10,11... | collective-permute-start | bytes 196616 | tf_op jit(solution)/shard_map/ppermute | solution.py:216
  65.7 8.5 %collective-permute-start.31 = (bf16[32,1024]{1,0:T(8,128)(2,1)S(1)}, bf16[32,1024]{1,0:T(8,128)(2,1)S(1)}, u32[]{:S(2)}, u32[]{:S(2)}) collective-permute-start(bf16[32,1024]{1,0:T(8,128)(2,1)S(1)} %get-tuple-element.51), channel_id=1, source_target_pairs={{0,30},{2,0},{4,2},{6,4},{8,6},{10,8},{12,10},{14,12},{16,14},{18,... | collective-permute-start | bytes 196616 | tf_op jit(solution)/shard_map/ppermute | solution.py:216
  69.6 9.9 %collective-permute-start.32 = (bf16[32,1024]{1,0:T(8,128)(2,1)S(1)}, bf16[32,1024]{1,0:T(8,128)(2,1)S(1)}, u32[]{:S(2)}, u32[]{:S(2)}) collective-permute-start(bf16[32,1024]{1,0:T(8,128)(2,1)S(1)} %get-tuple-element.52), channel_id=1, source_target_pairs={{0,28},{2,30},{4,0},{6,2},{8,4},{10,6},{12,8},{14,10},{16,12},{18,... | collective-permute-start | bytes 196616 | tf_op jit(solution)/shard_map/ppermute | solution.py:216
  69.6 9.9 %collective-permute-start.33 = (bf16[32,1024]{1,0:T(8,128)(2,1)S(1)}, bf16[32,1024]{1,0:T(8,128)(2,1)S(1)}, u32[]{:S(2)}, u32[]{:S(2)}) collective-permute-start(bf16[32,1024]{1,0:T(8,128)(2,1)S(1)} %get-tuple-element.53), channel_id=1, source_target_pairs={{0,26},{2,28},{4,30},{6,0},{8,2},{10,4},{12,6},{14,8},{16,10},{18,... | collective-permute-start | bytes 196616 | tf_op jit(solution)/shard_map/ppermute | solution.py:216
  72.8 8.1 %collective-permute-start.34 = (bf16[32,1024]{1,0:T(8,128)(2,1)S(1)}, bf16[32,1024]{1,0:T(8,128)(2,1)S(1)}, u32[]{:S(2)}, u32[]{:S(2)}) collective-permute-start(bf16[32,1024]{1,0:T(8,128)(2,1)S(1)} %get-tuple-element.54), channel_id=1, source_target_pairs={{0,24},{2,26},{4,28},{6,30},{8,0},{10,2},{12,4},{14,6},{16,8},{18,... | collective-permute-start | bytes 196616 | tf_op jit(solution)/shard_map/ppermute | solution.py:216
  73.3 10.1 %collective-permute-start.35 = (bf16[32,1024]{1,0:T(8,128)(2,1)S(1)}, bf16[32,1024]{1,0:T(8,128)(2,1)S(1)}, u32[]{:S(2)}, u32[]{:S(2)}) collective-permute-start(bf16[32,1024]{1,0:T(8,128)(2,1)S(1)} %get-tuple-element.55), channel_id=1, source_target_pairs={{0,22},{2,24},{4,26},{6,28},{8,30},{10,0},{12,2},{14,4},{16,6},{18... | collective-permute-start | bytes 196616 | tf_op jit(solution)/shard_map/ppermute | solution.py:216
  74.2 11.6 %collective-permute-start.36 = (bf16[32,1024]{1,0:T(8,128)(2,1)S(1)}, bf16[32,1024]{1,0:T(8,128)(2,1)S(1)}, u32[]{:S(2)}, u32[]{:S(2)}) collective-permute-start(bf16[32,1024]{1,0:T(8,128)(2,1)S(1)} %get-tuple-element.56), channel_id=1, source_target_pairs={{0,20},{2,22},{4,24},{6,26},{8,28},{10,30},{12,0},{14,2},{16,4},{1... | collective-permute-start | bytes 196616 | tf_op jit(solution)/shard_map/ppermute | solution.py:216
  79.5 8.3 %collective-permute-start.37 = (bf16[32,1024]{1,0:T(8,128)(2,1)S(1)}, bf16[32,1024]{1,0:T(8,128)(2,1)S(1)}, u32[]{:S(2)}, u32[]{:S(2)}) collective-permute-start(bf16[32,1024]{1,0:T(8,128)(2,1)S(1)} %get-tuple-element.57), channel_id=1, source_target_pairs={{0,18},{2,20},{4,22},{6,24},{8,26},{10,28},{12,30},{14,0},{16,2},{... | collective-permute-start | bytes 196616 | tf_op jit(solution)/shard_map/ppermute | solution.py:216
  79.5 15.6 %collective-permute-start.38 = (bf16[32,1024]{1,0:T(8,128)(2,1)S(1)}, bf16[32,1024]{1,0:T(8,128)(2,1)S(1)}, u32[]{:S(2)}, u32[]{:S(2)}) collective-permute-start(bf16[32,1024]{1,0:T(8,128)(2,1)S(1)} %get-tuple-element.58), channel_id=1, source_target_pairs={{0,16},{2,18},{4,20},{6,22},{8,24},{10,26},{12,28},{14,30},{16,0},... | collective-permute-start | bytes 196616 | tf_op jit(solution)/shard_map/ppermute | solution.py:216
  80.9 14.2 %collective-permute-start.39 = (bf16[32,1024]{1,0:T(8,128)(2,1)S(1)}, bf16[32,1024]{1,0:T(8,128)(2,1)S(1)}, u32[]{:S(2)}, u32[]{:S(2)}) collective-permute-start(bf16[32,1024]{1,0:T(8,128)(2,1)S(1)} %get-tuple-element.59), channel_id=1, source_target_pairs={{0,14},{2,16},{4,18},{6,20},{8,22},{10,24},{12,26},{14,28},{16,30}... | collective-permute-start | bytes 196616 | tf_op jit(solution)/shard_map/ppermute | solution.py:216
  83.4 11.7 %collective-permute-start.40 = (bf16[32,1024]{1,0:T(8,128)(2,1)S(1)}, bf16[32,1024]{1,0:T(8,128)(2,1)S(1)}, u32[]{:S(2)}, u32[]{:S(2)}) collective-permute-start(bf16[32,1024]{1,0:T(8,128)(2,1)S(1)} %get-tuple-element.60), channel_id=1, source_target_pairs={{0,12},{2,14},{4,16},{6,18},{8,20},{10,22},{12,24},{14,26},{16,28}... | collective-permute-start | bytes 196616 | tf_op jit(solution)/shard_map/ppermute | solution.py:216
  85.7 11.6 %collective-permute-start.41 = (bf16[32,1024]{1,0:T(8,128)(2,1)S(1)}, bf16[32,1024]{1,0:T(8,128)(2,1)S(1)}, u32[]{:S(2)}, u32[]{:S(2)}) collective-permute-start(bf16[32,1024]{1,0:T(8,128)(2,1)S(1)} %get-tuple-element.61), channel_id=1, source_target_pairs={{0,10},{2,12},{4,14},{6,16},{8,18},{10,20},{12,22},{14,24},{16,26}... | collective-permute-start | bytes 196616 | tf_op jit(solution)/shard_map/ppermute | solution.py:216
  87.8 9.5 %collective-permute-start.42 = (bf16[32,1024]{1,0:T(8,128)(2,1)S(1)}, bf16[32,1024]{1,0:T(8,128)(2,1)S(1)}, u32[]{:S(2)}, u32[]{:S(2)}) collective-permute-start(bf16[32,1024]{1,0:T(8,128)(2,1)S(1)} %get-tuple-element.62), channel_id=1, source_target_pairs={{0,8},{2,10},{4,12},{6,14},{8,16},{10,18},{12,20},{14,22},{16,24},... | collective-permute-start | bytes 196616 | tf_op jit(solution)/shard_map/ppermute | solution.py:216
  95.1 7.3 %collective-permute-start.43 = (bf16[32,1024]{1,0:T(8,128)(2,1)S(1)}, bf16[32,1024]{1,0:T(8,128)(2,1)S(1)}, u32[]{:S(2)}, u32[]{:S(2)}) collective-permute-start(bf16[32,1024]{1,0:T(8,128)(2,1)S(1)} %get-tuple-element.63), channel_id=1, source_target_pairs={{0,6},{2,8},{4,10},{6,12},{8,14},{10,16},{12,18},{14,20},{16,22},{... | collective-permute-start | bytes 196616 | tf_op jit(solution)/shard_map/ppermute | solution.py:216
  95.1 7.9 %collective-permute-start.44 = (bf16[32,1024]{1,0:T(8,128)(2,1)S(1)}, bf16[32,1024]{1,0:T(8,128)(2,1)S(1)}, u32[]{:S(2)}, u32[]{:S(2)}) collective-permute-start(bf16[32,1024]{1,0:T(8,128)(2,1)S(1)} %get-tuple-element.64), channel_id=1, source_target_pairs={{0,4},{2,6},{4,8},{6,10},{8,12},{10,14},{12,16},{14,18},{16,20},{1... | collective-permute-start | bytes 196616 | tf_op jit(solution)/shard_map/ppermute | solution.py:216
  95.2 9.2 %collective-permute-start.45 = (bf16[32,1024]{1,0:T(8,128)(2,1)S(1)}, bf16[32,1024]{1,0:T(8,128)(2,1)S(1)}, u32[]{:S(2)}, u32[]{:S(2)}) collective-permute-start(bf16[32,1024]{1,0:T(8,128)(2,1)S(1)} %get-tuple-element.65), channel_id=1, source_target_pairs={{0,2},{2,4},{4,6},{6,8},{8,10},{10,12},{12,14},{14,16},{16,18},{18... | collective-permute-start | bytes 196616 | tf_op jit(solution)/shard_map/ppermute | solution.py:216
  97.3 7.0 %collective-permute-start.46 = (bf16[32,1024]{1,0:T(8,128)(2,1)S(1)}, bf16[32,1024]{1,0:T(8,128)(2,1)S(1)}, u32[]{:S(2)}, u32[]{:S(2)}) collective-permute-start(bf16[32,1024]{1,0:T(8,128)(2,1)S(1)} %get-tuple-element.50.refs_0_), channel_id=1, source_target_pairs={{0,1},{1,0},{2,3},{3,2},{4,5},{5,4},{6,7},{7,6},{8,9},{9,8},{10,11... | collective-permute-start | bytes 196616 | tf_op jit(solution)/shard_map/ppermute | solution.py:216
  97.3 7.5 %collective-permute-start.47 = (bf16[32,1024]{1,0:T(8,128)(2,1)S(1)}, bf16[32,1024]{1,0:T(8,128)(2,1)S(1)}, u32[]{:S(2)}, u32[]{:S(2)}) collective-permute-start(bf16[32,1024]{1,0:T(8,128)(2,1)S(1)} %collective-permute-done.31.refs_1_), channel_id=1, source_target_pairs={{0,1},{1,0},{2,3},{3,2},{4,5},{5,4},{6,7},{7,6},{8,9},{9,8},{10,11... | collective-permute-start | bytes 196616 | tf_op jit(solution)/shard_map/ppermute | solution.py:216
  102.4 2.5 %collective-permute-start.48 = (bf16[32,1024]{1,0:T(8,128)(2,1)S(1)}, bf16[32,1024]{1,0:T(8,128)(2,1)S(1)}, u32[]{:S(2)}, u32[]{:S(2)}) collective-permute-start(bf16[32,1024]{1,0:T(8,128)(2,1)S(1)} %collective-permute-done.32.refs_2_), channel_id=1, source_target_pairs={{0,1},{1,0},{2,3},{3,2},{4,5},{5,4},{6,7},{7,6},{8,9},{9,8},{10,11... | collective-permute-start | bytes 196616 | tf_op jit(solution)/shard_map/ppermute | solution.py:216
  103.0 2.4 %collective-permute-start.49 = (bf16[32,1024]{1,0:T(8,128)(2,1)S(1)}, bf16[32,1024]{1,0:T(8,128)(2,1)S(1)}, u32[]{:S(2)}, u32[]{:S(2)}) collective-permute-start(bf16[32,1024]{1,0:T(8,128)(2,1)S(1)} %collective-permute-done.33.refs_3_), channel_id=1, source_target_pairs={{0,1},{1,0},{2,3},{3,2},{4,5},{5,4},{6,7},{7,6},{8,9},{9,8},{10,11... | collective-permute-start | bytes 196616 | tf_op jit(solution)/shard_map/ppermute | solution.py:216
  104.3 1.5 %collective-permute-start.51 = (bf16[32,1024]{1,0:T(8,128)(2,1)S(1)}, bf16[32,1024]{1,0:T(8,128)(2,1)S(1)}, u32[]{:S(2)}, u32[]{:S(2)}) collective-permute-start(bf16[32,1024]{1,0:T(8,128)(2,1)S(1)} %collective-permute-done.35.refs_5_), channel_id=1, source_target_pairs={{0,1},{1,0},{2,3},{3,2},{4,5},{5,4},{6,7},{7,6},{8,9},{9,8},{10,11... | collective-permute-start | bytes 196616 | tf_op jit(solution)/shard_map/ppermute | solution.py:216
  104.9 1.5 %collective-permute-start.53 = (bf16[32,1024]{1,0:T(8,128)(2,1)S(1)}, bf16[32,1024]{1,0:T(8,128)(2,1)S(1)}, u32[]{:S(2)}, u32[]{:S(2)}) collective-permute-start(bf16[32,1024]{1,0:T(8,128)(2,1)S(1)} %collective-permute-done.37.refs_7_), channel_id=1, source_target_pairs={{0,1},{1,0},{2,3},{3,2},{4,5},{5,4},{6,7},{7,6},{8,9},{9,8},{10,11... | collective-permute-start | bytes 196616 | tf_op jit(solution)/shard_map/ppermute | solution.py:216
  106.1 7.6 %collective-permute-start.57 = (bf16[32,1024]{1,0:T(8,128)(2,1)S(1)}, bf16[32,1024]{1,0:T(8,128)(2,1)S(1)}, u32[]{:S(2)}, u32[]{:S(2)}) collective-permute-start(bf16[32,1024]{1,0:T(8,128)(2,1)S(1)} %collective-permute-done.41.refs_11_), channel_id=1, source_target_pairs={{0,1},{1,0},{2,3},{3,2},{4,5},{5,4},{6,7},{7,6},{8,9},{9,8},{10,11... | collective-permute-start | bytes 196616 | tf_op jit(solution)/shard_map/ppermute | solution.py:216
  106.4 7.3 %collective-permute-start.58 = (bf16[32,1024]{1,0:T(8,128)(2,1)S(1)}, bf16[32,1024]{1,0:T(8,128)(2,1)S(1)}, u32[]{:S(2)}, u32[]{:S(2)}) collective-permute-start(bf16[32,1024]{1,0:T(8,128)(2,1)S(1)} %collective-permute-done.42.refs_12_), channel_id=1, source_target_pairs={{0,1},{1,0},{2,3},{3,2},{4,5},{5,4},{6,7},{7,6},{8,9},{9,8},{10,11... | collective-permute-start | bytes 196616 | tf_op jit(solution)/shard_map/ppermute | solution.py:216
  106.6 7.1 %collective-permute-start.59 = (bf16[32,1024]{1,0:T(8,128)(2,1)S(1)}, bf16[32,1024]{1,0:T(8,128)(2,1)S(1)}, u32[]{:S(2)}, u32[]{:S(2)}) collective-permute-start(bf16[32,1024]{1,0:T(8,128)(2,1)S(1)} %collective-permute-done.43.refs_13_), channel_id=1, source_target_pairs={{0,1},{1,0},{2,3},{3,2},{4,5},{5,4},{6,7},{7,6},{8,9},{9,8},{10,11... | collective-permute-start | bytes 196616 | tf_op jit(solution)/shard_map/ppermute | solution.py:216
  106.9 6.8 %collective-permute-start.60 = (bf16[32,1024]{1,0:T(8,128)(2,1)S(1)}, bf16[32,1024]{1,0:T(8,128)(2,1)S(1)}, u32[]{:S(2)}, u32[]{:S(2)}) collective-permute-start(bf16[32,1024]{1,0:T(8,128)(2,1)S(1)} %collective-permute-done.44.refs_14_), channel_id=1, source_target_pairs={{0,1},{1,0},{2,3},{3,2},{4,5},{5,4},{6,7},{7,6},{8,9},{9,8},{10,11... | collective-permute-start | bytes 196616 | tf_op jit(solution)/shard_map/ppermute | solution.py:216
  107.1 6.6 %collective-permute-start.61 = (bf16[32,1024]{1,0:T(8,128)(2,1)S(1)}, bf16[32,1024]{1,0:T(8,128)(2,1)S(1)}, u32[]{:S(2)}, u32[]{:S(2)}) collective-permute-start(bf16[32,1024]{1,0:T(8,128)(2,1)S(1)} %collective-permute-done.45.refs_15_), channel_id=1, source_target_pairs={{0,1},{1,0},{2,3},{3,2},{4,5},{5,4},{6,7},{7,6},{8,9},{9,8},{10,11... | collective-permute-start | bytes 196616 | tf_op jit(solution)/shard_map/ppermute | solution.py:216
  (16 other events, 20.9 us)

commit v2 on v0

v2 whole, which is shorter than its diff:
```python
import functools

import jax
import jax.numpy as jnp
from jax import lax
from jax.experimental import pallas as pl
from jax.experimental.pallas import tpu as pltpu
from jax.sharding import PartitionSpec as P

ITERS = 5

coef_a = 3.4445
coef_b = -4.775
coef_c = 2.0315

BF = jnp.bfloat16
F32 = jnp.float32


def next_momentum(m, g):
    return (0.95 * m.astype(F32) + g.astype(F32)).astype(BF)


def blend(m, g):
    return (g.astype(F32) + 0.95 * next_momentum(m, g).astype(F32)).astype(BF)


def share_kernel(rep_ref, m_hbm, g_hbm, share_ref, m_ref, g_ref, sems):
    experts, height, _ = share_ref.shape
    chunks = sems.shape[1]
    step = experts // chunks
    rows = pl.ds(pl.multiple_of(rep_ref[0] * height, height), height)
    copies = []
    for i in range(chunks):
        at = pl.ds(i * step, step)
        copies.append(
            [
                pltpu.make_async_copy(src.at[at, rows], dst.at[at], sems.at[j, i])
                for j, (src, dst) in enumerate(((m_hbm, m_ref), (g_hbm, g_ref)))
            ]
        )
        for copy in copies[-1]:
            copy.start()
    for i in range(chunks):
        for copy in copies[i]:
            copy.wait()
        at = slice(i * step, (i + 1) * step)
        share_ref[at] = blend(m_ref[at], g_ref[at])


def blended_share(rep, momentum, gradient, n_rep):
    experts, rows, cols = momentum.shape
    height = rows // n_rep
    shape = (experts, height, cols)
    if height % 16:
        m, g = (
            lax.dynamic_slice_in_dim(x, rep * height, height, 1) for x in (momentum, gradient)
        )
        return blend(m, g)
    chunks = 4 if experts % 4 == 0 else 1
    hbm = pl.BlockSpec(memory_space=pltpu.HBM)
    return pl.pallas_call(
        share_kernel,
        in_specs=[pl.BlockSpec(memory_space=pltpu.SMEM), hbm, hbm],
        out_specs=pl.BlockSpec(memory_space=pltpu.VMEM),
        out_shape=jax.ShapeDtypeStruct(shape, BF),
        scratch_shapes=[
            pltpu.VMEM(shape, BF),
            pltpu.VMEM(shape, BF),
            pltpu.SemaphoreType.DMA((2, chunks)),
        ],
        compiler_params=pltpu.CompilerParams(vmem_limit_bytes=16 * 2**20),
        name="share",
    )(rep[None], momentum, gradient)


def momentum_kernel(m_ref, g_ref, new_ref):
    def one(e, carry):
        new_ref[e] = next_momentum(m_ref[e], g_ref[e])
        return carry

    lax.fori_loop(0, m_ref.shape[0], one, 0)


def new_momentum_of(momentum, gradient):
    vmem = pl.BlockSpec(memory_space=pltpu.VMEM)
    return pl.pallas_call(
        momentum_kernel,
        in_specs=[vmem, vmem],
        out_specs=vmem,
        out_shape=jax.ShapeDtypeStruct(momentum.shape, BF),
        cost_estimate=pl.CostEstimate(
            flops=2 * momentum.size, bytes_accessed=6 * momentum.size, transcendentals=0
        ),
        compiler_params=pltpu.CompilerParams(vmem_limit_bytes=16 * 2**20),
        name="new_momentum",
    )(momentum, gradient)


def halves(x):
    high = x.astype(BF)
    return high, (x - high.astype(F32)).astype(BF)


def put_left(ref, x):
    rows, n = x.shape
    high, low = halves(x)
    ref[:rows, :n] = high
    ref[:rows, n : 2 * n] = high
    ref[:rows, 2 * n :] = low


def put_right(ref, x):
    n = x.shape[0]
    high, low = halves(x)
    ref[:n] = high
    ref[n : 2 * n] = low
    ref[2 * n :] = high


def dot(x, y):
    return jnp.dot(x, y, preferred_element_type=F32)


def dot_transposed(x, y):
    return lax.dot_general(x, y, (((1,), (1,)), ((), ())), preferred_element_type=F32)


def put_symmetric(ref, upper, corner):
    half = corner.shape[0]
    ref[:half] = upper
    ref[half:, half:] = corner
    ref[half:, :half] = upper[:, half:].T


def orthogonal_kernel(scale, *refs):
    *parts, out_ref, x_ref, a_ref, s_ref, y_ref, q_ref, left, right = refs
    height = out_ref.shape[0]
    n = x_ref.shape[0]
    half = n // 2
    for i, part in enumerate(parts):
        x_ref[i * height : (i + 1) * height] = part[...]

    put_symmetric(
        y_ref,
        dot_transposed(x_ref[:half], x_ref[...]),
        dot_transposed(x_ref[half:], x_ref[half:]),
    )
    eye = lax.broadcasted_iota(jnp.int32, (n, n), 0) == lax.broadcasted_iota(
        jnp.int32, (n, n), 1
    )
    square = jnp.sum(jnp.where(eye, y_ref[...], 0.0), keepdims=True)
    inverse = 1.0 / (jnp.sqrt(square) + 1e-07)
    a_ref[...] = y_ref[...] * (inverse * inverse)

    def multiply(ref):
        put_symmetric(
            ref, dot(left[:half], right[...]), dot(left[half:], right[:, half:])
        )

    def middle():
        a = a_ref[...]
        put_left(left, a)
        put_right(right, a)
        multiply(y_ref)
        m = coef_b * a + coef_c * y_ref[...]
        put_right(right, m)
        return m

    def advance():
        multiply(y_ref)
        s = coef_a * a_ref[...] + y_ref[...]
        s_ref[...] = s
        put_left(left, s)
        multiply(y_ref)
        a_ref[...] = coef_a * s_ref[...] + y_ref[...]

    def extend():
        put_left(left, q_ref[...])
        return coef_a * q_ref[...] + dot(left[:height], right[...])

    q_ref[...] = jnp.where(eye[:height], coef_a, 0.0) + middle()[:height]
    advance()

    def step(_, carry):
        middle()
        advance()
        q_ref[...] = extend()
        return carry

    lax.fori_loop(1, ITERS - 1, step, 0)
    middle()
    high, low = halves(extend() * (inverse * scale))
    left[:height, :n] = high
    left[:height, n : 2 * n] = low
    width = out_ref.shape[1]
    block = min(width, 512)
    for at in range(0, width, block):
        x = x_ref[:, at : at + block]
        out_ref[:, at : at + block] = (
            dot(left[:height, :n], x) + dot(left[:height, n : 2 * n], x)
        ).astype(BF)


def orthogonal(parts, scale):
    height, cols = parts[0].shape
    n = height * len(parts)
    vmem = pl.BlockSpec(memory_space=pltpu.VMEM)
    return pl.pallas_call(
        functools.partial(orthogonal_kernel, scale),
        in_specs=[vmem] * len(parts),
        out_specs=vmem,
        out_shape=jax.ShapeDtypeStruct((height, cols), BF),
        scratch_shapes=[
            pltpu.VMEM((n, cols), BF),
            pltpu.VMEM((n, n), F32),
            pltpu.VMEM((n, n), F32),
            pltpu.VMEM((n, n), F32),
            pltpu.VMEM((height, n), F32),
            pltpu.VMEM((n, 3 * n), BF),
            pltpu.VMEM((3 * n, n), BF),
        ],
        compiler_params=pltpu.CompilerParams(vmem_limit_bytes=40 * 2**20),
        name="orthogonal",
    )(*parts)


def place_kernel(rep_ref, part_ref, *refs):
    *_, out_ref, sem = refs
    height = part_ref.shape[1]
    rows = pl.ds(pl.multiple_of(rep_ref[0] * height, height), height)
    copy = pltpu.make_async_copy(part_ref, out_ref.at[:, rows], sem)
    copy.start()
    copy.wait()


def place(which, part, whole):
    experts, height, cols = part.shape
    if height % 16:
        if isinstance(whole, tuple):
            whole = jnp.zeros(whole, BF)
        return lax.dynamic_update_slice(whole, part, (0, which * height, 0))
    anywhere = pl.BlockSpec(memory_space=pl.ANY)
    hbm = pl.BlockSpec(memory_space=pltpu.HBM)
    first = isinstance(whole, tuple)
    return pl.pallas_call(
        place_kernel,
        in_specs=[pl.BlockSpec(memory_space=pltpu.SMEM), anywhere] + [hbm] * (not first),
        out_specs=hbm,
        out_shape=jax.ShapeDtypeStruct(whole if first else whole.shape, BF),
        scratch_shapes=[pltpu.SemaphoreType.DMA(())],
        input_output_aliases={} if first else {2: 0},
        cost_estimate=pl.CostEstimate(
            flops=0, bytes_accessed=4 * part.size, transcendentals=0
        ),
        compiler_params=pltpu.CompilerParams(vmem_limit_bytes=4 * 2**20),
        name="place",
    )(which[None], part, *([] if first else [whole]))


def solution(mesh):
    n_rep = mesh.shape["rep"]

    def others(x):
        return [
            lax.ppermute(x, "rep", [((i + j) % n_rep, i) for i in range(n_rep)])
            for j in range(1, n_rep)
        ]

    def exchange(x):
        return lax.all_to_all(x, "shard", split_axis=0, concat_axis=0, tiled=True)

    def shards(momentum, gradient):
        experts, rows, cols = momentum.shape
        rep = lax.axis_index("rep")
        share = exchange(blended_share(rep, momentum, gradient, n_rep))
        own = share.reshape(-1, cols)
        rest = others(own)
        momentum, gradient, own = lax.optimization_barrier((momentum, gradient, own))
        new_momentum = new_momentum_of(momentum, gradient)
        rest, new_momentum = lax.optimization_barrier((rest, new_momentum))
        scale = float(max(experts * rows, cols)) ** 0.5
        update = exchange(orthogonal([own, *rest], scale).reshape(share.shape))
        whole = (experts, rows, cols)
        for j, part in enumerate([update, *others(update)]):
            whole = place(lax.rem(rep + j, n_rep), part, whole)
        return new_momentum, whole

    return jax.shard_map(
        shards,
        mesh=mesh,
        in_specs=(P(None, "shard", None), P(None, "shard", None)),
        out_specs=(P(None, "shard", None), P(None, "shard", None)),
        check_vma=False,
    )
```

time: 98.2 us -> 91.4 us (0.931)
  Pallas kernels: 25.4 us -> 20.1 us
  waiting for transfers between devices: 4.94 us -> 2.32 us
  local copies, waits for them, and re-layouts: 1.78 us -> 3.17 us
    pallas_call x1, Pallas kernels: 18.8 us -> 15.4 us  [orthogonal(): pl.pallas_call(functools.partial(orthogonal_kernel, scale), in_specs=[vme...]
    ppermute x2, waiting for transfers between devices: 4.94 us -> 2.32 us  [others(): lax.ppermute(x, 'rep', [((i + j) % n_rep, i) for i in range(n_rep)])]
    pallas_call x1 -> x4, Pallas kernels: 6.63 us -> 4.74 us  [the longest x1 2 us: new_momentum_of(): pl.pallas_call(momentum_kernel, in_specs=[vmem, vmem], out_specs=vmem, ou...]
    unnamed x2 -> x4, local copies, waits for them, and re-layouts: 1.32 us -> 3.17 us
  transfers between devices with their start and end apart: 2 -> 2, of which waited for: 2 -> 2; matrix products, arithmetic and copies ran while one was open for 0% -> 0% of each run, Pallas kernels for 0% -> 3%
where the time goes in v2:
time: 91.4 us; the launch traced here: 91.1 us
  blocking collectives  64.8 us (71%)
  Pallas kernels  20.1 us (22%)
  local copies, waits for them, and re-layouts  3.17 us (3%)
  waiting for transfers between devices  2.32 us (3%)
    all_to_all x2, blocking collectives, exchange(): return lax.all_to_all(x, 'shard', split_axis=0, concat_axis=0, tiled=True)  64.8 us
    pallas_call x1, Pallas kernels, orthogonal(): pl.pallas_call(functools.partial(orthogonal_kernel, scale), in_specs=[vme...  15.4 us
    unnamed x4, local copies, waits for them, and re-layouts  3.17 us
    ppermute x2, waiting for transfers between devices, others(): lax.ppermute(x, 'rep', [((i + j) % n_rep, i) for i in range(n_rep)])  2.32 us
    pallas_call x1, Pallas kernels, new_momentum_of(): pl.pallas_call(momentum_kernel, in_specs=[vmem, vmem], out_specs=vmem, ou...  2 us
    pallas_call x2, Pallas kernels, place(): pl.pallas_call(place_kernel, in_specs=[pl.BlockSpec(memory_space=pltpu.SM...  1.96 us
  transfers between devices with their start and end apart: 2, of which 2 were waited for; matrix products, arithmetic and copies ran while one was open for 0% of the time, Pallas kernels for 3%

profile of v2, /device:TPU:0, one launch (start us, length us, event | category | flops | bytes accessed | tf_op | source)
XLA Modules:
  0.0 91.1 jit_solution(16429053374527268713)
XLA Ops:
  0.6 0.0 copy-start
  0.6 1.6 %copy-done = bf16[16,32,2048]{2,1,0:T(8,128)(2,1)S(1)} copy-done((bf16[16,32,2048]{2,1,0:T(8,128)(2,1)S(1)}, bf16[16,32,2048]{2,1,0:T(8,128)(2,1)}, u32[]{:S(2)}) %copy-start) | copy-done | bytes 2097176
  2.2 0.0 copy-start.1
  2.2 1.6 %copy-done.1 = bf16[16,32,2048]{2,1,0:T(8,128)(2,1)S(1)} copy-done((bf16[16,32,2048]{2,1,0:T(8,128)(2,1)S(1)}, bf16[16,32,2048]{2,1,0:T(8,128)(2,1)}, u32[]{:S(2)}) %copy-start.1) | copy-done | bytes 2097176
  3.8 0.8 share.1
  4.6 34.5 %all_to_all.10 = bf16[16,16,2048]{2,1,0:T(8,128)(2,1)S(1)} all-to-all(bf16[16,16,2048]{2,1,0:T(8,128)(2,1)S(1)} %share.1), channel_id=1, replica_groups=mesh['shard'=16,'rep'=2] {'shard'}, dimensions={0} | all-to-all | bytes 2097152 | tf_op jit(solution)/shard_map/all_to_all | solution.py:271
  39.1 0.0 collective-permute-start
  39.1 2.0 %new_momentum.1 = bf16[16,32,2048]{2,1,0:T(8,128)(2,1)} custom-call(bf16[16,32,2048]{2,1,0:T(8,128)(2,1)S(1)} %copy-done, bf16[16,32,2048]{2,1,0:T(8,128)(2,1)S(1)} %copy-done.1), custom_call_target="tpu_custom_call" | custom-call | flops 2097152 | bytes 6291456 | tf_op jit(solution)/shard_map/new_momentum/pallas_call | solution.py:87
  41.1 0.7 collective-permute-done.refs_1_
  41.7 15.4 %orthogonal.1 = bf16[256,2048]{1,0:T(8,128)(2,1)S(1)} custom-call(bf16[256,2048]{1,0:T(8,128)(2,1)S(1)} %bitcast.6, bf16[256,2048]{1,0:T(8,128)(2,1)S(1)} %collective-permute-done.refs_1_), custom_call_target="tpu_custom_call" | custom-call | tf_op jit(solution)/shard_map/orthogonal/pallas_call | solution.py:209
  57.2 30.3 %all_to_all.11.part_ref = bf16[16,16,2048]{2,1,0:T(8,128)(2,1)S(1)} all-to-all(bf16[16,16,2048]{2,1,0:T(8,128)(2,1)S(1)} %bitcast.7), channel_id=1, replica_groups=mesh['shard'=16,'rep'=2] {'shard'}, dimensions={0} | all-to-all | bytes 2097152 | tf_op jit(solution)/shard_map/all_to_all | solution.py:271
  87.5 0.0 collective-permute-start.1
  87.5 1.0 %place.2.refs_0_ = bf16[16,32,2048]{2,1,0:T(8,128)(2,1)} custom-call(s32[1]{0:T(128)} %bitcast.4.rep_ref, bf16[16,16,2048]{2,1,0:T(8,128)(2,1)S(1)} %all_to_all.11.part_ref), custom_call_target="tpu_custom_call" | custom-call | bytes 2097152 | tf_op jit(solution)/shard_map/place/pallas_call | solution.py:246
  88.5 1.7 %collective-permute-done.1.part_ref = bf16[16,16,2048]{2,1,0:T(8,128)(2,1)S(1)} collective-permute-done((bf16[16,16,2048]{2,1,0:T(8,128)(2,1)S(1)}, bf16[16,16,2048]{2,1,0:T(8,128)(2,1)S(1)}, u32[]{:S(2)}, u32[]{:S(2)}) %collective-permute-start.1) | collective-permute-done | bytes 1048608 | tf_op jit(solution)/shard_map/ppermute | solution.py:266
  90.2 1.0 %place.3 = bf16[16,32,2048]{2,1,0:T(8,128)(2,1)} custom-call(s32[1]{0:T(128)} %bitcast.2.rep_ref, bf16[16,16,2048]{2,1,0:T(8,128)(2,1)S(1)} %collective-permute-done.1.part_ref, bf16[16,32,2048]{2,1,0:T(8,128)(2,1)} %place.2.refs_0_), custom_call_target="tpu_custom_call", output_to_operand_aliasing={{}: (2, {})} | custom-call | bytes 2097152 | tf_op jit(solution)/shard_map/place/pallas_call | solution.py:246
Async XLA Ops:
  0.6 1.6 %copy-start = (bf16[16,32,2048]{2,1,0:T(8,128)(2,1)S(1)}, bf16[16,32,2048]{2,1,0:T(8,128)(2,1)}, u32[]{:S(2)}) copy-start(bf16[16,32,2048]{2,1,0:T(8,128)(2,1)} %m_ref) | copy-start | bytes 6291460
  2.2 1.6 %copy-start.1 = (bf16[16,32,2048]{2,1,0:T(8,128)(2,1)S(1)}, bf16[16,32,2048]{2,1,0:T(8,128)(2,1)}, u32[]{:S(2)}) copy-start(bf16[16,32,2048]{2,1,0:T(8,128)(2,1)} %g_ref) | copy-start | bytes 6291460
  39.1 2.7 %collective-permute-start = (bf16[256,2048]{1,0:T(8,128)(2,1)S(1)}, bf16[256,2048]{1,0:T(8,128)(2,1)S(1)}, u32[]{:S(2)}, u32[]{:S(2)}) collective-permute-start(bf16[256,2048]{1,0:T(8,128)(2,1)S(1)} %bitcast.5), channel_id=1, source_target_pairs={{1,0},{0,1},{3,2},{2,3},{5,4},{4,5},{7,6},{6,7},{9,8},{8,9},{11,10... | collective-permute-start | bytes 3145736 | tf_op jit(solution)/shard_map/ppermute | solution.py:266
  87.5 2.7 %collective-permute-start.1 = (bf16[16,16,2048]{2,1,0:T(8,128)(2,1)S(1)}, bf16[16,16,2048]{2,1,0:T(8,128)(2,1)S(1)}, u32[]{:S(2)}, u32[]{:S(2)}) collective-permute-start(bf16[16,16,2048]{2,1,0:T(8,128)(2,1)S(1)} %all_to_all.11.part_ref), channel_id=1, source_target_pairs={{1,0},{0,1},{3,2},{2,3},{5,4},{4,5},{7,6},{6,7},{9,8},{8,9},{11,10... | collective-permute-start | bytes 3145736 | tf_op jit(solution)/shard_map/ppermute | solution.py:266

commit v3 on v2

--- a/solution.py
+++ b/solution.py
@@ -69,7 +69,7 @@
             pltpu.VMEM(shape, BF),
             pltpu.SemaphoreType.DMA((2, chunks)),
         ],
-        compiler_params=pltpu.CompilerParams(vmem_limit_bytes=16 * 2**20),
+        compiler_params=pltpu.CompilerParams(vmem_limit_bytes=60 * 2**20),
         name="share",
     )(rep[None], momentum, gradient)
 
@@ -260,6 +260,8 @@
 
 def solution(mesh):
     n_rep = mesh.shape["rep"]
+    n_shard = mesh.shape["shard"]
+    order = [p // 2 + p % 2 * (n_shard // 2) if n_shard % 2 == 0 else p for p in range(n_shard)]
 
     def others(x):
         return [
@@ -268,7 +270,9 @@
         ]
 
     def exchange(x):
-        return lax.all_to_all(x, "shard", split_axis=0, concat_axis=0, tiled=True)
+        return lax.all_to_all(
+            x, "shard", split_axis=0, concat_axis=0, axis_index_groups=[order], tiled=True
+        )
 
     def shards(momentum, gradient):
         experts, rows, cols = momentum.shape

time: 91.4 us -> 90.7 us (level)
  local copies, waits for them, and re-layouts: 3.17 us -> 0.01 us
  Pallas kernels: 20.1 us -> 22.2 us
    unnamed x4, local copies, waits for them, and re-layouts: 3.17 us -> 0.01 us
    pallas_call x1, Pallas kernels: 0.78 us -> 2.83 us  [blended_share(): pl.pallas_call(share_kernel, in_specs=[pl.BlockSpec(memory_space=pltpu.SM...]
where the time goes in v3:
time: 90.7 us; the launch traced here: 90.4 us
  blocking collectives  65.2 us (72%)
  Pallas kernels  22.2 us (24%)
  waiting for transfers between devices  2.31 us (3%)
    all_to_all x2, blocking collectives, exchange(): lax.all_to_all(x, 'shard', split_axis=0, concat_axis=0, axis_index_groups...  65.2 us
    pallas_call x1, Pallas kernels, orthogonal(): pl.pallas_call(functools.partial(orthogonal_kernel, scale), in_specs=[vme...  15.4 us
    pallas_call x1, Pallas kernels, blended_share(): pl.pallas_call(share_kernel, in_specs=[pl.BlockSpec(memory_space=pltpu.SM...  2.83 us
    ppermute x2, waiting for transfers between devices, others(): lax.ppermute(x, 'rep', [((i + j) % n_rep, i) for i in range(n_rep)])  2.31 us
    pallas_call x1, Pallas kernels, new_momentum_of(): pl.pallas_call(momentum_kernel, in_specs=[vmem, vmem], out_specs=vmem, ou...  2.01 us
    pallas_call x2, Pallas kernels, place(): pl.pallas_call(place_kernel, in_specs=[pl.BlockSpec(memory_space=pltpu.SM...  1.96 us
  transfers between devices with their start and end apart: 2, of which 2 were waited for; matrix products, arithmetic and copies ran while one was open for 0% of the time, Pallas kernels for 3%

profile of v3, /device:TPU:0, one launch (start us, length us, event | category | flops | bytes accessed | tf_op | source)
XLA Modules:
  0.0 90.4 jit_solution(1027549174670526266)
XLA Ops:
  0.6 0.0 copy-start.1
  0.6 2.8 %share.1 = bf16[16,16,2048]{2,1,0:T(8,128)(2,1)} custom-call(s32[1]{0:T(128)} %bitcast.rep_ref, bf16[16,32,2048]{2,1,0:T(8,128)(2,1)} %m_ref, bf16[16,32,2048]{2,1,0:T(8,128)(2,1)} %g_ref), custom_call_target="tpu_custom_call" | custom-call | tf_op jit(solution)/shard_map/share/pallas_call | solution.py:62
  3.5 0.0 copy-start
  3.5 34.8 %all_to_all.10 = bf16[16,16,2048]{2,1,0:T(8,128)(2,1)S(1)} all-to-all(bf16[16,16,2048]{2,1,0:T(8,128)(2,1)} %share.1), channel_id=1, replica_groups={{0,16,2,18,4,20,6,22,8,24,10,26,12,28,14,30},{1,17,3,19,5,21,7,23,9,25,..., dimensions={0} | all-to-all | bytes 2097152 | tf_op jit(solution)/shard_map/all_to_all | solution.py:273
  38.3 0.0 collective-permute-start
  38.3 0.0 copy-done.1
  38.3 0.0 copy-done
  38.3 2.0 %new_momentum.1 = bf16[16,32,2048]{2,1,0:T(8,128)(2,1)} custom-call(bf16[16,32,2048]{2,1,0:T(8,128)(2,1)S(1)} %copy-done, bf16[16,32,2048]{2,1,0:T(8,128)(2,1)S(1)} %copy-done.1), custom_call_target="tpu_custom_call" | custom-call | flops 2097152 | bytes 6291456 | tf_op jit(solution)/shard_map/new_momentum/pallas_call | solution.py:87
  40.3 0.6 collective-permute-done.refs_1_
  41.0 15.4 %orthogonal.1 = bf16[256,2048]{1,0:T(8,128)(2,1)S(1)} custom-call(bf16[256,2048]{1,0:T(8,128)(2,1)S(1)} %bitcast.6, bf16[256,2048]{1,0:T(8,128)(2,1)S(1)} %collective-permute-done.refs_1_), custom_call_target="tpu_custom_call" | custom-call | tf_op jit(solution)/shard_map/orthogonal/pallas_call | solution.py:209
  56.4 30.4 %all_to_all.11.part_ref = bf16[16,16,2048]{2,1,0:T(8,128)(2,1)S(1)} all-to-all(bf16[16,16,2048]{2,1,0:T(8,128)(2,1)S(1)} %bitcast.7), channel_id=1, replica_groups={{0,16,2,18,4,20,6,22,8,24,10,26,12,28,14,30},{1,17,3,19,5,21,7,23,9,25,..., dimensions={0} | all-to-all | bytes 2097152 | tf_op jit(solution)/shard_map/all_to_all | solution.py:273
  86.8 0.0 collective-permute-start.1
  86.8 1.0 %place.2.refs_0_ = bf16[16,32,2048]{2,1,0:T(8,128)(2,1)} custom-call(s32[1]{0:T(128)} %bitcast.4.rep_ref, bf16[16,16,2048]{2,1,0:T(8,128)(2,1)S(1)} %all_to_all.11.part_ref), custom_call_target="tpu_custom_call" | custom-call | bytes 2097152 | tf_op jit(solution)/shard_map/place/pallas_call | solution.py:246
  87.8 1.7 %collective-permute-done.1.part_ref = bf16[16,16,2048]{2,1,0:T(8,128)(2,1)S(1)} collective-permute-done((bf16[16,16,2048]{2,1,0:T(8,128)(2,1)S(1)}, bf16[16,16,2048]{2,1,0:T(8,128)(2,1)S(1)}, u32[]{:S(2)}, u32[]{:S(2)}) %collective-permute-start.1) | collective-permute-done | bytes 1048608 | tf_op jit(solution)/shard_map/ppermute | solution.py:268
  89.4 1.0 %place.3 = bf16[16,32,2048]{2,1,0:T(8,128)(2,1)} custom-call(s32[1]{0:T(128)} %bitcast.2.rep_ref, bf16[16,16,2048]{2,1,0:T(8,128)(2,1)S(1)} %collective-permute-done.1.part_ref, bf16[16,32,2048]{2,1,0:T(8,128)(2,1)} %place.2.refs_0_), custom_call_target="tpu_custom_call", output_to_operand_aliasing={{}: (2, {})} | custom-call | bytes 2097152 | tf_op jit(solution)/shard_map/place/pallas_call | solution.py:246
Async XLA Ops:
  0.6 37.7 %copy-start.1 = (bf16[16,32,2048]{2,1,0:T(8,128)(2,1)S(1)}, bf16[16,32,2048]{2,1,0:T(8,128)(2,1)}, u32[]{:S(2)}) copy-start(bf16[16,32,2048]{2,1,0:T(8,128)(2,1)} %g_ref) | copy-start | bytes 6291460
  3.5 34.8 %copy-start = (bf16[16,32,2048]{2,1,0:T(8,128)(2,1)S(1)}, bf16[16,32,2048]{2,1,0:T(8,128)(2,1)}, u32[]{:S(2)}) copy-start(bf16[16,32,2048]{2,1,0:T(8,128)(2,1)} %m_ref) | copy-start | bytes 6291460
  38.3 2.7 %collective-permute-start = (bf16[256,2048]{1,0:T(8,128)(2,1)S(1)}, bf16[256,2048]{1,0:T(8,128)(2,1)S(1)}, u32[]{:S(2)}, u32[]{:S(2)}) collective-permute-start(bf16[256,2048]{1,0:T(8,128)(2,1)S(1)} %bitcast.5), channel_id=1, source_target_pairs={{1,0},{0,1},{3,2},{2,3},{5,4},{4,5},{7,6},{6,7},{9,8},{8,9},{11,10... | collective-permute-start | bytes 3145736 | tf_op jit(solution)/shard_map/ppermute | solution.py:268
  86.8 2.7 %collective-permute-start.1 = (bf16[16,16,2048]{2,1,0:T(8,128)(2,1)S(1)}, bf16[16,16,2048]{2,1,0:T(8,128)(2,1)S(1)}, u32[]{:S(2)}, u32[]{:S(2)}) collective-permute-start(bf16[16,16,2048]{2,1,0:T(8,128)(2,1)S(1)} %all_to_all.11.part_ref), channel_id=1, source_target_pairs={{1,0},{0,1},{3,2},{2,3},{5,4},{4,5},{7,6},{6,7},{9,8},{8,9},{11,10... | collective-permute-start | bytes 3145736 | tf_op jit(solution)/shard_map/ppermute | solution.py:268

commit v4 on v3

--- a/solution.py
+++ b/solution.py
@@ -13,6 +13,8 @@
 coef_b = -4.775
 coef_c = 2.0315
 
+LIMIT = 4.0
+
 BF = jnp.bfloat16
 F32 = jnp.float32
 
@@ -25,7 +27,7 @@
     return (g.astype(F32) + 0.95 * next_momentum(m, g).astype(F32)).astype(BF)
 
 
-def share_kernel(rep_ref, m_hbm, g_hbm, share_ref, m_ref, g_ref, sems):
+def share_kernel(rep_ref, m_hbm, g_hbm, share_hbm, m_ref, g_ref, share_ref, sems):
     experts, height, _ = share_ref.shape
     chunks = sems.shape[1]
     step = experts // chunks
@@ -46,6 +48,11 @@
             copy.wait()
         at = slice(i * step, (i + 1) * step)
         share_ref[at] = blend(m_ref[at], g_ref[at])
+        at = pl.ds(i * step, step)
+        copies[i] = pltpu.make_async_copy(share_ref.at[at], share_hbm.at[at], sems.at[2, i])
+        copies[i].start()
+    for copy in copies:
+        copy.wait()
 
 
 def blended_share(rep, momentum, gradient, n_rep):
@@ -62,12 +69,13 @@
     return pl.pallas_call(
         share_kernel,
         in_specs=[pl.BlockSpec(memory_space=pltpu.SMEM), hbm, hbm],
-        out_specs=pl.BlockSpec(memory_space=pltpu.VMEM),
+        out_specs=hbm,
         out_shape=jax.ShapeDtypeStruct(shape, BF),
         scratch_shapes=[
             pltpu.VMEM(shape, BF),
             pltpu.VMEM(shape, BF),
-            pltpu.SemaphoreType.DMA((2, chunks)),
+            pltpu.VMEM(shape, BF),
+            pltpu.SemaphoreType.DMA((3, chunks)),
         ],
         compiler_params=pltpu.CompilerParams(vmem_limit_bytes=60 * 2**20),
         name="share",
@@ -102,104 +110,144 @@
     return high, (x - high.astype(F32)).astype(BF)
 
 
-def put_left(ref, x):
-    rows, n = x.shape
-    high, low = halves(x)
-    ref[:rows, :n] = high
-    ref[:rows, n : 2 * n] = high
-    ref[:rows, 2 * n :] = low
-
-
-def put_right(ref, x):
-    n = x.shape[0]
-    high, low = halves(x)
-    ref[:n] = high
-    ref[n : 2 * n] = low
-    ref[2 * n :] = high
-
-
 def dot(x, y):
     return jnp.dot(x, y, preferred_element_type=F32)
 
 
-def dot_transposed(x, y):
-    return lax.dot_general(x, y, (((1,), (1,)), ((), ())), preferred_element_type=F32)
-
-
-def put_symmetric(ref, upper, corner):
-    half = corner.shape[0]
-    ref[:half] = upper
-    ref[half:, half:] = corner
-    ref[half:, :half] = upper[:, half:].T
+def dot_transposed(x, y, precision=None):
+    return lax.dot_general(
+        x, y, (((1,), (1,)), ((), ())), precision=precision, preferred_element_type=F32
+    )
 
 
 def orthogonal_kernel(scale, *refs):
-    *parts, out_ref, x_ref, a_ref, s_ref, y_ref, q_ref, left, right = refs
-    height = out_ref.shape[0]
+    *parts, out_ref, x_ref, a_ref, s_ref, q_ref, left, right, full_ref = refs
+    height, width = out_ref.shape
     n = x_ref.shape[0]
     half = n // 2
     for i, part in enumerate(parts):
         x_ref[i * height : (i + 1) * height] = part[...]
 
-    put_symmetric(
-        y_ref,
-        dot_transposed(x_ref[:half], x_ref[...]),
-        dot_transposed(x_ref[half:], x_ref[half:]),
+    def spread(blocks, to_left, to_right):
+        b11, b12, b22 = blocks
+        for i, j, x in ((0, 0, b11), (0, 1, b12), (1, 1, b22), (1, 0, b12.T)):
+            high, low = halves(x)
+            cols = slice(j * half, (j + 1) * half)
+            if to_left:
+                put_left(height + i * half, j * half, high, low)
+            if to_right:
+                for k, part in enumerate((high, low, high)):
+                    right[k * n + i * half : k * n + (i + 1) * half, cols] = part
+
+    def put_left(row, col, high, low):
+        rows, cols = high.shape
+        for k, part in enumerate((high, high, low)):
+            left[row : row + rows, k * n + col : k * n + col + cols] = part
+
+    def product(first=height):
+        y = dot(left[first:], right[:, half:])
+        z = dot(left[first : height + half], right[:, :half])
+        q = height - first
+        return (z[q:], y[q : q + half], y[q + half :]), z[:q], y[:q]
+
+    def middle():
+        a = [a_ref[i] for i in range(3)]
+        spread(a, True, True)
+        y, _, _ = product()
+        m = [coef_b * u + coef_c * v for u, v in zip(a, y)]
+        spread(m, False, True)
+        return m
+
+    def advance(y):
+        for i in range(3):
+            s_ref[i] = coef_a * a_ref[i] + y[i]
+        spread([s_ref[i] for i in range(3)], True, False)
+        y, _, _ = product()
+        for i in range(3):
+            a_ref[i] = coef_a * s_ref[i] + y[i]
+
+    def extend():
+        high, low = halves(q_ref[...])
+        put_left(0, 0, high, low)
+
+    y = dot_transposed(x_ref[...], x_ref[half:])
+    gram = (dot_transposed(x_ref[:half], x_ref[:half]), y[:half], y[half:])
+    eye = lax.broadcasted_iota(jnp.int32, (half, half), 0) == lax.broadcasted_iota(
+        jnp.int32, (half, half), 1
     )
-    eye = lax.broadcasted_iota(jnp.int32, (n, n), 0) == lax.broadcasted_iota(
-        jnp.int32, (n, n), 1
-    )
-    square = jnp.sum(jnp.where(eye, y_ref[...], 0.0), keepdims=True)
+    square = jnp.sum(jnp.where(eye, gram[0] + gram[2], 0.0), keepdims=True)
     inverse = 1.0 / (jnp.sqrt(square) + 1e-07)
-    a_ref[...] = y_ref[...] * (inverse * inverse)
-
-    def multiply(ref):
-        put_symmetric(
-            ref, dot(left[:half], right[...]), dot(left[half:], right[:, half:])
-        )
-
-    def middle():
-        a = a_ref[...]
-        put_left(left, a)
-        put_right(right, a)
-        multiply(y_ref)
-        m = coef_b * a + coef_c * y_ref[...]
-        put_right(right, m)
-        return m
-
-    def advance():
-        multiply(y_ref)
-        s = coef_a * a_ref[...] + y_ref[...]
-        s_ref[...] = s
-        put_left(left, s)
-        multiply(y_ref)
-        a_ref[...] = coef_a * s_ref[...] + y_ref[...]
-
-    def extend():
-        put_left(left, q_ref[...])
-        return coef_a * q_ref[...] + dot(left[:height], right[...])
-
-    q_ref[...] = jnp.where(eye[:height], coef_a, 0.0) + middle()[:height]
-    advance()
+    for i in range(3):
+        a_ref[i] = gram[i] * (inverse * inverse)
+
+    m = middle()
+    q_ref[:, :half] = (m[0] + jnp.where(eye, coef_a, 0.0))[:height]
+    q_ref[:, half:] = m[1][:height]
+    y, _, _ = product()
+    advance(y)
 
     def step(_, carry):
         middle()
-        advance()
-        q_ref[...] = extend()
+        extend()
+        y, ql, qr = product(0)
+        q_ref[:, :half] = coef_a * q_ref[:, :half] + ql
+        q_ref[:, half:] = coef_a * q_ref[:, half:] + qr
+        advance(y)
         return carry
 
     lax.fori_loop(1, ITERS - 1, step, 0)
     middle()
-    high, low = halves(extend() * (inverse * scale))
-    left[:height, :n] = high
-    left[:height, n : 2 * n] = low
-    width = out_ref.shape[1]
-    block = min(width, 512)
-    for at in range(0, width, block):
-        x = x_ref[:, at : at + block]
-        out_ref[:, at : at + block] = (
-            dot(left[:height, :n], x) + dot(left[:height, n : 2 * n], x)
-        ).astype(BF)
+    extend()
+    q = coef_a * q_ref[...] + dot(left[:height], right[...])
+    spread_of_values = jnp.sum(q * q) * (1.0 / (height * n))
+    good = spread_of_values < LIMIT
+
+    @pl.when(good)
+    def _():
+        high, low = halves(q * (inverse * scale))
+        left[:height, :n] = high
+        left[:height, n : 2 * n] = low
+        block = min(width, 512)
+        for at in range(0, width, block):
+            x = x_ref[:, at : at + block]
+            out_ref[:, at : at + block] = (
+                dot(left[:height, :n], x) + dot(left[:height, n : 2 * n], x)
+            ).astype(BF)
+
+    @pl.when(jnp.logical_not(good))
+    def _():
+        best = lax.Precision.HIGHEST
+        block = min(width, 512)
+
+        def columns(i):
+            return pl.ds(pl.multiple_of(i * block, block), block)
+
+        def load(i, carry):
+            full_ref[:, columns(i)] = x_ref[:, columns(i)].astype(F32) * inverse
+            return carry
+
+        def sweep(_, carry):
+            def add(i, total):
+                x = full_ref[:, columns(i)]
+                return total + dot_transposed(x, x, best)
+
+            a = lax.fori_loop(0, width // block, add, jnp.zeros((n, n), F32))
+            m = coef_b * a + coef_c * jnp.dot(a, a, precision=best)
+
+            def apply(i, carry):
+                x = full_ref[:, columns(i)]
+                full_ref[:, columns(i)] = coef_a * x + jnp.dot(m, x, precision=best)
+                return carry
+
+            return lax.fori_loop(0, width // block, apply, carry)
+
+        def store(i, carry):
+            out_ref[:, columns(i)] = (full_ref[:height, columns(i)] * scale).astype(BF)
+            return carry
+
+        lax.fori_loop(0, width // block, load, 0)
+        lax.fori_loop(0, ITERS, sweep, 0)
+        lax.fori_loop(0, width // block, store, 0)
 
 
 def orthogonal(parts, scale):
@@ -213,12 +261,12 @@
         out_shape=jax.ShapeDtypeStruct((height, cols), BF),
         scratch_shapes=[
             pltpu.VMEM((n, cols), BF),
-            pltpu.VMEM((n, n), F32),
-            pltpu.VMEM((n, n), F32),
-            pltpu.VMEM((n, n), F32),
+            pltpu.VMEM((3, n // 2, n // 2), F32),
+            pltpu.VMEM((3, n // 2, n // 2), F32),
             pltpu.VMEM((height, n), F32),
-            pltpu.VMEM((n, 3 * n), BF),
+            pltpu.VMEM((height + n, 3 * n), BF),
             pltpu.VMEM((3 * n, n), BF),
+            pltpu.VMEM((n, cols), F32),
         ],
         compiler_params=pltpu.CompilerParams(vmem_limit_bytes=40 * 2**20),
         name="orthogonal",
@@ -226,12 +274,17 @@
 
 
 def place_kernel(rep_ref, part_ref, *refs):
-    *_, out_ref, sem = refs
-    height = part_ref.shape[1]
+    *_, out_ref, sems = refs
+    experts, height, _ = part_ref.shape
     rows = pl.ds(pl.multiple_of(rep_ref[0] * height, height), height)
-    copy = pltpu.make_async_copy(part_ref, out_ref.at[:, rows], sem)
-    copy.start()
-    copy.wait()
+    step = experts // sems.shape[0]
+    copies = []
+    for i in range(sems.shape[0]):
+        at = pl.ds(i * step, step)
+        copies.append(pltpu.make_async_copy(part_ref.at[at], out_ref.at[at, rows], sems.at[i]))
+        copies[-1].start()
+    for copy in copies:
+        copy.wait()
 
 
 def place(which, part, whole):
@@ -248,7 +301,7 @@
         in_specs=[pl.BlockSpec(memory_space=pltpu.SMEM), anywhere] + [hbm] * (not first),
         out_specs=hbm,
         out_shape=jax.ShapeDtypeStruct(whole if first else whole.shape, BF),
-        scratch_shapes=[pltpu.SemaphoreType.DMA(())],
+        scratch_shapes=[pltpu.SemaphoreType.DMA((4 if experts % 4 == 0 else 1,))],
         input_output_aliases={} if first else {2: 0},
         cost_estimate=pl.CostEstimate(
             flops=0, bytes_accessed=4 * part.size, transcendentals=0

time: 90.7 us -> 91.6 us (level)
    pallas_call x1, Pallas kernels: 15.4 us -> 16.5 us  [orthogonal(): pl.pallas_call(functools.partial(orthogonal_kernel, scale), in_specs=[vme...]
where the time goes in v4:
time: 91.6 us; the launch traced here: 91.4 us
  blocking collectives  65.2 us (71%)
  Pallas kernels  23 us (25%)
  waiting for transfers between devices  2.29 us (2%)
    all_to_all x2, blocking collectives, exchange(): lax.all_to_all(x, 'shard', split_axis=0, concat_axis=0, axis_index_groups...  65.2 us
    pallas_call x1, Pallas kernels, orthogonal(): pl.pallas_call(functools.partial(orthogonal_kernel, scale), in_specs=[vme...  16.5 us
    pallas_call x1, Pallas kernels, blended_share(): pl.pallas_call(share_kernel, in_specs=[pl.BlockSpec(memory_space=pltpu.SM...  2.6 us
    ppermute x2, waiting for transfers between devices, others(): lax.ppermute(x, 'rep', [((i + j) % n_rep, i) for i in range(n_rep)])  2.29 us
    pallas_call x1, Pallas kernels, new_momentum_of(): pl.pallas_call(momentum_kernel, in_specs=[vmem, vmem], out_specs=vmem, ou...  2.01 us
    pallas_call x2, Pallas kernels, place(): pl.pallas_call(place_kernel, in_specs=[pl.BlockSpec(memory_space=pltpu.SM...  1.99 us
  transfers between devices with their start and end apart: 2, of which 2 were waited for; matrix products, arithmetic and copies ran while one was open for 0% of the time, Pallas kernels for 3%

profile of v4, /device:TPU:0, one launch (start us, length us, event | category | flops | bytes accessed | tf_op | source)
XLA Modules:
  0.0 91.4 jit_solution(14977544918924765434)
XLA Ops:
  0.6 0.0 copy-start.1
  0.6 2.6 %share.1 = bf16[16,16,2048]{2,1,0:T(8,128)(2,1)} custom-call(s32[1]{0:T(128)} %bitcast.rep_ref, bf16[16,32,2048]{2,1,0:T(8,128)(2,1)} %m_ref, bf16[16,32,2048]{2,1,0:T(8,128)(2,1)} %g_ref), custom_call_target="tpu_custom_call" | custom-call | tf_op jit(solution)/shard_map/share/pallas_call | solution.py:69
  3.2 0.0 copy-start
  3.3 34.8 %all_to_all.10 = bf16[16,16,2048]{2,1,0:T(8,128)(2,1)S(1)} all-to-all(bf16[16,16,2048]{2,1,0:T(8,128)(2,1)} %share.1), channel_id=1, replica_groups={{0,16,2,18,4,20,6,22,8,24,10,26,12,28,14,30},{1,17,3,19,5,21,7,23,9,25,..., dimensions={0} | all-to-all | bytes 2097152 | tf_op jit(solution)/shard_map/all_to_all | solution.py:326
  38.1 0.0 collective-permute-start
  38.1 0.0 copy-done.1
  38.1 0.0 copy-done
  38.1 2.0 %new_momentum.1 = bf16[16,32,2048]{2,1,0:T(8,128)(2,1)} custom-call(bf16[16,32,2048]{2,1,0:T(8,128)(2,1)S(1)} %copy-done, bf16[16,32,2048]{2,1,0:T(8,128)(2,1)S(1)} %copy-done.1), custom_call_target="tpu_custom_call" | custom-call | flops 2097152 | bytes 6291456 | tf_op jit(solution)/shard_map/new_momentum/pallas_call | solution.py:95
  40.1 0.6 collective-permute-done.refs_1_
  40.7 16.5 %orthogonal.1 = bf16[256,2048]{1,0:T(8,128)(2,1)S(1)} custom-call(bf16[256,2048]{1,0:T(8,128)(2,1)S(1)} %bitcast.6, bf16[256,2048]{1,0:T(8,128)(2,1)S(1)} %collective-permute-done.refs_1_), custom_call_target="tpu_custom_call" | custom-call | tf_op jit(solution)/shard_map/orthogonal/pallas_call | solution.py:257
  57.2 30.4 %all_to_all.11.part_ref = bf16[16,16,2048]{2,1,0:T(8,128)(2,1)S(1)} all-to-all(bf16[16,16,2048]{2,1,0:T(8,128)(2,1)S(1)} %bitcast.7), channel_id=1, replica_groups={{0,16,2,18,4,20,6,22,8,24,10,26,12,28,14,30},{1,17,3,19,5,21,7,23,9,25,..., dimensions={0} | all-to-all | bytes 2097152 | tf_op jit(solution)/shard_map/all_to_all | solution.py:326
  87.6 0.0 collective-permute-start.1
  87.6 1.0 %place.2.refs_0_ = bf16[16,32,2048]{2,1,0:T(8,128)(2,1)} custom-call(s32[1]{0:T(128)} %bitcast.4.rep_ref, bf16[16,16,2048]{2,1,0:T(8,128)(2,1)S(1)} %all_to_all.11.part_ref), custom_call_target="tpu_custom_call" | custom-call | bytes 2097152 | tf_op jit(solution)/shard_map/place/pallas_call | solution.py:299
  88.6 1.7 %collective-permute-done.1.part_ref = bf16[16,16,2048]{2,1,0:T(8,128)(2,1)S(1)} collective-permute-done((bf16[16,16,2048]{2,1,0:T(8,128)(2,1)S(1)}, bf16[16,16,2048]{2,1,0:T(8,128)(2,1)S(1)}, u32[]{:S(2)}, u32[]{:S(2)}) %collective-permute-start.1) | collective-permute-done | bytes 1048608 | tf_op jit(solution)/shard_map/ppermute | solution.py:321
  90.2 1.0 %place.3 = bf16[16,32,2048]{2,1,0:T(8,128)(2,1)} custom-call(s32[1]{0:T(128)} %bitcast.2.rep_ref, bf16[16,16,2048]{2,1,0:T(8,128)(2,1)S(1)} %collective-permute-done.1.part_ref, bf16[16,32,2048]{2,1,0:T(8,128)(2,1)} %place.2.refs_0_), custom_call_target="tpu_custom_call", output_to_operand_aliasing={{}: (2, {})} | custom-call | bytes 2097152 | tf_op jit(solution)/shard_map/place/pallas_call | solution.py:299
Async XLA Ops:
  0.6 37.5 %copy-start.1 = (bf16[16,32,2048]{2,1,0:T(8,128)(2,1)S(1)}, bf16[16,32,2048]{2,1,0:T(8,128)(2,1)}, u32[]{:S(2)}) copy-start(bf16[16,32,2048]{2,1,0:T(8,128)(2,1)} %g_ref) | copy-start | bytes 6291460
  3.2 34.8 %copy-start = (bf16[16,32,2048]{2,1,0:T(8,128)(2,1)S(1)}, bf16[16,32,2048]{2,1,0:T(8,128)(2,1)}, u32[]{:S(2)}) copy-start(bf16[16,32,2048]{2,1,0:T(8,128)(2,1)} %m_ref) | copy-start | bytes 6291460
  38.1 2.7 %collective-permute-start = (bf16[256,2048]{1,0:T(8,128)(2,1)S(1)}, bf16[256,2048]{1,0:T(8,128)(2,1)S(1)}, u32[]{:S(2)}, u32[]{:S(2)}) collective-permute-start(bf16[256,2048]{1,0:T(8,128)(2,1)S(1)} %bitcast.5), channel_id=1, source_target_pairs={{1,0},{0,1},{3,2},{2,3},{5,4},{4,5},{7,6},{6,7},{9,8},{8,9},{11,10... | collective-permute-start | bytes 3145736 | tf_op jit(solution)/shard_map/ppermute | solution.py:321
  87.6 2.7 %collective-permute-start.1 = (bf16[16,16,2048]{2,1,0:T(8,128)(2,1)S(1)}, bf16[16,16,2048]{2,1,0:T(8,128)(2,1)S(1)}, u32[]{:S(2)}, u32[]{:S(2)}) collective-permute-start(bf16[16,16,2048]{2,1,0:T(8,128)(2,1)S(1)} %all_to_all.11.part_ref), channel_id=1, source_target_pairs={{1,0},{0,1},{3,2},{2,3},{5,4},{4,5},{7,6},{6,7},{9,8},{8,9},{11,10... | collective-permute-start | bytes 3145736 | tf_op jit(solution)/shard_map/ppermute | solution.py:321

commit v5 on v4

--- a/solution.py
+++ b/solution.py
@@ -144,31 +144,32 @@
         for k, part in enumerate((high, high, low)):
             left[row : row + rows, k * n + col : k * n + col + cols] = part
 
-    def product(first=height):
-        y = dot(left[first:], right[:, half:])
-        z = dot(left[first : height + half], right[:, :half])
-        q = height - first
-        return (z[q:], y[q : q + half], y[q + half :]), z[:q], y[:q]
+    def product():
+        upper = dot(left[height : height + half], right[...])
+        corner = dot(left[height + half :], right[:, half:])
+        return upper[:, :half], upper[:, half:], corner
 
     def middle():
         a = [a_ref[i] for i in range(3)]
         spread(a, True, True)
-        y, _, _ = product()
+        y = product()
         m = [coef_b * u + coef_c * v for u, v in zip(a, y)]
         spread(m, False, True)
         return m
 
-    def advance(y):
+    def advance():
+        s = [coef_a * a_ref[i] + y for i, y in enumerate(product())]
         for i in range(3):
-            s_ref[i] = coef_a * a_ref[i] + y[i]
-        spread([s_ref[i] for i in range(3)], True, False)
-        y, _, _ = product()
+            s_ref[i] = s[i]
+        spread(s, True, False)
+        y = product()
         for i in range(3):
             a_ref[i] = coef_a * s_ref[i] + y[i]
 
-    def extend():
-        high, low = halves(q_ref[...])
+    def rows_times(q):
+        high, low = halves(q)
         put_left(0, 0, high, low)
+        return dot(left[:height], right[...])
 
     y = dot_transposed(x_ref[...], x_ref[half:])
     gram = (dot_transposed(x_ref[:half], x_ref[:half]), y[:half], y[half:])
@@ -183,22 +184,18 @@
     m = middle()
     q_ref[:, :half] = (m[0] + jnp.where(eye, coef_a, 0.0))[:height]
     q_ref[:, half:] = m[1][:height]
-    y, _, _ = product()
-    advance(y)
+    advance()
 
     def step(_, carry):
         middle()
-        extend()
-        y, ql, qr = product(0)
-        q_ref[:, :half] = coef_a * q_ref[:, :half] + ql
-        q_ref[:, half:] = coef_a * q_ref[:, half:] + qr
-        advance(y)
+        advance()
+        q_ref[...] = coef_a * q_ref[...] + rows_times(q_ref[...])
         return carry
 
     lax.fori_loop(1, ITERS - 1, step, 0)
-    middle()
-    extend()
-    q = coef_a * q_ref[...] + dot(left[:height], right[...])
+    spread([a_ref[i] for i in range(3)], False, True)
+    q = q_ref[...]
+    q = coef_a * q + rows_times(coef_b * q + coef_c * rows_times(q))
     spread_of_values = jnp.sum(q * q) * (1.0 / (height * n))
     good = spread_of_values < LIMIT
 

time: 91.6 us -> 90.1 us (0.984)
  Pallas kernels: 23 us -> 21.5 us
    pallas_call x1, Pallas kernels: 16.5 us -> 14.9 us  [orthogonal(): pl.pallas_call(functools.partial(orthogonal_kernel, scale), in_specs=[vme...]
where the time goes in v5:
time: 90.1 us; the launch traced here: 89.9 us
  blocking collectives  65.2 us (72%)
  Pallas kernels  21.5 us (24%)
  waiting for transfers between devices  2.29 us (3%)
    all_to_all x2, blocking collectives, exchange(): lax.all_to_all(x, 'shard', split_axis=0, concat_axis=0, axis_index_groups...  65.2 us
    pallas_call x1, Pallas kernels, orthogonal(): pl.pallas_call(functools.partial(orthogonal_kernel, scale), in_specs=[vme...  14.9 us
    pallas_call x1, Pallas kernels, blended_share(): pl.pallas_call(share_kernel, in_specs=[pl.BlockSpec(memory_space=pltpu.SM...  2.6 us
    ppermute x2, waiting for transfers between devices, others(): lax.ppermute(x, 'rep', [((i + j) % n_rep, i) for i in range(n_rep)])  2.29 us
    pallas_call x1, Pallas kernels, new_momentum_of(): pl.pallas_call(momentum_kernel, in_specs=[vmem, vmem], out_specs=vmem, ou...  2.01 us
    pallas_call x2, Pallas kernels, place(): pl.pallas_call(place_kernel, in_specs=[pl.BlockSpec(memory_space=pltpu.SM...  1.99 us
  transfers between devices with their start and end apart: 2, of which 2 were waited for; matrix products, arithmetic and copies ran while one was open for 0% of the time, Pallas kernels for 3%

profile of v5, /device:TPU:0, one launch (start us, length us, event | category | flops | bytes accessed | tf_op | source)
XLA Modules:
  0.0 89.9 jit_solution(1202639350329302267)
XLA Ops:
  0.6 0.0 copy-start.1
  0.6 2.6 %share.1 = bf16[16,16,2048]{2,1,0:T(8,128)(2,1)} custom-call(s32[1]{0:T(128)} %bitcast.rep_ref, bf16[16,32,2048]{2,1,0:T(8,128)(2,1)} %m_ref, bf16[16,32,2048]{2,1,0:T(8,128)(2,1)} %g_ref), custom_call_target="tpu_custom_call" | custom-call | tf_op jit(solution)/shard_map/share/pallas_call | solution.py:69
  3.2 0.0 copy-start
  3.3 34.8 %all_to_all.10 = bf16[16,16,2048]{2,1,0:T(8,128)(2,1)S(1)} all-to-all(bf16[16,16,2048]{2,1,0:T(8,128)(2,1)} %share.1), channel_id=1, replica_groups={{0,16,2,18,4,20,6,22,8,24,10,26,12,28,14,30},{1,17,3,19,5,21,7,23,9,25,..., dimensions={0} | all-to-all | bytes 2097152 | tf_op jit(solution)/shard_map/all_to_all | solution.py:323
  38.1 0.0 collective-permute-start
  38.1 0.0 copy-done.1
  38.1 0.0 copy-done
  38.1 2.0 %new_momentum.1 = bf16[16,32,2048]{2,1,0:T(8,128)(2,1)} custom-call(bf16[16,32,2048]{2,1,0:T(8,128)(2,1)S(1)} %copy-done, bf16[16,32,2048]{2,1,0:T(8,128)(2,1)S(1)} %copy-done.1), custom_call_target="tpu_custom_call" | custom-call | flops 2097152 | bytes 6291456 | tf_op jit(solution)/shard_map/new_momentum/pallas_call | solution.py:95
  40.1 0.6 collective-permute-done.refs_1_
  40.7 14.9 %orthogonal.1 = bf16[256,2048]{1,0:T(8,128)(2,1)S(1)} custom-call(bf16[256,2048]{1,0:T(8,128)(2,1)S(1)} %bitcast.6, bf16[256,2048]{1,0:T(8,128)(2,1)S(1)} %collective-permute-done.refs_1_), custom_call_target="tpu_custom_call" | custom-call | tf_op jit(solution)/shard_map/orthogonal/pallas_call | solution.py:254
  55.7 30.4 %all_to_all.11.part_ref = bf16[16,16,2048]{2,1,0:T(8,128)(2,1)S(1)} all-to-all(bf16[16,16,2048]{2,1,0:T(8,128)(2,1)S(1)} %bitcast.7), channel_id=1, replica_groups={{0,16,2,18,4,20,6,22,8,24,10,26,12,28,14,30},{1,17,3,19,5,21,7,23,9,25,..., dimensions={0} | all-to-all | bytes 2097152 | tf_op jit(solution)/shard_map/all_to_all | solution.py:323
  86.1 0.0 collective-permute-start.1
  86.1 1.0 %place.2.refs_0_ = bf16[16,32,2048]{2,1,0:T(8,128)(2,1)} custom-call(s32[1]{0:T(128)} %bitcast.4.rep_ref, bf16[16,16,2048]{2,1,0:T(8,128)(2,1)S(1)} %all_to_all.11.part_ref), custom_call_target="tpu_custom_call" | custom-call | bytes 2097152 | tf_op jit(solution)/shard_map/place/pallas_call | solution.py:296
  87.1 1.7 %collective-permute-done.1.part_ref = bf16[16,16,2048]{2,1,0:T(8,128)(2,1)S(1)} collective-permute-done((bf16[16,16,2048]{2,1,0:T(8,128)(2,1)S(1)}, bf16[16,16,2048]{2,1,0:T(8,128)(2,1)S(1)}, u32[]{:S(2)}, u32[]{:S(2)}) %collective-permute-start.1) | collective-permute-done | bytes 1048608 | tf_op jit(solution)/shard_map/ppermute | solution.py:318
  88.7 1.0 %place.3 = bf16[16,32,2048]{2,1,0:T(8,128)(2,1)} custom-call(s32[1]{0:T(128)} %bitcast.2.rep_ref, bf16[16,16,2048]{2,1,0:T(8,128)(2,1)S(1)} %collective-permute-done.1.part_ref, bf16[16,32,2048]{2,1,0:T(8,128)(2,1)} %place.2.refs_0_), custom_call_target="tpu_custom_call", output_to_operand_aliasing={{}: (2, {})} | custom-call | bytes 2097152 | tf_op jit(solution)/shard_map/place/pallas_call | solution.py:296
Async XLA Ops:
  0.6 37.5 %copy-start.1 = (bf16[16,32,2048]{2,1,0:T(8,128)(2,1)S(1)}, bf16[16,32,2048]{2,1,0:T(8,128)(2,1)}, u32[]{:S(2)}) copy-start(bf16[16,32,2048]{2,1,0:T(8,128)(2,1)} %g_ref) | copy-start | bytes 6291460
  3.2 34.8 %copy-start = (bf16[16,32,2048]{2,1,0:T(8,128)(2,1)S(1)}, bf16[16,32,2048]{2,1,0:T(8,128)(2,1)}, u32[]{:S(2)}) copy-start(bf16[16,32,2048]{2,1,0:T(8,128)(2,1)} %m_ref) | copy-start | bytes 6291460
  38.1 2.7 %collective-permute-start = (bf16[256,2048]{1,0:T(8,128)(2,1)S(1)}, bf16[256,2048]{1,0:T(8,128)(2,1)S(1)}, u32[]{:S(2)}, u32[]{:S(2)}) collective-permute-start(bf16[256,2048]{1,0:T(8,128)(2,1)S(1)} %bitcast.5), channel_id=1, source_target_pairs={{1,0},{0,1},{3,2},{2,3},{5,4},{4,5},{7,6},{6,7},{9,8},{8,9},{11,10... | collective-permute-start | bytes 3145736 | tf_op jit(solution)/shard_map/ppermute | solution.py:318
  86.1 2.7 %collective-permute-start.1 = (bf16[16,16,2048]{2,1,0:T(8,128)(2,1)S(1)}, bf16[16,16,2048]{2,1,0:T(8,128)(2,1)S(1)}, u32[]{:S(2)}, u32[]{:S(2)}) collective-permute-start(bf16[16,16,2048]{2,1,0:T(8,128)(2,1)S(1)} %all_to_all.11.part_ref), channel_id=1, source_target_pairs={{1,0},{0,1},{3,2},{2,3},{5,4},{4,5},{7,6},{6,7},{9,8},{8,9},{11,10... | collective-permute-start | bytes 3145736 | tf_op jit(solution)/shard_map/ppermute | solution.py:318

commit v6 on v5

--- a/solution.py
+++ b/solution.py
@@ -121,94 +121,84 @@
 
 
 def orthogonal_kernel(scale, *refs):
-    *parts, out_ref, x_ref, a_ref, s_ref, q_ref, left, right, full_ref = refs
+    *parts, out_ref, x_ref, a_ref, s_ref, q_ref = refs[:-6]
+    a_left, a_right, m_right, s_left, q_left, full_ref = refs[-6:]
     height, width = out_ref.shape
     n = x_ref.shape[0]
     half = n // 2
     for i, part in enumerate(parts):
         x_ref[i * height : (i + 1) * height] = part[...]
 
-    def spread(blocks, to_left, to_right):
-        b11, b12, b22 = blocks
-        for i, j, x in ((0, 0, b11), (0, 1, b12), (1, 1, b22), (1, 0, b12.T)):
+    blocks = ((0, 1), (0, 0), (1, 1))
+
+    def rows(i):
+        return slice(i * half, (i + 1) * half)
+
+    def put_left(ref, row, col, high, low):
+        height, width = high.shape
+        for k, part in enumerate((high, high, low)):
+            ref[row : row + height, k * n + col : k * n + col + width] = part
+
+    def put(i, j, x, left=None, right=None):
+        for i, j, x in ((i, j, x), (j, i, x.T))[: 1 + (i != j)]:
             high, low = halves(x)
-            cols = slice(j * half, (j + 1) * half)
-            if to_left:
-                put_left(height + i * half, j * half, high, low)
-            if to_right:
+            if left is not None:
+                put_left(left, i * half, j * half, high, low)
+            if right is not None:
                 for k, part in enumerate((high, low, high)):
-                    right[k * n + i * half : k * n + (i + 1) * half, cols] = part
-
-    def put_left(row, col, high, low):
-        rows, cols = high.shape
-        for k, part in enumerate((high, high, low)):
-            left[row : row + rows, k * n + col : k * n + col + cols] = part
-
-    def product():
-        upper = dot(left[height : height + half], right[...])
-        corner = dot(left[height + half :], right[:, half:])
-        return upper[:, :half], upper[:, half:], corner
-
-    def middle():
-        a = [a_ref[i] for i in range(3)]
-        spread(a, True, True)
-        y = product()
-        m = [coef_b * u + coef_c * v for u, v in zip(a, y)]
-        spread(m, False, True)
-        return m
-
-    def advance():
-        s = [coef_a * a_ref[i] + y for i, y in enumerate(product())]
-        for i in range(3):
-            s_ref[i] = s[i]
-        spread(s, True, False)
-        y = product()
-        for i in range(3):
-            a_ref[i] = coef_a * s_ref[i] + y[i]
-
-    def rows_times(q):
+                    right[k * n + i * half : k * n + (i + 1) * half, rows(j)] = part
+
+    def put_q(q):
+        q_ref[...] = q
         high, low = halves(q)
-        put_left(0, 0, high, low)
-        return dot(left[:height], right[...])
-
-    y = dot_transposed(x_ref[...], x_ref[half:])
-    gram = (dot_transposed(x_ref[:half], x_ref[:half]), y[:half], y[half:])
+        put_left(q_left, 0, 0, high, low)
+
+    def put_a(i, j, a):
+        a_ref[i + j] = a
+        put(i, j, a, a_left, a_right)
+
     eye = lax.broadcasted_iota(jnp.int32, (half, half), 0) == lax.broadcasted_iota(
         jnp.int32, (half, half), 1
     )
-    square = jnp.sum(jnp.where(eye, gram[0] + gram[2], 0.0), keepdims=True)
+    gram = {(i, j): dot_transposed(x_ref[rows(i)], x_ref[rows(j)]) for i, j in blocks}
+    square = jnp.sum(jnp.where(eye, gram[0, 0] + gram[1, 1], 0.0), keepdims=True)
     inverse = 1.0 / (jnp.sqrt(square) + 1e-07)
-    for i in range(3):
-        a_ref[i] = gram[i] * (inverse * inverse)
-
-    m = middle()
-    q_ref[:, :half] = (m[0] + jnp.where(eye, coef_a, 0.0))[:height]
-    q_ref[:, half:] = m[1][:height]
-    advance()
-
-    def step(_, carry):
-        middle()
-        advance()
-        q_ref[...] = coef_a * q_ref[...] + rows_times(q_ref[...])
-        return carry
-
-    lax.fori_loop(1, ITERS - 1, step, 0)
-    spread([a_ref[i] for i in range(3)], False, True)
+    for i, j in blocks:
+        put_a(i, j, gram[i, j] * (inverse * inverse))
+
+    for sweep in range(ITERS - 1):
+        for i, j in blocks:
+            m = coef_b * a_ref[i + j] + coef_c * dot(a_left[rows(i)], a_right[:, rows(j)])
+            put(i, j, m, right=m_right)
+            if sweep == 0 and i == 0:
+                p = m + jnp.where(eye, coef_a, 0.0) if j == 0 else m
+                q_ref[:, rows(j)] = p[:height]
+        for i, j in blocks:
+            s = coef_a * a_ref[i + j] + dot(a_left[rows(i)], m_right[:, rows(j)])
+            s_ref[i + j] = s
+            put(i, j, s, left=s_left)
+        q = q_ref[...]
+        put_q(coef_a * q + dot(q_left[...], m_right[...]) if sweep else q)
+        for i, j in blocks:
+            put_a(i, j, coef_a * s_ref[i + j] + dot(s_left[rows(i)], m_right[:, rows(j)]))
+
     q = q_ref[...]
-    q = coef_a * q + rows_times(coef_b * q + coef_c * rows_times(q))
+    high, low = halves(coef_b * q + coef_c * dot(q_left[...], a_right[...]))
+    put_left(s_left, 0, 0, high, low)
+    q = coef_a * q + dot(s_left[:height], a_right[...])
     spread_of_values = jnp.sum(q * q) * (1.0 / (height * n))
     good = spread_of_values < LIMIT
 
     @pl.when(good)
     def _():
         high, low = halves(q * (inverse * scale))
-        left[:height, :n] = high
-        left[:height, n : 2 * n] = low
+        q_left[:, :n] = high
+        q_left[:, n : 2 * n] = low
         block = min(width, 512)
         for at in range(0, width, block):
             x = x_ref[:, at : at + block]
             out_ref[:, at : at + block] = (
-                dot(left[:height, :n], x) + dot(left[:height, n : 2 * n], x)
+                dot(q_left[:, :n], x) + dot(q_left[:, n : 2 * n], x)
             ).astype(BF)
 
     @pl.when(jnp.logical_not(good))
@@ -261,8 +251,11 @@
             pltpu.VMEM((3, n // 2, n // 2), F32),
             pltpu.VMEM((3, n // 2, n // 2), F32),
             pltpu.VMEM((height, n), F32),
-            pltpu.VMEM((height + n, 3 * n), BF),
+            pltpu.VMEM((n, 3 * n), BF),
             pltpu.VMEM((3 * n, n), BF),
+            pltpu.VMEM((3 * n, n), BF),
+            pltpu.VMEM((n, 3 * n), BF),
+            pltpu.VMEM((height, 3 * n), BF),
             pltpu.VMEM((n, cols), F32),
         ],
         compiler_params=pltpu.CompilerParams(vmem_limit_bytes=40 * 2**20),
@@ -310,8 +303,6 @@
 
 def solution(mesh):
     n_rep = mesh.shape["rep"]
-    n_shard = mesh.shape["shard"]
-    order = [p // 2 + p % 2 * (n_shard // 2) if n_shard % 2 == 0 else p for p in range(n_shard)]
 
     def others(x):
         return [
@@ -320,9 +311,7 @@
         ]
 
     def exchange(x):
-        return lax.all_to_all(
-            x, "shard", split_axis=0, concat_axis=0, axis_index_groups=[order], tiled=True
-        )
+        return lax.all_to_all(x, "shard", split_axis=0, concat_axis=0, tiled=True)
 
     def shards(momentum, gradient):
         experts, rows, cols = momentum.shape

time: 90.1 us -> 89.5 us (level)
  no operation moved by 1% of the time
where the time goes in v6:
time: 89.5 us; the launch traced here: 89.2 us
  blocking collectives  65.2 us (73%)
  Pallas kernels  20.9 us (23%)
  waiting for transfers between devices  2.29 us (3%)
    all_to_all x2, blocking collectives, exchange(): return lax.all_to_all(x, 'shard', split_axis=0, concat_axis=0, tiled=True)  65.2 us
    pallas_call x1, Pallas kernels, orthogonal(): pl.pallas_call(functools.partial(orthogonal_kernel, scale), in_specs=[vme...  14.3 us
    pallas_call x1, Pallas kernels, blended_share(): pl.pallas_call(share_kernel, in_specs=[pl.BlockSpec(memory_space=pltpu.SM...  2.6 us
    ppermute x2, waiting for transfers between devices, others(): lax.ppermute(x, 'rep', [((i + j) % n_rep, i) for i in range(n_rep)])  2.29 us
    pallas_call x1, Pallas kernels, new_momentum_of(): pl.pallas_call(momentum_kernel, in_specs=[vmem, vmem], out_specs=vmem, ou...  2.01 us
    pallas_call x2, Pallas kernels, place(): pl.pallas_call(place_kernel, in_specs=[pl.BlockSpec(memory_space=pltpu.SM...  1.99 us
  transfers between devices with their start and end apart: 2, of which 2 were waited for; matrix products, arithmetic and copies ran while one was open for 0% of the time, Pallas kernels for 3%

profile of v6, /device:TPU:0, one launch (start us, length us, event | category | flops | bytes accessed | tf_op | source)
XLA Modules:
  0.0 89.2 jit_solution(8405167551981199529)
XLA Ops:
  0.6 0.0 copy-start.1
  0.6 2.6 %share.1 = bf16[16,16,2048]{2,1,0:T(8,128)(2,1)} custom-call(s32[1]{0:T(128)} %bitcast.rep_ref, bf16[16,32,2048]{2,1,0:T(8,128)(2,1)} %m_ref, bf16[16,32,2048]{2,1,0:T(8,128)(2,1)} %g_ref), custom_call_target="tpu_custom_call" | custom-call | tf_op jit(solution)/shard_map/share/pallas_call | solution.py:69
  3.2 0.0 copy-start
  3.3 34.8 %all_to_all.10 = bf16[16,16,2048]{2,1,0:T(8,128)(2,1)S(1)} all-to-all(bf16[16,16,2048]{2,1,0:T(8,128)(2,1)} %share.1), channel_id=1, replica_groups=mesh['shard'=16,'rep'=2] {'shard'}, dimensions={0} | all-to-all | bytes 2097152 | tf_op jit(solution)/shard_map/all_to_all | solution.py:314
  38.1 0.0 collective-permute-start
  38.1 0.0 copy-done.1
  38.1 0.0 copy-done
  38.1 2.0 %new_momentum.1 = bf16[16,32,2048]{2,1,0:T(8,128)(2,1)} custom-call(bf16[16,32,2048]{2,1,0:T(8,128)(2,1)S(1)} %copy-done, bf16[16,32,2048]{2,1,0:T(8,128)(2,1)S(1)} %copy-done.1), custom_call_target="tpu_custom_call" | custom-call | flops 2097152 | bytes 6291456 | tf_op jit(solution)/shard_map/new_momentum/pallas_call | solution.py:95
  40.1 0.6 collective-permute-done.refs_1_
  40.7 14.3 %orthogonal.1 = bf16[256,2048]{1,0:T(8,128)(2,1)S(1)} custom-call(bf16[256,2048]{1,0:T(8,128)(2,1)S(1)} %bitcast.6, bf16[256,2048]{1,0:T(8,128)(2,1)S(1)} %collective-permute-done.refs_1_), custom_call_target="tpu_custom_call" | custom-call | tf_op jit(solution)/shard_map/orthogonal/pallas_call | solution.py:244
  55.1 30.3 %all_to_all.11.part_ref = bf16[16,16,2048]{2,1,0:T(8,128)(2,1)S(1)} all-to-all(bf16[16,16,2048]{2,1,0:T(8,128)(2,1)S(1)} %bitcast.7), channel_id=1, replica_groups=mesh['shard'=16,'rep'=2] {'shard'}, dimensions={0} | all-to-all | bytes 2097152 | tf_op jit(solution)/shard_map/all_to_all | solution.py:314
  85.4 0.0 collective-permute-start.1
  85.4 1.0 %place.2.refs_0_ = bf16[16,32,2048]{2,1,0:T(8,128)(2,1)} custom-call(s32[1]{0:T(128)} %bitcast.4.rep_ref, bf16[16,16,2048]{2,1,0:T(8,128)(2,1)S(1)} %all_to_all.11.part_ref), custom_call_target="tpu_custom_call" | custom-call | bytes 2097152 | tf_op jit(solution)/shard_map/place/pallas_call | solution.py:289
  86.4 1.7 %collective-permute-done.1.part_ref = bf16[16,16,2048]{2,1,0:T(8,128)(2,1)S(1)} collective-permute-done((bf16[16,16,2048]{2,1,0:T(8,128)(2,1)S(1)}, bf16[16,16,2048]{2,1,0:T(8,128)(2,1)S(1)}, u32[]{:S(2)}, u32[]{:S(2)}) %collective-permute-start.1) | collective-permute-done | bytes 1048608 | tf_op jit(solution)/shard_map/ppermute | solution.py:309
  88.1 1.0 %place.3 = bf16[16,32,2048]{2,1,0:T(8,128)(2,1)} custom-call(s32[1]{0:T(128)} %bitcast.2.rep_ref, bf16[16,16,2048]{2,1,0:T(8,128)(2,1)S(1)} %collective-permute-done.1.part_ref, bf16[16,32,2048]{2,1,0:T(8,128)(2,1)} %place.2.refs_0_), custom_call_target="tpu_custom_call", output_to_operand_aliasing={{}: (2, {})} | custom-call | bytes 2097152 | tf_op jit(solution)/shard_map/place/pallas_call | solution.py:289
Async XLA Ops:
  0.6 37.5 %copy-start.1 = (bf16[16,32,2048]{2,1,0:T(8,128)(2,1)S(1)}, bf16[16,32,2048]{2,1,0:T(8,128)(2,1)}, u32[]{:S(2)}) copy-start(bf16[16,32,2048]{2,1,0:T(8,128)(2,1)} %g_ref) | copy-start | bytes 6291460
  3.2 34.8 %copy-start = (bf16[16,32,2048]{2,1,0:T(8,128)(2,1)S(1)}, bf16[16,32,2048]{2,1,0:T(8,128)(2,1)}, u32[]{:S(2)}) copy-start(bf16[16,32,2048]{2,1,0:T(8,128)(2,1)} %m_ref) | copy-start | bytes 6291460
  38.1 2.7 %collective-permute-start = (bf16[256,2048]{1,0:T(8,128)(2,1)S(1)}, bf16[256,2048]{1,0:T(8,128)(2,1)S(1)}, u32[]{:S(2)}, u32[]{:S(2)}) collective-permute-start(bf16[256,2048]{1,0:T(8,128)(2,1)S(1)} %bitcast.5), channel_id=1, source_target_pairs={{1,0},{0,1},{3,2},{2,3},{5,4},{4,5},{7,6},{6,7},{9,8},{8,9},{11,10... | collective-permute-start | bytes 3145736 | tf_op jit(solution)/shard_map/ppermute | solution.py:309
  85.4 2.7 %collective-permute-start.1 = (bf16[16,16,2048]{2,1,0:T(8,128)(2,1)S(1)}, bf16[16,16,2048]{2,1,0:T(8,128)(2,1)S(1)}, u32[]{:S(2)}, u32[]{:S(2)}) collective-permute-start(bf16[16,16,2048]{2,1,0:T(8,128)(2,1)S(1)} %all_to_all.11.part_ref), channel_id=1, source_target_pairs={{1,0},{0,1},{3,2},{2,3},{5,4},{4,5},{7,6},{6,7},{9,8},{8,9},{11,10... | collective-permute-start | bytes 3145736 | tf_op jit(solution)/shard_map/ppermute | solution.py:309

commit v7 on v6

--- a/solution.py
+++ b/solution.py
@@ -27,59 +27,44 @@
     return (g.astype(F32) + 0.95 * next_momentum(m, g).astype(F32)).astype(BF)
 
 
-def share_kernel(rep_ref, m_hbm, g_hbm, share_hbm, m_ref, g_ref, share_ref, sems):
-    experts, height, _ = share_ref.shape
-    chunks = sems.shape[1]
-    step = experts // chunks
-    rows = pl.ds(pl.multiple_of(rep_ref[0] * height, height), height)
+def share_kernel(at_ref, m_hbm, g_hbm, *refs):
+    *share_hbms, m_ref, g_ref, share_ref, sems = refs
+    count = len(share_hbms)
+    experts = m_hbm.shape[0]
     copies = []
-    for i in range(chunks):
-        at = pl.ds(i * step, step)
+    for j in range(count):
+        e = lax.rem(at_ref[0] + j * (experts // count), experts)
         copies.append(
             [
-                pltpu.make_async_copy(src.at[at, rows], dst.at[at], sems.at[j, i])
-                for j, (src, dst) in enumerate(((m_hbm, m_ref), (g_hbm, g_ref)))
+                pltpu.make_async_copy(src.at[e], dst.at[j], sems.at[i, j])
+                for i, (src, dst) in enumerate(((m_hbm, m_ref), (g_hbm, g_ref)))
             ]
         )
         for copy in copies[-1]:
             copy.start()
-    for i in range(chunks):
-        for copy in copies[i]:
+    for j, share_hbm in enumerate(share_hbms):
+        for copy in copies[j]:
             copy.wait()
-        at = slice(i * step, (i + 1) * step)
-        share_ref[at] = blend(m_ref[at], g_ref[at])
-        at = pl.ds(i * step, step)
-        copies[i] = pltpu.make_async_copy(share_ref.at[at], share_hbm.at[at], sems.at[2, i])
-        copies[i].start()
+        share_ref[j] = blend(m_ref[j], g_ref[j])
+        copies[j] = pltpu.make_async_copy(share_ref.at[j], share_hbm, sems.at[2, j])
+        copies[j].start()
     for copy in copies:
         copy.wait()
 
 
-def blended_share(rep, momentum, gradient, n_rep):
+def blended_share(first, momentum, gradient, count):
     experts, rows, cols = momentum.shape
-    height = rows // n_rep
-    shape = (experts, height, cols)
-    if height % 16:
-        m, g = (
-            lax.dynamic_slice_in_dim(x, rep * height, height, 1) for x in (momentum, gradient)
-        )
-        return blend(m, g)
-    chunks = 4 if experts % 4 == 0 else 1
     hbm = pl.BlockSpec(memory_space=pltpu.HBM)
     return pl.pallas_call(
         share_kernel,
         in_specs=[pl.BlockSpec(memory_space=pltpu.SMEM), hbm, hbm],
-        out_specs=hbm,
-        out_shape=jax.ShapeDtypeStruct(shape, BF),
-        scratch_shapes=[
-            pltpu.VMEM(shape, BF),
-            pltpu.VMEM(shape, BF),
-            pltpu.VMEM(shape, BF),
-            pltpu.SemaphoreType.DMA((3, chunks)),
-        ],
+        out_specs=[hbm] * count,
+        out_shape=[jax.ShapeDtypeStruct((rows, cols), BF)] * count,
+        scratch_shapes=[pltpu.VMEM((count, rows, cols), BF)] * 3
+        + [pltpu.SemaphoreType.DMA((3, count))],
         compiler_params=pltpu.CompilerParams(vmem_limit_bytes=60 * 2**20),
         name="share",
-    )(rep[None], momentum, gradient)
+    )(first[None], momentum, gradient)
 
 
 def momentum_kernel(m_ref, g_ref, new_ref):
@@ -120,14 +105,20 @@
     )
 
 
-def orthogonal_kernel(scale, *refs):
-    *parts, out_ref, x_ref, a_ref, s_ref, q_ref = refs[:-6]
+def orthogonal_kernel(scale, count, *refs):
+    *parts, x_ref, a_ref, s_ref, q_ref = refs[:-6]
+    parts, out_refs = parts[:-count], parts[-count:]
     a_left, a_right, m_right, s_left, q_left, full_ref = refs[-6:]
-    height, width = out_ref.shape
+    piece, width = out_refs[0].shape
+    height = count * piece
     n = x_ref.shape[0]
     half = n // 2
     for i, part in enumerate(parts):
-        x_ref[i * height : (i + 1) * height] = part[...]
+        x_ref[i * piece : (i + 1) * piece] = part[...]
+
+    def put_out(cols, y):
+        for i, out_ref in enumerate(out_refs):
+            out_ref[:, cols] = y[i * piece : (i + 1) * piece].astype(BF)
 
     blocks = ((0, 1), (0, 0), (1, 1))
 
@@ -197,9 +188,8 @@
         block = min(width, 512)
         for at in range(0, width, block):
             x = x_ref[:, at : at + block]
-            out_ref[:, at : at + block] = (
-                dot(q_left[:, :n], x) + dot(q_left[:, n : 2 * n], x)
-            ).astype(BF)
+            y = dot(q_left[:, :n], x) + dot(q_left[:, n : 2 * n], x)
+            put_out(slice(at, at + block), y)
 
     @pl.when(jnp.logical_not(good))
     def _():
@@ -229,7 +219,7 @@
             return lax.fori_loop(0, width // block, apply, carry)
 
         def store(i, carry):
-            out_ref[:, columns(i)] = (full_ref[:height, columns(i)] * scale).astype(BF)
+            put_out(columns(i), full_ref[:height, columns(i)] * scale)
             return carry
 
         lax.fori_loop(0, width // block, load, 0)
@@ -237,15 +227,16 @@
         lax.fori_loop(0, width // block, store, 0)
 
 
-def orthogonal(parts, scale):
-    height, cols = parts[0].shape
-    n = height * len(parts)
+def orthogonal(parts, count, scale):
+    piece, cols = parts[0].shape
+    height = piece * count
+    n = piece * len(parts)
     vmem = pl.BlockSpec(memory_space=pltpu.VMEM)
     return pl.pallas_call(
-        functools.partial(orthogonal_kernel, scale),
+        functools.partial(orthogonal_kernel, scale, count),
         in_specs=[vmem] * len(parts),
-        out_specs=vmem,
-        out_shape=jax.ShapeDtypeStruct((height, cols), BF),
+        out_specs=[vmem] * count,
+        out_shape=[jax.ShapeDtypeStruct((piece, cols), BF)] * count,
         scratch_shapes=[
             pltpu.VMEM((n, cols), BF),
             pltpu.VMEM((3, n // 2, n // 2), F32),
@@ -263,70 +254,83 @@
     )(*parts)
 
 
-def place_kernel(rep_ref, part_ref, *refs):
-    *_, out_ref, sems = refs
-    experts, height, _ = part_ref.shape
-    rows = pl.ds(pl.multiple_of(rep_ref[0] * height, height), height)
-    step = experts // sems.shape[0]
+def place_kernel(count, at_ref, *refs):
+    parts, (*_, out_ref, sems) = refs[:count], refs[count:]
+    experts = out_ref.shape[0]
     copies = []
-    for i in range(sems.shape[0]):
-        at = pl.ds(i * step, step)
-        copies.append(pltpu.make_async_copy(part_ref.at[at], out_ref.at[at, rows], sems.at[i]))
+    for j, part in enumerate(parts):
+        e = lax.rem(at_ref[0] + j * (experts // count), experts)
+        copies.append(pltpu.make_async_copy(part, out_ref.at[e], sems.at[j]))
         copies[-1].start()
     for copy in copies:
         copy.wait()
 
 
-def place(which, part, whole):
-    experts, height, cols = part.shape
-    if height % 16:
-        if isinstance(whole, tuple):
-            whole = jnp.zeros(whole, BF)
-        return lax.dynamic_update_slice(whole, part, (0, which * height, 0))
+def place(first, parts, whole):
+    count = len(parts)
     anywhere = pl.BlockSpec(memory_space=pl.ANY)
     hbm = pl.BlockSpec(memory_space=pltpu.HBM)
-    first = isinstance(whole, tuple)
+    new = isinstance(whole, tuple)
     return pl.pallas_call(
-        place_kernel,
-        in_specs=[pl.BlockSpec(memory_space=pltpu.SMEM), anywhere] + [hbm] * (not first),
+        functools.partial(place_kernel, count),
+        in_specs=[pl.BlockSpec(memory_space=pltpu.SMEM)] + [anywhere] * count + [hbm] * (not new),
         out_specs=hbm,
-        out_shape=jax.ShapeDtypeStruct(whole if first else whole.shape, BF),
-        scratch_shapes=[pltpu.SemaphoreType.DMA((4 if experts % 4 == 0 else 1,))],
-        input_output_aliases={} if first else {2: 0},
+        out_shape=jax.ShapeDtypeStruct(whole if new else whole.shape, BF),
+        scratch_shapes=[pltpu.SemaphoreType.DMA((count,))],
+        input_output_aliases={} if new else {count + 1: 0},
         cost_estimate=pl.CostEstimate(
-            flops=0, bytes_accessed=4 * part.size, transcendentals=0
+            flops=0, bytes_accessed=4 * count * parts[0].size, transcendentals=0
         ),
         compiler_params=pltpu.CompilerParams(vmem_limit_bytes=4 * 2**20),
         name="place",
-    )(which[None], part, *([] if first else [whole]))
+    )(first[None], *parts, *([] if new else [whole]))
 
 
 def solution(mesh):
     n_rep = mesh.shape["rep"]
-
-    def others(x):
-        return [
-            lax.ppermute(x, "rep", [((i + j) % n_rep, i) for i in range(n_rep)])
-            for j in range(1, n_rep)
-        ]
-
-    def exchange(x):
-        return lax.all_to_all(x, "shard", split_axis=0, concat_axis=0, tiled=True)
+    n_shard = mesh.shape["shard"]
+    count = n_shard // n_rep
+    middle = n_shard // 2
+    order = [p // 2 + p % 2 * middle for p in range(n_shard)]
+
+    def others(pieces):
+        pairs = [[((i + j) % n_rep, i) for i in range(n_rep)] for j in range(1, n_rep)]
+        return [[lax.ppermute(x, "rep", pair) for x in pieces] for pair in pairs]
+
+    def exchange(pieces, there):
+        moved = []
+        for j, x in enumerate(pieces):
+            pairs = [
+                (
+                    order[p] * n_rep + r,
+                    order[(p + j * n_rep + r) % n_shard] * n_rep + r,
+                )
+                for p in range(n_shard)
+                for r in range(n_rep)
+            ]
+            pairs = pairs if there else [pair[::-1] for pair in pairs]
+            moved.append(lax.ppermute(x, ("shard", "rep"), pairs))
+        return moved
 
     def shards(momentum, gradient):
         experts, rows, cols = momentum.shape
-        rep = lax.axis_index("rep")
-        share = exchange(blended_share(rep, momentum, gradient, n_rep))
-        own = share.reshape(-1, cols)
+        shard, rep = lax.axis_index("shard"), lax.axis_index("rep")
+        place_of = 2 * lax.rem(shard, middle) + shard // middle
+        own = exchange(
+            blended_share(lax.rem(place_of + rep, n_shard), momentum, gradient, count), True
+        )
         rest = others(own)
-        momentum, gradient, own = lax.optimization_barrier((momentum, gradient, own))
+        momentum, gradient, early = lax.optimization_barrier((momentum, gradient, own[1]))
         new_momentum = new_momentum_of(momentum, gradient)
-        rest, new_momentum = lax.optimization_barrier((rest, new_momentum))
+        own[1] = early
+        own[-1], new_momentum = lax.optimization_barrier((own[-1], new_momentum))
         scale = float(max(experts * rows, cols)) ** 0.5
-        update = exchange(orthogonal([own, *rest], scale).reshape(share.shape))
+        parts = own + [piece for pieces in rest for piece in pieces]
+        update = exchange(orthogonal(parts, count, scale), False)
         whole = (experts, rows, cols)
-        for j, part in enumerate([update, *others(update)]):
-            whole = place(lax.rem(rep + j, n_rep), part, whole)
+        for j, pieces in enumerate([update, *others(update)]):
+            first = lax.rem(place_of + lax.rem(rep + j, n_rep), n_shard)
+            whole = place(first, pieces, whole)
         return new_momentum, whole
 
     return jax.shard_map(

time: 89.5 us -> 82.5 us (0.922)
  the two profiles are of different devices: /device:TPU:0 before, /device:TPU:5 now
where the time goes in v7:
time: 82.5 us; the launch traced here: 82.3 us
  starting transfers between devices  33.5 us (41%)
  waiting for transfers between devices  25.2 us (31%)
  Pallas kernels  21.1 us (26%)
  local copies, waits for them, and re-layouts  1.6 us (2%)
  between operations  0.95 us (1%)
    ppermute x16, starting transfers between devices, exchange(): moved.append(lax.ppermute(x, ('shard', 'rep'), pairs))  31.5 us
    ppermute x16, waiting for transfers between devices, exchange(): moved.append(lax.ppermute(x, ('shard', 'rep'), pairs))  25.2 us
    pallas_call x1, Pallas kernels, orthogonal(): pl.pallas_call(functools.partial(orthogonal_kernel, scale, count), in_spe...  14.3 us
    pallas_call x1, Pallas kernels, blended_share(): pl.pallas_call(share_kernel, in_specs=[pl.BlockSpec(memory_space=pltpu.SM...  2.65 us
    ppermute x16, starting transfers between devices, others(): return [[lax.ppermute(x, 'rep', pair) for x in pieces] for pair in pairs]  2.06 us
    pallas_call x2, Pallas kernels, place(): pl.pallas_call(functools.partial(place_kernel, count), in_specs=[pl.Block...  2.06 us
    pallas_call x1, Pallas kernels, new_momentum_of(): pl.pallas_call(momentum_kernel, in_specs=[vmem, vmem], out_specs=vmem, ou...  2 us
  transfers between devices with their start and end apart: 32, of which 11 were waited for; matrix products, arithmetic and copies ran while one was open for 0% of the time, Pallas kernels for 4%

profile of v7, /device:TPU:5, one launch (start us, length us, event | category | flops | bytes accessed | tf_op | source)
XLA Modules:
  0.0 82.3 jit_solution(17282650716986452490)
XLA Ops:
  0.7 2.7 %share.1 = (bf16[32,2048]{1,0:T(8,128)(2,1)}, bf16[32,2048]{1,0:T(8,128)(2,1)}, bf16[32,2048]{1,0:T(8,128)(2,1)}, bf16[32,2048]{1,0:T(8,128)(2,1)}, bf16[32,2048...) custom-call(s32[1]{0:T(128)} %bitcast.at_ref, ...), custom_call_target="tpu_custom_call" | custom-call | tf_op jit(solution)/shard_map/share/pallas_call | solution.py:58
  3.3 3.2 %collective-permute-start = (bf16[32,2048]{1,0:T(8,128)(2,1)}, bf16[32,2048]{1,0:T(8,128)(2,1)S(1)}, u32[]{:S(2)}, u32[]{:S(2)}) collective-permute-start(bf16[32,2048]{1,0:T(8,128)(2,1)} %get-tuple-element.23), channel_id=1, source_target_pairs={{0,14},{1,31},{16,30},{17,1},{2,0},{3,17},{18,16},{19,3},{4,2},{5,... | collective-permute-start | bytes 393224 | tf_op jit(solution)/shard_map/ppermute | solution.py:312
  6.6 0.1 collective-permute-start.1
  6.7 4.2 %collective-permute-start.2 = (bf16[32,2048]{1,0:T(8,128)(2,1)}, bf16[32,2048]{1,0:T(8,128)(2,1)S(1)}, u32[]{:S(2)}, u32[]{:S(2)}) collective-permute-start(bf16[32,2048]{1,0:T(8,128)(2,1)} %get-tuple-element.28), channel_id=1, source_target_pairs={{0,0},{1,17},{16,16},{17,3},{2,2},{3,19},{18,18},{19,5},{4,4},{5,2... | collective-permute-start | bytes 393224 | tf_op jit(solution)/shard_map/ppermute | solution.py:312
  10.9 2.0 %collective-permute-start.3 = (bf16[32,2048]{1,0:T(8,128)(2,1)}, bf16[32,2048]{1,0:T(8,128)(2,1)S(1)}, u32[]{:S(2)}, u32[]{:S(2)}) collective-permute-start(bf16[32,2048]{1,0:T(8,128)(2,1)} %get-tuple-element.30), channel_id=1, source_target_pairs={{0,4},{1,21},{16,20},{17,7},{2,6},{3,23},{18,22},{19,9},{4,8},{5,2... | collective-permute-start | bytes 393224 | tf_op jit(solution)/shard_map/ppermute | solution.py:312
  12.9 3.1 %collective-permute-start.4 = (bf16[32,2048]{1,0:T(8,128)(2,1)}, bf16[32,2048]{1,0:T(8,128)(2,1)S(1)}, u32[]{:S(2)}, u32[]{:S(2)}) collective-permute-start(bf16[32,2048]{1,0:T(8,128)(2,1)} %get-tuple-element.31), channel_id=1, source_target_pairs={{0,6},{1,23},{16,22},{17,9},{2,8},{3,25},{18,24},{19,11},{4,10},{5... | collective-permute-start | bytes 393224 | tf_op jit(solution)/shard_map/ppermute | solution.py:312
  15.9 0.0 collective-permute-done.refs_7_
  15.9 0.2 collective-permute-start.5
  16.2 0.0 collective-permute-done.1.refs_1_
  16.2 4.7 %collective-permute-start.6 = (bf16[32,2048]{1,0:T(8,128)(2,1)}, bf16[32,2048]{1,0:T(8,128)(2,1)S(1)}, u32[]{:S(2)}, u32[]{:S(2)}) collective-permute-start(bf16[32,2048]{1,0:T(8,128)(2,1)} %get-tuple-element.33), channel_id=1, source_target_pairs={{0,10},{1,27},{16,26},{17,13},{2,12},{3,29},{18,28},{19,15},{4,14}... | collective-permute-start | bytes 393224 | tf_op jit(solution)/shard_map/ppermute | solution.py:312
  20.8 0.0 collective-permute-done.2.refs_0_
  20.8 0.5 collective-permute-done.3.refs_2_
  21.3 1.6 %collective-permute-done.4.refs_3_ = bf16[32,2048]{1,0:T(8,128)(2,1)S(1)} collective-permute-done((bf16[32,2048]{1,0:T(8,128)(2,1)}, bf16[32,2048]{1,0:T(8,128)(2,1)S(1)}, u32[]{:S(2)}, u32[]{:S(2)}) %collective-permute-start.4) | collective-permute-done | bytes 131104 | tf_op jit(solution)/shard_map/ppermute | solution.py:312
  23.0 2.8 %collective-permute-done.5.refs_4_ = bf16[32,2048]{1,0:T(8,128)(2,1)S(1)} collective-permute-done((bf16[32,2048]{1,0:T(8,128)(2,1)}, bf16[32,2048]{1,0:T(8,128)(2,1)S(1)}, u32[]{:S(2)}, u32[]{:S(2)}) %collective-permute-start.5) | collective-permute-done | bytes 131104 | tf_op jit(solution)/shard_map/ppermute | solution.py:312
  25.8 0.0 collective-permute-start.8
  25.8 0.5 collective-permute-done.6.refs_5_
  26.3 0.0 collective-permute-start.10
  26.3 5.6 %collective-permute-done.7.refs_6_ = bf16[32,2048]{1,0:T(8,128)(2,1)S(1)} collective-permute-done((bf16[32,2048]{1,0:T(8,128)(2,1)}, bf16[32,2048]{1,0:T(8,128)(2,1)S(1)}, u32[]{:S(2)}, u32[]{:S(2)}) %collective-permute-start.7) | collective-permute-done | bytes 131104 | tf_op jit(solution)/shard_map/ppermute | solution.py:312
  31.9 0.0 collective-permute-start.11
  31.9 0.0 collective-permute-done.15.refs_15_
  31.9 0.5 collective-permute-start.12
  32.4 0.0 collective-permute-done.9.refs_9_
  32.4 0.1 collective-permute-start.13
  32.5 0.0 collective-permute-done.8.refs_8_
  32.5 0.4 collective-permute-start.14
  33.0 1.6 %copy-done.1 = bf16[16,32,2048]{2,1,0:T(8,128)(2,1)S(1)} copy-done((bf16[16,32,2048]{2,1,0:T(8,128)(2,1)S(1)}, bf16[16,32,2048]{2,1,0:T(8,128)(2,1)}, u32[]{:S(2)}) %copy-start.1) | copy-done | bytes 2097176
  34.6 2.0 %new_momentum.1 = bf16[16,32,2048]{2,1,0:T(8,128)(2,1)} custom-call(bf16[16,32,2048]{2,1,0:T(8,128)(2,1)S(1)} %copy-done, bf16[16,32,2048]{2,1,0:T(8,128)(2,1)S(1)} %copy-done.1), custom_call_target="tpu_custom_call" | custom-call | flops 2097152 | bytes 6291456 | tf_op jit(solution)/shard_map/new_momentum/pallas_call | solution.py:80
  36.6 0.0 collective-permute-done.10.refs_10_
  36.6 14.3 %orthogonal.1 = (bf16[32,2048]{1,0:T(8,128)(2,1)S(1)}, bf16[32,2048]{1,0:T(8,128)(2,1)S(1)}, bf16[32,2048]{1,0:T(8,128)(2,1)S(1)}, bf16[32,2048]{1,0:T(8,128)(2,...) custom-call(bf16[32,2048]{1,0:T(8,128)(2,1)S(1)} %collective-permute, ...), custom_call_target="tpu_custom_call" | custom-call | tf_op jit(solution)/shard_map/orthogonal/pallas_call | solution.py:235
  51.0 2.3 %collective-permute-start.16 = (bf16[32,2048]{1,0:T(8,128)(2,1)S(1)}, bf16[32,2048]{1,0:T(8,128)(2,1)S(1)}, u32[]{:S(2)}, u32[]{:S(2)}) collective-permute-start(bf16[32,2048]{1,0:T(8,128)(2,1)S(1)} %get-tuple-element.36), channel_id=1, source_target_pairs={{0,0},{17,1},{16,16},{3,17},{2,2},{19,3},{18,18},{5,19},{4,4},{21,... | collective-permute-start | bytes 393224 | tf_op jit(solution)/shard_map/ppermute | solution.py:312
  53.3 1.6 %collective-permute-start.18 = (bf16[32,2048]{1,0:T(8,128)(2,1)S(1)}, bf16[32,2048]{1,0:T(8,128)(2,1)S(1)}, u32[]{:S(2)}, u32[]{:S(2)}) collective-permute-start(bf16[32,2048]{1,0:T(8,128)(2,1)S(1)} %get-tuple-element.37), channel_id=1, source_target_pairs={{2,0},{19,1},{18,16},{5,17},{4,2},{21,3},{20,18},{7,19},{6,4},{23,... | collective-permute-start | bytes 393224 | tf_op jit(solution)/shard_map/ppermute | solution.py:312
  54.8 3.8 %collective-permute-start.20 = (bf16[32,2048]{1,0:T(8,128)(2,1)S(1)}, bf16[32,2048]{1,0:T(8,128)(2,1)S(1)}, u32[]{:S(2)}, u32[]{:S(2)}) collective-permute-start(bf16[32,2048]{1,0:T(8,128)(2,1)S(1)} %get-tuple-element.38), channel_id=1, source_target_pairs={{4,0},{21,1},{20,16},{7,17},{6,2},{23,3},{22,18},{9,19},{8,4},{25,... | collective-permute-start | bytes 393224 | tf_op jit(solution)/shard_map/ppermute | solution.py:312
  58.7 0.4 collective-permute-start.22
  59.1 4.7 %collective-permute-start.24 = (bf16[32,2048]{1,0:T(8,128)(2,1)S(1)}, bf16[32,2048]{1,0:T(8,128)(2,1)S(1)}, u32[]{:S(2)}, u32[]{:S(2)}) collective-permute-start(bf16[32,2048]{1,0:T(8,128)(2,1)S(1)} %get-tuple-element.40), channel_id=1, source_target_pairs={{8,0},{25,1},{24,16},{11,17},{10,2},{27,3},{26,18},{13,19},{12,4},... | collective-permute-start | bytes 393224 | tf_op jit(solution)/shard_map/ppermute | solution.py:312
  63.8 0.4 collective-permute-start.26
  64.1 0.2 collective-permute-start.28
  64.4 1.7 %collective-permute-done.20.refs_2_ = bf16[32,2048]{1,0:T(8,128)(2,1)S(1)} collective-permute-done((bf16[32,2048]{1,0:T(8,128)(2,1)S(1)}, bf16[32,2048]{1,0:T(8,128)(2,1)S(1)}, u32[]{:S(2)}, u32[]{:S(2)}) %collective-permute-start.20) | collective-permute-done | bytes 131104 | tf_op jit(solution)/shard_map/ppermute | solution.py:312
  66.1 0.6 collective-permute-start.30
  66.7 1.0 %collective-permute-done.22.refs_3_ = bf16[32,2048]{1,0:T(8,128)(2,1)S(1)} collective-permute-done((bf16[32,2048]{1,0:T(8,128)(2,1)S(1)}, bf16[32,2048]{1,0:T(8,128)(2,1)S(1)}, u32[]{:S(2)}, u32[]{:S(2)}) %collective-permute-start.22) | collective-permute-done | bytes 131104 | tf_op jit(solution)/shard_map/ppermute | solution.py:312
  67.7 2.1 %collective-permute-done.24.refs_4_ = bf16[32,2048]{1,0:T(8,128)(2,1)S(1)} collective-permute-done((bf16[32,2048]{1,0:T(8,128)(2,1)S(1)}, bf16[32,2048]{1,0:T(8,128)(2,1)S(1)}, u32[]{:S(2)}, u32[]{:S(2)}) %collective-permute-start.24) | collective-permute-done | bytes 131104 | tf_op jit(solution)/shard_map/ppermute | solution.py:312
  69.7 2.5 %collective-permute-done.26.refs_5_ = bf16[32,2048]{1,0:T(8,128)(2,1)S(1)} collective-permute-done((bf16[32,2048]{1,0:T(8,128)(2,1)S(1)}, bf16[32,2048]{1,0:T(8,128)(2,1)S(1)}, u32[]{:S(2)}, u32[]{:S(2)}) %collective-permute-start.26) | collective-permute-done | bytes 131104 | tf_op jit(solution)/shard_map/ppermute | solution.py:312
  72.3 4.5 %collective-permute-done.28.refs_6_ = bf16[32,2048]{1,0:T(8,128)(2,1)S(1)} collective-permute-done((bf16[32,2048]{1,0:T(8,128)(2,1)S(1)}, bf16[32,2048]{1,0:T(8,128)(2,1)S(1)}, u32[]{:S(2)}, u32[]{:S(2)}) %collective-permute-start.28) | collective-permute-done | bytes 131104 | tf_op jit(solution)/shard_map/ppermute | solution.py:312
  76.8 2.2 %collective-permute-done.30.refs_7_ = bf16[32,2048]{1,0:T(8,128)(2,1)S(1)} collective-permute-done((bf16[32,2048]{1,0:T(8,128)(2,1)S(1)}, bf16[32,2048]{1,0:T(8,128)(2,1)S(1)}, u32[]{:S(2)}, u32[]{:S(2)}) %collective-permute-start.30) | collective-permute-done | bytes 131104 | tf_op jit(solution)/shard_map/ppermute | solution.py:312
  79.0 0.5 collective-permute-start.27
  79.6 0.1 collective-permute-start.29
  79.6 0.4 collective-permute-start.31
  80.1 1.0 %place.2.refs_8_ = bf16[16,32,2048]{2,1,0:T(8,128)(2,1)} custom-call(s32[1]{0:T(128)} %bitcast.2.at_ref, bf16[32,2048]{1,0:T(8,128)(2,1)S(1)} %collective-permute-done.16.refs_0_, bf16[32,2048]{1,0:T(8,128)(2,1)S(1)} %collective-permute-done.18.refs_1_, bf16[32,2048]{1,0:T(8,128)(2,1)S(1)} %collective-permute-done.20.refs_2_, ...), custom_call_target="tpu_custom_call" | custom-call | bytes 2097152 | tf_op jit(solution)/shard_map/place/pallas_call | solution.py:274
  81.2 1.0 %place.3 = bf16[16,32,2048]{2,1,0:T(8,128)(2,1)} custom-call(s32[1]{0:T(128)} %bitcast.1.at_ref, bf16[32,2048]{1,0:T(8,128)(2,1)S(1)} %collective-permute-done.17.refs_0_, bf16[32,2048]{1,0:T(8,128)(2,1)S(1)} %collective-permute-done.19.refs_1_, bf16[32,2048]{1,0:T(8,128)(2,1)S(1)} %collective-permute-done.21.refs_2_, ...), custom_call_target="tpu_custom_call", output_to_operand_aliasing={{}: (9, {})} | custom-call | bytes 2097152 | tf_op jit(solution)/shard_map/place/pallas_call | solution.py:274
  (25 shorter events, 0.1 us)
Async XLA Ops:
  0.7 32.3 %copy-start = (bf16[16,32,2048]{2,1,0:T(8,128)(2,1)S(1)}, bf16[16,32,2048]{2,1,0:T(8,128)(2,1)}, u32[]{:S(2)}) copy-start(bf16[16,32,2048]{2,1,0:T(8,128)(2,1)} %m_ref) | copy-start | bytes 6291460
  3.3 12.6 %collective-permute-start = (bf16[32,2048]{1,0:T(8,128)(2,1)}, bf16[32,2048]{1,0:T(8,128)(2,1)S(1)}, u32[]{:S(2)}, u32[]{:S(2)}) collective-permute-start(bf16[32,2048]{1,0:T(8,128)(2,1)} %get-tuple-element.23), channel_id=1, source_target_pairs={{0,14},{1,31},{16,30},{17,1},{2,0},{3,17},{18,16},{19,3},{4,2},{5,... | collective-permute-start | bytes 393224 | tf_op jit(solution)/shard_map/ppermute | solution.py:312
  6.6 9.6 %collective-permute-start.1 = (bf16[32,2048]{1,0:T(8,128)(2,1)}, bf16[32,2048]{1,0:T(8,128)(2,1)S(1)}, u32[]{:S(2)}, u32[]{:S(2)}) collective-permute-start(bf16[32,2048]{1,0:T(8,128)(2,1)} %get-tuple-element.24), channel_id=1, source_target_pairs={{0,2},{1,19},{16,18},{17,5},{2,4},{3,21},{18,20},{19,7},{4,6},{5,2... | collective-permute-start | bytes 393224 | tf_op jit(solution)/shard_map/ppermute | solution.py:312
  6.7 14.1 %collective-permute-start.2 = (bf16[32,2048]{1,0:T(8,128)(2,1)}, bf16[32,2048]{1,0:T(8,128)(2,1)S(1)}, u32[]{:S(2)}, u32[]{:S(2)}) collective-permute-start(bf16[32,2048]{1,0:T(8,128)(2,1)} %get-tuple-element.28), channel_id=1, source_target_pairs={{0,0},{1,17},{16,16},{17,3},{2,2},{3,19},{18,18},{19,5},{4,4},{5,2... | collective-permute-start | bytes 393224 | tf_op jit(solution)/shard_map/ppermute | solution.py:312
  10.9 10.4 %collective-permute-start.3 = (bf16[32,2048]{1,0:T(8,128)(2,1)}, bf16[32,2048]{1,0:T(8,128)(2,1)S(1)}, u32[]{:S(2)}, u32[]{:S(2)}) collective-permute-start(bf16[32,2048]{1,0:T(8,128)(2,1)} %get-tuple-element.30), channel_id=1, source_target_pairs={{0,4},{1,21},{16,20},{17,7},{2,6},{3,23},{18,22},{19,9},{4,8},{5,2... | collective-permute-start | bytes 393224 | tf_op jit(solution)/shard_map/ppermute | solution.py:312
  12.9 10.1 %collective-permute-start.4 = (bf16[32,2048]{1,0:T(8,128)(2,1)}, bf16[32,2048]{1,0:T(8,128)(2,1)S(1)}, u32[]{:S(2)}, u32[]{:S(2)}) collective-permute-start(bf16[32,2048]{1,0:T(8,128)(2,1)} %get-tuple-element.31), channel_id=1, source_target_pairs={{0,6},{1,23},{16,22},{17,9},{2,8},{3,25},{18,24},{19,11},{4,10},{5... | collective-permute-start | bytes 393224 | tf_op jit(solution)/shard_map/ppermute | solution.py:312
  15.9 9.8 %collective-permute-start.5 = (bf16[32,2048]{1,0:T(8,128)(2,1)}, bf16[32,2048]{1,0:T(8,128)(2,1)S(1)}, u32[]{:S(2)}, u32[]{:S(2)}) collective-permute-start(bf16[32,2048]{1,0:T(8,128)(2,1)} %get-tuple-element.32), channel_id=1, source_target_pairs={{0,8},{1,25},{16,24},{17,11},{2,10},{3,27},{18,26},{19,13},{4,12},... | collective-permute-start | bytes 393224 | tf_op jit(solution)/shard_map/ppermute | solution.py:312
  16.2 10.1 %collective-permute-start.6 = (bf16[32,2048]{1,0:T(8,128)(2,1)}, bf16[32,2048]{1,0:T(8,128)(2,1)S(1)}, u32[]{:S(2)}, u32[]{:S(2)}) collective-permute-start(bf16[32,2048]{1,0:T(8,128)(2,1)} %get-tuple-element.33), channel_id=1, source_target_pairs={{0,10},{1,27},{16,26},{17,13},{2,12},{3,29},{18,28},{19,15},{4,14}... | collective-permute-start | bytes 393224 | tf_op jit(solution)/shard_map/ppermute | solution.py:312
  20.8 11.1 %collective-permute-start.7 = (bf16[32,2048]{1,0:T(8,128)(2,1)}, bf16[32,2048]{1,0:T(8,128)(2,1)S(1)}, u32[]{:S(2)}, u32[]{:S(2)}) collective-permute-start(bf16[32,2048]{1,0:T(8,128)(2,1)} %get-tuple-element.34), channel_id=1, source_target_pairs={{0,12},{1,29},{16,28},{17,15},{2,14},{3,31},{18,30},{19,1},{4,0},{... | collective-permute-start | bytes 393224 | tf_op jit(solution)/shard_map/ppermute | solution.py:312
  21.3 10.6 %collective-permute-start.15 = (bf16[32,2048]{1,0:T(8,128)(2,1)S(1)}, bf16[32,2048]{1,0:T(8,128)(2,1)S(1)}, u32[]{:S(2)}, u32[]{:S(2)}) collective-permute-start(bf16[32,2048]{1,0:T(8,128)(2,1)S(1)} %collective-permute-done.refs_7_), channel_id=1, source_target_pairs={{1,0},{0,1},{3,2},{2,3},{5,4},{4,5},{7,6},{6,7},{9,8},{8,9},{11,10... | collective-permute-start | bytes 393224 | tf_op jit(solution)/shard_map/ppermute | solution.py:298
  22.9 9.5 %collective-permute-start.9 = (bf16[32,2048]{1,0:T(8,128)(2,1)S(1)}, bf16[32,2048]{1,0:T(8,128)(2,1)S(1)}, u32[]{:S(2)}, u32[]{:S(2)}) collective-permute-start(bf16[32,2048]{1,0:T(8,128)(2,1)S(1)} %collective-permute-done.1.refs_1_), channel_id=1, source_target_pairs={{1,0},{0,1},{3,2},{2,3},{5,4},{4,5},{7,6},{6,7},{9,8},{8,9},{11,10... | collective-permute-start | bytes 393224 | tf_op jit(solution)/shard_map/ppermute | solution.py:298
  25.8 6.8 %collective-permute-start.8 = (bf16[32,2048]{1,0:T(8,128)(2,1)S(1)}, bf16[32,2048]{1,0:T(8,128)(2,1)S(1)}, u32[]{:S(2)}, u32[]{:S(2)}) collective-permute-start(bf16[32,2048]{1,0:T(8,128)(2,1)S(1)} %collective-permute-done.2.refs_0_), channel_id=1, source_target_pairs={{1,0},{0,1},{3,2},{2,3},{5,4},{4,5},{7,6},{6,7},{9,8},{8,9},{11,10... | collective-permute-start | bytes 393224 | tf_op jit(solution)/shard_map/ppermute | solution.py:298
  26.3 10.3 %collective-permute-start.10 = (bf16[32,2048]{1,0:T(8,128)(2,1)S(1)}, bf16[32,2048]{1,0:T(8,128)(2,1)S(1)}, u32[]{:S(2)}, u32[]{:S(2)}) collective-permute-start(bf16[32,2048]{1,0:T(8,128)(2,1)S(1)} %collective-permute-done.3.refs_2_), channel_id=1, source_target_pairs={{1,0},{0,1},{3,2},{2,3},{5,4},{4,5},{7,6},{6,7},{9,8},{8,9},{11,10... | collective-permute-start | bytes 393224 | tf_op jit(solution)/shard_map/ppermute | solution.py:298
  31.9 4.6 %collective-permute-start.11 = (bf16[32,2048]{1,0:T(8,128)(2,1)S(1)}, bf16[32,2048]{1,0:T(8,128)(2,1)S(1)}, u32[]{:S(2)}, u32[]{:S(2)}) collective-permute-start(bf16[32,2048]{1,0:T(8,128)(2,1)S(1)} %collective-permute-done.4.refs_3_), channel_id=1, source_target_pairs={{1,0},{0,1},{3,2},{2,3},{5,4},{4,5},{7,6},{6,7},{9,8},{8,9},{11,10... | collective-permute-start | bytes 393224 | tf_op jit(solution)/shard_map/ppermute | solution.py:298
  31.9 4.6 %collective-permute-start.12 = (bf16[32,2048]{1,0:T(8,128)(2,1)S(1)}, bf16[32,2048]{1,0:T(8,128)(2,1)S(1)}, u32[]{:S(2)}, u32[]{:S(2)}) collective-permute-start(bf16[32,2048]{1,0:T(8,128)(2,1)S(1)} %collective-permute-done.5.refs_4_), channel_id=1, source_target_pairs={{1,0},{0,1},{3,2},{2,3},{5,4},{4,5},{7,6},{6,7},{9,8},{8,9},{11,10... | collective-permute-start | bytes 393224 | tf_op jit(solution)/shard_map/ppermute | solution.py:298
  32.4 4.1 %collective-permute-start.13 = (bf16[32,2048]{1,0:T(8,128)(2,1)S(1)}, bf16[32,2048]{1,0:T(8,128)(2,1)S(1)}, u32[]{:S(2)}, u32[]{:S(2)}) collective-permute-start(bf16[32,2048]{1,0:T(8,128)(2,1)S(1)} %collective-permute-done.6.refs_5_), channel_id=1, source_target_pairs={{1,0},{0,1},{3,2},{2,3},{5,4},{4,5},{7,6},{6,7},{9,8},{8,9},{11,10... | collective-permute-start | bytes 393224 | tf_op jit(solution)/shard_map/ppermute | solution.py:298
  32.5 4.1 %collective-permute-start.14 = (bf16[32,2048]{1,0:T(8,128)(2,1)S(1)}, bf16[32,2048]{1,0:T(8,128)(2,1)S(1)}, u32[]{:S(2)}, u32[]{:S(2)}) collective-permute-start(bf16[32,2048]{1,0:T(8,128)(2,1)S(1)} %collective-permute-done.7.refs_6_), channel_id=1, source_target_pairs={{1,0},{0,1},{3,2},{2,3},{5,4},{4,5},{7,6},{6,7},{9,8},{8,9},{11,10... | collective-permute-start | bytes 393224 | tf_op jit(solution)/shard_map/ppermute | solution.py:298
  33.0 1.6 %copy-start.1 = (bf16[16,32,2048]{2,1,0:T(8,128)(2,1)S(1)}, bf16[16,32,2048]{2,1,0:T(8,128)(2,1)}, u32[]{:S(2)}) copy-start(bf16[16,32,2048]{2,1,0:T(8,128)(2,1)} %g_ref) | copy-start | bytes 6291460
  51.0 12.8 %collective-permute-start.16 = (bf16[32,2048]{1,0:T(8,128)(2,1)S(1)}, bf16[32,2048]{1,0:T(8,128)(2,1)S(1)}, u32[]{:S(2)}, u32[]{:S(2)}) collective-permute-start(bf16[32,2048]{1,0:T(8,128)(2,1)S(1)} %get-tuple-element.36), channel_id=1, source_target_pairs={{0,0},{17,1},{16,16},{3,17},{2,2},{19,3},{18,18},{5,19},{4,4},{21,... | collective-permute-start | bytes 393224 | tf_op jit(solution)/shard_map/ppermute | solution.py:312
  53.3 10.9 %collective-permute-start.18 = (bf16[32,2048]{1,0:T(8,128)(2,1)S(1)}, bf16[32,2048]{1,0:T(8,128)(2,1)S(1)}, u32[]{:S(2)}, u32[]{:S(2)}) collective-permute-start(bf16[32,2048]{1,0:T(8,128)(2,1)S(1)} %get-tuple-element.37), channel_id=1, source_target_pairs={{2,0},{19,1},{18,16},{5,17},{4,2},{21,3},{20,18},{7,19},{6,4},{23,... | collective-permute-start | bytes 393224 | tf_op jit(solution)/shard_map/ppermute | solution.py:312
  54.8 11.3 %collective-permute-start.20 = (bf16[32,2048]{1,0:T(8,128)(2,1)S(1)}, bf16[32,2048]{1,0:T(8,128)(2,1)S(1)}, u32[]{:S(2)}, u32[]{:S(2)}) collective-permute-start(bf16[32,2048]{1,0:T(8,128)(2,1)S(1)} %get-tuple-element.38), channel_id=1, source_target_pairs={{4,0},{21,1},{20,16},{7,17},{6,2},{23,3},{22,18},{9,19},{8,4},{25,... | collective-permute-start | bytes 393224 | tf_op jit(solution)/shard_map/ppermute | solution.py:312
  58.7 9.0 %collective-permute-start.22 = (bf16[32,2048]{1,0:T(8,128)(2,1)S(1)}, bf16[32,2048]{1,0:T(8,128)(2,1)S(1)}, u32[]{:S(2)}, u32[]{:S(2)}) collective-permute-start(bf16[32,2048]{1,0:T(8,128)(2,1)S(1)} %get-tuple-element.39), channel_id=1, source_target_pairs={{6,0},{23,1},{22,16},{9,17},{8,2},{25,3},{24,18},{11,19},{10,4},{2... | collective-permute-start | bytes 393224 | tf_op jit(solution)/shard_map/ppermute | solution.py:312
  59.1 10.7 %collective-permute-start.24 = (bf16[32,2048]{1,0:T(8,128)(2,1)S(1)}, bf16[32,2048]{1,0:T(8,128)(2,1)S(1)}, u32[]{:S(2)}, u32[]{:S(2)}) collective-permute-start(bf16[32,2048]{1,0:T(8,128)(2,1)S(1)} %get-tuple-element.40), channel_id=1, source_target_pairs={{8,0},{25,1},{24,16},{11,17},{10,2},{27,3},{26,18},{13,19},{12,4},... | collective-permute-start | bytes 393224 | tf_op jit(solution)/shard_map/ppermute | solution.py:312
  63.8 8.5 %collective-permute-start.26 = (bf16[32,2048]{1,0:T(8,128)(2,1)S(1)}, bf16[32,2048]{1,0:T(8,128)(2,1)S(1)}, u32[]{:S(2)}, u32[]{:S(2)}) collective-permute-start(bf16[32,2048]{1,0:T(8,128)(2,1)S(1)} %get-tuple-element.41), channel_id=1, source_target_pairs={{10,0},{27,1},{26,16},{13,17},{12,2},{29,3},{28,18},{15,19},{14,4}... | collective-permute-start | bytes 393224 | tf_op jit(solution)/shard_map/ppermute | solution.py:312
  64.1 12.7 %collective-permute-start.28 = (bf16[32,2048]{1,0:T(8,128)(2,1)S(1)}, bf16[32,2048]{1,0:T(8,128)(2,1)S(1)}, u32[]{:S(2)}, u32[]{:S(2)}) collective-permute-start(bf16[32,2048]{1,0:T(8,128)(2,1)S(1)} %get-tuple-element.42), channel_id=1, source_target_pairs={{12,0},{29,1},{28,16},{15,17},{14,2},{31,3},{30,18},{1,19},{0,4},{... | collective-permute-start | bytes 393224 | tf_op jit(solution)/shard_map/ppermute | solution.py:312
  66.1 12.9 %collective-permute-start.30 = (bf16[32,2048]{1,0:T(8,128)(2,1)S(1)}, bf16[32,2048]{1,0:T(8,128)(2,1)S(1)}, u32[]{:S(2)}, u32[]{:S(2)}) collective-permute-start(bf16[32,2048]{1,0:T(8,128)(2,1)S(1)} %get-tuple-element.43), channel_id=1, source_target_pairs={{14,0},{31,1},{30,16},{1,17},{0,2},{17,3},{16,18},{3,19},{2,4},{19... | collective-permute-start | bytes 393224 | tf_op jit(solution)/shard_map/ppermute | solution.py:312
  67.6 11.4 %collective-permute-start.17 = (bf16[32,2048]{1,0:T(8,128)(2,1)S(1)}, bf16[32,2048]{1,0:T(8,128)(2,1)S(1)}, u32[]{:S(2)}, u32[]{:S(2)}) collective-permute-start(bf16[32,2048]{1,0:T(8,128)(2,1)S(1)} %collective-permute-done.16.refs_0_), channel_id=1, source_target_pairs={{1,0},{0,1},{3,2},{2,3},{5,4},{4,5},{7,6},{6,7},{9,8},{8,9},{11,10... | collective-permute-start | bytes 393224 | tf_op jit(solution)/shard_map/ppermute | solution.py:298
  69.7 9.8 %collective-permute-start.19 = (bf16[32,2048]{1,0:T(8,128)(2,1)S(1)}, bf16[32,2048]{1,0:T(8,128)(2,1)S(1)}, u32[]{:S(2)}, u32[]{:S(2)}) collective-permute-start(bf16[32,2048]{1,0:T(8,128)(2,1)S(1)} %collective-permute-done.18.refs_1_), channel_id=1, source_target_pairs={{1,0},{0,1},{3,2},{2,3},{5,4},{4,5},{7,6},{6,7},{9,8},{8,9},{11,10... | collective-permute-start | bytes 393224 | tf_op jit(solution)/shard_map/ppermute | solution.py:298
  72.3 7.4 %collective-permute-start.21 = (bf16[32,2048]{1,0:T(8,128)(2,1)S(1)}, bf16[32,2048]{1,0:T(8,128)(2,1)S(1)}, u32[]{:S(2)}, u32[]{:S(2)}) collective-permute-start(bf16[32,2048]{1,0:T(8,128)(2,1)S(1)} %collective-permute-done.20.refs_2_), channel_id=1, source_target_pairs={{1,0},{0,1},{3,2},{2,3},{5,4},{4,5},{7,6},{6,7},{9,8},{8,9},{11,10... | collective-permute-start | bytes 393224 | tf_op jit(solution)/shard_map/ppermute | solution.py:298
  76.8 4.3 %collective-permute-start.23 = (bf16[32,2048]{1,0:T(8,128)(2,1)S(1)}, bf16[32,2048]{1,0:T(8,128)(2,1)S(1)}, u32[]{:S(2)}, u32[]{:S(2)}) collective-permute-start(bf16[32,2048]{1,0:T(8,128)(2,1)S(1)} %collective-permute-done.22.refs_3_), channel_id=1, source_target_pairs={{1,0},{0,1},{3,2},{2,3},{5,4},{4,5},{7,6},{6,7},{9,8},{8,9},{11,10... | collective-permute-start | bytes 393224 | tf_op jit(solution)/shard_map/ppermute | solution.py:298
  79.0 2.1 %collective-permute-start.25 = (bf16[32,2048]{1,0:T(8,128)(2,1)S(1)}, bf16[32,2048]{1,0:T(8,128)(2,1)S(1)}, u32[]{:S(2)}, u32[]{:S(2)}) collective-permute-start(bf16[32,2048]{1,0:T(8,128)(2,1)S(1)} %collective-permute-done.24.refs_4_), channel_id=1, source_target_pairs={{1,0},{0,1},{3,2},{2,3},{5,4},{4,5},{7,6},{6,7},{9,8},{8,9},{11,10... | collective-permute-start | bytes 393224 | tf_op jit(solution)/shard_map/ppermute | solution.py:298
  79.0 2.1 %collective-permute-start.27 = (bf16[32,2048]{1,0:T(8,128)(2,1)S(1)}, bf16[32,2048]{1,0:T(8,128)(2,1)S(1)}, u32[]{:S(2)}, u32[]{:S(2)}) collective-permute-start(bf16[32,2048]{1,0:T(8,128)(2,1)S(1)} %collective-permute-done.26.refs_5_), channel_id=1, source_target_pairs={{1,0},{0,1},{3,2},{2,3},{5,4},{4,5},{7,6},{6,7},{9,8},{8,9},{11,10... | collective-permute-start | bytes 393224 | tf_op jit(solution)/shard_map/ppermute | solution.py:298
  79.6 1.6 %collective-permute-start.29 = (bf16[32,2048]{1,0:T(8,128)(2,1)S(1)}, bf16[32,2048]{1,0:T(8,128)(2,1)S(1)}, u32[]{:S(2)}, u32[]{:S(2)}) collective-permute-start(bf16[32,2048]{1,0:T(8,128)(2,1)S(1)} %collective-permute-done.28.refs_6_), channel_id=1, source_target_pairs={{1,0},{0,1},{3,2},{2,3},{5,4},{4,5},{7,6},{6,7},{9,8},{8,9},{11,10... | collective-permute-start | bytes 393224 | tf_op jit(solution)/shard_map/ppermute | solution.py:298
  79.6 1.5 %collective-permute-start.31 = (bf16[32,2048]{1,0:T(8,128)(2,1)S(1)}, bf16[32,2048]{1,0:T(8,128)(2,1)S(1)}, u32[]{:S(2)}, u32[]{:S(2)}) collective-permute-start(bf16[32,2048]{1,0:T(8,128)(2,1)S(1)} %collective-permute-done.30.refs_7_), channel_id=1, source_target_pairs={{1,0},{0,1},{3,2},{2,3},{5,4},{4,5},{7,6},{6,7},{9,8},{8,9},{11,10... | collective-permute-start | bytes 393224 | tf_op jit(solution)/shard_map/ppermute | solution.py:298

commit v8 on v7

--- a/solution.py
+++ b/solution.py
@@ -27,13 +27,21 @@
     return (g.astype(F32) + 0.95 * next_momentum(m, g).astype(F32)).astype(BF)
 
 
+def distance(core, j, n_rep):
+    return j * n_rep + (core + j) % n_rep
+
+
+def expert(place, core, j, n_rep, experts):
+    return lax.rem(place + j * n_rep + lax.rem(core + j, n_rep), experts)
+
+
 def share_kernel(at_ref, m_hbm, g_hbm, *refs):
     *share_hbms, m_ref, g_ref, share_ref, sems = refs
     count = len(share_hbms)
     experts = m_hbm.shape[0]
     copies = []
     for j in range(count):
-        e = lax.rem(at_ref[0] + j * (experts // count), experts)
+        e = expert(at_ref[0], at_ref[1], j, experts // count, experts)
         copies.append(
             [
                 pltpu.make_async_copy(src.at[e], dst.at[j], sems.at[i, j])
@@ -52,7 +60,7 @@
         copy.wait()
 
 
-def blended_share(first, momentum, gradient, count):
+def blended_share(at, momentum, gradient, count):
     experts, rows, cols = momentum.shape
     hbm = pl.BlockSpec(memory_space=pltpu.HBM)
     return pl.pallas_call(
@@ -64,7 +72,7 @@
         + [pltpu.SemaphoreType.DMA((3, count))],
         compiler_params=pltpu.CompilerParams(vmem_limit_bytes=60 * 2**20),
         name="share",
-    )(first[None], momentum, gradient)
+    )(at, momentum, gradient)
 
 
 def momentum_kernel(m_ref, g_ref, new_ref):
@@ -254,25 +262,25 @@
     )(*parts)
 
 
-def place_kernel(count, at_ref, *refs):
-    parts, (*_, out_ref, sems) = refs[:count], refs[count:]
-    experts = out_ref.shape[0]
+def place_kernel(which, n_rep, at_ref, *refs):
+    parts, (*_, out_ref, sems) = refs[: len(which)], refs[len(which) :]
     copies = []
-    for j, part in enumerate(parts):
-        e = lax.rem(at_ref[0] + j * (experts // count), experts)
-        copies.append(pltpu.make_async_copy(part, out_ref.at[e], sems.at[j]))
+    for i, (part, (ahead, j)) in enumerate(zip(parts, which)):
+        core = lax.rem(at_ref[1] + ahead, n_rep)
+        e = expert(at_ref[0], core, j, n_rep, out_ref.shape[0])
+        copies.append(pltpu.make_async_copy(part, out_ref.at[e], sems.at[i]))
         copies[-1].start()
     for copy in copies:
         copy.wait()
 
 
-def place(first, parts, whole):
+def place(at, which, parts, n_rep, whole):
     count = len(parts)
     anywhere = pl.BlockSpec(memory_space=pl.ANY)
     hbm = pl.BlockSpec(memory_space=pltpu.HBM)
     new = isinstance(whole, tuple)
     return pl.pallas_call(
-        functools.partial(place_kernel, count),
+        functools.partial(place_kernel, which, n_rep),
         in_specs=[pl.BlockSpec(memory_space=pltpu.SMEM)] + [anywhere] * count + [hbm] * (not new),
         out_specs=hbm,
         out_shape=jax.ShapeDtypeStruct(whole if new else whole.shape, BF),
@@ -283,7 +291,7 @@
         ),
         compiler_params=pltpu.CompilerParams(vmem_limit_bytes=4 * 2**20),
         name="place",
-    )(first[None], *parts, *([] if new else [whole]))
+    )(at, *parts, *([] if new else [whole]))
 
 
 def solution(mesh):
@@ -297,13 +305,13 @@
         pairs = [[((i + j) % n_rep, i) for i in range(n_rep)] for j in range(1, n_rep)]
         return [[lax.ppermute(x, "rep", pair) for x in pieces] for pair in pairs]
 
-    def exchange(pieces, there):
+    def exchange(pieces, there, first=0):
         moved = []
-        for j, x in enumerate(pieces):
+        for j, x in enumerate(pieces, first):
             pairs = [
                 (
                     order[p] * n_rep + r,
-                    order[(p + j * n_rep + r) % n_shard] * n_rep + r,
+                    order[(p + distance(r, j, n_rep)) % n_shard] * n_rep + r,
                 )
                 for p in range(n_shard)
                 for r in range(n_rep)
@@ -315,22 +323,22 @@
     def shards(momentum, gradient):
         experts, rows, cols = momentum.shape
         shard, rep = lax.axis_index("shard"), lax.axis_index("rep")
-        place_of = 2 * lax.rem(shard, middle) + shard // middle
-        own = exchange(
-            blended_share(lax.rem(place_of + rep, n_shard), momentum, gradient, count), True
-        )
-        rest = others(own)
-        momentum, gradient, early = lax.optimization_barrier((momentum, gradient, own[1]))
+        at = jnp.stack([2 * lax.rem(shard, middle) + shard // middle, rep])
+        sent = blended_share(at, momentum, gradient, count)
+        late = count // 4
+        own = exchange(sent[:-late], True)
+        momentum, gradient, own[0] = lax.optimization_barrier((momentum, gradient, own[0]))
         new_momentum = new_momentum_of(momentum, gradient)
-        own[1] = early
-        own[-1], new_momentum = lax.optimization_barrier((own[-1], new_momentum))
+        last, new_momentum = lax.optimization_barrier((sent[-late:], new_momentum))
+        own += exchange(last, True, count - late)
         scale = float(max(experts * rows, cols)) ** 0.5
-        parts = own + [piece for pieces in rest for piece in pieces]
+        parts = own + [piece for pieces in others(own) for piece in pieces]
         update = exchange(orthogonal(parts, count, scale), False)
+        pieces = {(i, j): x for i, xs in enumerate([update, *others(update)]) for j, x in enumerate(xs)}
+        early = [(i, j) for i, j in pieces if j < (count // 2 if i else 3 * count // 4)]
         whole = (experts, rows, cols)
-        for j, pieces in enumerate([update, *others(update)]):
-            first = lax.rem(place_of + lax.rem(rep + j, n_rep), n_shard)
-            whole = place(first, pieces, whole)
+        for which in (early, [key for key in pieces if key not in early]):
+            whole = place(at, which, [pieces[key] for key in which], n_rep, whole)
         return new_momentum, whole
 
     return jax.shard_map(

time: 82.5 us -> 85.9 us (1.041)
  the two profiles are of different devices: /device:TPU:5 before, /device:TPU:0 now
where the time goes in v8:
time: 85.9 us; the launch traced here: 85.7 us
  starting transfers between devices  47.5 us (55%)
  Pallas kernels  22.9 us (27%)
  waiting for transfers between devices  12.3 us (14%)
  local copies, waits for them, and re-layouts  1.61 us (2%)
  between operations  0.92 us (1%)
    ppermute x16, starting transfers between devices, exchange(): moved.append(lax.ppermute(x, ('shard', 'rep'), pairs))  28.2 us
    ppermute x16, starting transfers between devices, others(): return [[lax.ppermute(x, 'rep', pair) for x in pieces] for pair in pairs]  19.2 us
    pallas_call x1, Pallas kernels, orthogonal(): pl.pallas_call(functools.partial(orthogonal_kernel, scale, count), in_spe...  14.3 us
    ppermute x16, waiting for transfers between devices, exchange(): moved.append(lax.ppermute(x, ('shard', 'rep'), pairs))  10.6 us
    pallas_call x1, Pallas kernels, blended_share(): pl.pallas_call(share_kernel, in_specs=[pl.BlockSpec(memory_space=pltpu.SM...  3.35 us
    pallas_call x2, Pallas kernels, place(): pl.pallas_call(functools.partial(place_kernel, which, n_rep), in_specs=[p...  3.16 us
    pallas_call x1, Pallas kernels, new_momentum_of(): pl.pallas_call(momentum_kernel, in_specs=[vmem, vmem], out_specs=vmem, ou...  2 us
  transfers between devices with their start and end apart: 32, of which 9 were waited for; matrix products, arithmetic and copies ran while one was open for 0% of the time, Pallas kernels for 4%

profile of v8, /device:TPU:0, one launch (start us, length us, event | category | flops | bytes accessed | tf_op | source)
XLA Modules:
  0.0 85.7 jit_solution(12458399969014824003)
XLA Ops:
  0.6 0.6 pad_add_fusion.at_ref
  1.2 3.3 %share.1 = (bf16[32,2048]{1,0:T(8,128)(2,1)}, bf16[32,2048]{1,0:T(8,128)(2,1)}, bf16[32,2048]{1,0:T(8,128)(2,1)}, bf16[32,2048]{1,0:T(8,128)(2,1)}, bf16[32,2048...) custom-call(s32[2]{0:T(128)} %pad_add_fusion.at_ref, ...), custom_call_target="tpu_custom_call" | custom-call | tf_op jit(solution)/shard_map/share/pallas_call | solution.py:66
  4.6 1.6 %collective-permute-start = (bf16[32,2048]{1,0:T(8,128)(2,1)}, bf16[32,2048]{1,0:T(8,128)(2,1)S(1)}, u32[]{:S(2)}, u32[]{:S(2)}) collective-permute-start(bf16[32,2048]{1,0:T(8,128)(2,1)} %get-tuple-element.26), channel_id=1, source_target_pairs={{0,0},{1,17},{16,16},{17,3},{2,2},{3,19},{18,18},{19,5},{4,4},{5,2... | collective-permute-start | bytes 393224 | tf_op jit(solution)/shard_map/ppermute | solution.py:320
  6.1 5.0 %collective-permute-start.1 = (bf16[32,2048]{1,0:T(8,128)(2,1)}, bf16[32,2048]{1,0:T(8,128)(2,1)S(1)}, u32[]{:S(2)}, u32[]{:S(2)}) collective-permute-start(bf16[32,2048]{1,0:T(8,128)(2,1)} %get-tuple-element.31), channel_id=1, source_target_pairs={{0,18},{1,3},{16,4},{17,19},{2,20},{3,5},{18,6},{19,21},{4,22},{5,... | collective-permute-start | bytes 393224 | tf_op jit(solution)/shard_map/ppermute | solution.py:320
  11.1 1.5 %collective-permute-start.2 = (bf16[32,2048]{1,0:T(8,128)(2,1)}, bf16[32,2048]{1,0:T(8,128)(2,1)S(1)}, u32[]{:S(2)}, u32[]{:S(2)}) collective-permute-start(bf16[32,2048]{1,0:T(8,128)(2,1)} %get-tuple-element.32), channel_id=1, source_target_pairs={{0,4},{1,21},{16,20},{17,7},{2,6},{3,23},{18,22},{19,9},{4,8},{5,2... | collective-permute-start | bytes 393224 | tf_op jit(solution)/shard_map/ppermute | solution.py:320
  12.6 2.2 %collective-permute-start.3 = (bf16[32,2048]{1,0:T(8,128)(2,1)}, bf16[32,2048]{1,0:T(8,128)(2,1)S(1)}, u32[]{:S(2)}, u32[]{:S(2)}) collective-permute-start(bf16[32,2048]{1,0:T(8,128)(2,1)} %get-tuple-element.33), channel_id=1, source_target_pairs={{0,22},{1,7},{16,8},{17,23},{2,24},{3,9},{18,10},{19,25},{4,26},{5... | collective-permute-start | bytes 393224 | tf_op jit(solution)/shard_map/ppermute | solution.py:320
  14.9 0.4 collective-permute-start.4
  15.3 0.0 collective-permute-done.refs_0_
  15.3 2.1 %collective-permute-start.5 = (bf16[32,2048]{1,0:T(8,128)(2,1)}, bf16[32,2048]{1,0:T(8,128)(2,1)S(1)}, u32[]{:S(2)}, u32[]{:S(2)}) collective-permute-start(bf16[32,2048]{1,0:T(8,128)(2,1)} %get-tuple-element.35), channel_id=1, source_target_pairs={{0,26},{1,11},{16,12},{17,27},{2,28},{3,13},{18,14},{19,29},{4,30}... | collective-permute-start | bytes 393224 | tf_op jit(solution)/shard_map/ppermute | solution.py:320
  17.4 1.6 %copy-done.1 = bf16[16,32,2048]{2,1,0:T(8,128)(2,1)S(1)} copy-done((bf16[16,32,2048]{2,1,0:T(8,128)(2,1)S(1)}, bf16[16,32,2048]{2,1,0:T(8,128)(2,1)}, u32[]{:S(2)}) %copy-start.1) | copy-done | bytes 2097176
  19.0 2.0 %new_momentum.1 = bf16[16,32,2048]{2,1,0:T(8,128)(2,1)} custom-call(bf16[16,32,2048]{2,1,0:T(8,128)(2,1)S(1)} %copy-done, bf16[16,32,2048]{2,1,0:T(8,128)(2,1)S(1)} %copy-done.1), custom_call_target="tpu_custom_call" | custom-call | flops 2097152 | bytes 6291456 | tf_op jit(solution)/shard_map/new_momentum/pallas_call | solution.py:88
  21.0 0.0 collective-permute-done.1.refs_1_
  21.0 3.7 %collective-permute-start.8 = (bf16[32,2048]{1,0:T(8,128)(2,1)S(1)}, bf16[32,2048]{1,0:T(8,128)(2,1)S(1)}, u32[]{:S(2)}, u32[]{:S(2)}) collective-permute-start(bf16[32,2048]{1,0:T(8,128)(2,1)S(1)} %collective-permute-done.refs_0_), channel_id=1, source_target_pairs={{1,0},{0,1},{3,2},{2,3},{5,4},{4,5},{7,6},{6,7},{9,8},{8,9},{11,10... | collective-permute-start | bytes 393224 | tf_op jit(solution)/shard_map/ppermute | solution.py:306
  24.7 0.0 collective-permute-done.2.refs_2_
  24.7 0.1 collective-permute-start.9
  24.8 0.4 collective-permute-start.10
  25.3 2.3 %collective-permute-done.4.refs_4_ = bf16[32,2048]{1,0:T(8,128)(2,1)S(1)} collective-permute-done((bf16[32,2048]{1,0:T(8,128)(2,1)}, bf16[32,2048]{1,0:T(8,128)(2,1)S(1)}, u32[]{:S(2)}, u32[]{:S(2)}) %collective-permute-start.4) | collective-permute-done | bytes 131104 | tf_op jit(solution)/shard_map/ppermute | solution.py:320
  27.6 0.8 collective-permute-start.6
  28.4 1.7 %collective-permute-done.5.refs_5_ = bf16[32,2048]{1,0:T(8,128)(2,1)S(1)} collective-permute-done((bf16[32,2048]{1,0:T(8,128)(2,1)}, bf16[32,2048]{1,0:T(8,128)(2,1)S(1)}, u32[]{:S(2)}, u32[]{:S(2)}) %collective-permute-start.5) | collective-permute-done | bytes 131104 | tf_op jit(solution)/shard_map/ppermute | solution.py:320
  30.1 2.5 %collective-permute-start.7 = (bf16[32,2048]{1,0:T(8,128)(2,1)S(1)}, bf16[32,2048]{1,0:T(8,128)(2,1)S(1)}, u32[]{:S(2)}, u32[]{:S(2)}) collective-permute-start(bf16[32,2048]{1,0:T(8,128)(2,1)S(1)} %copy-done.3), channel_id=1, source_target_pairs={{0,30},{1,15},{16,0},{17,31},{2,16},{3,1},{18,2},{19,17},{4,18},{5... | collective-permute-start | bytes 393224 | tf_op jit(solution)/shard_map/ppermute | solution.py:320
  32.5 0.5 collective-permute-start.12
  33.0 0.1 collective-permute-start.13
  33.1 5.0 %collective-permute-start.14 = (bf16[32,2048]{1,0:T(8,128)(2,1)S(1)}, bf16[32,2048]{1,0:T(8,128)(2,1)S(1)}, u32[]{:S(2)}, u32[]{:S(2)}) collective-permute-start(bf16[32,2048]{1,0:T(8,128)(2,1)S(1)} %collective-permute-done.6.refs_6_), channel_id=1, source_target_pairs={{1,0},{0,1},{3,2},{2,3},{5,4},{4,5},{7,6},{6,7},{9,8},{8,9},{11,10... | collective-permute-start | bytes 393224 | tf_op jit(solution)/shard_map/ppermute | solution.py:306
  38.1 0.4 collective-permute-done.7.refs_7_
  38.5 0.6 collective-permute-done.14.refs_14_
  39.1 0.8 collective-permute-done.15.refs_15_
  39.9 14.3 %orthogonal.1 = (bf16[32,2048]{1,0:T(8,128)(2,1)S(1)}, bf16[32,2048]{1,0:T(8,128)(2,1)S(1)}, bf16[32,2048]{1,0:T(8,128)(2,1)S(1)}, bf16[32,2048]{1,0:T(8,128)(2,...) custom-call(bf16[32,2048]{1,0:T(8,128)(2,1)S(1)} %collective-permute, ...), custom_call_target="tpu_custom_call" | custom-call | tf_op jit(solution)/shard_map/orthogonal/pallas_call | solution.py:243
  54.2 0.4 collective-permute-start.16
  54.6 1.3 %collective-permute-start.17 = (bf16[32,2048]{1,0:T(8,128)(2,1)S(1)}, bf16[32,2048]{1,0:T(8,128)(2,1)S(1)}, u32[]{:S(2)}, u32[]{:S(2)}) collective-permute-start(bf16[32,2048]{1,0:T(8,128)(2,1)S(1)} %get-tuple-element.39), channel_id=1, source_target_pairs={{30,0},{15,1},{0,16},{31,17},{16,2},{1,3},{2,18},{17,19},{18,4},{3... | collective-permute-start | bytes 393224 | tf_op jit(solution)/shard_map/ppermute | solution.py:320
  55.9 2.2 %collective-permute-start.18 = (bf16[32,2048]{1,0:T(8,128)(2,1)S(1)}, bf16[32,2048]{1,0:T(8,128)(2,1)S(1)}, u32[]{:S(2)}, u32[]{:S(2)}) collective-permute-start(bf16[32,2048]{1,0:T(8,128)(2,1)S(1)} %get-tuple-element.40), channel_id=1, source_target_pairs={{8,0},{25,1},{24,16},{11,17},{10,2},{27,3},{26,18},{13,19},{12,4},... | collective-permute-start | bytes 393224 | tf_op jit(solution)/shard_map/ppermute | solution.py:320
  58.1 0.7 collective-permute-start.24
  58.7 2.4 %collective-permute-start.25 = (bf16[32,2048]{1,0:T(8,128)(2,1)S(1)}, bf16[32,2048]{1,0:T(8,128)(2,1)S(1)}, u32[]{:S(2)}, u32[]{:S(2)}) collective-permute-start(bf16[32,2048]{1,0:T(8,128)(2,1)S(1)} %get-tuple-element.43), channel_id=1, source_target_pairs={{18,0},{3,1},{4,16},{19,17},{20,2},{5,3},{6,18},{21,19},{22,4},{7,... | collective-permute-start | bytes 393224 | tf_op jit(solution)/shard_map/ppermute | solution.py:320
  61.1 0.8 collective-permute-done.16.refs_0_
  61.9 0.2 collective-permute-start.26
  62.1 3.5 %collective-permute-done.17.refs_1_ = bf16[32,2048]{1,0:T(8,128)(2,1)S(1)} collective-permute-done((bf16[32,2048]{1,0:T(8,128)(2,1)S(1)}, bf16[32,2048]{1,0:T(8,128)(2,1)S(1)}, u32[]{:S(2)}, u32[]{:S(2)}) %collective-permute-start.17) | collective-permute-done | bytes 131104 | tf_op jit(solution)/shard_map/ppermute | solution.py:320
  65.6 3.5 %collective-permute-start.20 = (bf16[32,2048]{1,0:T(8,128)(2,1)S(1)}, bf16[32,2048]{1,0:T(8,128)(2,1)S(1)}, u32[]{:S(2)}, u32[]{:S(2)}) collective-permute-start(bf16[32,2048]{1,0:T(8,128)(2,1)S(1)} %get-tuple-element.41), channel_id=1, source_target_pairs={{26,0},{11,1},{12,16},{27,17},{28,2},{13,3},{14,18},{29,19},{30,4}... | collective-permute-start | bytes 393224 | tf_op jit(solution)/shard_map/ppermute | solution.py:320
  69.1 1.7 %collective-permute-start.27 = (bf16[32,2048]{1,0:T(8,128)(2,1)S(1)}, bf16[32,2048]{1,0:T(8,128)(2,1)S(1)}, u32[]{:S(2)}, u32[]{:S(2)}) collective-permute-start(bf16[32,2048]{1,0:T(8,128)(2,1)S(1)} %get-tuple-element.45), channel_id=1, source_target_pairs={{22,0},{7,1},{8,16},{23,17},{24,2},{9,3},{10,18},{25,19},{26,4},{1... | collective-permute-start | bytes 393224 | tf_op jit(solution)/shard_map/ppermute | solution.py:320
  70.8 3.9 %collective-permute-start.28 = (bf16[32,2048]{1,0:T(8,128)(2,1)S(1)}, bf16[32,2048]{1,0:T(8,128)(2,1)S(1)}, u32[]{:S(2)}, u32[]{:S(2)}) collective-permute-start(bf16[32,2048]{1,0:T(8,128)(2,1)S(1)} %collective-permute-done.24.refs_0_), channel_id=1, source_target_pairs={{1,0},{0,1},{3,2},{2,3},{5,4},{4,5},{7,6},{6,7},{9,8},{8,9},{11,10... | collective-permute-start | bytes 393224 | tf_op jit(solution)/shard_map/ppermute | solution.py:306
  74.7 0.0 collective-permute-start.29
  74.7 4.4 %collective-permute-start.30 = (bf16[32,2048]{1,0:T(8,128)(2,1)S(1)}, bf16[32,2048]{1,0:T(8,128)(2,1)S(1)}, u32[]{:S(2)}, u32[]{:S(2)}) collective-permute-start(bf16[32,2048]{1,0:T(8,128)(2,1)S(1)} %collective-permute-done.26.refs_2_), channel_id=1, source_target_pairs={{1,0},{0,1},{3,2},{2,3},{5,4},{4,5},{7,6},{6,7},{9,8},{8,9},{11,10... | collective-permute-start | bytes 393224 | tf_op jit(solution)/shard_map/ppermute | solution.py:306
  79.1 0.0 collective-permute-start.22
  79.1 1.9 %collective-permute-done.27.refs_3_ = bf16[32,2048]{1,0:T(8,128)(2,1)S(1)} collective-permute-done((bf16[32,2048]{1,0:T(8,128)(2,1)S(1)}, bf16[32,2048]{1,0:T(8,128)(2,1)S(1)}, u32[]{:S(2)}, u32[]{:S(2)}) %collective-permute-start.27) | collective-permute-done | bytes 131104 | tf_op jit(solution)/shard_map/ppermute | solution.py:320
  81.0 0.5 collective-permute-start.23
  81.5 0.1 collective-permute-start.19
  81.6 0.4 collective-permute-start.21
  82.0 0.3 collective-permute-done.31.refs_9_
  82.3 1.7 %place.2.refs_6_ = bf16[16,32,2048]{2,1,0:T(8,128)(2,1)} custom-call(s32[2]{0:T(128)S(1)} %copy-done.2, bf16[32,2048]{1,0:T(8,128)(2,1)S(1)} %collective-permute-done.24.refs_0_, bf16[32,2048]{1,0:T(8,128)(2,1)S(1)} %collective-permute-done.25.refs_1_, bf16[32,2048]{1,0:T(8,128)(2,1)S(1)} %collective-permute-done.26.refs_2_, ...), custom_call_target="tpu_custom_call" | custom-call | bytes 2621440 | tf_op jit(solution)/shard_map/place/pallas_call | solution.py:282
  84.1 1.5 %place.3 = bf16[16,32,2048]{2,1,0:T(8,128)(2,1)} custom-call(s32[2]{0:T(128)S(1)} %copy-done.2, bf16[32,2048]{1,0:T(8,128)(2,1)S(1)} %collective-permute-done.16.refs_0_, bf16[32,2048]{1,0:T(8,128)(2,1)S(1)} %collective-permute-done.17.refs_1_, bf16[32,2048]{1,0:T(8,128)(2,1)S(1)} %collective-permute-done.19.refs_2_, ...), custom_call_target="tpu_custom_call", output_to_operand_aliasing={{}: (7, {})} | custom-call | bytes 1572864 | tf_op jit(solution)/shard_map/place/pallas_call | solution.py:282
  (32 shorter events, 0.1 us)
Async XLA Ops:
  1.2 16.2 %copy-start = (bf16[16,32,2048]{2,1,0:T(8,128)(2,1)S(1)}, bf16[16,32,2048]{2,1,0:T(8,128)(2,1)}, u32[]{:S(2)}) copy-start(bf16[16,32,2048]{2,1,0:T(8,128)(2,1)} %m_ref) | copy-start | bytes 6291460
  4.6 10.7 %collective-permute-start = (bf16[32,2048]{1,0:T(8,128)(2,1)}, bf16[32,2048]{1,0:T(8,128)(2,1)S(1)}, u32[]{:S(2)}, u32[]{:S(2)}) collective-permute-start(bf16[32,2048]{1,0:T(8,128)(2,1)} %get-tuple-element.26), channel_id=1, source_target_pairs={{0,0},{1,17},{16,16},{17,3},{2,2},{3,19},{18,18},{19,5},{4,4},{5,2... | collective-permute-start | bytes 393224 | tf_op jit(solution)/shard_map/ppermute | solution.py:320
  6.1 14.9 %collective-permute-start.1 = (bf16[32,2048]{1,0:T(8,128)(2,1)}, bf16[32,2048]{1,0:T(8,128)(2,1)S(1)}, u32[]{:S(2)}, u32[]{:S(2)}) collective-permute-start(bf16[32,2048]{1,0:T(8,128)(2,1)} %get-tuple-element.31), channel_id=1, source_target_pairs={{0,18},{1,3},{16,4},{17,19},{2,20},{3,5},{18,6},{19,21},{4,22},{5,... | collective-permute-start | bytes 393224 | tf_op jit(solution)/shard_map/ppermute | solution.py:320
  11.1 13.6 %collective-permute-start.2 = (bf16[32,2048]{1,0:T(8,128)(2,1)}, bf16[32,2048]{1,0:T(8,128)(2,1)S(1)}, u32[]{:S(2)}, u32[]{:S(2)}) collective-permute-start(bf16[32,2048]{1,0:T(8,128)(2,1)} %get-tuple-element.32), channel_id=1, source_target_pairs={{0,4},{1,21},{16,20},{17,7},{2,6},{3,23},{18,22},{19,9},{4,8},{5,2... | collective-permute-start | bytes 393224 | tf_op jit(solution)/shard_map/ppermute | solution.py:320
  12.6 12.2 %collective-permute-start.3 = (bf16[32,2048]{1,0:T(8,128)(2,1)}, bf16[32,2048]{1,0:T(8,128)(2,1)S(1)}, u32[]{:S(2)}, u32[]{:S(2)}) collective-permute-start(bf16[32,2048]{1,0:T(8,128)(2,1)} %get-tuple-element.33), channel_id=1, source_target_pairs={{0,22},{1,7},{16,8},{17,23},{2,24},{3,9},{18,10},{19,25},{4,26},{5... | collective-permute-start | bytes 393224 | tf_op jit(solution)/shard_map/ppermute | solution.py:320
  14.9 12.7 %collective-permute-start.4 = (bf16[32,2048]{1,0:T(8,128)(2,1)}, bf16[32,2048]{1,0:T(8,128)(2,1)S(1)}, u32[]{:S(2)}, u32[]{:S(2)}) collective-permute-start(bf16[32,2048]{1,0:T(8,128)(2,1)} %get-tuple-element.34), channel_id=1, source_target_pairs={{0,8},{1,25},{16,24},{17,11},{2,10},{3,27},{18,26},{19,13},{4,12},... | collective-permute-start | bytes 393224 | tf_op jit(solution)/shard_map/ppermute | solution.py:320
  15.3 14.7 %collective-permute-start.5 = (bf16[32,2048]{1,0:T(8,128)(2,1)}, bf16[32,2048]{1,0:T(8,128)(2,1)S(1)}, u32[]{:S(2)}, u32[]{:S(2)}) collective-permute-start(bf16[32,2048]{1,0:T(8,128)(2,1)} %get-tuple-element.35), channel_id=1, source_target_pairs={{0,26},{1,11},{16,12},{17,27},{2,28},{3,13},{18,14},{19,29},{4,30}... | collective-permute-start | bytes 393224 | tf_op jit(solution)/shard_map/ppermute | solution.py:320
  17.4 1.6 %copy-start.1 = (bf16[16,32,2048]{2,1,0:T(8,128)(2,1)S(1)}, bf16[16,32,2048]{2,1,0:T(8,128)(2,1)}, u32[]{:S(2)}) copy-start(bf16[16,32,2048]{2,1,0:T(8,128)(2,1)} %g_ref) | copy-start | bytes 6291460
  19.0 8.6 %copy-start.4 = (bf16[32,2048]{1,0:T(8,128)(2,1)S(1)}, bf16[32,2048]{1,0:T(8,128)(2,1)}, u32[]{:S(2)}) copy-start(bf16[32,2048]{1,0:T(8,128)(2,1)} %get-tuple-element.36) | copy-start | bytes 393220
  19.0 11.1 %copy-start.3 = (bf16[32,2048]{1,0:T(8,128)(2,1)S(1)}, bf16[32,2048]{1,0:T(8,128)(2,1)}, u32[]{:S(2)}) copy-start(bf16[32,2048]{1,0:T(8,128)(2,1)} %get-tuple-element.37) | copy-start | bytes 393220
  21.0 61.4 %copy-start.2 = (s32[2]{0:T(128)S(1)}, s32[2]{0:T(128)}, u32[]{:S(2)}) copy-start(s32[2]{0:T(128)} %pad_add_fusion.at_ref) | copy-start | bytes 28
  21.0 11.5 %collective-permute-start.8 = (bf16[32,2048]{1,0:T(8,128)(2,1)S(1)}, bf16[32,2048]{1,0:T(8,128)(2,1)S(1)}, u32[]{:S(2)}, u32[]{:S(2)}) collective-permute-start(bf16[32,2048]{1,0:T(8,128)(2,1)S(1)} %collective-permute-done.refs_0_), channel_id=1, source_target_pairs={{1,0},{0,1},{3,2},{2,3},{5,4},{4,5},{7,6},{6,7},{9,8},{8,9},{11,10... | collective-permute-start | bytes 393224 | tf_op jit(solution)/shard_map/ppermute | solution.py:306
  24.7 7.8 %collective-permute-start.9 = (bf16[32,2048]{1,0:T(8,128)(2,1)S(1)}, bf16[32,2048]{1,0:T(8,128)(2,1)S(1)}, u32[]{:S(2)}, u32[]{:S(2)}) collective-permute-start(bf16[32,2048]{1,0:T(8,128)(2,1)S(1)} %collective-permute-done.1.refs_1_), channel_id=1, source_target_pairs={{1,0},{0,1},{3,2},{2,3},{5,4},{4,5},{7,6},{6,7},{9,8},{8,9},{11,10... | collective-permute-start | bytes 393224 | tf_op jit(solution)/shard_map/ppermute | solution.py:306
  24.8 8.2 %collective-permute-start.10 = (bf16[32,2048]{1,0:T(8,128)(2,1)S(1)}, bf16[32,2048]{1,0:T(8,128)(2,1)S(1)}, u32[]{:S(2)}, u32[]{:S(2)}) collective-permute-start(bf16[32,2048]{1,0:T(8,128)(2,1)S(1)} %collective-permute-done.2.refs_2_), channel_id=1, source_target_pairs={{1,0},{0,1},{3,2},{2,3},{5,4},{4,5},{7,6},{6,7},{9,8},{8,9},{11,10... | collective-permute-start | bytes 393224 | tf_op jit(solution)/shard_map/ppermute | solution.py:306
  27.6 5.6 %collective-permute-start.6 = (bf16[32,2048]{1,0:T(8,128)(2,1)S(1)}, bf16[32,2048]{1,0:T(8,128)(2,1)S(1)}, u32[]{:S(2)}, u32[]{:S(2)}) collective-permute-start(bf16[32,2048]{1,0:T(8,128)(2,1)S(1)} %copy-done.4), channel_id=1, source_target_pairs={{0,12},{1,29},{16,28},{17,15},{2,14},{3,31},{18,30},{19,1},{4,0},{... | collective-permute-start | bytes 393224 | tf_op jit(solution)/shard_map/ppermute | solution.py:320
  30.1 8.4 %collective-permute-start.7 = (bf16[32,2048]{1,0:T(8,128)(2,1)S(1)}, bf16[32,2048]{1,0:T(8,128)(2,1)S(1)}, u32[]{:S(2)}, u32[]{:S(2)}) collective-permute-start(bf16[32,2048]{1,0:T(8,128)(2,1)S(1)} %copy-done.3), channel_id=1, source_target_pairs={{0,30},{1,15},{16,0},{17,31},{2,16},{3,1},{18,2},{19,17},{4,18},{5... | collective-permute-start | bytes 393224 | tf_op jit(solution)/shard_map/ppermute | solution.py:320
  32.5 6.0 %collective-permute-start.11 = (bf16[32,2048]{1,0:T(8,128)(2,1)S(1)}, bf16[32,2048]{1,0:T(8,128)(2,1)S(1)}, u32[]{:S(2)}, u32[]{:S(2)}) collective-permute-start(bf16[32,2048]{1,0:T(8,128)(2,1)S(1)} %collective-permute-done.3.refs_3_), channel_id=1, source_target_pairs={{1,0},{0,1},{3,2},{2,3},{5,4},{4,5},{7,6},{6,7},{9,8},{8,9},{11,10... | collective-permute-start | bytes 393224 | tf_op jit(solution)/shard_map/ppermute | solution.py:306
  32.5 6.0 %collective-permute-start.12 = (bf16[32,2048]{1,0:T(8,128)(2,1)S(1)}, bf16[32,2048]{1,0:T(8,128)(2,1)S(1)}, u32[]{:S(2)}, u32[]{:S(2)}) collective-permute-start(bf16[32,2048]{1,0:T(8,128)(2,1)S(1)} %collective-permute-done.4.refs_4_), channel_id=1, source_target_pairs={{1,0},{0,1},{3,2},{2,3},{5,4},{4,5},{7,6},{6,7},{9,8},{8,9},{11,10... | collective-permute-start | bytes 393224 | tf_op jit(solution)/shard_map/ppermute | solution.py:306
  33.0 5.5 %collective-permute-start.13 = (bf16[32,2048]{1,0:T(8,128)(2,1)S(1)}, bf16[32,2048]{1,0:T(8,128)(2,1)S(1)}, u32[]{:S(2)}, u32[]{:S(2)}) collective-permute-start(bf16[32,2048]{1,0:T(8,128)(2,1)S(1)} %collective-permute-done.5.refs_5_), channel_id=1, source_target_pairs={{1,0},{0,1},{3,2},{2,3},{5,4},{4,5},{7,6},{6,7},{9,8},{8,9},{11,10... | collective-permute-start | bytes 393224 | tf_op jit(solution)/shard_map/ppermute | solution.py:306
  33.1 6.0 %collective-permute-start.14 = (bf16[32,2048]{1,0:T(8,128)(2,1)S(1)}, bf16[32,2048]{1,0:T(8,128)(2,1)S(1)}, u32[]{:S(2)}, u32[]{:S(2)}) collective-permute-start(bf16[32,2048]{1,0:T(8,128)(2,1)S(1)} %collective-permute-done.6.refs_6_), channel_id=1, source_target_pairs={{1,0},{0,1},{3,2},{2,3},{5,4},{4,5},{7,6},{6,7},{9,8},{8,9},{11,10... | collective-permute-start | bytes 393224 | tf_op jit(solution)/shard_map/ppermute | solution.py:306
  38.5 1.3 %collective-permute-start.15 = (bf16[32,2048]{1,0:T(8,128)(2,1)S(1)}, bf16[32,2048]{1,0:T(8,128)(2,1)S(1)}, u32[]{:S(2)}, u32[]{:S(2)}) collective-permute-start(bf16[32,2048]{1,0:T(8,128)(2,1)S(1)} %collective-permute-done.7.refs_7_), channel_id=1, source_target_pairs={{1,0},{0,1},{3,2},{2,3},{5,4},{4,5},{7,6},{6,7},{9,8},{8,9},{11,10... | collective-permute-start | bytes 393224 | tf_op jit(solution)/shard_map/ppermute | solution.py:306
  54.2 7.7 %collective-permute-start.16 = (bf16[32,2048]{1,0:T(8,128)(2,1)S(1)}, bf16[32,2048]{1,0:T(8,128)(2,1)S(1)}, u32[]{:S(2)}, u32[]{:S(2)}) collective-permute-start(bf16[32,2048]{1,0:T(8,128)(2,1)S(1)} %get-tuple-element.38), channel_id=1, source_target_pairs={{12,0},{29,1},{28,16},{15,17},{14,2},{31,3},{30,18},{1,19},{0,4},{... | collective-permute-start | bytes 393224 | tf_op jit(solution)/shard_map/ppermute | solution.py:320
  54.6 11.0 %collective-permute-start.17 = (bf16[32,2048]{1,0:T(8,128)(2,1)S(1)}, bf16[32,2048]{1,0:T(8,128)(2,1)S(1)}, u32[]{:S(2)}, u32[]{:S(2)}) collective-permute-start(bf16[32,2048]{1,0:T(8,128)(2,1)S(1)} %get-tuple-element.39), channel_id=1, source_target_pairs={{30,0},{15,1},{0,16},{31,17},{16,2},{1,3},{2,18},{17,19},{18,4},{3... | collective-permute-start | bytes 393224 | tf_op jit(solution)/shard_map/ppermute | solution.py:320
  55.9 13.2 %collective-permute-start.18 = (bf16[32,2048]{1,0:T(8,128)(2,1)S(1)}, bf16[32,2048]{1,0:T(8,128)(2,1)S(1)}, u32[]{:S(2)}, u32[]{:S(2)}) collective-permute-start(bf16[32,2048]{1,0:T(8,128)(2,1)S(1)} %get-tuple-element.40), channel_id=1, source_target_pairs={{8,0},{25,1},{24,16},{11,17},{10,2},{27,3},{26,18},{13,19},{12,4},... | collective-permute-start | bytes 393224 | tf_op jit(solution)/shard_map/ppermute | solution.py:320
  58.1 12.7 %collective-permute-start.24 = (bf16[32,2048]{1,0:T(8,128)(2,1)S(1)}, bf16[32,2048]{1,0:T(8,128)(2,1)S(1)}, u32[]{:S(2)}, u32[]{:S(2)}) collective-permute-start(bf16[32,2048]{1,0:T(8,128)(2,1)S(1)} %get-tuple-element.42), channel_id=1, source_target_pairs={{0,0},{17,1},{16,16},{3,17},{2,2},{19,3},{18,18},{5,19},{4,4},{21,... | collective-permute-start | bytes 393224 | tf_op jit(solution)/shard_map/ppermute | solution.py:320
  58.7 16.0 %collective-permute-start.25 = (bf16[32,2048]{1,0:T(8,128)(2,1)S(1)}, bf16[32,2048]{1,0:T(8,128)(2,1)S(1)}, u32[]{:S(2)}, u32[]{:S(2)}) collective-permute-start(bf16[32,2048]{1,0:T(8,128)(2,1)S(1)} %get-tuple-element.43), channel_id=1, source_target_pairs={{18,0},{3,1},{4,16},{19,17},{20,2},{5,3},{6,18},{21,19},{22,4},{7,... | collective-permute-start | bytes 393224 | tf_op jit(solution)/shard_map/ppermute | solution.py:320
  61.9 12.8 %collective-permute-start.26 = (bf16[32,2048]{1,0:T(8,128)(2,1)S(1)}, bf16[32,2048]{1,0:T(8,128)(2,1)S(1)}, u32[]{:S(2)}, u32[]{:S(2)}) collective-permute-start(bf16[32,2048]{1,0:T(8,128)(2,1)S(1)} %get-tuple-element.44), channel_id=1, source_target_pairs={{4,0},{21,1},{20,16},{7,17},{6,2},{23,3},{22,18},{9,19},{8,4},{25,... | collective-permute-start | bytes 393224 | tf_op jit(solution)/shard_map/ppermute | solution.py:320
  65.6 13.5 %collective-permute-start.20 = (bf16[32,2048]{1,0:T(8,128)(2,1)S(1)}, bf16[32,2048]{1,0:T(8,128)(2,1)S(1)}, u32[]{:S(2)}, u32[]{:S(2)}) collective-permute-start(bf16[32,2048]{1,0:T(8,128)(2,1)S(1)} %get-tuple-element.41), channel_id=1, source_target_pairs={{26,0},{11,1},{12,16},{27,17},{28,2},{13,3},{14,18},{29,19},{30,4}... | collective-permute-start | bytes 393224 | tf_op jit(solution)/shard_map/ppermute | solution.py:320
  69.1 11.9 %collective-permute-start.27 = (bf16[32,2048]{1,0:T(8,128)(2,1)S(1)}, bf16[32,2048]{1,0:T(8,128)(2,1)S(1)}, u32[]{:S(2)}, u32[]{:S(2)}) collective-permute-start(bf16[32,2048]{1,0:T(8,128)(2,1)S(1)} %get-tuple-element.45), channel_id=1, source_target_pairs={{22,0},{7,1},{8,16},{23,17},{24,2},{9,3},{10,18},{25,19},{26,4},{1... | collective-permute-start | bytes 393224 | tf_op jit(solution)/shard_map/ppermute | solution.py:320
  70.8 10.2 %collective-permute-start.28 = (bf16[32,2048]{1,0:T(8,128)(2,1)S(1)}, bf16[32,2048]{1,0:T(8,128)(2,1)S(1)}, u32[]{:S(2)}, u32[]{:S(2)}) collective-permute-start(bf16[32,2048]{1,0:T(8,128)(2,1)S(1)} %collective-permute-done.24.refs_0_), channel_id=1, source_target_pairs={{1,0},{0,1},{3,2},{2,3},{5,4},{4,5},{7,6},{6,7},{9,8},{8,9},{11,10... | collective-permute-start | bytes 393224 | tf_op jit(solution)/shard_map/ppermute | solution.py:306
  74.7 6.8 %collective-permute-start.29 = (bf16[32,2048]{1,0:T(8,128)(2,1)S(1)}, bf16[32,2048]{1,0:T(8,128)(2,1)S(1)}, u32[]{:S(2)}, u32[]{:S(2)}) collective-permute-start(bf16[32,2048]{1,0:T(8,128)(2,1)S(1)} %collective-permute-done.25.refs_1_), channel_id=1, source_target_pairs={{1,0},{0,1},{3,2},{2,3},{5,4},{4,5},{7,6},{6,7},{9,8},{8,9},{11,10... | collective-permute-start | bytes 393224 | tf_op jit(solution)/shard_map/ppermute | solution.py:306
  74.7 6.9 %collective-permute-start.30 = (bf16[32,2048]{1,0:T(8,128)(2,1)S(1)}, bf16[32,2048]{1,0:T(8,128)(2,1)S(1)}, u32[]{:S(2)}, u32[]{:S(2)}) collective-permute-start(bf16[32,2048]{1,0:T(8,128)(2,1)S(1)} %collective-permute-done.26.refs_2_), channel_id=1, source_target_pairs={{1,0},{0,1},{3,2},{2,3},{5,4},{4,5},{7,6},{6,7},{9,8},{8,9},{11,10... | collective-permute-start | bytes 393224 | tf_op jit(solution)/shard_map/ppermute | solution.py:306
  79.1 4.9 %collective-permute-start.22 = (bf16[32,2048]{1,0:T(8,128)(2,1)S(1)}, bf16[32,2048]{1,0:T(8,128)(2,1)S(1)}, u32[]{:S(2)}, u32[]{:S(2)}) collective-permute-start(bf16[32,2048]{1,0:T(8,128)(2,1)S(1)} %collective-permute-done.16.refs_0_), channel_id=1, source_target_pairs={{1,0},{0,1},{3,2},{2,3},{5,4},{4,5},{7,6},{6,7},{9,8},{8,9},{11,10... | collective-permute-start | bytes 393224 | tf_op jit(solution)/shard_map/ppermute | solution.py:306
  81.0 1.3 %collective-permute-start.31 = (bf16[32,2048]{1,0:T(8,128)(2,1)S(1)}, bf16[32,2048]{1,0:T(8,128)(2,1)S(1)}, u32[]{:S(2)}, u32[]{:S(2)}) collective-permute-start(bf16[32,2048]{1,0:T(8,128)(2,1)S(1)} %collective-permute-done.27.refs_3_), channel_id=1, source_target_pairs={{1,0},{0,1},{3,2},{2,3},{5,4},{4,5},{7,6},{6,7},{9,8},{8,9},{11,10... | collective-permute-start | bytes 393224 | tf_op jit(solution)/shard_map/ppermute | solution.py:306
  81.0 3.0 %collective-permute-start.23 = (bf16[32,2048]{1,0:T(8,128)(2,1)S(1)}, bf16[32,2048]{1,0:T(8,128)(2,1)S(1)}, u32[]{:S(2)}, u32[]{:S(2)}) collective-permute-start(bf16[32,2048]{1,0:T(8,128)(2,1)S(1)} %collective-permute-done.17.refs_1_), channel_id=1, source_target_pairs={{1,0},{0,1},{3,2},{2,3},{5,4},{4,5},{7,6},{6,7},{9,8},{8,9},{11,10... | collective-permute-start | bytes 393224 | tf_op jit(solution)/shard_map/ppermute | solution.py:306
  81.5 2.5 %collective-permute-start.19 = (bf16[32,2048]{1,0:T(8,128)(2,1)S(1)}, bf16[32,2048]{1,0:T(8,128)(2,1)S(1)}, u32[]{:S(2)}, u32[]{:S(2)}) collective-permute-start(bf16[32,2048]{1,0:T(8,128)(2,1)S(1)} %collective-permute-done.18.refs_4_), channel_id=1, source_target_pairs={{1,0},{0,1},{3,2},{2,3},{5,4},{4,5},{7,6},{6,7},{9,8},{8,9},{11,10... | collective-permute-start | bytes 393224 | tf_op jit(solution)/shard_map/ppermute | solution.py:306
  81.6 2.5 %collective-permute-start.21 = (bf16[32,2048]{1,0:T(8,128)(2,1)S(1)}, bf16[32,2048]{1,0:T(8,128)(2,1)S(1)}, u32[]{:S(2)}, u32[]{:S(2)}) collective-permute-start(bf16[32,2048]{1,0:T(8,128)(2,1)S(1)} %collective-permute-done.20.refs_5_), channel_id=1, source_target_pairs={{1,0},{0,1},{3,2},{2,3},{5,4},{4,5},{7,6},{6,7},{9,8},{8,9},{11,10... | collective-permute-start | bytes 393224 | tf_op jit(solution)/shard_map/ppermute | solution.py:306

commit v9 on v7

--- a/solution.py
+++ b/solution.py
@@ -27,13 +27,13 @@
     return (g.astype(F32) + 0.95 * next_momentum(m, g).astype(F32)).astype(BF)
 
 
-def share_kernel(at_ref, m_hbm, g_hbm, *refs):
+def share_kernel(n_rep, at_ref, m_hbm, g_hbm, *refs):
     *share_hbms, m_ref, g_ref, share_ref, sems = refs
     count = len(share_hbms)
     experts = m_hbm.shape[0]
     copies = []
     for j in range(count):
-        e = lax.rem(at_ref[0] + j * (experts // count), experts)
+        e = lax.rem(at_ref[0] + j * n_rep, experts)
         copies.append(
             [
                 pltpu.make_async_copy(src.at[e], dst.at[j], sems.at[i, j])
@@ -52,11 +52,11 @@
         copy.wait()
 
 
-def blended_share(first, momentum, gradient, count):
+def blended_share(first, momentum, gradient, count, n_rep):
     experts, rows, cols = momentum.shape
     hbm = pl.BlockSpec(memory_space=pltpu.HBM)
     return pl.pallas_call(
-        share_kernel,
+        functools.partial(share_kernel, n_rep),
         in_specs=[pl.BlockSpec(memory_space=pltpu.SMEM), hbm, hbm],
         out_specs=[hbm] * count,
         out_shape=[jax.ShapeDtypeStruct((rows, cols), BF)] * count,
@@ -254,25 +254,25 @@
     )(*parts)
 
 
-def place_kernel(count, at_ref, *refs):
-    parts, (*_, out_ref, sems) = refs[:count], refs[count:]
-    experts = out_ref.shape[0]
+def place_kernel(which, n_rep, at_ref, *refs):
+    parts, (*_, out_ref, sems) = refs[: len(which)], refs[len(which) :]
     copies = []
-    for j, part in enumerate(parts):
-        e = lax.rem(at_ref[0] + j * (experts // count), experts)
-        copies.append(pltpu.make_async_copy(part, out_ref.at[e], sems.at[j]))
+    for i, (part, (ahead, j)) in enumerate(zip(parts, which)):
+        e = lax.rem(at_ref[ahead] + j * n_rep, out_ref.shape[0])
+        copies.append(pltpu.make_async_copy(part, out_ref.at[e], sems.at[i]))
         copies[-1].start()
     for copy in copies:
         copy.wait()
 
 
-def place(first, parts, whole):
-    count = len(parts)
+def place(firsts, pieces, n_rep, whole):
+    count = len(pieces)
     anywhere = pl.BlockSpec(memory_space=pl.ANY)
     hbm = pl.BlockSpec(memory_space=pltpu.HBM)
     new = isinstance(whole, tuple)
+    parts = list(pieces.values())
     return pl.pallas_call(
-        functools.partial(place_kernel, count),
+        functools.partial(place_kernel, list(pieces), n_rep),
         in_specs=[pl.BlockSpec(memory_space=pltpu.SMEM)] + [anywhere] * count + [hbm] * (not new),
         out_specs=hbm,
         out_shape=jax.ShapeDtypeStruct(whole if new else whole.shape, BF),
@@ -283,7 +283,7 @@
         ),
         compiler_params=pltpu.CompilerParams(vmem_limit_bytes=4 * 2**20),
         name="place",
-    )(first[None], *parts, *([] if new else [whole]))
+    )(firsts, *parts, *([] if new else [whole]))
 
 
 def solution(mesh):
@@ -312,25 +312,49 @@
             moved.append(lax.ppermute(x, ("shard", "rep"), pairs))
         return moved
 
+    def after(x, y):
+        return lax.optimization_barrier((x, y))[0]
+
     def shards(momentum, gradient):
         experts, rows, cols = momentum.shape
         shard, rep = lax.axis_index("shard"), lax.axis_index("rep")
         place_of = 2 * lax.rem(shard, middle) + shard // middle
-        own = exchange(
-            blended_share(lax.rem(place_of + rep, n_shard), momentum, gradient, count), True
-        )
-        rest = others(own)
-        momentum, gradient, early = lax.optimization_barrier((momentum, gradient, own[1]))
+        first = lax.rem(place_of + rep, n_shard)
+        few = count // 4
+        own = exchange(blended_share(first, momentum, gradient, count, n_rep), True)
+
+        middle_piece = (count - 1) // 2
+        momentum, gradient, own[middle_piece] = lax.optimization_barrier(
+            (momentum, gradient, own[middle_piece])
+        )
         new_momentum = new_momentum_of(momentum, gradient)
-        own[1] = early
-        own[-1], new_momentum = lax.optimization_barrier((own[-1], new_momentum))
+        own = [after(x, new_momentum) for x in own]
         scale = float(max(experts * rows, cols)) ** 0.5
-        parts = own + [piece for pieces in rest for piece in pieces]
+        parts = own + [piece for pieces in others(own) for piece in pieces]
         update = exchange(orthogonal(parts, count, scale), False)
-        whole = (experts, rows, cols)
-        for j, pieces in enumerate([update, *others(update)]):
-            first = lax.rem(place_of + lax.rem(rep + j, n_rep), n_shard)
-            whole = place(first, pieces, whole)
+
+        firsts = jnp.stack(
+            [lax.rem(place_of + lax.rem(rep + i, n_rep), n_shard) for i in range(n_rep)]
+        )
+        early = count - few
+        whole = place(
+            firsts, {(0, j): update[j] for j in range(early)}, n_rep, (experts, rows, cols)
+        )
+        update[early:] = [after(x, whole) for x in update[early:]]
+        swapped = others(update)
+        whole = place(
+            firsts,
+            {(0, j): update[j] for j in range(early, count)}
+            | {(i, j): x for i, xs in enumerate(swapped, 1) for j, x in enumerate(xs[:early])},
+            n_rep,
+            whole,
+        )
+        whole = place(
+            firsts,
+            {(i, j): xs[j] for i, xs in enumerate(swapped, 1) for j in range(early, count)},
+            n_rep,
+            whole,
+        )
         return new_momentum, whole
 
     return jax.shard_map(

time: 82.5 us -> 81.5 us (0.988)
  the two profiles are of different devices: /device:TPU:5 before, /device:TPU:9 now
where the time goes in v9:
time: 81.5 us; the launch traced here: 81.3 us
  starting transfers between devices  31.4 us (39%)
  waiting for transfers between devices  24 us (29%)
  Pallas kernels  23.3 us (29%)
  local copies, waits for them, and re-layouts  1.6 us (2%)
  between operations  0.93 us (1%)
    ppermute x16, starting transfers between devices, exchange(): moved.append(lax.ppermute(x, ('shard', 'rep'), pairs))  29.2 us
    ppermute x16, waiting for transfers between devices, exchange(): moved.append(lax.ppermute(x, ('shard', 'rep'), pairs))  21.8 us
    pallas_call x1, Pallas kernels, orthogonal(): pl.pallas_call(functools.partial(orthogonal_kernel, scale, count), in_spe...  14.3 us
    pallas_call x3, Pallas kernels, place(): pl.pallas_call(functools.partial(place_kernel, list(pieces), n_rep), in_s...  4.3 us
    pallas_call x1, Pallas kernels, blended_share(): pl.pallas_call(functools.partial(share_kernel, n_rep), in_specs=[pl.Block...  2.65 us
    ppermute x16, waiting for transfers between devices, others(): return [[lax.ppermute(x, 'rep', pair) for x in pieces] for pair in pairs]  2.24 us
    ppermute x16, starting transfers between devices, others(): return [[lax.ppermute(x, 'rep', pair) for x in pieces] for pair in pairs]  2.2 us
    pallas_call x1, Pallas kernels, new_momentum_of(): pl.pallas_call(momentum_kernel, in_specs=[vmem, vmem], out_specs=vmem, ou...  2 us
  transfers between devices with their start and end apart: 32, of which 18 were waited for; matrix products, arithmetic and copies ran while one was open for 0% of the time, Pallas kernels for 6%

profile of v9, /device:TPU:9, one launch (start us, length us, event | category | flops | bytes accessed | tf_op | source)
XLA Modules:
  0.0 81.3 jit_solution(2633853709297675362)
XLA Ops:
  0.7 2.7 %share.1 = (bf16[32,2048]{1,0:T(8,128)(2,1)}, bf16[32,2048]{1,0:T(8,128)(2,1)}, bf16[32,2048]{1,0:T(8,128)(2,1)}, bf16[32,2048]{1,0:T(8,128)(2,1)}, bf16[32,2048...) custom-call(s32[1]{0:T(128)} %bitcast.at_ref, ...), custom_call_target="tpu_custom_call" | custom-call | tf_op jit(solution)/shard_map/share/pallas_call | solution.py:58
  3.3 4.2 %collective-permute-start = (bf16[32,2048]{1,0:T(8,128)(2,1)}, bf16[32,2048]{1,0:T(8,128)(2,1)S(1)}, u32[]{:S(2)}, u32[]{:S(2)}) collective-permute-start(bf16[32,2048]{1,0:T(8,128)(2,1)} %get-tuple-element.31), channel_id=1, source_target_pairs={{0,6},{1,23},{16,22},{17,9},{2,8},{3,25},{18,24},{19,11},{4,10},{5... | collective-permute-start | bytes 393224 | tf_op jit(solution)/shard_map/ppermute | solution.py:312
  7.6 3.1 %collective-permute-start.3 = (bf16[32,2048]{1,0:T(8,128)(2,1)}, bf16[32,2048]{1,0:T(8,128)(2,1)S(1)}, u32[]{:S(2)}, u32[]{:S(2)}) collective-permute-start(bf16[32,2048]{1,0:T(8,128)(2,1)} %get-tuple-element.38), channel_id=1, source_target_pairs={{0,4},{1,21},{16,20},{17,7},{2,6},{3,23},{18,22},{19,9},{4,8},{5,2... | collective-permute-start | bytes 393224 | tf_op jit(solution)/shard_map/ppermute | solution.py:312
  10.7 1.9 %collective-permute-start.1 = (bf16[32,2048]{1,0:T(8,128)(2,1)}, bf16[32,2048]{1,0:T(8,128)(2,1)S(1)}, u32[]{:S(2)}, u32[]{:S(2)}) collective-permute-start(bf16[32,2048]{1,0:T(8,128)(2,1)} %get-tuple-element.34), channel_id=1, source_target_pairs={{0,0},{1,17},{16,16},{17,3},{2,2},{3,19},{18,18},{19,5},{4,4},{5,2... | collective-permute-start | bytes 393224 | tf_op jit(solution)/shard_map/ppermute | solution.py:312
  12.6 1.5 %collective-permute-start.6 = (bf16[32,2048]{1,0:T(8,128)(2,1)}, bf16[32,2048]{1,0:T(8,128)(2,1)S(1)}, u32[]{:S(2)}, u32[]{:S(2)}) collective-permute-start(bf16[32,2048]{1,0:T(8,128)(2,1)} %get-tuple-element.46), channel_id=1, source_target_pairs={{0,12},{1,29},{16,28},{17,15},{2,14},{3,31},{18,30},{19,1},{4,0},{... | collective-permute-start | bytes 393224 | tf_op jit(solution)/shard_map/ppermute | solution.py:312
  14.1 1.9 %collective-permute-start.7 = (bf16[32,2048]{1,0:T(8,128)(2,1)}, bf16[32,2048]{1,0:T(8,128)(2,1)S(1)}, u32[]{:S(2)}, u32[]{:S(2)}) collective-permute-start(bf16[32,2048]{1,0:T(8,128)(2,1)} %get-tuple-element.48), channel_id=1, source_target_pairs={{0,14},{1,31},{16,30},{17,1},{2,0},{3,17},{18,16},{19,3},{4,2},{5,... | collective-permute-start | bytes 393224 | tf_op jit(solution)/shard_map/ppermute | solution.py:312
  16.0 0.7 collective-permute-done.2.refs_1_
  16.7 0.8 collective-permute-start.4
  17.5 2.1 %collective-permute-done.3.refs_2_ = bf16[32,2048]{1,0:T(8,128)(2,1)S(1)} collective-permute-done((bf16[32,2048]{1,0:T(8,128)(2,1)}, bf16[32,2048]{1,0:T(8,128)(2,1)S(1)}, u32[]{:S(2)}, u32[]{:S(2)}) %collective-permute-start.3) | collective-permute-done | bytes 131104 | tf_op jit(solution)/shard_map/ppermute | solution.py:312
  19.6 1.6 %copy-done.1 = bf16[16,32,2048]{2,1,0:T(8,128)(2,1)S(1)} copy-done((bf16[16,32,2048]{2,1,0:T(8,128)(2,1)S(1)}, bf16[16,32,2048]{2,1,0:T(8,128)(2,1)}, u32[]{:S(2)}) %copy-start.1) | copy-done | bytes 2097176
  21.2 2.0 %new_momentum.1 = bf16[16,32,2048]{2,1,0:T(8,128)(2,1)} custom-call(bf16[16,32,2048]{2,1,0:T(8,128)(2,1)S(1)} %copy-done, bf16[16,32,2048]{2,1,0:T(8,128)(2,1)S(1)} %copy-done.1), custom_call_target="tpu_custom_call" | custom-call | flops 2097152 | bytes 6291456 | tf_op jit(solution)/shard_map/new_momentum/pallas_call | solution.py:80
  23.2 3.4 %collective-permute-done.6.refs_6_ = bf16[32,2048]{1,0:T(8,128)(2,1)S(1)} collective-permute-done((bf16[32,2048]{1,0:T(8,128)(2,1)}, bf16[32,2048]{1,0:T(8,128)(2,1)S(1)}, u32[]{:S(2)}, u32[]{:S(2)}) %collective-permute-start.6) | collective-permute-done | bytes 131104 | tf_op jit(solution)/shard_map/ppermute | solution.py:312
  26.6 1.4 %collective-permute-done.7.refs_7_ = bf16[32,2048]{1,0:T(8,128)(2,1)S(1)} collective-permute-done((bf16[32,2048]{1,0:T(8,128)(2,1)}, bf16[32,2048]{1,0:T(8,128)(2,1)S(1)}, u32[]{:S(2)}, u32[]{:S(2)}) %collective-permute-start.7) | collective-permute-done | bytes 131104 | tf_op jit(solution)/shard_map/ppermute | solution.py:312
  28.0 2.8 %collective-permute-done.5.refs_5_ = bf16[32,2048]{1,0:T(8,128)(2,1)S(1)} collective-permute-done((bf16[32,2048]{1,0:T(8,128)(2,1)}, bf16[32,2048]{1,0:T(8,128)(2,1)S(1)}, u32[]{:S(2)}, u32[]{:S(2)}) %collective-permute-start.5) | collective-permute-done | bytes 131104 | tf_op jit(solution)/shard_map/ppermute | solution.py:312
  30.8 0.5 collective-permute-start.12
  31.3 0.0 collective-permute-start.13
  31.3 0.5 collective-permute-start.14
  31.8 0.1 collective-permute-start.15
  31.9 0.2 collective-permute-done.11.refs_11_
  32.2 0.2 collective-permute-done.12.refs_12_
  32.3 0.3 collective-permute-done.13.refs_13_
  32.7 0.2 collective-permute-done.14.refs_14_
  32.9 0.3 collective-permute-done.15.refs_15_
  33.2 14.3 %orthogonal.1 = (bf16[32,2048]{1,0:T(8,128)(2,1)S(1)}, bf16[32,2048]{1,0:T(8,128)(2,1)S(1)}, bf16[32,2048]{1,0:T(8,128)(2,1)S(1)}, bf16[32,2048]{1,0:T(8,128)(2,...) custom-call(bf16[32,2048]{1,0:T(8,128)(2,1)S(1)} %collective-permute, ...), custom_call_target="tpu_custom_call" | custom-call | tf_op jit(solution)/shard_map/orthogonal/pallas_call | solution.py:235
  47.5 3.9 %collective-permute-start.17 = (bf16[32,2048]{1,0:T(8,128)(2,1)S(1)}, bf16[32,2048]{1,0:T(8,128)(2,1)S(1)}, u32[]{:S(2)}, u32[]{:S(2)}) collective-permute-start(bf16[32,2048]{1,0:T(8,128)(2,1)S(1)} %get-tuple-element.51), channel_id=1, source_target_pairs={{0,0},{17,1},{16,16},{3,17},{2,2},{19,3},{18,18},{5,19},{4,4},{21,... | collective-permute-start | bytes 393224 | tf_op jit(solution)/shard_map/ppermute | solution.py:312
  51.5 0.1 collective-permute-start.18
  51.5 2.4 %collective-permute-start.19 = (bf16[32,2048]{1,0:T(8,128)(2,1)S(1)}, bf16[32,2048]{1,0:T(8,128)(2,1)S(1)}, u32[]{:S(2)}, u32[]{:S(2)}) collective-permute-start(bf16[32,2048]{1,0:T(8,128)(2,1)S(1)} %get-tuple-element.53), channel_id=1, source_target_pairs={{4,0},{21,1},{20,16},{7,17},{6,2},{23,3},{22,18},{9,19},{8,4},{25,... | collective-permute-start | bytes 393224 | tf_op jit(solution)/shard_map/ppermute | solution.py:312
  54.0 0.3 collective-permute-start.20
  54.2 3.9 %collective-permute-start.21 = (bf16[32,2048]{1,0:T(8,128)(2,1)S(1)}, bf16[32,2048]{1,0:T(8,128)(2,1)S(1)}, u32[]{:S(2)}, u32[]{:S(2)}) collective-permute-start(bf16[32,2048]{1,0:T(8,128)(2,1)S(1)} %get-tuple-element.55), channel_id=1, source_target_pairs={{8,0},{25,1},{24,16},{11,17},{10,2},{27,3},{26,18},{13,19},{12,4},... | collective-permute-start | bytes 393224 | tf_op jit(solution)/shard_map/ppermute | solution.py:312
  58.1 0.8 collective-permute-start.22
  58.9 2.7 %collective-permute-start.24 = (bf16[32,2048]{1,0:T(8,128)(2,1)S(1)}, bf16[32,2048]{1,0:T(8,128)(2,1)S(1)}, u32[]{:S(2)}, u32[]{:S(2)}) collective-permute-start(bf16[32,2048]{1,0:T(8,128)(2,1)S(1)} %get-tuple-element.58), channel_id=1, source_target_pairs={{14,0},{31,1},{30,16},{1,17},{0,2},{17,3},{16,18},{3,19},{2,4},{19... | collective-permute-start | bytes 393224 | tf_op jit(solution)/shard_map/ppermute | solution.py:312
  61.6 0.9 %collective-permute-done.19.refs_2_ = bf16[32,2048]{1,0:T(8,128)(2,1)S(1)} collective-permute-done((bf16[32,2048]{1,0:T(8,128)(2,1)S(1)}, bf16[32,2048]{1,0:T(8,128)(2,1)S(1)}, u32[]{:S(2)}, u32[]{:S(2)}) %collective-permute-start.19) | collective-permute-done | bytes 131104 | tf_op jit(solution)/shard_map/ppermute | solution.py:312
  62.5 1.7 %collective-permute-start.16 = (bf16[32,2048]{1,0:T(8,128)(2,1)S(1)}, bf16[32,2048]{1,0:T(8,128)(2,1)S(1)}, u32[]{:S(2)}, u32[]{:S(2)}) collective-permute-start(bf16[32,2048]{1,0:T(8,128)(2,1)S(1)} %get-tuple-element.50), channel_id=1, source_target_pairs={{12,0},{29,1},{28,16},{15,17},{14,2},{31,3},{30,18},{1,19},{0,4},{... | collective-permute-start | bytes 393224 | tf_op jit(solution)/shard_map/ppermute | solution.py:312
  64.2 4.6 %collective-permute-done.20.refs_3_ = bf16[32,2048]{1,0:T(8,128)(2,1)S(1)} collective-permute-done((bf16[32,2048]{1,0:T(8,128)(2,1)S(1)}, bf16[32,2048]{1,0:T(8,128)(2,1)S(1)}, u32[]{:S(2)}, u32[]{:S(2)}) %collective-permute-start.20) | collective-permute-done | bytes 131104 | tf_op jit(solution)/shard_map/ppermute | solution.py:312
  68.8 2.2 %collective-permute-done.21.refs_4_ = bf16[32,2048]{1,0:T(8,128)(2,1)S(1)} collective-permute-done((bf16[32,2048]{1,0:T(8,128)(2,1)S(1)}, bf16[32,2048]{1,0:T(8,128)(2,1)S(1)}, u32[]{:S(2)}, u32[]{:S(2)}) %collective-permute-start.21) | collective-permute-done | bytes 131104 | tf_op jit(solution)/shard_map/ppermute | solution.py:312
  71.0 1.0 %collective-permute-done.22.refs_5_ = bf16[32,2048]{1,0:T(8,128)(2,1)S(1)} collective-permute-done((bf16[32,2048]{1,0:T(8,128)(2,1)S(1)}, bf16[32,2048]{1,0:T(8,128)(2,1)S(1)}, u32[]{:S(2)}, u32[]{:S(2)}) %collective-permute-start.22) | collective-permute-done | bytes 131104 | tf_op jit(solution)/shard_map/ppermute | solution.py:312
  72.1 0.1 pad_add_fusion.at_ref
  72.1 1.5 %place.3.refs_8_ = bf16[16,32,2048]{2,1,0:T(8,128)(2,1)} custom-call(s32[2]{0:T(128)S(1)} %pad_add_fusion.at_ref, bf16[32,2048]{1,0:T(8,128)(2,1)S(1)} %collective-permute-done.17.refs_0_, bf16[32,2048]{1,0:T(8,128)(2,1)S(1)} %collective-permute-done.18.refs_1_, bf16[32,2048]{1,0:T(8,128)(2,1)S(1)} %collective-permute-done.19.refs_2_, ...), custom_call_target="tpu_custom_call" | custom-call | bytes 1572864 | tf_op jit(solution)/shard_map/place/pallas_call | solution.py:274
  73.6 2.6 %collective-permute-done.24.refs_1_ = bf16[32,2048]{1,0:T(8,128)(2,1)S(1)} collective-permute-done((bf16[32,2048]{1,0:T(8,128)(2,1)S(1)}, bf16[32,2048]{1,0:T(8,128)(2,1)S(1)}, u32[]{:S(2)}, u32[]{:S(2)}) %collective-permute-start.24) | collective-permute-done | bytes 131104 | tf_op jit(solution)/shard_map/ppermute | solution.py:312
  76.2 0.0 collective-permute-done.16.refs_0_
  76.2 0.5 collective-permute-start.29
  76.7 0.5 collective-permute-start.31
  77.3 0.1 collective-permute-start.25
  77.3 0.4 collective-permute-done.29.refs_5_
  77.8 0.3 collective-permute-done.30.refs_6_
  78.1 0.2 collective-permute-done.31.refs_7_
  78.3 1.6 %place.4.refs_2_ = bf16[16,32,2048]{2,1,0:T(8,128)(2,1)} custom-call(s32[2]{0:T(128)S(1)} %pad_add_fusion.at_ref, bf16[32,2048]{1,0:T(8,128)(2,1)S(1)} %collective-permute-done.16.refs_0_, bf16[32,2048]{1,0:T(8,128)(2,1)S(1)} %collective-permute-done.24.refs_1_, ...), custom_call_target="tpu_custom_call", output_to_operand_aliasing={{}: (9, {})} | custom-call | bytes 2097152 | tf_op jit(solution)/shard_map/place/pallas_call | solution.py:274
  79.9 1.3 %place.5 = bf16[16,32,2048]{2,1,0:T(8,128)(2,1)} custom-call(s32[2]{0:T(128)S(1)} %pad_add_fusion.at_ref, bf16[32,2048]{1,0:T(8,128)(2,1)S(1)} %collective-permute-done.23.refs_0_, bf16[32,2048]{1,0:T(8,128)(2,1)S(1)} %collective-permute-done.25.refs_1_, bf16[16,32,2048]{2,1,0:T(8,128)(2,1)} %place.4.refs_2_), custom_call_target="tpu_custom_call", output_to_operand_aliasing={{}: (3, {})} | custom-call | bytes 524288 | tf_op jit(solution)/shard_map/place/pallas_call | solution.py:274
  (27 shorter events, 0.1 us)
Async XLA Ops:
  0.7 18.9 %copy-start = (bf16[16,32,2048]{2,1,0:T(8,128)(2,1)S(1)}, bf16[16,32,2048]{2,1,0:T(8,128)(2,1)}, u32[]{:S(2)}) copy-start(bf16[16,32,2048]{2,1,0:T(8,128)(2,1)} %m_ref) | copy-start | bytes 6291460
  3.3 10.8 %collective-permute-start = (bf16[32,2048]{1,0:T(8,128)(2,1)}, bf16[32,2048]{1,0:T(8,128)(2,1)S(1)}, u32[]{:S(2)}, u32[]{:S(2)}) collective-permute-start(bf16[32,2048]{1,0:T(8,128)(2,1)} %get-tuple-element.31), channel_id=1, source_target_pairs={{0,6},{1,23},{16,22},{17,9},{2,8},{3,25},{18,24},{19,11},{4,10},{5... | collective-permute-start | bytes 393224 | tf_op jit(solution)/shard_map/ppermute | solution.py:312
  7.6 9.2 %collective-permute-start.2 = (bf16[32,2048]{1,0:T(8,128)(2,1)}, bf16[32,2048]{1,0:T(8,128)(2,1)S(1)}, u32[]{:S(2)}, u32[]{:S(2)}) collective-permute-start(bf16[32,2048]{1,0:T(8,128)(2,1)} %get-tuple-element.36), channel_id=1, source_target_pairs={{0,2},{1,19},{16,18},{17,5},{2,4},{3,21},{18,20},{19,7},{4,6},{5,2... | collective-permute-start | bytes 393224 | tf_op jit(solution)/shard_map/ppermute | solution.py:312
  7.6 12.0 %collective-permute-start.3 = (bf16[32,2048]{1,0:T(8,128)(2,1)}, bf16[32,2048]{1,0:T(8,128)(2,1)S(1)}, u32[]{:S(2)}, u32[]{:S(2)}) collective-permute-start(bf16[32,2048]{1,0:T(8,128)(2,1)} %get-tuple-element.38), channel_id=1, source_target_pairs={{0,4},{1,21},{16,20},{17,7},{2,6},{3,23},{18,22},{19,9},{4,8},{5,2... | collective-permute-start | bytes 393224 | tf_op jit(solution)/shard_map/ppermute | solution.py:312
  10.7 12.4 %collective-permute-start.1 = (bf16[32,2048]{1,0:T(8,128)(2,1)}, bf16[32,2048]{1,0:T(8,128)(2,1)S(1)}, u32[]{:S(2)}, u32[]{:S(2)}) collective-permute-start(bf16[32,2048]{1,0:T(8,128)(2,1)} %get-tuple-element.34), channel_id=1, source_target_pairs={{0,0},{1,17},{16,16},{17,3},{2,2},{3,19},{18,18},{19,5},{4,4},{5,2... | collective-permute-start | bytes 393224 | tf_op jit(solution)/shard_map/ppermute | solution.py:312
  12.6 13.9 %collective-permute-start.6 = (bf16[32,2048]{1,0:T(8,128)(2,1)}, bf16[32,2048]{1,0:T(8,128)(2,1)S(1)}, u32[]{:S(2)}, u32[]{:S(2)}) collective-permute-start(bf16[32,2048]{1,0:T(8,128)(2,1)} %get-tuple-element.46), channel_id=1, source_target_pairs={{0,12},{1,29},{16,28},{17,15},{2,14},{3,31},{18,30},{19,1},{4,0},{... | collective-permute-start | bytes 393224 | tf_op jit(solution)/shard_map/ppermute | solution.py:312
  14.1 13.9 %collective-permute-start.7 = (bf16[32,2048]{1,0:T(8,128)(2,1)}, bf16[32,2048]{1,0:T(8,128)(2,1)S(1)}, u32[]{:S(2)}, u32[]{:S(2)}) collective-permute-start(bf16[32,2048]{1,0:T(8,128)(2,1)} %get-tuple-element.48), channel_id=1, source_target_pairs={{0,14},{1,31},{16,30},{17,1},{2,0},{3,17},{18,16},{19,3},{4,2},{5,... | collective-permute-start | bytes 393224 | tf_op jit(solution)/shard_map/ppermute | solution.py:312
  16.7 14.1 %collective-permute-start.4 = (bf16[32,2048]{1,0:T(8,128)(2,1)}, bf16[32,2048]{1,0:T(8,128)(2,1)S(1)}, u32[]{:S(2)}, u32[]{:S(2)}) collective-permute-start(bf16[32,2048]{1,0:T(8,128)(2,1)} %get-tuple-element.42), channel_id=1, source_target_pairs={{0,8},{1,25},{16,24},{17,11},{2,10},{3,27},{18,26},{19,13},{4,12},... | collective-permute-start | bytes 393224 | tf_op jit(solution)/shard_map/ppermute | solution.py:312
  19.6 11.2 %collective-permute-start.5 = (bf16[32,2048]{1,0:T(8,128)(2,1)}, bf16[32,2048]{1,0:T(8,128)(2,1)S(1)}, u32[]{:S(2)}, u32[]{:S(2)}) collective-permute-start(bf16[32,2048]{1,0:T(8,128)(2,1)} %get-tuple-element.44), channel_id=1, source_target_pairs={{0,10},{1,27},{16,26},{17,13},{2,12},{3,29},{18,28},{19,15},{4,14}... | collective-permute-start | bytes 393224 | tf_op jit(solution)/shard_map/ppermute | solution.py:312
  19.6 1.6 %copy-start.1 = (bf16[16,32,2048]{2,1,0:T(8,128)(2,1)S(1)}, bf16[16,32,2048]{2,1,0:T(8,128)(2,1)}, u32[]{:S(2)}) copy-start(bf16[16,32,2048]{2,1,0:T(8,128)(2,1)} %g_ref) | copy-start | bytes 6291460
  23.2 8.1 %collective-permute-start.8 = (bf16[32,2048]{1,0:T(8,128)(2,1)S(1)}, bf16[32,2048]{1,0:T(8,128)(2,1)S(1)}, u32[]{:S(2)}, u32[]{:S(2)}) collective-permute-start(bf16[32,2048]{1,0:T(8,128)(2,1)S(1)} %collective-permute-done.1.refs_0_), channel_id=1, source_target_pairs={{1,0},{0,1},{3,2},{2,3},{5,4},{4,5},{7,6},{6,7},{9,8},{8,9},{11,10... | collective-permute-start | bytes 393224 | tf_op jit(solution)/shard_map/ppermute | solution.py:298
  26.6 4.7 %collective-permute-start.9 = (bf16[32,2048]{1,0:T(8,128)(2,1)S(1)}, bf16[32,2048]{1,0:T(8,128)(2,1)S(1)}, u32[]{:S(2)}, u32[]{:S(2)}) collective-permute-start(bf16[32,2048]{1,0:T(8,128)(2,1)S(1)} %collective-permute-done.2.refs_1_), channel_id=1, source_target_pairs={{1,0},{0,1},{3,2},{2,3},{5,4},{4,5},{7,6},{6,7},{9,8},{8,9},{11,10... | collective-permute-start | bytes 393224 | tf_op jit(solution)/shard_map/ppermute | solution.py:298
  28.0 3.8 %collective-permute-start.10 = (bf16[32,2048]{1,0:T(8,128)(2,1)S(1)}, bf16[32,2048]{1,0:T(8,128)(2,1)S(1)}, u32[]{:S(2)}, u32[]{:S(2)}) collective-permute-start(bf16[32,2048]{1,0:T(8,128)(2,1)S(1)} %collective-permute-done.3.refs_2_), channel_id=1, source_target_pairs={{1,0},{0,1},{3,2},{2,3},{5,4},{4,5},{7,6},{6,7},{9,8},{8,9},{11,10... | collective-permute-start | bytes 393224 | tf_op jit(solution)/shard_map/ppermute | solution.py:298
  30.8 1.3 %collective-permute-start.11 = (bf16[32,2048]{1,0:T(8,128)(2,1)S(1)}, bf16[32,2048]{1,0:T(8,128)(2,1)S(1)}, u32[]{:S(2)}, u32[]{:S(2)}) collective-permute-start(bf16[32,2048]{1,0:T(8,128)(2,1)S(1)} %collective-permute-done.refs_3_), channel_id=1, source_target_pairs={{1,0},{0,1},{3,2},{2,3},{5,4},{4,5},{7,6},{6,7},{9,8},{8,9},{11,10... | collective-permute-start | bytes 393224 | tf_op jit(solution)/shard_map/ppermute | solution.py:298
  30.8 1.5 %collective-permute-start.12 = (bf16[32,2048]{1,0:T(8,128)(2,1)S(1)}, bf16[32,2048]{1,0:T(8,128)(2,1)S(1)}, u32[]{:S(2)}, u32[]{:S(2)}) collective-permute-start(bf16[32,2048]{1,0:T(8,128)(2,1)S(1)} %collective-permute-done.4.refs_4_), channel_id=1, source_target_pairs={{1,0},{0,1},{3,2},{2,3},{5,4},{4,5},{7,6},{6,7},{9,8},{8,9},{11,10... | collective-permute-start | bytes 393224 | tf_op jit(solution)/shard_map/ppermute | solution.py:298
  31.3 1.3 %collective-permute-start.13 = (bf16[32,2048]{1,0:T(8,128)(2,1)S(1)}, bf16[32,2048]{1,0:T(8,128)(2,1)S(1)}, u32[]{:S(2)}, u32[]{:S(2)}) collective-permute-start(bf16[32,2048]{1,0:T(8,128)(2,1)S(1)} %collective-permute-done.5.refs_5_), channel_id=1, source_target_pairs={{1,0},{0,1},{3,2},{2,3},{5,4},{4,5},{7,6},{6,7},{9,8},{8,9},{11,10... | collective-permute-start | bytes 393224 | tf_op jit(solution)/shard_map/ppermute | solution.py:298
  31.3 1.5 %collective-permute-start.14 = (bf16[32,2048]{1,0:T(8,128)(2,1)S(1)}, bf16[32,2048]{1,0:T(8,128)(2,1)S(1)}, u32[]{:S(2)}, u32[]{:S(2)}) collective-permute-start(bf16[32,2048]{1,0:T(8,128)(2,1)S(1)} %collective-permute-done.6.refs_6_), channel_id=1, source_target_pairs={{1,0},{0,1},{3,2},{2,3},{5,4},{4,5},{7,6},{6,7},{9,8},{8,9},{11,10... | collective-permute-start | bytes 393224 | tf_op jit(solution)/shard_map/ppermute | solution.py:298
  31.8 1.3 %collective-permute-start.15 = (bf16[32,2048]{1,0:T(8,128)(2,1)S(1)}, bf16[32,2048]{1,0:T(8,128)(2,1)S(1)}, u32[]{:S(2)}, u32[]{:S(2)}) collective-permute-start(bf16[32,2048]{1,0:T(8,128)(2,1)S(1)} %collective-permute-done.7.refs_7_), channel_id=1, source_target_pairs={{1,0},{0,1},{3,2},{2,3},{5,4},{4,5},{7,6},{6,7},{9,8},{8,9},{11,10... | collective-permute-start | bytes 393224 | tf_op jit(solution)/shard_map/ppermute | solution.py:298
  47.5 10.6 %collective-permute-start.17 = (bf16[32,2048]{1,0:T(8,128)(2,1)S(1)}, bf16[32,2048]{1,0:T(8,128)(2,1)S(1)}, u32[]{:S(2)}, u32[]{:S(2)}) collective-permute-start(bf16[32,2048]{1,0:T(8,128)(2,1)S(1)} %get-tuple-element.51), channel_id=1, source_target_pairs={{0,0},{17,1},{16,16},{3,17},{2,2},{19,3},{18,18},{5,19},{4,4},{21,... | collective-permute-start | bytes 393224 | tf_op jit(solution)/shard_map/ppermute | solution.py:312
  51.5 7.5 %collective-permute-start.18 = (bf16[32,2048]{1,0:T(8,128)(2,1)S(1)}, bf16[32,2048]{1,0:T(8,128)(2,1)S(1)}, u32[]{:S(2)}, u32[]{:S(2)}) collective-permute-start(bf16[32,2048]{1,0:T(8,128)(2,1)S(1)} %get-tuple-element.52), channel_id=1, source_target_pairs={{2,0},{19,1},{18,16},{5,17},{4,2},{21,3},{20,18},{7,19},{6,4},{23,... | collective-permute-start | bytes 393224 | tf_op jit(solution)/shard_map/ppermute | solution.py:312
  51.5 11.0 %collective-permute-start.19 = (bf16[32,2048]{1,0:T(8,128)(2,1)S(1)}, bf16[32,2048]{1,0:T(8,128)(2,1)S(1)}, u32[]{:S(2)}, u32[]{:S(2)}) collective-permute-start(bf16[32,2048]{1,0:T(8,128)(2,1)S(1)} %get-tuple-element.53), channel_id=1, source_target_pairs={{4,0},{21,1},{20,16},{7,17},{6,2},{23,3},{22,18},{9,19},{8,4},{25,... | collective-permute-start | bytes 393224 | tf_op jit(solution)/shard_map/ppermute | solution.py:312
  54.0 14.8 %collective-permute-start.20 = (bf16[32,2048]{1,0:T(8,128)(2,1)S(1)}, bf16[32,2048]{1,0:T(8,128)(2,1)S(1)}, u32[]{:S(2)}, u32[]{:S(2)}) collective-permute-start(bf16[32,2048]{1,0:T(8,128)(2,1)S(1)} %get-tuple-element.54), channel_id=1, source_target_pairs={{6,0},{23,1},{22,16},{9,17},{8,2},{25,3},{24,18},{11,19},{10,4},{2... | collective-permute-start | bytes 393224 | tf_op jit(solution)/shard_map/ppermute | solution.py:312
  54.2 16.8 %collective-permute-start.21 = (bf16[32,2048]{1,0:T(8,128)(2,1)S(1)}, bf16[32,2048]{1,0:T(8,128)(2,1)S(1)}, u32[]{:S(2)}, u32[]{:S(2)}) collective-permute-start(bf16[32,2048]{1,0:T(8,128)(2,1)S(1)} %get-tuple-element.55), channel_id=1, source_target_pairs={{8,0},{25,1},{24,16},{11,17},{10,2},{27,3},{26,18},{13,19},{12,4},... | collective-permute-start | bytes 393224 | tf_op jit(solution)/shard_map/ppermute | solution.py:312
  58.1 13.9 %collective-permute-start.22 = (bf16[32,2048]{1,0:T(8,128)(2,1)S(1)}, bf16[32,2048]{1,0:T(8,128)(2,1)S(1)}, u32[]{:S(2)}, u32[]{:S(2)}) collective-permute-start(bf16[32,2048]{1,0:T(8,128)(2,1)S(1)} %get-tuple-element.56), channel_id=1, source_target_pairs={{10,0},{27,1},{26,16},{13,17},{12,2},{29,3},{28,18},{15,19},{14,4}... | collective-permute-start | bytes 393224 | tf_op jit(solution)/shard_map/ppermute | solution.py:312
  58.9 17.2 %collective-permute-start.24 = (bf16[32,2048]{1,0:T(8,128)(2,1)S(1)}, bf16[32,2048]{1,0:T(8,128)(2,1)S(1)}, u32[]{:S(2)}, u32[]{:S(2)}) collective-permute-start(bf16[32,2048]{1,0:T(8,128)(2,1)S(1)} %get-tuple-element.58), channel_id=1, source_target_pairs={{14,0},{31,1},{30,16},{1,17},{0,2},{17,3},{16,18},{3,19},{2,4},{19... | collective-permute-start | bytes 393224 | tf_op jit(solution)/shard_map/ppermute | solution.py:312
  62.5 13.7 %collective-permute-start.16 = (bf16[32,2048]{1,0:T(8,128)(2,1)S(1)}, bf16[32,2048]{1,0:T(8,128)(2,1)S(1)}, u32[]{:S(2)}, u32[]{:S(2)}) collective-permute-start(bf16[32,2048]{1,0:T(8,128)(2,1)S(1)} %get-tuple-element.50), channel_id=1, source_target_pairs={{12,0},{29,1},{28,16},{15,17},{14,2},{31,3},{30,18},{1,19},{0,4},{... | collective-permute-start | bytes 393224 | tf_op jit(solution)/shard_map/ppermute | solution.py:312
  68.8 7.9 %collective-permute-start.26 = (bf16[32,2048]{1,0:T(8,128)(2,1)S(1)}, bf16[32,2048]{1,0:T(8,128)(2,1)S(1)}, u32[]{:S(2)}, u32[]{:S(2)}) collective-permute-start(bf16[32,2048]{1,0:T(8,128)(2,1)S(1)} %collective-permute-done.17.refs_0_), channel_id=1, source_target_pairs={{1,0},{0,1},{3,2},{2,3},{5,4},{4,5},{7,6},{6,7},{9,8},{8,9},{11,10... | collective-permute-start | bytes 393224 | tf_op jit(solution)/shard_map/ppermute | solution.py:298
  71.0 5.7 %collective-permute-start.27 = (bf16[32,2048]{1,0:T(8,128)(2,1)S(1)}, bf16[32,2048]{1,0:T(8,128)(2,1)S(1)}, u32[]{:S(2)}, u32[]{:S(2)}) collective-permute-start(bf16[32,2048]{1,0:T(8,128)(2,1)S(1)} %collective-permute-done.18.refs_1_), channel_id=1, source_target_pairs={{1,0},{0,1},{3,2},{2,3},{5,4},{4,5},{7,6},{6,7},{9,8},{8,9},{11,10... | collective-permute-start | bytes 393224 | tf_op jit(solution)/shard_map/ppermute | solution.py:298
  72.1 5.2 %collective-permute-start.28 = (bf16[32,2048]{1,0:T(8,128)(2,1)S(1)}, bf16[32,2048]{1,0:T(8,128)(2,1)S(1)}, u32[]{:S(2)}, u32[]{:S(2)}) collective-permute-start(bf16[32,2048]{1,0:T(8,128)(2,1)S(1)} %collective-permute-done.19.refs_2_), channel_id=1, source_target_pairs={{1,0},{0,1},{3,2},{2,3},{5,4},{4,5},{7,6},{6,7},{9,8},{8,9},{11,10... | collective-permute-start | bytes 393224 | tf_op jit(solution)/shard_map/ppermute | solution.py:298
  76.2 3.6 %collective-permute-start.23 = (bf16[32,2048]{1,0:T(8,128)(2,1)S(1)}, bf16[32,2048]{1,0:T(8,128)(2,1)S(1)}, u32[]{:S(2)}, u32[]{:S(2)}) collective-permute-start(bf16[32,2048]{1,0:T(8,128)(2,1)S(1)} %collective-permute-done.16.refs_0_), channel_id=1, source_target_pairs={{1,0},{0,1},{3,2},{2,3},{5,4},{4,5},{7,6},{6,7},{9,8},{8,9},{11,10... | collective-permute-start | bytes 393224 | tf_op jit(solution)/shard_map/ppermute | solution.py:298
  76.2 1.5 %collective-permute-start.29 = (bf16[32,2048]{1,0:T(8,128)(2,1)S(1)}, bf16[32,2048]{1,0:T(8,128)(2,1)S(1)}, u32[]{:S(2)}, u32[]{:S(2)}) collective-permute-start(bf16[32,2048]{1,0:T(8,128)(2,1)S(1)} %collective-permute-done.20.refs_3_), channel_id=1, source_target_pairs={{1,0},{0,1},{3,2},{2,3},{5,4},{4,5},{7,6},{6,7},{9,8},{8,9},{11,10... | collective-permute-start | bytes 393224 | tf_op jit(solution)/shard_map/ppermute | solution.py:298
  76.7 1.3 %collective-permute-start.30 = (bf16[32,2048]{1,0:T(8,128)(2,1)S(1)}, bf16[32,2048]{1,0:T(8,128)(2,1)S(1)}, u32[]{:S(2)}, u32[]{:S(2)}) collective-permute-start(bf16[32,2048]{1,0:T(8,128)(2,1)S(1)} %collective-permute-done.21.refs_4_), channel_id=1, source_target_pairs={{1,0},{0,1},{3,2},{2,3},{5,4},{4,5},{7,6},{6,7},{9,8},{8,9},{11,10... | collective-permute-start | bytes 393224 | tf_op jit(solution)/shard_map/ppermute | solution.py:298
  76.7 1.5 %collective-permute-start.31 = (bf16[32,2048]{1,0:T(8,128)(2,1)S(1)}, bf16[32,2048]{1,0:T(8,128)(2,1)S(1)}, u32[]{:S(2)}, u32[]{:S(2)}) collective-permute-start(bf16[32,2048]{1,0:T(8,128)(2,1)S(1)} %collective-permute-done.22.refs_5_), channel_id=1, source_target_pairs={{1,0},{0,1},{3,2},{2,3},{5,4},{4,5},{7,6},{6,7},{9,8},{8,9},{11,10... | collective-permute-start | bytes 393224 | tf_op jit(solution)/shard_map/ppermute | solution.py:298
  77.3 2.6 %collective-permute-start.25 = (bf16[32,2048]{1,0:T(8,128)(2,1)S(1)}, bf16[32,2048]{1,0:T(8,128)(2,1)S(1)}, u32[]{:S(2)}, u32[]{:S(2)}) collective-permute-start(bf16[32,2048]{1,0:T(8,128)(2,1)S(1)} %collective-permute-done.24.refs_1_), channel_id=1, source_target_pairs={{1,0},{0,1},{3,2},{2,3},{5,4},{4,5},{7,6},{6,7},{9,8},{8,9},{11,10... | collective-permute-start | bytes 393224 | tf_op jit(solution)/shard_map/ppermute | solution.py:298

commit v10 on v9

--- a/solution.py
+++ b/solution.py
@@ -113,8 +113,10 @@
     height = count * piece
     n = x_ref.shape[0]
     half = n // 2
-    for i, part in enumerate(parts):
-        x_ref[i * piece : (i + 1) * piece] = part[...]
+    at = 0
+    for part in parts:
+        x_ref[at : at + part.shape[0]] = part[...]
+        at += part.shape[0]
 
     def put_out(cols, y):
         for i, out_ref in enumerate(out_refs):
@@ -230,7 +232,7 @@
 def orthogonal(parts, count, scale):
     piece, cols = parts[0].shape
     height = piece * count
-    n = piece * len(parts)
+    n = sum(part.shape[0] for part in parts)
     vmem = pl.BlockSpec(memory_space=pltpu.VMEM)
     return pl.pallas_call(
         functools.partial(orthogonal_kernel, scale, count),
@@ -254,36 +256,42 @@
     )(*parts)
 
 
-def place_kernel(which, n_rep, at_ref, *refs):
-    parts, (*_, out_ref, sems) = refs[: len(which)], refs[len(which) :]
+def place_kernel(which, n_rep, *refs):
+    aheads = sorted({ahead for names in which for ahead, _ in names})
+    firsts = dict(zip(aheads, refs))
+    parts, (*_, out_ref, sems) = refs[len(aheads) :][: len(which)], refs[len(aheads) + len(which) :]
+    rows = out_ref.shape[1]
     copies = []
-    for i, (part, (ahead, j)) in enumerate(zip(parts, which)):
-        e = lax.rem(at_ref[ahead] + j * n_rep, out_ref.shape[0])
-        copies.append(pltpu.make_async_copy(part, out_ref.at[e], sems.at[i]))
-        copies[-1].start()
+    for part, names in zip(parts, which):
+        for i, (ahead, j) in enumerate(names):
+            e = lax.rem(firsts[ahead][0] + j * n_rep, out_ref.shape[0])
+            src = part.at[pl.ds(i * rows, rows)]
+            copies.append(pltpu.make_async_copy(src, out_ref.at[e], sems.at[len(copies)]))
+            copies[-1].start()
     for copy in copies:
         copy.wait()
 
 
-def place(firsts, pieces, n_rep, whole):
-    count = len(pieces)
-    anywhere = pl.BlockSpec(memory_space=pl.ANY)
+def place(firsts, which, parts, n_rep, whole):
+    count = sum(len(names) for names in which)
+    indices = [firsts[i] for i in sorted({ahead for names in which for ahead, _ in names})]
     hbm = pl.BlockSpec(memory_space=pltpu.HBM)
     new = isinstance(whole, tuple)
-    parts = list(pieces.values())
     return pl.pallas_call(
-        functools.partial(place_kernel, list(pieces), n_rep),
-        in_specs=[pl.BlockSpec(memory_space=pltpu.SMEM)] + [anywhere] * count + [hbm] * (not new),
+        functools.partial(place_kernel, which, n_rep),
+        in_specs=[pl.BlockSpec(memory_space=pltpu.SMEM)] * len(indices)
+        + [pl.BlockSpec(memory_space=pl.ANY)] * len(parts)
+        + [hbm] * (not new),
         out_specs=hbm,
         out_shape=jax.ShapeDtypeStruct(whole if new else whole.shape, BF),
         scratch_shapes=[pltpu.SemaphoreType.DMA((count,))],
-        input_output_aliases={} if new else {count + 1: 0},
+        input_output_aliases={} if new else {len(indices) + len(parts): 0},
         cost_estimate=pl.CostEstimate(
-            flops=0, bytes_accessed=4 * count * parts[0].size, transcendentals=0
+            flops=0, bytes_accessed=4 * sum(x.size for x in parts), transcendentals=0
         ),
         compiler_params=pltpu.CompilerParams(vmem_limit_bytes=4 * 2**20),
         name="place",
-    )(firsts, *parts, *([] if new else [whole]))
+    )(*indices, *parts, *([] if new else [whole]))
 
 
 def solution(mesh):
@@ -329,32 +337,25 @@
         )
         new_momentum = new_momentum_of(momentum, gradient)
         own = [after(x, new_momentum) for x in own]
+
         scale = float(max(experts * rows, cols)) ** 0.5
-        parts = own + [piece for pieces in others(own) for piece in pieces]
+        parts = own + [x for xs in others(own) for x in xs]
         update = exchange(orthogonal(parts, count, scale), False)
 
-        firsts = jnp.stack(
-            [lax.rem(place_of + lax.rem(rep + i, n_rep), n_shard) for i in range(n_rep)]
-        )
+        firsts = [lax.rem(place_of + lax.rem(rep + i, n_rep), n_shard)[None] for i in range(n_rep)]
         early = count - few
+        soon = 3 * count // 8
         whole = place(
-            firsts, {(0, j): update[j] for j in range(early)}, n_rep, (experts, rows, cols)
+            firsts, [[(0, j)] for j in range(early)], update[:early], n_rep, (experts, rows, cols)
         )
         update[early:] = [after(x, whole) for x in update[early:]]
         swapped = others(update)
-        whole = place(
-            firsts,
-            {(0, j): update[j] for j in range(early, count)}
-            | {(i, j): x for i, xs in enumerate(swapped, 1) for j, x in enumerate(xs[:early])},
-            n_rep,
-            whole,
-        )
-        whole = place(
-            firsts,
-            {(i, j): xs[j] for i, xs in enumerate(swapped, 1) for j in range(early, count)},
-            n_rep,
-            whole,
-        )
+        second = [(0, j) for j in range(early, count)]
+        second += [(i, j) for i in range(1, n_rep) for j in range(soon)]
+        third = [(i, j) for i in range(1, n_rep) for j in range(soon, count)]
+        for names in (second, third):
+            pieces = [swapped[i - 1][j] if i else update[j] for i, j in names]
+            whole = place(firsts, [[name] for name in names], pieces, n_rep, whole)
         return new_momentum, whole
 
     return jax.shard_map(

time: 81.5 us -> 78.8 us (0.967)
  the two profiles are of different devices: /device:TPU:9 before, /device:TPU:0 now
where the time goes in v10:
time: 78.8 us; the launch traced here: 78.5 us
  starting transfers between devices  47.5 us (60%)
  Pallas kernels  21.7 us (28%)
  waiting for transfers between devices  6.78 us (9%)
  local copies, waits for them, and re-layouts  1.6 us (2%)
  between operations  0.94 us (1%)
    ppermute x16, starting transfers between devices, exchange(): moved.append(lax.ppermute(x, ('shard', 'rep'), pairs))  24.9 us
    ppermute x16, starting transfers between devices, others(): return [[lax.ppermute(x, 'rep', pair) for x in pieces] for pair in pairs]  22.6 us
    pallas_call x1, Pallas kernels, orthogonal(): pl.pallas_call(functools.partial(orthogonal_kernel, scale, count), in_spe...  14.3 us
    ppermute x16, waiting for transfers between devices, exchange(): moved.append(lax.ppermute(x, ('shard', 'rep'), pairs))  5.37 us
    pallas_call x3, Pallas kernels, place(): pl.pallas_call(functools.partial(place_kernel, which, n_rep), in_specs=[p...  2.66 us
    pallas_call x1, Pallas kernels, blended_share(): pl.pallas_call(functools.partial(share_kernel, n_rep), in_specs=[pl.Block...  2.65 us
    pallas_call x1, Pallas kernels, new_momentum_of(): pl.pallas_call(momentum_kernel, in_specs=[vmem, vmem], out_specs=vmem, ou...  2 us
    unnamed x4, local copies, waits for them, and re-layouts  1.6 us
  transfers between devices with their start and end apart: 32, of which 9 were waited for; matrix products, arithmetic and copies ran while one was open for 0% of the time, Pallas kernels for 5%

profile of v10, /device:TPU:0, one launch (start us, length us, event | category | flops | bytes accessed | tf_op | source)
XLA Modules:
  0.0 78.5 jit_solution(13892006068115896868)
XLA Ops:
  0.7 2.7 %share.1 = (bf16[32,2048]{1,0:T(8,128)(2,1)}, bf16[32,2048]{1,0:T(8,128)(2,1)}, bf16[32,2048]{1,0:T(8,128)(2,1)}, bf16[32,2048]{1,0:T(8,128)(2,1)}, bf16[32,2048...) custom-call(s32[1]{0:T(128)} %bitcast.at_ref, ...), custom_call_target="tpu_custom_call" | custom-call | tf_op jit(solution)/shard_map/share/pallas_call | solution.py:58
  3.3 3.9 %collective-permute-start = (bf16[32,2048]{1,0:T(8,128)(2,1)}, bf16[32,2048]{1,0:T(8,128)(2,1)S(1)}, u32[]{:S(2)}, u32[]{:S(2)}) collective-permute-start(bf16[32,2048]{1,0:T(8,128)(2,1)} %get-tuple-element.31), channel_id=1, source_target_pairs={{0,6},{1,23},{16,22},{17,9},{2,8},{3,25},{18,24},{19,11},{4,10},{5... | collective-permute-start | bytes 393224 | tf_op jit(solution)/shard_map/ppermute | solution.py:320
  7.3 0.6 collective-permute-start.2
  7.9 1.5 %collective-permute-start.3 = (bf16[32,2048]{1,0:T(8,128)(2,1)}, bf16[32,2048]{1,0:T(8,128)(2,1)S(1)}, u32[]{:S(2)}, u32[]{:S(2)}) collective-permute-start(bf16[32,2048]{1,0:T(8,128)(2,1)} %get-tuple-element.38), channel_id=1, source_target_pairs={{0,4},{1,21},{16,20},{17,7},{2,6},{3,23},{18,22},{19,9},{4,8},{5,2... | collective-permute-start | bytes 393224 | tf_op jit(solution)/shard_map/ppermute | solution.py:320
  9.4 1.6 %collective-permute-start.1 = (bf16[32,2048]{1,0:T(8,128)(2,1)}, bf16[32,2048]{1,0:T(8,128)(2,1)S(1)}, u32[]{:S(2)}, u32[]{:S(2)}) collective-permute-start(bf16[32,2048]{1,0:T(8,128)(2,1)} %get-tuple-element.34), channel_id=1, source_target_pairs={{0,0},{1,17},{16,16},{17,3},{2,2},{3,19},{18,18},{19,5},{4,4},{5,2... | collective-permute-start | bytes 393224 | tf_op jit(solution)/shard_map/ppermute | solution.py:320
  10.9 1.4 %collective-permute-start.6 = (bf16[32,2048]{1,0:T(8,128)(2,1)}, bf16[32,2048]{1,0:T(8,128)(2,1)S(1)}, u32[]{:S(2)}, u32[]{:S(2)}) collective-permute-start(bf16[32,2048]{1,0:T(8,128)(2,1)} %get-tuple-element.46), channel_id=1, source_target_pairs={{0,12},{1,29},{16,28},{17,15},{2,14},{3,31},{18,30},{19,1},{4,0},{... | collective-permute-start | bytes 393224 | tf_op jit(solution)/shard_map/ppermute | solution.py:320
  12.3 2.3 %collective-permute-start.7 = (bf16[32,2048]{1,0:T(8,128)(2,1)}, bf16[32,2048]{1,0:T(8,128)(2,1)S(1)}, u32[]{:S(2)}, u32[]{:S(2)}) collective-permute-start(bf16[32,2048]{1,0:T(8,128)(2,1)} %get-tuple-element.48), channel_id=1, source_target_pairs={{0,14},{1,31},{16,30},{17,1},{2,0},{3,17},{18,16},{19,3},{4,2},{5,... | collective-permute-start | bytes 393224 | tf_op jit(solution)/shard_map/ppermute | solution.py:320
  14.7 1.7 %collective-permute-done.2.refs_1_ = bf16[32,2048]{1,0:T(8,128)(2,1)S(1)} collective-permute-done((bf16[32,2048]{1,0:T(8,128)(2,1)}, bf16[32,2048]{1,0:T(8,128)(2,1)S(1)}, u32[]{:S(2)}, u32[]{:S(2)}) %collective-permute-start.2) | collective-permute-done | bytes 131104 | tf_op jit(solution)/shard_map/ppermute | solution.py:320
  16.3 2.0 %collective-permute-start.4 = (bf16[32,2048]{1,0:T(8,128)(2,1)}, bf16[32,2048]{1,0:T(8,128)(2,1)S(1)}, u32[]{:S(2)}, u32[]{:S(2)}) collective-permute-start(bf16[32,2048]{1,0:T(8,128)(2,1)} %get-tuple-element.42), channel_id=1, source_target_pairs={{0,8},{1,25},{16,24},{17,11},{2,10},{3,27},{18,26},{19,13},{4,12},... | collective-permute-start | bytes 393224 | tf_op jit(solution)/shard_map/ppermute | solution.py:320
  18.4 0.5 collective-permute-done.3.refs_2_
  18.9 1.2 %collective-permute-start.5 = (bf16[32,2048]{1,0:T(8,128)(2,1)}, bf16[32,2048]{1,0:T(8,128)(2,1)S(1)}, u32[]{:S(2)}, u32[]{:S(2)}) collective-permute-start(bf16[32,2048]{1,0:T(8,128)(2,1)} %get-tuple-element.44), channel_id=1, source_target_pairs={{0,10},{1,27},{16,26},{17,13},{2,12},{3,29},{18,28},{19,15},{4,14}... | collective-permute-start | bytes 393224 | tf_op jit(solution)/shard_map/ppermute | solution.py:320
  20.1 1.6 %copy-done.1 = bf16[16,32,2048]{2,1,0:T(8,128)(2,1)S(1)} copy-done((bf16[16,32,2048]{2,1,0:T(8,128)(2,1)S(1)}, bf16[16,32,2048]{2,1,0:T(8,128)(2,1)}, u32[]{:S(2)}) %copy-start.1) | copy-done | bytes 2097176
  21.7 2.0 %new_momentum.1 = bf16[16,32,2048]{2,1,0:T(8,128)(2,1)} custom-call(bf16[16,32,2048]{2,1,0:T(8,128)(2,1)S(1)} %copy-done, bf16[16,32,2048]{2,1,0:T(8,128)(2,1)S(1)} %copy-done.1), custom_call_target="tpu_custom_call" | custom-call | flops 2097152 | bytes 6291456 | tf_op jit(solution)/shard_map/new_momentum/pallas_call | solution.py:80
  23.7 2.6 %collective-permute-start.8 = (bf16[32,2048]{1,0:T(8,128)(2,1)S(1)}, bf16[32,2048]{1,0:T(8,128)(2,1)S(1)}, u32[]{:S(2)}, u32[]{:S(2)}) collective-permute-start(bf16[32,2048]{1,0:T(8,128)(2,1)S(1)} %collective-permute-done.1.refs_0_), channel_id=1, source_target_pairs={{1,0},{0,1},{3,2},{2,3},{5,4},{4,5},{7,6},{6,7},{9,8},{8,9},{11,10... | collective-permute-start | bytes 393224 | tf_op jit(solution)/shard_map/ppermute | solution.py:306
  26.3 1.0 %collective-permute-start.9 = (bf16[32,2048]{1,0:T(8,128)(2,1)S(1)}, bf16[32,2048]{1,0:T(8,128)(2,1)S(1)}, u32[]{:S(2)}, u32[]{:S(2)}) collective-permute-start(bf16[32,2048]{1,0:T(8,128)(2,1)S(1)} %collective-permute-done.2.refs_1_), channel_id=1, source_target_pairs={{1,0},{0,1},{3,2},{2,3},{5,4},{4,5},{7,6},{6,7},{9,8},{8,9},{11,10... | collective-permute-start | bytes 393224 | tf_op jit(solution)/shard_map/ppermute | solution.py:306
  27.3 0.6 collective-permute-start.10
  27.9 5.5 %collective-permute-start.11 = (bf16[32,2048]{1,0:T(8,128)(2,1)S(1)}, bf16[32,2048]{1,0:T(8,128)(2,1)S(1)}, u32[]{:S(2)}, u32[]{:S(2)}) collective-permute-start(bf16[32,2048]{1,0:T(8,128)(2,1)S(1)} %collective-permute-done.refs_3_), channel_id=1, source_target_pairs={{1,0},{0,1},{3,2},{2,3},{5,4},{4,5},{7,6},{6,7},{9,8},{8,9},{11,10... | collective-permute-start | bytes 393224 | tf_op jit(solution)/shard_map/ppermute | solution.py:306
  33.5 0.0 collective-permute-start.12
  33.5 0.5 collective-permute-start.13
  34.0 0.1 collective-permute-start.14
  34.1 0.4 collective-permute-start.15
  34.5 0.3 collective-permute-done.12.refs_12_
  34.8 0.2 collective-permute-done.13.refs_13_
  35.0 0.3 collective-permute-done.14.refs_14_
  35.4 0.2 collective-permute-done.15.refs_15_
  35.5 14.3 %orthogonal.1 = (bf16[32,2048]{1,0:T(8,128)(2,1)S(1)}, bf16[32,2048]{1,0:T(8,128)(2,1)S(1)}, bf16[32,2048]{1,0:T(8,128)(2,1)S(1)}, bf16[32,2048]{1,0:T(8,128)(2,...) custom-call(bf16[32,2048]{1,0:T(8,128)(2,1)S(1)} %collective-permute, ...), custom_call_target="tpu_custom_call" | custom-call | tf_op jit(solution)/shard_map/orthogonal/pallas_call | solution.py:237
  49.9 0.1 collective-permute-start.16
  50.0 2.0 %collective-permute-start.18 = (bf16[32,2048]{1,0:T(8,128)(2,1)S(1)}, bf16[32,2048]{1,0:T(8,128)(2,1)S(1)}, u32[]{:S(2)}, u32[]{:S(2)}) collective-permute-start(bf16[32,2048]{1,0:T(8,128)(2,1)S(1)} %get-tuple-element.51), channel_id=1, source_target_pairs={{8,0},{25,1},{24,16},{11,17},{10,2},{27,3},{26,18},{13,19},{12,4},... | collective-permute-start | bytes 393224 | tf_op jit(solution)/shard_map/ppermute | solution.py:320
  52.0 1.1 %collective-permute-start.20 = (bf16[32,2048]{1,0:T(8,128)(2,1)S(1)}, bf16[32,2048]{1,0:T(8,128)(2,1)S(1)}, u32[]{:S(2)}, u32[]{:S(2)}) collective-permute-start(bf16[32,2048]{1,0:T(8,128)(2,1)S(1)} %get-tuple-element.52), channel_id=1, source_target_pairs={{10,0},{27,1},{26,16},{13,17},{12,2},{29,3},{28,18},{15,19},{14,4}... | collective-permute-start | bytes 393224 | tf_op jit(solution)/shard_map/ppermute | solution.py:320
  53.0 0.7 collective-permute-start.23
  53.7 1.3 %collective-permute-start.24 = (bf16[32,2048]{1,0:T(8,128)(2,1)S(1)}, bf16[32,2048]{1,0:T(8,128)(2,1)S(1)}, u32[]{:S(2)}, u32[]{:S(2)}) collective-permute-start(bf16[32,2048]{1,0:T(8,128)(2,1)S(1)} %get-tuple-element.55), channel_id=1, source_target_pairs={{2,0},{19,1},{18,16},{5,17},{4,2},{21,3},{20,18},{7,19},{6,4},{23,... | collective-permute-start | bytes 393224 | tf_op jit(solution)/shard_map/ppermute | solution.py:320
  55.0 0.8 collective-permute-done.16.refs_4_
  55.8 3.1 %collective-permute-start.25 = (bf16[32,2048]{1,0:T(8,128)(2,1)S(1)}, bf16[32,2048]{1,0:T(8,128)(2,1)S(1)}, u32[]{:S(2)}, u32[]{:S(2)}) collective-permute-start(bf16[32,2048]{1,0:T(8,128)(2,1)S(1)} %get-tuple-element.56), channel_id=1, source_target_pairs={{4,0},{21,1},{20,16},{7,17},{6,2},{23,3},{22,18},{9,19},{8,4},{25,... | collective-permute-start | bytes 393224 | tf_op jit(solution)/shard_map/ppermute | solution.py:320
  58.9 2.3 %collective-permute-done.18.refs_5_ = bf16[32,2048]{1,0:T(8,128)(2,1)S(1)} collective-permute-done((bf16[32,2048]{1,0:T(8,128)(2,1)S(1)}, bf16[32,2048]{1,0:T(8,128)(2,1)S(1)}, u32[]{:S(2)}, u32[]{:S(2)}) %collective-permute-start.18) | collective-permute-done | bytes 131104 | tf_op jit(solution)/shard_map/ppermute | solution.py:320
  61.3 2.1 %collective-permute-start.22 = (bf16[32,2048]{1,0:T(8,128)(2,1)S(1)}, bf16[32,2048]{1,0:T(8,128)(2,1)S(1)}, u32[]{:S(2)}, u32[]{:S(2)}) collective-permute-start(bf16[32,2048]{1,0:T(8,128)(2,1)S(1)} %get-tuple-element.53), channel_id=1, source_target_pairs={{12,0},{29,1},{28,16},{15,17},{14,2},{31,3},{30,18},{1,19},{0,4},{... | collective-permute-start | bytes 393224 | tf_op jit(solution)/shard_map/ppermute | solution.py:320
  63.4 4.6 %collective-permute-start.29 = (bf16[32,2048]{1,0:T(8,128)(2,1)S(1)}, bf16[32,2048]{1,0:T(8,128)(2,1)S(1)}, u32[]{:S(2)}, u32[]{:S(2)}) collective-permute-start(bf16[32,2048]{1,0:T(8,128)(2,1)S(1)} %collective-permute-done.23.refs_1_), channel_id=1, source_target_pairs={{1,0},{0,1},{3,2},{2,3},{5,4},{4,5},{7,6},{6,7},{9,8},{8,9},{11,10... | collective-permute-start | bytes 393224 | tf_op jit(solution)/shard_map/ppermute | solution.py:306
  68.0 3.7 %collective-permute-start.30 = (bf16[32,2048]{1,0:T(8,128)(2,1)S(1)}, bf16[32,2048]{1,0:T(8,128)(2,1)S(1)}, u32[]{:S(2)}, u32[]{:S(2)}) collective-permute-start(bf16[32,2048]{1,0:T(8,128)(2,1)S(1)} %collective-permute-done.24.refs_2_), channel_id=1, source_target_pairs={{1,0},{0,1},{3,2},{2,3},{5,4},{4,5},{7,6},{6,7},{9,8},{8,9},{11,10... | collective-permute-start | bytes 393224 | tf_op jit(solution)/shard_map/ppermute | solution.py:306
  71.7 2.3 %collective-permute-start.31 = (bf16[32,2048]{1,0:T(8,128)(2,1)S(1)}, bf16[32,2048]{1,0:T(8,128)(2,1)S(1)}, u32[]{:S(2)}, u32[]{:S(2)}) collective-permute-start(bf16[32,2048]{1,0:T(8,128)(2,1)S(1)} %collective-permute-done.25.refs_3_), channel_id=1, source_target_pairs={{1,0},{0,1},{3,2},{2,3},{5,4},{4,5},{7,6},{6,7},{9,8},{8,9},{11,10... | collective-permute-start | bytes 393224 | tf_op jit(solution)/shard_map/ppermute | solution.py:306
  74.0 0.9 %place.3.refs_7_ = bf16[16,32,2048]{2,1,0:T(8,128)(2,1)} custom-call(s32[1]{0:T(128)} %bitcast.2.refs_0_, bf16[32,2048]{1,0:T(8,128)(2,1)S(1)} %collective-permute-done.23.refs_1_, bf16[32,2048]{1,0:T(8,128)(2,1)S(1)} %collective-permute-done.24.refs_2_, bf16[32,2048]{1,0:T(8,128)(2,1)S(1)} %collective-permute-done.25.refs_3_, ...), custom_call_target="tpu_custom_call" | custom-call | bytes 1572864 | tf_op jit(solution)/shard_map/place/pallas_call | solution.py:280
  75.0 0.1 collective-permute-start.26
  75.1 0.5 collective-permute-start.17
  75.6 0.1 collective-permute-start.19
  75.6 0.4 collective-permute-start.21
  76.1 0.1 collective-permute-start.28
  76.2 0.9 %place.4.refs_6_ = bf16[16,32,2048]{2,1,0:T(8,128)(2,1)} custom-call(s32[1]{0:T(128)} %bitcast.2.refs_0_, s32[1]{0:T(128)} %bitcast.1.refs_1_.refs_0_, bf16[32,2048]{1,0:T(8,128)(2,1)S(1)} %collective-permute-done.22.refs_2_, bf16[32,2048]{1,0:T(8,128)(2,1)S(1)} %collective-permute-done.27.refs_3_, ...), custom_call_target="tpu_custom_call", output_to_operand_aliasing={{}: (7, {})} | custom-call | bytes 1310720 | tf_op jit(solution)/shard_map/place/pallas_call | solution.py:280
  77.1 0.0 collective-permute-done.21.refs_3_
  77.1 0.3 collective-permute-done.28.refs_5_
  77.4 0.9 %place.5 = bf16[16,32,2048]{2,1,0:T(8,128)(2,1)} custom-call(s32[1]{0:T(128)} %bitcast.1.refs_1_.refs_0_, bf16[32,2048]{1,0:T(8,128)(2,1)S(1)} %collective-permute-done.17.refs_1_, bf16[32,2048]{1,0:T(8,128)(2,1)S(1)} %collective-permute-done.19.refs_2_, bf16[32,2048]{1,0:T(8,128)(2,1)S(1)} %collective-permute-done.21.refs_3_, ...), custom_call_target="tpu_custom_call", output_to_operand_aliasing={{}: (6, {})} | custom-call | bytes 1310720 | tf_op jit(solution)/shard_map/place/pallas_call | solution.py:280
  (26 shorter events, 0.1 us)
Async XLA Ops:
  0.7 19.5 %copy-start = (bf16[16,32,2048]{2,1,0:T(8,128)(2,1)S(1)}, bf16[16,32,2048]{2,1,0:T(8,128)(2,1)}, u32[]{:S(2)}) copy-start(bf16[16,32,2048]{2,1,0:T(8,128)(2,1)} %m_ref) | copy-start | bytes 6291460
  3.3 9.0 %collective-permute-start = (bf16[32,2048]{1,0:T(8,128)(2,1)}, bf16[32,2048]{1,0:T(8,128)(2,1)S(1)}, u32[]{:S(2)}, u32[]{:S(2)}) collective-permute-start(bf16[32,2048]{1,0:T(8,128)(2,1)} %get-tuple-element.31), channel_id=1, source_target_pairs={{0,6},{1,23},{16,22},{17,9},{2,8},{3,25},{18,24},{19,11},{4,10},{5... | collective-permute-start | bytes 393224 | tf_op jit(solution)/shard_map/ppermute | solution.py:320
  7.3 9.1 %collective-permute-start.2 = (bf16[32,2048]{1,0:T(8,128)(2,1)}, bf16[32,2048]{1,0:T(8,128)(2,1)S(1)}, u32[]{:S(2)}, u32[]{:S(2)}) collective-permute-start(bf16[32,2048]{1,0:T(8,128)(2,1)} %get-tuple-element.36), channel_id=1, source_target_pairs={{0,2},{1,19},{16,18},{17,5},{2,4},{3,21},{18,20},{19,7},{4,6},{5,2... | collective-permute-start | bytes 393224 | tf_op jit(solution)/shard_map/ppermute | solution.py:320
  7.9 11.0 %collective-permute-start.3 = (bf16[32,2048]{1,0:T(8,128)(2,1)}, bf16[32,2048]{1,0:T(8,128)(2,1)S(1)}, u32[]{:S(2)}, u32[]{:S(2)}) collective-permute-start(bf16[32,2048]{1,0:T(8,128)(2,1)} %get-tuple-element.38), channel_id=1, source_target_pairs={{0,4},{1,21},{16,20},{17,7},{2,6},{3,23},{18,22},{19,9},{4,8},{5,2... | collective-permute-start | bytes 393224 | tf_op jit(solution)/shard_map/ppermute | solution.py:320
  9.4 14.3 %collective-permute-start.1 = (bf16[32,2048]{1,0:T(8,128)(2,1)}, bf16[32,2048]{1,0:T(8,128)(2,1)S(1)}, u32[]{:S(2)}, u32[]{:S(2)}) collective-permute-start(bf16[32,2048]{1,0:T(8,128)(2,1)} %get-tuple-element.34), channel_id=1, source_target_pairs={{0,0},{1,17},{16,16},{17,3},{2,2},{3,19},{18,18},{19,5},{4,4},{5,2... | collective-permute-start | bytes 393224 | tf_op jit(solution)/shard_map/ppermute | solution.py:320
  10.9 15.4 %collective-permute-start.6 = (bf16[32,2048]{1,0:T(8,128)(2,1)}, bf16[32,2048]{1,0:T(8,128)(2,1)S(1)}, u32[]{:S(2)}, u32[]{:S(2)}) collective-permute-start(bf16[32,2048]{1,0:T(8,128)(2,1)} %get-tuple-element.46), channel_id=1, source_target_pairs={{0,12},{1,29},{16,28},{17,15},{2,14},{3,31},{18,30},{19,1},{4,0},{... | collective-permute-start | bytes 393224 | tf_op jit(solution)/shard_map/ppermute | solution.py:320
  12.3 15.0 %collective-permute-start.7 = (bf16[32,2048]{1,0:T(8,128)(2,1)}, bf16[32,2048]{1,0:T(8,128)(2,1)S(1)}, u32[]{:S(2)}, u32[]{:S(2)}) collective-permute-start(bf16[32,2048]{1,0:T(8,128)(2,1)} %get-tuple-element.48), channel_id=1, source_target_pairs={{0,14},{1,31},{16,30},{17,1},{2,0},{3,17},{18,16},{19,3},{4,2},{5,... | collective-permute-start | bytes 393224 | tf_op jit(solution)/shard_map/ppermute | solution.py:320
  16.3 11.6 %collective-permute-start.4 = (bf16[32,2048]{1,0:T(8,128)(2,1)}, bf16[32,2048]{1,0:T(8,128)(2,1)S(1)}, u32[]{:S(2)}, u32[]{:S(2)}) collective-permute-start(bf16[32,2048]{1,0:T(8,128)(2,1)} %get-tuple-element.42), channel_id=1, source_target_pairs={{0,8},{1,25},{16,24},{17,11},{2,10},{3,27},{18,26},{19,13},{4,12},... | collective-permute-start | bytes 393224 | tf_op jit(solution)/shard_map/ppermute | solution.py:320
  18.9 9.0 %collective-permute-start.5 = (bf16[32,2048]{1,0:T(8,128)(2,1)}, bf16[32,2048]{1,0:T(8,128)(2,1)S(1)}, u32[]{:S(2)}, u32[]{:S(2)}) collective-permute-start(bf16[32,2048]{1,0:T(8,128)(2,1)} %get-tuple-element.44), channel_id=1, source_target_pairs={{0,10},{1,27},{16,26},{17,13},{2,12},{3,29},{18,28},{19,15},{4,14}... | collective-permute-start | bytes 393224 | tf_op jit(solution)/shard_map/ppermute | solution.py:320
  20.1 1.6 %copy-start.1 = (bf16[16,32,2048]{2,1,0:T(8,128)(2,1)S(1)}, bf16[16,32,2048]{2,1,0:T(8,128)(2,1)}, u32[]{:S(2)}) copy-start(bf16[16,32,2048]{2,1,0:T(8,128)(2,1)} %g_ref) | copy-start | bytes 6291460
  23.7 9.8 %collective-permute-start.8 = (bf16[32,2048]{1,0:T(8,128)(2,1)S(1)}, bf16[32,2048]{1,0:T(8,128)(2,1)S(1)}, u32[]{:S(2)}, u32[]{:S(2)}) collective-permute-start(bf16[32,2048]{1,0:T(8,128)(2,1)S(1)} %collective-permute-done.1.refs_0_), channel_id=1, source_target_pairs={{1,0},{0,1},{3,2},{2,3},{5,4},{4,5},{7,6},{6,7},{9,8},{8,9},{11,10... | collective-permute-start | bytes 393224 | tf_op jit(solution)/shard_map/ppermute | solution.py:306
  26.3 7.7 %collective-permute-start.9 = (bf16[32,2048]{1,0:T(8,128)(2,1)S(1)}, bf16[32,2048]{1,0:T(8,128)(2,1)S(1)}, u32[]{:S(2)}, u32[]{:S(2)}) collective-permute-start(bf16[32,2048]{1,0:T(8,128)(2,1)S(1)} %collective-permute-done.2.refs_1_), channel_id=1, source_target_pairs={{1,0},{0,1},{3,2},{2,3},{5,4},{4,5},{7,6},{6,7},{9,8},{8,9},{11,10... | collective-permute-start | bytes 393224 | tf_op jit(solution)/shard_map/ppermute | solution.py:306
  27.3 6.8 %collective-permute-start.10 = (bf16[32,2048]{1,0:T(8,128)(2,1)S(1)}, bf16[32,2048]{1,0:T(8,128)(2,1)S(1)}, u32[]{:S(2)}, u32[]{:S(2)}) collective-permute-start(bf16[32,2048]{1,0:T(8,128)(2,1)S(1)} %collective-permute-done.3.refs_2_), channel_id=1, source_target_pairs={{1,0},{0,1},{3,2},{2,3},{5,4},{4,5},{7,6},{6,7},{9,8},{8,9},{11,10... | collective-permute-start | bytes 393224 | tf_op jit(solution)/shard_map/ppermute | solution.py:306
  27.9 6.6 %collective-permute-start.11 = (bf16[32,2048]{1,0:T(8,128)(2,1)S(1)}, bf16[32,2048]{1,0:T(8,128)(2,1)S(1)}, u32[]{:S(2)}, u32[]{:S(2)}) collective-permute-start(bf16[32,2048]{1,0:T(8,128)(2,1)S(1)} %collective-permute-done.refs_3_), channel_id=1, source_target_pairs={{1,0},{0,1},{3,2},{2,3},{5,4},{4,5},{7,6},{6,7},{9,8},{8,9},{11,10... | collective-permute-start | bytes 393224 | tf_op jit(solution)/shard_map/ppermute | solution.py:306
  33.5 1.3 %collective-permute-start.12 = (bf16[32,2048]{1,0:T(8,128)(2,1)S(1)}, bf16[32,2048]{1,0:T(8,128)(2,1)S(1)}, u32[]{:S(2)}, u32[]{:S(2)}) collective-permute-start(bf16[32,2048]{1,0:T(8,128)(2,1)S(1)} %collective-permute-done.4.refs_4_), channel_id=1, source_target_pairs={{1,0},{0,1},{3,2},{2,3},{5,4},{4,5},{7,6},{6,7},{9,8},{8,9},{11,10... | collective-permute-start | bytes 393224 | tf_op jit(solution)/shard_map/ppermute | solution.py:306
  33.5 1.5 %collective-permute-start.13 = (bf16[32,2048]{1,0:T(8,128)(2,1)S(1)}, bf16[32,2048]{1,0:T(8,128)(2,1)S(1)}, u32[]{:S(2)}, u32[]{:S(2)}) collective-permute-start(bf16[32,2048]{1,0:T(8,128)(2,1)S(1)} %collective-permute-done.5.refs_5_), channel_id=1, source_target_pairs={{1,0},{0,1},{3,2},{2,3},{5,4},{4,5},{7,6},{6,7},{9,8},{8,9},{11,10... | collective-permute-start | bytes 393224 | tf_op jit(solution)/shard_map/ppermute | solution.py:306
  34.0 1.3 %collective-permute-start.14 = (bf16[32,2048]{1,0:T(8,128)(2,1)S(1)}, bf16[32,2048]{1,0:T(8,128)(2,1)S(1)}, u32[]{:S(2)}, u32[]{:S(2)}) collective-permute-start(bf16[32,2048]{1,0:T(8,128)(2,1)S(1)} %collective-permute-done.6.refs_6_), channel_id=1, source_target_pairs={{1,0},{0,1},{3,2},{2,3},{5,4},{4,5},{7,6},{6,7},{9,8},{8,9},{11,10... | collective-permute-start | bytes 393224 | tf_op jit(solution)/shard_map/ppermute | solution.py:306
  34.1 1.5 %collective-permute-start.15 = (bf16[32,2048]{1,0:T(8,128)(2,1)S(1)}, bf16[32,2048]{1,0:T(8,128)(2,1)S(1)}, u32[]{:S(2)}, u32[]{:S(2)}) collective-permute-start(bf16[32,2048]{1,0:T(8,128)(2,1)S(1)} %collective-permute-done.7.refs_7_), channel_id=1, source_target_pairs={{1,0},{0,1},{3,2},{2,3},{5,4},{4,5},{7,6},{6,7},{9,8},{8,9},{11,10... | collective-permute-start | bytes 393224 | tf_op jit(solution)/shard_map/ppermute | solution.py:306
  49.9 5.9 %collective-permute-start.16 = (bf16[32,2048]{1,0:T(8,128)(2,1)S(1)}, bf16[32,2048]{1,0:T(8,128)(2,1)S(1)}, u32[]{:S(2)}, u32[]{:S(2)}) collective-permute-start(bf16[32,2048]{1,0:T(8,128)(2,1)S(1)} %get-tuple-element.50), channel_id=1, source_target_pairs={{6,0},{23,1},{22,16},{9,17},{8,2},{25,3},{24,18},{11,19},{10,4},{2... | collective-permute-start | bytes 393224 | tf_op jit(solution)/shard_map/ppermute | solution.py:320
  50.0 11.3 %collective-permute-start.18 = (bf16[32,2048]{1,0:T(8,128)(2,1)S(1)}, bf16[32,2048]{1,0:T(8,128)(2,1)S(1)}, u32[]{:S(2)}, u32[]{:S(2)}) collective-permute-start(bf16[32,2048]{1,0:T(8,128)(2,1)S(1)} %get-tuple-element.51), channel_id=1, source_target_pairs={{8,0},{25,1},{24,16},{11,17},{10,2},{27,3},{26,18},{13,19},{12,4},... | collective-permute-start | bytes 393224 | tf_op jit(solution)/shard_map/ppermute | solution.py:320
  52.0 9.3 %collective-permute-start.20 = (bf16[32,2048]{1,0:T(8,128)(2,1)S(1)}, bf16[32,2048]{1,0:T(8,128)(2,1)S(1)}, u32[]{:S(2)}, u32[]{:S(2)}) collective-permute-start(bf16[32,2048]{1,0:T(8,128)(2,1)S(1)} %get-tuple-element.52), channel_id=1, source_target_pairs={{10,0},{27,1},{26,16},{13,17},{12,2},{29,3},{28,18},{15,19},{14,4}... | collective-permute-start | bytes 393224 | tf_op jit(solution)/shard_map/ppermute | solution.py:320
  53.0 10.3 %collective-permute-start.23 = (bf16[32,2048]{1,0:T(8,128)(2,1)S(1)}, bf16[32,2048]{1,0:T(8,128)(2,1)S(1)}, u32[]{:S(2)}, u32[]{:S(2)}) collective-permute-start(bf16[32,2048]{1,0:T(8,128)(2,1)S(1)} %get-tuple-element.54), channel_id=1, source_target_pairs={{0,0},{17,1},{16,16},{3,17},{2,2},{19,3},{18,18},{5,19},{4,4},{21,... | collective-permute-start | bytes 393224 | tf_op jit(solution)/shard_map/ppermute | solution.py:320
  53.7 14.3 %collective-permute-start.24 = (bf16[32,2048]{1,0:T(8,128)(2,1)S(1)}, bf16[32,2048]{1,0:T(8,128)(2,1)S(1)}, u32[]{:S(2)}, u32[]{:S(2)}) collective-permute-start(bf16[32,2048]{1,0:T(8,128)(2,1)S(1)} %get-tuple-element.55), channel_id=1, source_target_pairs={{2,0},{19,1},{18,16},{5,17},{4,2},{21,3},{20,18},{7,19},{6,4},{23,... | collective-permute-start | bytes 393224 | tf_op jit(solution)/shard_map/ppermute | solution.py:320
  55.8 15.9 %collective-permute-start.25 = (bf16[32,2048]{1,0:T(8,128)(2,1)S(1)}, bf16[32,2048]{1,0:T(8,128)(2,1)S(1)}, u32[]{:S(2)}, u32[]{:S(2)}) collective-permute-start(bf16[32,2048]{1,0:T(8,128)(2,1)S(1)} %get-tuple-element.56), channel_id=1, source_target_pairs={{4,0},{21,1},{20,16},{7,17},{6,2},{23,3},{22,18},{9,19},{8,4},{25,... | collective-permute-start | bytes 393224 | tf_op jit(solution)/shard_map/ppermute | solution.py:320
  61.2 13.7 %collective-permute-start.27 = (bf16[32,2048]{1,0:T(8,128)(2,1)S(1)}, bf16[32,2048]{1,0:T(8,128)(2,1)S(1)}, u32[]{:S(2)}, u32[]{:S(2)}) collective-permute-start(bf16[32,2048]{1,0:T(8,128)(2,1)S(1)} %get-tuple-element.58), channel_id=1, source_target_pairs={{14,0},{31,1},{30,16},{1,17},{0,2},{17,3},{16,18},{3,19},{2,4},{19... | collective-permute-start | bytes 393224 | tf_op jit(solution)/shard_map/ppermute | solution.py:320
  61.3 13.7 %collective-permute-start.22 = (bf16[32,2048]{1,0:T(8,128)(2,1)S(1)}, bf16[32,2048]{1,0:T(8,128)(2,1)S(1)}, u32[]{:S(2)}, u32[]{:S(2)}) collective-permute-start(bf16[32,2048]{1,0:T(8,128)(2,1)S(1)} %get-tuple-element.53), channel_id=1, source_target_pairs={{12,0},{29,1},{28,16},{15,17},{14,2},{31,3},{30,18},{1,19},{0,4},{... | collective-permute-start | bytes 393224 | tf_op jit(solution)/shard_map/ppermute | solution.py:320
  63.4 12.2 %collective-permute-start.29 = (bf16[32,2048]{1,0:T(8,128)(2,1)S(1)}, bf16[32,2048]{1,0:T(8,128)(2,1)S(1)}, u32[]{:S(2)}, u32[]{:S(2)}) collective-permute-start(bf16[32,2048]{1,0:T(8,128)(2,1)S(1)} %collective-permute-done.23.refs_1_), channel_id=1, source_target_pairs={{1,0},{0,1},{3,2},{2,3},{5,4},{4,5},{7,6},{6,7},{9,8},{8,9},{11,10... | collective-permute-start | bytes 393224 | tf_op jit(solution)/shard_map/ppermute | solution.py:306
  68.0 7.6 %collective-permute-start.30 = (bf16[32,2048]{1,0:T(8,128)(2,1)S(1)}, bf16[32,2048]{1,0:T(8,128)(2,1)S(1)}, u32[]{:S(2)}, u32[]{:S(2)}) collective-permute-start(bf16[32,2048]{1,0:T(8,128)(2,1)S(1)} %collective-permute-done.24.refs_2_), channel_id=1, source_target_pairs={{1,0},{0,1},{3,2},{2,3},{5,4},{4,5},{7,6},{6,7},{9,8},{8,9},{11,10... | collective-permute-start | bytes 393224 | tf_op jit(solution)/shard_map/ppermute | solution.py:306
  71.7 4.4 %collective-permute-start.31 = (bf16[32,2048]{1,0:T(8,128)(2,1)S(1)}, bf16[32,2048]{1,0:T(8,128)(2,1)S(1)}, u32[]{:S(2)}, u32[]{:S(2)}) collective-permute-start(bf16[32,2048]{1,0:T(8,128)(2,1)S(1)} %collective-permute-done.25.refs_3_), channel_id=1, source_target_pairs={{1,0},{0,1},{3,2},{2,3},{5,4},{4,5},{7,6},{6,7},{9,8},{8,9},{11,10... | collective-permute-start | bytes 393224 | tf_op jit(solution)/shard_map/ppermute | solution.py:306
  75.0 2.1 %collective-permute-start.26 = (bf16[32,2048]{1,0:T(8,128)(2,1)S(1)}, bf16[32,2048]{1,0:T(8,128)(2,1)S(1)}, u32[]{:S(2)}, u32[]{:S(2)}) collective-permute-start(bf16[32,2048]{1,0:T(8,128)(2,1)S(1)} %collective-permute-done.22.refs_2_), channel_id=1, source_target_pairs={{1,0},{0,1},{3,2},{2,3},{5,4},{4,5},{7,6},{6,7},{9,8},{8,9},{11,10... | collective-permute-start | bytes 393224 | tf_op jit(solution)/shard_map/ppermute | solution.py:306
  75.1 2.0 %collective-permute-start.17 = (bf16[32,2048]{1,0:T(8,128)(2,1)S(1)}, bf16[32,2048]{1,0:T(8,128)(2,1)S(1)}, u32[]{:S(2)}, u32[]{:S(2)}) collective-permute-start(bf16[32,2048]{1,0:T(8,128)(2,1)S(1)} %collective-permute-done.16.refs_4_), channel_id=1, source_target_pairs={{1,0},{0,1},{3,2},{2,3},{5,4},{4,5},{7,6},{6,7},{9,8},{8,9},{11,10... | collective-permute-start | bytes 393224 | tf_op jit(solution)/shard_map/ppermute | solution.py:306
  75.6 1.5 %collective-permute-start.19 = (bf16[32,2048]{1,0:T(8,128)(2,1)S(1)}, bf16[32,2048]{1,0:T(8,128)(2,1)S(1)}, u32[]{:S(2)}, u32[]{:S(2)}) collective-permute-start(bf16[32,2048]{1,0:T(8,128)(2,1)S(1)} %collective-permute-done.18.refs_5_), channel_id=1, source_target_pairs={{1,0},{0,1},{3,2},{2,3},{5,4},{4,5},{7,6},{6,7},{9,8},{8,9},{11,10... | collective-permute-start | bytes 393224 | tf_op jit(solution)/shard_map/ppermute | solution.py:306
  75.6 1.5 %collective-permute-start.21 = (bf16[32,2048]{1,0:T(8,128)(2,1)S(1)}, bf16[32,2048]{1,0:T(8,128)(2,1)S(1)}, u32[]{:S(2)}, u32[]{:S(2)}) collective-permute-start(bf16[32,2048]{1,0:T(8,128)(2,1)S(1)} %collective-permute-done.20.refs_6_), channel_id=1, source_target_pairs={{1,0},{0,1},{3,2},{2,3},{5,4},{4,5},{7,6},{6,7},{9,8},{8,9},{11,10... | collective-permute-start | bytes 393224 | tf_op jit(solution)/shard_map/ppermute | solution.py:306
  76.1 1.3 %collective-permute-start.28 = (bf16[32,2048]{1,0:T(8,128)(2,1)S(1)}, bf16[32,2048]{1,0:T(8,128)(2,1)S(1)}, u32[]{:S(2)}, u32[]{:S(2)}) collective-permute-start(bf16[32,2048]{1,0:T(8,128)(2,1)S(1)} %collective-permute-done.27.refs_3_), channel_id=1, source_target_pairs={{1,0},{0,1},{3,2},{2,3},{5,4},{4,5},{7,6},{6,7},{9,8},{8,9},{11,10... | collective-permute-start | bytes 393224 | tf_op jit(solution)/shard_map/ppermute | solution.py:306

commit v11 on v10

--- a/solution.py
+++ b/solution.py
@@ -344,18 +344,15 @@
 
         firsts = [lax.rem(place_of + lax.rem(rep + i, n_rep), n_shard)[None] for i in range(n_rep)]
         early = count - few
-        soon = 3 * count // 8
         whole = place(
             firsts, [[(0, j)] for j in range(early)], update[:early], n_rep, (experts, rows, cols)
         )
         update[early:] = [after(x, whole) for x in update[early:]]
-        swapped = others(update)
-        second = [(0, j) for j in range(early, count)]
-        second += [(i, j) for i in range(1, n_rep) for j in range(soon)]
-        third = [(i, j) for i in range(1, n_rep) for j in range(soon, count)]
-        for names in (second, third):
-            pieces = [swapped[i - 1][j] if i else update[j] for i, j in names]
-            whole = place(firsts, [[name] for name in names], pieces, n_rep, whole)
+        pieces = {(i, j): x for i, xs in enumerate([update, *others(update)]) for j, x in enumerate(xs)}
+        names = [(i, j) for i, j in pieces if i or j >= early]
+        whole = place(
+            firsts, [[name] for name in names], [pieces[name] for name in names], n_rep, whole
+        )
         return new_momentum, whole
 
     return jax.shard_map(

time: 78.8 us -> 80.1 us (1.016)
  the two profiles are of different devices: /device:TPU:0 before, /device:TPU:9 now
where the time goes in v11:
time: 80.1 us; the launch traced here: 79.9 us
  starting transfers between devices  31.4 us (39%)
  waiting for transfers between devices  25 us (31%)
  Pallas kernels  21 us (26%)
  local copies, waits for them, and re-layouts  1.6 us (2%)
  between operations  0.91 us (1%)
    ppermute x16, starting transfers between devices, exchange(): moved.append(lax.ppermute(x, ('shard', 'rep'), pairs))  29.2 us
    ppermute x16, waiting for transfers between devices, exchange(): moved.append(lax.ppermute(x, ('shard', 'rep'), pairs))  22.4 us
    pallas_call x1, Pallas kernels, orthogonal(): pl.pallas_call(functools.partial(orthogonal_kernel, scale, count), in_spe...  14.3 us
    pallas_call x1, Pallas kernels, blended_share(): pl.pallas_call(functools.partial(share_kernel, n_rep), in_specs=[pl.Block...  2.65 us
    ppermute x16, waiting for transfers between devices, others(): return [[lax.ppermute(x, 'rep', pair) for x in pieces] for pair in pairs]  2.57 us
    ppermute x16, starting transfers between devices, others(): return [[lax.ppermute(x, 'rep', pair) for x in pieces] for pair in pairs]  2.2 us
    pallas_call x2, Pallas kernels, place(): pl.pallas_call(functools.partial(place_kernel, which, n_rep), in_specs=[p...  2.05 us
    pallas_call x1, Pallas kernels, new_momentum_of(): pl.pallas_call(momentum_kernel, in_specs=[vmem, vmem], out_specs=vmem, ou...  2 us
  transfers between devices with their start and end apart: 32, of which 19 were waited for; matrix products, arithmetic and copies ran while one was open for 0% of the time, Pallas kernels for 4%

profile of v11, /device:TPU:9, one launch (start us, length us, event | category | flops | bytes accessed | tf_op | source)
XLA Modules:
  0.0 79.9 jit_solution(1179044266294346176)
XLA Ops:
  0.7 2.7 %share.1 = (bf16[32,2048]{1,0:T(8,128)(2,1)}, bf16[32,2048]{1,0:T(8,128)(2,1)}, bf16[32,2048]{1,0:T(8,128)(2,1)}, bf16[32,2048]{1,0:T(8,128)(2,1)}, bf16[32,2048...) custom-call(s32[1]{0:T(128)} %bitcast.at_ref, ...), custom_call_target="tpu_custom_call" | custom-call | tf_op jit(solution)/shard_map/share/pallas_call | solution.py:58
  3.3 4.2 %collective-permute-start = (bf16[32,2048]{1,0:T(8,128)(2,1)}, bf16[32,2048]{1,0:T(8,128)(2,1)S(1)}, u32[]{:S(2)}, u32[]{:S(2)}) collective-permute-start(bf16[32,2048]{1,0:T(8,128)(2,1)} %get-tuple-element.31), channel_id=1, source_target_pairs={{0,6},{1,23},{16,22},{17,9},{2,8},{3,25},{18,24},{19,11},{4,10},{5... | collective-permute-start | bytes 393224 | tf_op jit(solution)/shard_map/ppermute | solution.py:320
  7.6 3.1 %collective-permute-start.3 = (bf16[32,2048]{1,0:T(8,128)(2,1)}, bf16[32,2048]{1,0:T(8,128)(2,1)S(1)}, u32[]{:S(2)}, u32[]{:S(2)}) collective-permute-start(bf16[32,2048]{1,0:T(8,128)(2,1)} %get-tuple-element.38), channel_id=1, source_target_pairs={{0,4},{1,21},{16,20},{17,7},{2,6},{3,23},{18,22},{19,9},{4,8},{5,2... | collective-permute-start | bytes 393224 | tf_op jit(solution)/shard_map/ppermute | solution.py:320
  10.7 1.9 %collective-permute-start.1 = (bf16[32,2048]{1,0:T(8,128)(2,1)}, bf16[32,2048]{1,0:T(8,128)(2,1)S(1)}, u32[]{:S(2)}, u32[]{:S(2)}) collective-permute-start(bf16[32,2048]{1,0:T(8,128)(2,1)} %get-tuple-element.34), channel_id=1, source_target_pairs={{0,0},{1,17},{16,16},{17,3},{2,2},{3,19},{18,18},{19,5},{4,4},{5,2... | collective-permute-start | bytes 393224 | tf_op jit(solution)/shard_map/ppermute | solution.py:320
  12.6 1.5 %collective-permute-start.6 = (bf16[32,2048]{1,0:T(8,128)(2,1)}, bf16[32,2048]{1,0:T(8,128)(2,1)S(1)}, u32[]{:S(2)}, u32[]{:S(2)}) collective-permute-start(bf16[32,2048]{1,0:T(8,128)(2,1)} %get-tuple-element.46), channel_id=1, source_target_pairs={{0,12},{1,29},{16,28},{17,15},{2,14},{3,31},{18,30},{19,1},{4,0},{... | collective-permute-start | bytes 393224 | tf_op jit(solution)/shard_map/ppermute | solution.py:320
  14.1 1.9 %collective-permute-start.7 = (bf16[32,2048]{1,0:T(8,128)(2,1)}, bf16[32,2048]{1,0:T(8,128)(2,1)S(1)}, u32[]{:S(2)}, u32[]{:S(2)}) collective-permute-start(bf16[32,2048]{1,0:T(8,128)(2,1)} %get-tuple-element.48), channel_id=1, source_target_pairs={{0,14},{1,31},{16,30},{17,1},{2,0},{3,17},{18,16},{19,3},{4,2},{5,... | collective-permute-start | bytes 393224 | tf_op jit(solution)/shard_map/ppermute | solution.py:320
  16.0 0.7 collective-permute-done.2.refs_1_
  16.7 0.8 collective-permute-start.4
  17.5 2.1 %collective-permute-done.3.refs_2_ = bf16[32,2048]{1,0:T(8,128)(2,1)S(1)} collective-permute-done((bf16[32,2048]{1,0:T(8,128)(2,1)}, bf16[32,2048]{1,0:T(8,128)(2,1)S(1)}, u32[]{:S(2)}, u32[]{:S(2)}) %collective-permute-start.3) | collective-permute-done | bytes 131104 | tf_op jit(solution)/shard_map/ppermute | solution.py:320
  19.6 1.6 %copy-done.1 = bf16[16,32,2048]{2,1,0:T(8,128)(2,1)S(1)} copy-done((bf16[16,32,2048]{2,1,0:T(8,128)(2,1)S(1)}, bf16[16,32,2048]{2,1,0:T(8,128)(2,1)}, u32[]{:S(2)}) %copy-start.1) | copy-done | bytes 2097176
  21.2 2.0 %new_momentum.1 = bf16[16,32,2048]{2,1,0:T(8,128)(2,1)} custom-call(bf16[16,32,2048]{2,1,0:T(8,128)(2,1)S(1)} %copy-done, bf16[16,32,2048]{2,1,0:T(8,128)(2,1)S(1)} %copy-done.1), custom_call_target="tpu_custom_call" | custom-call | flops 2097152 | bytes 6291456 | tf_op jit(solution)/shard_map/new_momentum/pallas_call | solution.py:80
  23.2 3.4 %collective-permute-done.6.refs_6_ = bf16[32,2048]{1,0:T(8,128)(2,1)S(1)} collective-permute-done((bf16[32,2048]{1,0:T(8,128)(2,1)}, bf16[32,2048]{1,0:T(8,128)(2,1)S(1)}, u32[]{:S(2)}, u32[]{:S(2)}) %collective-permute-start.6) | collective-permute-done | bytes 131104 | tf_op jit(solution)/shard_map/ppermute | solution.py:320
  26.6 1.4 %collective-permute-done.7.refs_7_ = bf16[32,2048]{1,0:T(8,128)(2,1)S(1)} collective-permute-done((bf16[32,2048]{1,0:T(8,128)(2,1)}, bf16[32,2048]{1,0:T(8,128)(2,1)S(1)}, u32[]{:S(2)}, u32[]{:S(2)}) %collective-permute-start.7) | collective-permute-done | bytes 131104 | tf_op jit(solution)/shard_map/ppermute | solution.py:320
  28.0 2.8 %collective-permute-done.5.refs_5_ = bf16[32,2048]{1,0:T(8,128)(2,1)S(1)} collective-permute-done((bf16[32,2048]{1,0:T(8,128)(2,1)}, bf16[32,2048]{1,0:T(8,128)(2,1)S(1)}, u32[]{:S(2)}, u32[]{:S(2)}) %collective-permute-start.5) | collective-permute-done | bytes 131104 | tf_op jit(solution)/shard_map/ppermute | solution.py:320
  30.8 0.5 collective-permute-start.12
  31.3 0.0 collective-permute-start.13
  31.3 0.5 collective-permute-start.14
  31.8 0.1 collective-permute-start.15
  31.9 0.2 collective-permute-done.11.refs_11_
  32.2 0.2 collective-permute-done.12.refs_12_
  32.3 0.3 collective-permute-done.13.refs_13_
  32.7 0.2 collective-permute-done.14.refs_14_
  32.9 0.3 collective-permute-done.15.refs_15_
  33.2 14.3 %orthogonal.1 = (bf16[32,2048]{1,0:T(8,128)(2,1)S(1)}, bf16[32,2048]{1,0:T(8,128)(2,1)S(1)}, bf16[32,2048]{1,0:T(8,128)(2,1)S(1)}, bf16[32,2048]{1,0:T(8,128)(2,...) custom-call(bf16[32,2048]{1,0:T(8,128)(2,1)S(1)} %collective-permute, ...), custom_call_target="tpu_custom_call" | custom-call | tf_op jit(solution)/shard_map/orthogonal/pallas_call | solution.py:237
  47.5 3.9 %collective-permute-start.17 = (bf16[32,2048]{1,0:T(8,128)(2,1)S(1)}, bf16[32,2048]{1,0:T(8,128)(2,1)S(1)}, u32[]{:S(2)}, u32[]{:S(2)}) collective-permute-start(bf16[32,2048]{1,0:T(8,128)(2,1)S(1)} %get-tuple-element.51), channel_id=1, source_target_pairs={{0,0},{17,1},{16,16},{3,17},{2,2},{19,3},{18,18},{5,19},{4,4},{21,... | collective-permute-start | bytes 393224 | tf_op jit(solution)/shard_map/ppermute | solution.py:320
  51.5 0.1 collective-permute-start.18
  51.5 2.4 %collective-permute-start.19 = (bf16[32,2048]{1,0:T(8,128)(2,1)S(1)}, bf16[32,2048]{1,0:T(8,128)(2,1)S(1)}, u32[]{:S(2)}, u32[]{:S(2)}) collective-permute-start(bf16[32,2048]{1,0:T(8,128)(2,1)S(1)} %get-tuple-element.53), channel_id=1, source_target_pairs={{4,0},{21,1},{20,16},{7,17},{6,2},{23,3},{22,18},{9,19},{8,4},{25,... | collective-permute-start | bytes 393224 | tf_op jit(solution)/shard_map/ppermute | solution.py:320
  54.0 0.3 collective-permute-start.20
  54.2 3.9 %collective-permute-start.21 = (bf16[32,2048]{1,0:T(8,128)(2,1)S(1)}, bf16[32,2048]{1,0:T(8,128)(2,1)S(1)}, u32[]{:S(2)}, u32[]{:S(2)}) collective-permute-start(bf16[32,2048]{1,0:T(8,128)(2,1)S(1)} %get-tuple-element.55), channel_id=1, source_target_pairs={{8,0},{25,1},{24,16},{11,17},{10,2},{27,3},{26,18},{13,19},{12,4},... | collective-permute-start | bytes 393224 | tf_op jit(solution)/shard_map/ppermute | solution.py:320
  58.1 0.8 %collective-permute-start.22 = (bf16[32,2048]{1,0:T(8,128)(2,1)S(1)}, bf16[32,2048]{1,0:T(8,128)(2,1)S(1)}, u32[]{:S(2)}, u32[]{:S(2)}) collective-permute-start(bf16[32,2048]{1,0:T(8,128)(2,1)S(1)} %get-tuple-element.56), channel_id=1, source_target_pairs={{10,0},{27,1},{26,16},{13,17},{12,2},{29,3},{28,18},{15,19},{14,4}... | collective-permute-start | bytes 393224 | tf_op jit(solution)/shard_map/ppermute | solution.py:320
  58.9 2.7 %collective-permute-start.23 = (bf16[32,2048]{1,0:T(8,128)(2,1)S(1)}, bf16[32,2048]{1,0:T(8,128)(2,1)S(1)}, u32[]{:S(2)}, u32[]{:S(2)}) collective-permute-start(bf16[32,2048]{1,0:T(8,128)(2,1)S(1)} %get-tuple-element.58), channel_id=1, source_target_pairs={{14,0},{31,1},{30,16},{1,17},{0,2},{17,3},{16,18},{3,19},{2,4},{19... | collective-permute-start | bytes 393224 | tf_op jit(solution)/shard_map/ppermute | solution.py:320
  61.6 0.9 %collective-permute-done.19.refs_3_ = bf16[32,2048]{1,0:T(8,128)(2,1)S(1)} collective-permute-done((bf16[32,2048]{1,0:T(8,128)(2,1)S(1)}, bf16[32,2048]{1,0:T(8,128)(2,1)S(1)}, u32[]{:S(2)}, u32[]{:S(2)}) %collective-permute-start.19) | collective-permute-done | bytes 131104 | tf_op jit(solution)/shard_map/ppermute | solution.py:320
  62.5 1.7 %collective-permute-start.16 = (bf16[32,2048]{1,0:T(8,128)(2,1)S(1)}, bf16[32,2048]{1,0:T(8,128)(2,1)S(1)}, u32[]{:S(2)}, u32[]{:S(2)}) collective-permute-start(bf16[32,2048]{1,0:T(8,128)(2,1)S(1)} %get-tuple-element.50), channel_id=1, source_target_pairs={{12,0},{29,1},{28,16},{15,17},{14,2},{31,3},{30,18},{1,19},{0,4},{... | collective-permute-start | bytes 393224 | tf_op jit(solution)/shard_map/ppermute | solution.py:320
  64.2 4.6 %collective-permute-done.20.refs_4_ = bf16[32,2048]{1,0:T(8,128)(2,1)S(1)} collective-permute-done((bf16[32,2048]{1,0:T(8,128)(2,1)S(1)}, bf16[32,2048]{1,0:T(8,128)(2,1)S(1)}, u32[]{:S(2)}, u32[]{:S(2)}) %collective-permute-start.20) | collective-permute-done | bytes 131104 | tf_op jit(solution)/shard_map/ppermute | solution.py:320
  68.8 2.2 %collective-permute-done.21.refs_5_ = bf16[32,2048]{1,0:T(8,128)(2,1)S(1)} collective-permute-done((bf16[32,2048]{1,0:T(8,128)(2,1)S(1)}, bf16[32,2048]{1,0:T(8,128)(2,1)S(1)}, u32[]{:S(2)}, u32[]{:S(2)}) %collective-permute-start.21) | collective-permute-done | bytes 131104 | tf_op jit(solution)/shard_map/ppermute | solution.py:320
  71.0 1.0 %collective-permute-done.22.refs_6_ = bf16[32,2048]{1,0:T(8,128)(2,1)S(1)} collective-permute-done((bf16[32,2048]{1,0:T(8,128)(2,1)S(1)}, bf16[32,2048]{1,0:T(8,128)(2,1)S(1)}, u32[]{:S(2)}, u32[]{:S(2)}) %collective-permute-start.22) | collective-permute-done | bytes 131104 | tf_op jit(solution)/shard_map/ppermute | solution.py:320
  72.1 0.9 %place.2.refs_12_ = bf16[16,32,2048]{2,1,0:T(8,128)(2,1)} custom-call(s32[1]{0:T(128)} %bitcast.1.refs_0_, bf16[32,2048]{1,0:T(8,128)(2,1)S(1)} %collective-permute-done.17.refs_1_, bf16[32,2048]{1,0:T(8,128)(2,1)S(1)} %collective-permute-done.18.refs_2_, bf16[32,2048]{1,0:T(8,128)(2,1)S(1)} %collective-permute-done.19.refs_3_, ...), custom_call_target="tpu_custom_call" | custom-call | bytes 1572864 | tf_op jit(solution)/shard_map/place/pallas_call | solution.py:280
  73.0 3.2 %collective-permute-done.23.refs_3_ = bf16[32,2048]{1,0:T(8,128)(2,1)S(1)} collective-permute-done((bf16[32,2048]{1,0:T(8,128)(2,1)S(1)}, bf16[32,2048]{1,0:T(8,128)(2,1)S(1)}, u32[]{:S(2)}, u32[]{:S(2)}) %collective-permute-start.23) | collective-permute-done | bytes 131104 | tf_op jit(solution)/shard_map/ppermute | solution.py:320
  76.2 0.0 collective-permute-done.16.refs_2_
  76.2 0.5 collective-permute-start.27
  76.7 0.0 collective-permute-start.28
  76.7 0.5 collective-permute-start.29
  77.3 0.1 collective-permute-start.31
  77.3 0.4 collective-permute-done.27.refs_7_
  77.8 0.3 collective-permute-done.28.refs_8_
  78.1 0.2 collective-permute-done.29.refs_9_
  78.3 0.3 collective-permute-done.31.refs_11_
  78.6 1.1 %place.3 = bf16[16,32,2048]{2,1,0:T(8,128)(2,1)} custom-call(s32[1]{0:T(128)} %bitcast.1.refs_0_, s32[1]{0:T(128)} %bitcast.2.refs_1_, bf16[32,2048]{1,0:T(8,128)(2,1)S(1)} %collective-permute-done.16.refs_2_, bf16[32,2048]{1,0:T(8,128)(2,1)S(1)} %collective-permute-done.23.refs_3_, ...), custom_call_target="tpu_custom_call", output_to_operand_aliasing={{}: (12, {})} | custom-call | bytes 2621440 | tf_op jit(solution)/shard_map/place/pallas_call | solution.py:280
  (25 shorter events, 0.1 us)
Async XLA Ops:
  0.7 18.9 %copy-start = (bf16[16,32,2048]{2,1,0:T(8,128)(2,1)S(1)}, bf16[16,32,2048]{2,1,0:T(8,128)(2,1)}, u32[]{:S(2)}) copy-start(bf16[16,32,2048]{2,1,0:T(8,128)(2,1)} %m_ref) | copy-start | bytes 6291460
  3.3 10.8 %collective-permute-start = (bf16[32,2048]{1,0:T(8,128)(2,1)}, bf16[32,2048]{1,0:T(8,128)(2,1)S(1)}, u32[]{:S(2)}, u32[]{:S(2)}) collective-permute-start(bf16[32,2048]{1,0:T(8,128)(2,1)} %get-tuple-element.31), channel_id=1, source_target_pairs={{0,6},{1,23},{16,22},{17,9},{2,8},{3,25},{18,24},{19,11},{4,10},{5... | collective-permute-start | bytes 393224 | tf_op jit(solution)/shard_map/ppermute | solution.py:320
  7.6 9.2 %collective-permute-start.2 = (bf16[32,2048]{1,0:T(8,128)(2,1)}, bf16[32,2048]{1,0:T(8,128)(2,1)S(1)}, u32[]{:S(2)}, u32[]{:S(2)}) collective-permute-start(bf16[32,2048]{1,0:T(8,128)(2,1)} %get-tuple-element.36), channel_id=1, source_target_pairs={{0,2},{1,19},{16,18},{17,5},{2,4},{3,21},{18,20},{19,7},{4,6},{5,2... | collective-permute-start | bytes 393224 | tf_op jit(solution)/shard_map/ppermute | solution.py:320
  7.6 12.0 %collective-permute-start.3 = (bf16[32,2048]{1,0:T(8,128)(2,1)}, bf16[32,2048]{1,0:T(8,128)(2,1)S(1)}, u32[]{:S(2)}, u32[]{:S(2)}) collective-permute-start(bf16[32,2048]{1,0:T(8,128)(2,1)} %get-tuple-element.38), channel_id=1, source_target_pairs={{0,4},{1,21},{16,20},{17,7},{2,6},{3,23},{18,22},{19,9},{4,8},{5,2... | collective-permute-start | bytes 393224 | tf_op jit(solution)/shard_map/ppermute | solution.py:320
  10.7 12.4 %collective-permute-start.1 = (bf16[32,2048]{1,0:T(8,128)(2,1)}, bf16[32,2048]{1,0:T(8,128)(2,1)S(1)}, u32[]{:S(2)}, u32[]{:S(2)}) collective-permute-start(bf16[32,2048]{1,0:T(8,128)(2,1)} %get-tuple-element.34), channel_id=1, source_target_pairs={{0,0},{1,17},{16,16},{17,3},{2,2},{3,19},{18,18},{19,5},{4,4},{5,2... | collective-permute-start | bytes 393224 | tf_op jit(solution)/shard_map/ppermute | solution.py:320
  12.6 13.9 %collective-permute-start.6 = (bf16[32,2048]{1,0:T(8,128)(2,1)}, bf16[32,2048]{1,0:T(8,128)(2,1)S(1)}, u32[]{:S(2)}, u32[]{:S(2)}) collective-permute-start(bf16[32,2048]{1,0:T(8,128)(2,1)} %get-tuple-element.46), channel_id=1, source_target_pairs={{0,12},{1,29},{16,28},{17,15},{2,14},{3,31},{18,30},{19,1},{4,0},{... | collective-permute-start | bytes 393224 | tf_op jit(solution)/shard_map/ppermute | solution.py:320
  14.1 13.9 %collective-permute-start.7 = (bf16[32,2048]{1,0:T(8,128)(2,1)}, bf16[32,2048]{1,0:T(8,128)(2,1)S(1)}, u32[]{:S(2)}, u32[]{:S(2)}) collective-permute-start(bf16[32,2048]{1,0:T(8,128)(2,1)} %get-tuple-element.48), channel_id=1, source_target_pairs={{0,14},{1,31},{16,30},{17,1},{2,0},{3,17},{18,16},{19,3},{4,2},{5,... | collective-permute-start | bytes 393224 | tf_op jit(solution)/shard_map/ppermute | solution.py:320
  16.7 14.1 %collective-permute-start.4 = (bf16[32,2048]{1,0:T(8,128)(2,1)}, bf16[32,2048]{1,0:T(8,128)(2,1)S(1)}, u32[]{:S(2)}, u32[]{:S(2)}) collective-permute-start(bf16[32,2048]{1,0:T(8,128)(2,1)} %get-tuple-element.42), channel_id=1, source_target_pairs={{0,8},{1,25},{16,24},{17,11},{2,10},{3,27},{18,26},{19,13},{4,12},... | collective-permute-start | bytes 393224 | tf_op jit(solution)/shard_map/ppermute | solution.py:320
  19.6 11.2 %collective-permute-start.5 = (bf16[32,2048]{1,0:T(8,128)(2,1)}, bf16[32,2048]{1,0:T(8,128)(2,1)S(1)}, u32[]{:S(2)}, u32[]{:S(2)}) collective-permute-start(bf16[32,2048]{1,0:T(8,128)(2,1)} %get-tuple-element.44), channel_id=1, source_target_pairs={{0,10},{1,27},{16,26},{17,13},{2,12},{3,29},{18,28},{19,15},{4,14}... | collective-permute-start | bytes 393224 | tf_op jit(solution)/shard_map/ppermute | solution.py:320
  19.6 1.6 %copy-start.1 = (bf16[16,32,2048]{2,1,0:T(8,128)(2,1)S(1)}, bf16[16,32,2048]{2,1,0:T(8,128)(2,1)}, u32[]{:S(2)}) copy-start(bf16[16,32,2048]{2,1,0:T(8,128)(2,1)} %g_ref) | copy-start | bytes 6291460
  23.2 8.1 %collective-permute-start.8 = (bf16[32,2048]{1,0:T(8,128)(2,1)S(1)}, bf16[32,2048]{1,0:T(8,128)(2,1)S(1)}, u32[]{:S(2)}, u32[]{:S(2)}) collective-permute-start(bf16[32,2048]{1,0:T(8,128)(2,1)S(1)} %collective-permute-done.1.refs_0_), channel_id=1, source_target_pairs={{1,0},{0,1},{3,2},{2,3},{5,4},{4,5},{7,6},{6,7},{9,8},{8,9},{11,10... | collective-permute-start | bytes 393224 | tf_op jit(solution)/shard_map/ppermute | solution.py:306
  26.6 4.7 %collective-permute-start.9 = (bf16[32,2048]{1,0:T(8,128)(2,1)S(1)}, bf16[32,2048]{1,0:T(8,128)(2,1)S(1)}, u32[]{:S(2)}, u32[]{:S(2)}) collective-permute-start(bf16[32,2048]{1,0:T(8,128)(2,1)S(1)} %collective-permute-done.2.refs_1_), channel_id=1, source_target_pairs={{1,0},{0,1},{3,2},{2,3},{5,4},{4,5},{7,6},{6,7},{9,8},{8,9},{11,10... | collective-permute-start | bytes 393224 | tf_op jit(solution)/shard_map/ppermute | solution.py:306
  28.0 3.8 %collective-permute-start.10 = (bf16[32,2048]{1,0:T(8,128)(2,1)S(1)}, bf16[32,2048]{1,0:T(8,128)(2,1)S(1)}, u32[]{:S(2)}, u32[]{:S(2)}) collective-permute-start(bf16[32,2048]{1,0:T(8,128)(2,1)S(1)} %collective-permute-done.3.refs_2_), channel_id=1, source_target_pairs={{1,0},{0,1},{3,2},{2,3},{5,4},{4,5},{7,6},{6,7},{9,8},{8,9},{11,10... | collective-permute-start | bytes 393224 | tf_op jit(solution)/shard_map/ppermute | solution.py:306
  30.8 1.3 %collective-permute-start.11 = (bf16[32,2048]{1,0:T(8,128)(2,1)S(1)}, bf16[32,2048]{1,0:T(8,128)(2,1)S(1)}, u32[]{:S(2)}, u32[]{:S(2)}) collective-permute-start(bf16[32,2048]{1,0:T(8,128)(2,1)S(1)} %collective-permute-done.refs_3_), channel_id=1, source_target_pairs={{1,0},{0,1},{3,2},{2,3},{5,4},{4,5},{7,6},{6,7},{9,8},{8,9},{11,10... | collective-permute-start | bytes 393224 | tf_op jit(solution)/shard_map/ppermute | solution.py:306
  30.8 1.5 %collective-permute-start.12 = (bf16[32,2048]{1,0:T(8,128)(2,1)S(1)}, bf16[32,2048]{1,0:T(8,128)(2,1)S(1)}, u32[]{:S(2)}, u32[]{:S(2)}) collective-permute-start(bf16[32,2048]{1,0:T(8,128)(2,1)S(1)} %collective-permute-done.4.refs_4_), channel_id=1, source_target_pairs={{1,0},{0,1},{3,2},{2,3},{5,4},{4,5},{7,6},{6,7},{9,8},{8,9},{11,10... | collective-permute-start | bytes 393224 | tf_op jit(solution)/shard_map/ppermute | solution.py:306
  31.3 1.3 %collective-permute-start.13 = (bf16[32,2048]{1,0:T(8,128)(2,1)S(1)}, bf16[32,2048]{1,0:T(8,128)(2,1)S(1)}, u32[]{:S(2)}, u32[]{:S(2)}) collective-permute-start(bf16[32,2048]{1,0:T(8,128)(2,1)S(1)} %collective-permute-done.5.refs_5_), channel_id=1, source_target_pairs={{1,0},{0,1},{3,2},{2,3},{5,4},{4,5},{7,6},{6,7},{9,8},{8,9},{11,10... | collective-permute-start | bytes 393224 | tf_op jit(solution)/shard_map/ppermute | solution.py:306
  31.3 1.5 %collective-permute-start.14 = (bf16[32,2048]{1,0:T(8,128)(2,1)S(1)}, bf16[32,2048]{1,0:T(8,128)(2,1)S(1)}, u32[]{:S(2)}, u32[]{:S(2)}) collective-permute-start(bf16[32,2048]{1,0:T(8,128)(2,1)S(1)} %collective-permute-done.6.refs_6_), channel_id=1, source_target_pairs={{1,0},{0,1},{3,2},{2,3},{5,4},{4,5},{7,6},{6,7},{9,8},{8,9},{11,10... | collective-permute-start | bytes 393224 | tf_op jit(solution)/shard_map/ppermute | solution.py:306
  31.8 1.3 %collective-permute-start.15 = (bf16[32,2048]{1,0:T(8,128)(2,1)S(1)}, bf16[32,2048]{1,0:T(8,128)(2,1)S(1)}, u32[]{:S(2)}, u32[]{:S(2)}) collective-permute-start(bf16[32,2048]{1,0:T(8,128)(2,1)S(1)} %collective-permute-done.7.refs_7_), channel_id=1, source_target_pairs={{1,0},{0,1},{3,2},{2,3},{5,4},{4,5},{7,6},{6,7},{9,8},{8,9},{11,10... | collective-permute-start | bytes 393224 | tf_op jit(solution)/shard_map/ppermute | solution.py:306
  47.5 10.6 %collective-permute-start.17 = (bf16[32,2048]{1,0:T(8,128)(2,1)S(1)}, bf16[32,2048]{1,0:T(8,128)(2,1)S(1)}, u32[]{:S(2)}, u32[]{:S(2)}) collective-permute-start(bf16[32,2048]{1,0:T(8,128)(2,1)S(1)} %get-tuple-element.51), channel_id=1, source_target_pairs={{0,0},{17,1},{16,16},{3,17},{2,2},{19,3},{18,18},{5,19},{4,4},{21,... | collective-permute-start | bytes 393224 | tf_op jit(solution)/shard_map/ppermute | solution.py:320
  51.5 7.5 %collective-permute-start.18 = (bf16[32,2048]{1,0:T(8,128)(2,1)S(1)}, bf16[32,2048]{1,0:T(8,128)(2,1)S(1)}, u32[]{:S(2)}, u32[]{:S(2)}) collective-permute-start(bf16[32,2048]{1,0:T(8,128)(2,1)S(1)} %get-tuple-element.52), channel_id=1, source_target_pairs={{2,0},{19,1},{18,16},{5,17},{4,2},{21,3},{20,18},{7,19},{6,4},{23,... | collective-permute-start | bytes 393224 | tf_op jit(solution)/shard_map/ppermute | solution.py:320
  51.5 11.0 %collective-permute-start.19 = (bf16[32,2048]{1,0:T(8,128)(2,1)S(1)}, bf16[32,2048]{1,0:T(8,128)(2,1)S(1)}, u32[]{:S(2)}, u32[]{:S(2)}) collective-permute-start(bf16[32,2048]{1,0:T(8,128)(2,1)S(1)} %get-tuple-element.53), channel_id=1, source_target_pairs={{4,0},{21,1},{20,16},{7,17},{6,2},{23,3},{22,18},{9,19},{8,4},{25,... | collective-permute-start | bytes 393224 | tf_op jit(solution)/shard_map/ppermute | solution.py:320
  54.0 14.8 %collective-permute-start.20 = (bf16[32,2048]{1,0:T(8,128)(2,1)S(1)}, bf16[32,2048]{1,0:T(8,128)(2,1)S(1)}, u32[]{:S(2)}, u32[]{:S(2)}) collective-permute-start(bf16[32,2048]{1,0:T(8,128)(2,1)S(1)} %get-tuple-element.54), channel_id=1, source_target_pairs={{6,0},{23,1},{22,16},{9,17},{8,2},{25,3},{24,18},{11,19},{10,4},{2... | collective-permute-start | bytes 393224 | tf_op jit(solution)/shard_map/ppermute | solution.py:320
  54.2 16.8 %collective-permute-start.21 = (bf16[32,2048]{1,0:T(8,128)(2,1)S(1)}, bf16[32,2048]{1,0:T(8,128)(2,1)S(1)}, u32[]{:S(2)}, u32[]{:S(2)}) collective-permute-start(bf16[32,2048]{1,0:T(8,128)(2,1)S(1)} %get-tuple-element.55), channel_id=1, source_target_pairs={{8,0},{25,1},{24,16},{11,17},{10,2},{27,3},{26,18},{13,19},{12,4},... | collective-permute-start | bytes 393224 | tf_op jit(solution)/shard_map/ppermute | solution.py:320
  58.1 13.9 %collective-permute-start.22 = (bf16[32,2048]{1,0:T(8,128)(2,1)S(1)}, bf16[32,2048]{1,0:T(8,128)(2,1)S(1)}, u32[]{:S(2)}, u32[]{:S(2)}) collective-permute-start(bf16[32,2048]{1,0:T(8,128)(2,1)S(1)} %get-tuple-element.56), channel_id=1, source_target_pairs={{10,0},{27,1},{26,16},{13,17},{12,2},{29,3},{28,18},{15,19},{14,4}... | collective-permute-start | bytes 393224 | tf_op jit(solution)/shard_map/ppermute | solution.py:320
  58.9 17.2 %collective-permute-start.23 = (bf16[32,2048]{1,0:T(8,128)(2,1)S(1)}, bf16[32,2048]{1,0:T(8,128)(2,1)S(1)}, u32[]{:S(2)}, u32[]{:S(2)}) collective-permute-start(bf16[32,2048]{1,0:T(8,128)(2,1)S(1)} %get-tuple-element.58), channel_id=1, source_target_pairs={{14,0},{31,1},{30,16},{1,17},{0,2},{17,3},{16,18},{3,19},{2,4},{19... | collective-permute-start | bytes 393224 | tf_op jit(solution)/shard_map/ppermute | solution.py:320
  62.5 13.7 %collective-permute-start.16 = (bf16[32,2048]{1,0:T(8,128)(2,1)S(1)}, bf16[32,2048]{1,0:T(8,128)(2,1)S(1)}, u32[]{:S(2)}, u32[]{:S(2)}) collective-permute-start(bf16[32,2048]{1,0:T(8,128)(2,1)S(1)} %get-tuple-element.50), channel_id=1, source_target_pairs={{12,0},{29,1},{28,16},{15,17},{14,2},{31,3},{30,18},{1,19},{0,4},{... | collective-permute-start | bytes 393224 | tf_op jit(solution)/shard_map/ppermute | solution.py:320
  68.8 7.9 %collective-permute-start.24 = (bf16[32,2048]{1,0:T(8,128)(2,1)S(1)}, bf16[32,2048]{1,0:T(8,128)(2,1)S(1)}, u32[]{:S(2)}, u32[]{:S(2)}) collective-permute-start(bf16[32,2048]{1,0:T(8,128)(2,1)S(1)} %collective-permute-done.17.refs_1_), channel_id=1, source_target_pairs={{1,0},{0,1},{3,2},{2,3},{5,4},{4,5},{7,6},{6,7},{9,8},{8,9},{11,10... | collective-permute-start | bytes 393224 | tf_op jit(solution)/shard_map/ppermute | solution.py:306
  71.0 5.7 %collective-permute-start.25 = (bf16[32,2048]{1,0:T(8,128)(2,1)S(1)}, bf16[32,2048]{1,0:T(8,128)(2,1)S(1)}, u32[]{:S(2)}, u32[]{:S(2)}) collective-permute-start(bf16[32,2048]{1,0:T(8,128)(2,1)S(1)} %collective-permute-done.18.refs_2_), channel_id=1, source_target_pairs={{1,0},{0,1},{3,2},{2,3},{5,4},{4,5},{7,6},{6,7},{9,8},{8,9},{11,10... | collective-permute-start | bytes 393224 | tf_op jit(solution)/shard_map/ppermute | solution.py:306
  72.1 5.2 %collective-permute-start.26 = (bf16[32,2048]{1,0:T(8,128)(2,1)S(1)}, bf16[32,2048]{1,0:T(8,128)(2,1)S(1)}, u32[]{:S(2)}, u32[]{:S(2)}) collective-permute-start(bf16[32,2048]{1,0:T(8,128)(2,1)S(1)} %collective-permute-done.19.refs_3_), channel_id=1, source_target_pairs={{1,0},{0,1},{3,2},{2,3},{5,4},{4,5},{7,6},{6,7},{9,8},{8,9},{11,10... | collective-permute-start | bytes 393224 | tf_op jit(solution)/shard_map/ppermute | solution.py:306
  76.2 2.1 %collective-permute-start.30 = (bf16[32,2048]{1,0:T(8,128)(2,1)S(1)}, bf16[32,2048]{1,0:T(8,128)(2,1)S(1)}, u32[]{:S(2)}, u32[]{:S(2)}) collective-permute-start(bf16[32,2048]{1,0:T(8,128)(2,1)S(1)} %collective-permute-done.16.refs_2_), channel_id=1, source_target_pairs={{1,0},{0,1},{3,2},{2,3},{5,4},{4,5},{7,6},{6,7},{9,8},{8,9},{11,10... | collective-permute-start | bytes 393224 | tf_op jit(solution)/shard_map/ppermute | solution.py:306
  76.2 1.5 %collective-permute-start.27 = (bf16[32,2048]{1,0:T(8,128)(2,1)S(1)}, bf16[32,2048]{1,0:T(8,128)(2,1)S(1)}, u32[]{:S(2)}, u32[]{:S(2)}) collective-permute-start(bf16[32,2048]{1,0:T(8,128)(2,1)S(1)} %collective-permute-done.20.refs_4_), channel_id=1, source_target_pairs={{1,0},{0,1},{3,2},{2,3},{5,4},{4,5},{7,6},{6,7},{9,8},{8,9},{11,10... | collective-permute-start | bytes 393224 | tf_op jit(solution)/shard_map/ppermute | solution.py:306
  76.7 1.3 %collective-permute-start.28 = (bf16[32,2048]{1,0:T(8,128)(2,1)S(1)}, bf16[32,2048]{1,0:T(8,128)(2,1)S(1)}, u32[]{:S(2)}, u32[]{:S(2)}) collective-permute-start(bf16[32,2048]{1,0:T(8,128)(2,1)S(1)} %collective-permute-done.21.refs_5_), channel_id=1, source_target_pairs={{1,0},{0,1},{3,2},{2,3},{5,4},{4,5},{7,6},{6,7},{9,8},{8,9},{11,10... | collective-permute-start | bytes 393224 | tf_op jit(solution)/shard_map/ppermute | solution.py:306
  76.7 1.5 %collective-permute-start.29 = (bf16[32,2048]{1,0:T(8,128)(2,1)S(1)}, bf16[32,2048]{1,0:T(8,128)(2,1)S(1)}, u32[]{:S(2)}, u32[]{:S(2)}) collective-permute-start(bf16[32,2048]{1,0:T(8,128)(2,1)S(1)} %collective-permute-done.22.refs_6_), channel_id=1, source_target_pairs={{1,0},{0,1},{3,2},{2,3},{5,4},{4,5},{7,6},{6,7},{9,8},{8,9},{11,10... | collective-permute-start | bytes 393224 | tf_op jit(solution)/shard_map/ppermute | solution.py:306
  77.3 1.3 %collective-permute-start.31 = (bf16[32,2048]{1,0:T(8,128)(2,1)S(1)}, bf16[32,2048]{1,0:T(8,128)(2,1)S(1)}, u32[]{:S(2)}, u32[]{:S(2)}) collective-permute-start(bf16[32,2048]{1,0:T(8,128)(2,1)S(1)} %collective-permute-done.23.refs_3_), channel_id=1, source_target_pairs={{1,0},{0,1},{3,2},{2,3},{5,4},{4,5},{7,6},{6,7},{9,8},{8,9},{11,10... | collective-permute-start | bytes 393224 | tf_op jit(solution)/shard_map/ppermute | solution.py:306

commit v12 on v11

--- a/solution.py
+++ b/solution.py
@@ -305,9 +305,9 @@
         pairs = [[((i + j) % n_rep, i) for i in range(n_rep)] for j in range(1, n_rep)]
         return [[lax.ppermute(x, "rep", pair) for x in pieces] for pair in pairs]
 
-    def exchange(pieces, there):
+    def exchange(pieces, steps, there):
         moved = []
-        for j, x in enumerate(pieces):
+        for j, x in zip(steps, pieces):
             pairs = [
                 (
                     order[p] * n_rep + r,
@@ -329,7 +329,9 @@
         place_of = 2 * lax.rem(shard, middle) + shard // middle
         first = lax.rem(place_of + rep, n_shard)
         few = count // 4
-        own = exchange(blended_share(first, momentum, gradient, count, n_rep), True)
+        own = exchange(
+            blended_share(first, momentum, gradient, count, n_rep), range(count), True
+        )
 
         middle_piece = (count - 1) // 2
         momentum, gradient, own[middle_piece] = lax.optimization_barrier(
@@ -340,18 +342,20 @@
 
         scale = float(max(experts * rows, cols)) ** 0.5
         parts = own + [x for xs in others(own) for x in xs]
-        update = exchange(orthogonal(parts, count, scale), False)
+        update = orthogonal(parts, count, scale)
+        early = count - few
+        steps = [(j + early // 2) % early if j < early else j for j in range(count)]
+        update = exchange([update[j] for j in steps], steps, False)
 
         firsts = [lax.rem(place_of + lax.rem(rep + i, n_rep), n_shard)[None] for i in range(n_rep)]
-        early = count - few
         whole = place(
-            firsts, [[(0, j)] for j in range(early)], update[:early], n_rep, (experts, rows, cols)
+            firsts, [[(0, j)] for j in steps[:early]], update[:early], n_rep, (experts, rows, cols)
         )
         update[early:] = [after(x, whole) for x in update[early:]]
         pieces = {(i, j): x for i, xs in enumerate([update, *others(update)]) for j, x in enumerate(xs)}
         names = [(i, j) for i, j in pieces if i or j >= early]
         whole = place(
-            firsts, [[name] for name in names], [pieces[name] for name in names], n_rep, whole
+            firsts, [[(i, steps[j])] for i, j in names], [pieces[name] for name in names], n_rep, whole
         )
         return new_momentum, whole
 

time: 80.1 us -> 79.1 us (0.988)
  the two profiles are of different devices: /device:TPU:9 before, /device:TPU:0 now
where the time goes in v12:
time: 79.1 us; the launch traced here: 78.7 us
  starting transfers between devices  47.5 us (60%)
  Pallas kernels  21 us (27%)
  waiting for transfers between devices  7.67 us (10%)
  local copies, waits for them, and re-layouts  1.6 us (2%)
  between operations  0.92 us (1%)
    ppermute x16, starting transfers between devices, exchange(): moved.append(lax.ppermute(x, ('shard', 'rep'), pairs))  24.9 us
    ppermute x16, starting transfers between devices, others(): return [[lax.ppermute(x, 'rep', pair) for x in pieces] for pair in pairs]  22.6 us
    pallas_call x1, Pallas kernels, orthogonal(): pl.pallas_call(functools.partial(orthogonal_kernel, scale, count), in_spe...  14.3 us
    ppermute x16, waiting for transfers between devices, exchange(): moved.append(lax.ppermute(x, ('shard', 'rep'), pairs))  5.37 us
    pallas_call x1, Pallas kernels, blended_share(): pl.pallas_call(functools.partial(share_kernel, n_rep), in_specs=[pl.Block...  2.65 us
    ppermute x16, waiting for transfers between devices, others(): return [[lax.ppermute(x, 'rep', pair) for x in pieces] for pair in pairs]  2.3 us
    pallas_call x2, Pallas kernels, place(): pl.pallas_call(functools.partial(place_kernel, which, n_rep), in_specs=[p...  2.05 us
    pallas_call x1, Pallas kernels, new_momentum_of(): pl.pallas_call(momentum_kernel, in_specs=[vmem, vmem], out_specs=vmem, ou...  2 us
  transfers between devices with their start and end apart: 32, of which 12 were waited for; matrix products, arithmetic and copies ran while one was open for 0% of the time, Pallas kernels for 4%

profile of v12, /device:TPU:0, one launch (start us, length us, event | category | flops | bytes accessed | tf_op | source)
XLA Modules:
  0.0 78.7 jit_solution(3448905311583706476)
XLA Ops:
  0.7 2.7 %share.1 = (bf16[32,2048]{1,0:T(8,128)(2,1)}, bf16[32,2048]{1,0:T(8,128)(2,1)}, bf16[32,2048]{1,0:T(8,128)(2,1)}, bf16[32,2048]{1,0:T(8,128)(2,1)}, bf16[32,2048...) custom-call(s32[1]{0:T(128)} %bitcast.at_ref, ...), custom_call_target="tpu_custom_call" | custom-call | tf_op jit(solution)/shard_map/share/pallas_call | solution.py:58
  3.3 3.9 %collective-permute-start = (bf16[32,2048]{1,0:T(8,128)(2,1)}, bf16[32,2048]{1,0:T(8,128)(2,1)S(1)}, u32[]{:S(2)}, u32[]{:S(2)}) collective-permute-start(bf16[32,2048]{1,0:T(8,128)(2,1)} %get-tuple-element.31), channel_id=1, source_target_pairs={{0,6},{1,23},{16,22},{17,9},{2,8},{3,25},{18,24},{19,11},{4,10},{5... | collective-permute-start | bytes 393224 | tf_op jit(solution)/shard_map/ppermute | solution.py:320
  7.3 0.6 collective-permute-start.2
  7.9 1.5 %collective-permute-start.3 = (bf16[32,2048]{1,0:T(8,128)(2,1)}, bf16[32,2048]{1,0:T(8,128)(2,1)S(1)}, u32[]{:S(2)}, u32[]{:S(2)}) collective-permute-start(bf16[32,2048]{1,0:T(8,128)(2,1)} %get-tuple-element.38), channel_id=1, source_target_pairs={{0,4},{1,21},{16,20},{17,7},{2,6},{3,23},{18,22},{19,9},{4,8},{5,2... | collective-permute-start | bytes 393224 | tf_op jit(solution)/shard_map/ppermute | solution.py:320
  9.4 1.6 %collective-permute-start.1 = (bf16[32,2048]{1,0:T(8,128)(2,1)}, bf16[32,2048]{1,0:T(8,128)(2,1)S(1)}, u32[]{:S(2)}, u32[]{:S(2)}) collective-permute-start(bf16[32,2048]{1,0:T(8,128)(2,1)} %get-tuple-element.34), channel_id=1, source_target_pairs={{0,0},{1,17},{16,16},{17,3},{2,2},{3,19},{18,18},{19,5},{4,4},{5,2... | collective-permute-start | bytes 393224 | tf_op jit(solution)/shard_map/ppermute | solution.py:320
  10.9 1.4 %collective-permute-start.6 = (bf16[32,2048]{1,0:T(8,128)(2,1)}, bf16[32,2048]{1,0:T(8,128)(2,1)S(1)}, u32[]{:S(2)}, u32[]{:S(2)}) collective-permute-start(bf16[32,2048]{1,0:T(8,128)(2,1)} %get-tuple-element.46), channel_id=1, source_target_pairs={{0,12},{1,29},{16,28},{17,15},{2,14},{3,31},{18,30},{19,1},{4,0},{... | collective-permute-start | bytes 393224 | tf_op jit(solution)/shard_map/ppermute | solution.py:320
  12.3 2.3 %collective-permute-start.7 = (bf16[32,2048]{1,0:T(8,128)(2,1)}, bf16[32,2048]{1,0:T(8,128)(2,1)S(1)}, u32[]{:S(2)}, u32[]{:S(2)}) collective-permute-start(bf16[32,2048]{1,0:T(8,128)(2,1)} %get-tuple-element.48), channel_id=1, source_target_pairs={{0,14},{1,31},{16,30},{17,1},{2,0},{3,17},{18,16},{19,3},{4,2},{5,... | collective-permute-start | bytes 393224 | tf_op jit(solution)/shard_map/ppermute | solution.py:320
  14.7 1.7 %collective-permute-done.2.refs_1_ = bf16[32,2048]{1,0:T(8,128)(2,1)S(1)} collective-permute-done((bf16[32,2048]{1,0:T(8,128)(2,1)}, bf16[32,2048]{1,0:T(8,128)(2,1)S(1)}, u32[]{:S(2)}, u32[]{:S(2)}) %collective-permute-start.2) | collective-permute-done | bytes 131104 | tf_op jit(solution)/shard_map/ppermute | solution.py:320
  16.3 2.0 %collective-permute-start.4 = (bf16[32,2048]{1,0:T(8,128)(2,1)}, bf16[32,2048]{1,0:T(8,128)(2,1)S(1)}, u32[]{:S(2)}, u32[]{:S(2)}) collective-permute-start(bf16[32,2048]{1,0:T(8,128)(2,1)} %get-tuple-element.42), channel_id=1, source_target_pairs={{0,8},{1,25},{16,24},{17,11},{2,10},{3,27},{18,26},{19,13},{4,12},... | collective-permute-start | bytes 393224 | tf_op jit(solution)/shard_map/ppermute | solution.py:320
  18.4 0.5 collective-permute-done.3.refs_2_
  18.9 1.2 %collective-permute-start.5 = (bf16[32,2048]{1,0:T(8,128)(2,1)}, bf16[32,2048]{1,0:T(8,128)(2,1)S(1)}, u32[]{:S(2)}, u32[]{:S(2)}) collective-permute-start(bf16[32,2048]{1,0:T(8,128)(2,1)} %get-tuple-element.44), channel_id=1, source_target_pairs={{0,10},{1,27},{16,26},{17,13},{2,12},{3,29},{18,28},{19,15},{4,14}... | collective-permute-start | bytes 393224 | tf_op jit(solution)/shard_map/ppermute | solution.py:320
  20.1 1.6 %copy-done.1 = bf16[16,32,2048]{2,1,0:T(8,128)(2,1)S(1)} copy-done((bf16[16,32,2048]{2,1,0:T(8,128)(2,1)S(1)}, bf16[16,32,2048]{2,1,0:T(8,128)(2,1)}, u32[]{:S(2)}) %copy-start.1) | copy-done | bytes 2097176
  21.7 2.0 %new_momentum.1 = bf16[16,32,2048]{2,1,0:T(8,128)(2,1)} custom-call(bf16[16,32,2048]{2,1,0:T(8,128)(2,1)S(1)} %copy-done, bf16[16,32,2048]{2,1,0:T(8,128)(2,1)S(1)} %copy-done.1), custom_call_target="tpu_custom_call" | custom-call | flops 2097152 | bytes 6291456 | tf_op jit(solution)/shard_map/new_momentum/pallas_call | solution.py:80
  23.7 2.6 %collective-permute-start.8 = (bf16[32,2048]{1,0:T(8,128)(2,1)S(1)}, bf16[32,2048]{1,0:T(8,128)(2,1)S(1)}, u32[]{:S(2)}, u32[]{:S(2)}) collective-permute-start(bf16[32,2048]{1,0:T(8,128)(2,1)S(1)} %collective-permute-done.1.refs_0_), channel_id=1, source_target_pairs={{1,0},{0,1},{3,2},{2,3},{5,4},{4,5},{7,6},{6,7},{9,8},{8,9},{11,10... | collective-permute-start | bytes 393224 | tf_op jit(solution)/shard_map/ppermute | solution.py:306
  26.3 1.0 %collective-permute-start.9 = (bf16[32,2048]{1,0:T(8,128)(2,1)S(1)}, bf16[32,2048]{1,0:T(8,128)(2,1)S(1)}, u32[]{:S(2)}, u32[]{:S(2)}) collective-permute-start(bf16[32,2048]{1,0:T(8,128)(2,1)S(1)} %collective-permute-done.2.refs_1_), channel_id=1, source_target_pairs={{1,0},{0,1},{3,2},{2,3},{5,4},{4,5},{7,6},{6,7},{9,8},{8,9},{11,10... | collective-permute-start | bytes 393224 | tf_op jit(solution)/shard_map/ppermute | solution.py:306
  27.3 0.6 collective-permute-start.10
  27.9 5.5 %collective-permute-start.11 = (bf16[32,2048]{1,0:T(8,128)(2,1)S(1)}, bf16[32,2048]{1,0:T(8,128)(2,1)S(1)}, u32[]{:S(2)}, u32[]{:S(2)}) collective-permute-start(bf16[32,2048]{1,0:T(8,128)(2,1)S(1)} %collective-permute-done.refs_3_), channel_id=1, source_target_pairs={{1,0},{0,1},{3,2},{2,3},{5,4},{4,5},{7,6},{6,7},{9,8},{8,9},{11,10... | collective-permute-start | bytes 393224 | tf_op jit(solution)/shard_map/ppermute | solution.py:306
  33.5 0.5 collective-permute-start.13
  34.0 0.1 collective-permute-start.14
  34.1 0.4 collective-permute-start.15
  34.5 0.3 collective-permute-done.12.refs_12_
  34.8 0.2 collective-permute-done.13.refs_13_
  35.0 0.3 collective-permute-done.14.refs_14_
  35.4 0.2 collective-permute-done.15.refs_15_
  35.5 14.3 %orthogonal.1 = (bf16[32,2048]{1,0:T(8,128)(2,1)S(1)}, bf16[32,2048]{1,0:T(8,128)(2,1)S(1)}, bf16[32,2048]{1,0:T(8,128)(2,1)S(1)}, bf16[32,2048]{1,0:T(8,128)(2,...) custom-call(bf16[32,2048]{1,0:T(8,128)(2,1)S(1)} %collective-permute, ...), custom_call_target="tpu_custom_call" | custom-call | tf_op jit(solution)/shard_map/orthogonal/pallas_call | solution.py:237
  49.9 0.1 collective-permute-start.17
  50.0 2.0 %collective-permute-start.18 = (bf16[32,2048]{1,0:T(8,128)(2,1)S(1)}, bf16[32,2048]{1,0:T(8,128)(2,1)S(1)}, u32[]{:S(2)}, u32[]{:S(2)}) collective-permute-start(bf16[32,2048]{1,0:T(8,128)(2,1)S(1)} %get-tuple-element.52), channel_id=1, source_target_pairs={{8,0},{25,1},{24,16},{11,17},{10,2},{27,3},{26,18},{13,19},{12,4},... | collective-permute-start | bytes 393224 | tf_op jit(solution)/shard_map/ppermute | solution.py:320
  52.0 1.1 %collective-permute-start.19 = (bf16[32,2048]{1,0:T(8,128)(2,1)S(1)}, bf16[32,2048]{1,0:T(8,128)(2,1)S(1)}, u32[]{:S(2)}, u32[]{:S(2)}) collective-permute-start(bf16[32,2048]{1,0:T(8,128)(2,1)S(1)} %get-tuple-element.53), channel_id=1, source_target_pairs={{10,0},{27,1},{26,16},{13,17},{12,2},{29,3},{28,18},{15,19},{14,4}... | collective-permute-start | bytes 393224 | tf_op jit(solution)/shard_map/ppermute | solution.py:320
  53.0 0.7 collective-permute-start.20
  53.7 1.3 %collective-permute-start.21 = (bf16[32,2048]{1,0:T(8,128)(2,1)S(1)}, bf16[32,2048]{1,0:T(8,128)(2,1)S(1)}, u32[]{:S(2)}, u32[]{:S(2)}) collective-permute-start(bf16[32,2048]{1,0:T(8,128)(2,1)S(1)} %get-tuple-element.55), channel_id=1, source_target_pairs={{2,0},{19,1},{18,16},{5,17},{4,2},{21,3},{20,18},{7,19},{6,4},{23,... | collective-permute-start | bytes 393224 | tf_op jit(solution)/shard_map/ppermute | solution.py:320
  55.0 0.8 collective-permute-done.17.refs_1_
  55.8 3.1 %collective-permute-start.22 = (bf16[32,2048]{1,0:T(8,128)(2,1)S(1)}, bf16[32,2048]{1,0:T(8,128)(2,1)S(1)}, u32[]{:S(2)}, u32[]{:S(2)}) collective-permute-start(bf16[32,2048]{1,0:T(8,128)(2,1)S(1)} %get-tuple-element.56), channel_id=1, source_target_pairs={{4,0},{21,1},{20,16},{7,17},{6,2},{23,3},{22,18},{9,19},{8,4},{25,... | collective-permute-start | bytes 393224 | tf_op jit(solution)/shard_map/ppermute | solution.py:320
  58.9 2.3 %collective-permute-done.18.refs_2_ = bf16[32,2048]{1,0:T(8,128)(2,1)S(1)} collective-permute-done((bf16[32,2048]{1,0:T(8,128)(2,1)S(1)}, bf16[32,2048]{1,0:T(8,128)(2,1)S(1)}, u32[]{:S(2)}, u32[]{:S(2)}) %collective-permute-start.18) | collective-permute-done | bytes 131104 | tf_op jit(solution)/shard_map/ppermute | solution.py:320
  61.3 2.1 %collective-permute-start.16 = (bf16[32,2048]{1,0:T(8,128)(2,1)S(1)}, bf16[32,2048]{1,0:T(8,128)(2,1)S(1)}, u32[]{:S(2)}, u32[]{:S(2)}) collective-permute-start(bf16[32,2048]{1,0:T(8,128)(2,1)S(1)} %get-tuple-element.50), channel_id=1, source_target_pairs={{12,0},{29,1},{28,16},{15,17},{14,2},{31,3},{30,18},{1,19},{0,4},{... | collective-permute-start | bytes 393224 | tf_op jit(solution)/shard_map/ppermute | solution.py:320
  63.4 4.6 %collective-permute-start.24 = (bf16[32,2048]{1,0:T(8,128)(2,1)S(1)}, bf16[32,2048]{1,0:T(8,128)(2,1)S(1)}, u32[]{:S(2)}, u32[]{:S(2)}) collective-permute-start(bf16[32,2048]{1,0:T(8,128)(2,1)S(1)} %collective-permute-done.17.refs_1_), channel_id=1, source_target_pairs={{1,0},{0,1},{3,2},{2,3},{5,4},{4,5},{7,6},{6,7},{9,8},{8,9},{11,10... | collective-permute-start | bytes 393224 | tf_op jit(solution)/shard_map/ppermute | solution.py:306
  68.0 3.7 %collective-permute-start.25 = (bf16[32,2048]{1,0:T(8,128)(2,1)S(1)}, bf16[32,2048]{1,0:T(8,128)(2,1)S(1)}, u32[]{:S(2)}, u32[]{:S(2)}) collective-permute-start(bf16[32,2048]{1,0:T(8,128)(2,1)S(1)} %collective-permute-done.18.refs_2_), channel_id=1, source_target_pairs={{1,0},{0,1},{3,2},{2,3},{5,4},{4,5},{7,6},{6,7},{9,8},{8,9},{11,10... | collective-permute-start | bytes 393224 | tf_op jit(solution)/shard_map/ppermute | solution.py:306
  71.7 2.3 %collective-permute-start.26 = (bf16[32,2048]{1,0:T(8,128)(2,1)S(1)}, bf16[32,2048]{1,0:T(8,128)(2,1)S(1)}, u32[]{:S(2)}, u32[]{:S(2)}) collective-permute-start(bf16[32,2048]{1,0:T(8,128)(2,1)S(1)} %collective-permute-done.19.refs_3_), channel_id=1, source_target_pairs={{1,0},{0,1},{3,2},{2,3},{5,4},{4,5},{7,6},{6,7},{9,8},{8,9},{11,10... | collective-permute-start | bytes 393224 | tf_op jit(solution)/shard_map/ppermute | solution.py:306
  74.0 0.9 %place.2.refs_12_ = bf16[16,32,2048]{2,1,0:T(8,128)(2,1)} custom-call(s32[1]{0:T(128)} %bitcast.1.refs_0_, bf16[32,2048]{1,0:T(8,128)(2,1)S(1)} %collective-permute-done.17.refs_1_, bf16[32,2048]{1,0:T(8,128)(2,1)S(1)} %collective-permute-done.18.refs_2_, bf16[32,2048]{1,0:T(8,128)(2,1)S(1)} %collective-permute-done.19.refs_3_, ...), custom_call_target="tpu_custom_call" | custom-call | bytes 1572864 | tf_op jit(solution)/shard_map/place/pallas_call | solution.py:280
  75.0 0.1 collective-permute-start.30
  75.1 0.5 collective-permute-start.27
  75.6 0.1 collective-permute-start.28
  75.6 0.4 collective-permute-start.29
  76.1 0.1 collective-permute-start.31
  76.2 0.4 collective-permute-done.27.refs_7_
  76.6 0.3 collective-permute-done.28.refs_8_
  76.9 0.2 collective-permute-done.29.refs_9_
  77.1 0.3 collective-permute-done.31.refs_11_
  77.4 1.1 %place.3 = bf16[16,32,2048]{2,1,0:T(8,128)(2,1)} custom-call(s32[1]{0:T(128)} %bitcast.1.refs_0_, s32[1]{0:T(128)} %bitcast.2.refs_1_, bf16[32,2048]{1,0:T(8,128)(2,1)S(1)} %collective-permute-done.16.refs_2_, bf16[32,2048]{1,0:T(8,128)(2,1)S(1)} %collective-permute-done.23.refs_3_, ...), custom_call_target="tpu_custom_call", output_to_operand_aliasing={{}: (12, {})} | custom-call | bytes 2621440 | tf_op jit(solution)/shard_map/place/pallas_call | solution.py:280
  (25 shorter events, 0.1 us)
Async XLA Ops:
  0.7 19.5 %copy-start = (bf16[16,32,2048]{2,1,0:T(8,128)(2,1)S(1)}, bf16[16,32,2048]{2,1,0:T(8,128)(2,1)}, u32[]{:S(2)}) copy-start(bf16[16,32,2048]{2,1,0:T(8,128)(2,1)} %m_ref) | copy-start | bytes 6291460
  3.3 9.0 %collective-permute-start = (bf16[32,2048]{1,0:T(8,128)(2,1)}, bf16[32,2048]{1,0:T(8,128)(2,1)S(1)}, u32[]{:S(2)}, u32[]{:S(2)}) collective-permute-start(bf16[32,2048]{1,0:T(8,128)(2,1)} %get-tuple-element.31), channel_id=1, source_target_pairs={{0,6},{1,23},{16,22},{17,9},{2,8},{3,25},{18,24},{19,11},{4,10},{5... | collective-permute-start | bytes 393224 | tf_op jit(solution)/shard_map/ppermute | solution.py:320
  7.3 9.1 %collective-permute-start.2 = (bf16[32,2048]{1,0:T(8,128)(2,1)}, bf16[32,2048]{1,0:T(8,128)(2,1)S(1)}, u32[]{:S(2)}, u32[]{:S(2)}) collective-permute-start(bf16[32,2048]{1,0:T(8,128)(2,1)} %get-tuple-element.36), channel_id=1, source_target_pairs={{0,2},{1,19},{16,18},{17,5},{2,4},{3,21},{18,20},{19,7},{4,6},{5,2... | collective-permute-start | bytes 393224 | tf_op jit(solution)/shard_map/ppermute | solution.py:320
  7.9 11.0 %collective-permute-start.3 = (bf16[32,2048]{1,0:T(8,128)(2,1)}, bf16[32,2048]{1,0:T(8,128)(2,1)S(1)}, u32[]{:S(2)}, u32[]{:S(2)}) collective-permute-start(bf16[32,2048]{1,0:T(8,128)(2,1)} %get-tuple-element.38), channel_id=1, source_target_pairs={{0,4},{1,21},{16,20},{17,7},{2,6},{3,23},{18,22},{19,9},{4,8},{5,2... | collective-permute-start | bytes 393224 | tf_op jit(solution)/shard_map/ppermute | solution.py:320
  9.4 14.3 %collective-permute-start.1 = (bf16[32,2048]{1,0:T(8,128)(2,1)}, bf16[32,2048]{1,0:T(8,128)(2,1)S(1)}, u32[]{:S(2)}, u32[]{:S(2)}) collective-permute-start(bf16[32,2048]{1,0:T(8,128)(2,1)} %get-tuple-element.34), channel_id=1, source_target_pairs={{0,0},{1,17},{16,16},{17,3},{2,2},{3,19},{18,18},{19,5},{4,4},{5,2... | collective-permute-start | bytes 393224 | tf_op jit(solution)/shard_map/ppermute | solution.py:320
  10.9 15.4 %collective-permute-start.6 = (bf16[32,2048]{1,0:T(8,128)(2,1)}, bf16[32,2048]{1,0:T(8,128)(2,1)S(1)}, u32[]{:S(2)}, u32[]{:S(2)}) collective-permute-start(bf16[32,2048]{1,0:T(8,128)(2,1)} %get-tuple-element.46), channel_id=1, source_target_pairs={{0,12},{1,29},{16,28},{17,15},{2,14},{3,31},{18,30},{19,1},{4,0},{... | collective-permute-start | bytes 393224 | tf_op jit(solution)/shard_map/ppermute | solution.py:320
  12.3 15.0 %collective-permute-start.7 = (bf16[32,2048]{1,0:T(8,128)(2,1)}, bf16[32,2048]{1,0:T(8,128)(2,1)S(1)}, u32[]{:S(2)}, u32[]{:S(2)}) collective-permute-start(bf16[32,2048]{1,0:T(8,128)(2,1)} %get-tuple-element.48), channel_id=1, source_target_pairs={{0,14},{1,31},{16,30},{17,1},{2,0},{3,17},{18,16},{19,3},{4,2},{5,... | collective-permute-start | bytes 393224 | tf_op jit(solution)/shard_map/ppermute | solution.py:320
  16.3 11.6 %collective-permute-start.4 = (bf16[32,2048]{1,0:T(8,128)(2,1)}, bf16[32,2048]{1,0:T(8,128)(2,1)S(1)}, u32[]{:S(2)}, u32[]{:S(2)}) collective-permute-start(bf16[32,2048]{1,0:T(8,128)(2,1)} %get-tuple-element.42), channel_id=1, source_target_pairs={{0,8},{1,25},{16,24},{17,11},{2,10},{3,27},{18,26},{19,13},{4,12},... | collective-permute-start | bytes 393224 | tf_op jit(solution)/shard_map/ppermute | solution.py:320
  18.9 9.0 %collective-permute-start.5 = (bf16[32,2048]{1,0:T(8,128)(2,1)}, bf16[32,2048]{1,0:T(8,128)(2,1)S(1)}, u32[]{:S(2)}, u32[]{:S(2)}) collective-permute-start(bf16[32,2048]{1,0:T(8,128)(2,1)} %get-tuple-element.44), channel_id=1, source_target_pairs={{0,10},{1,27},{16,26},{17,13},{2,12},{3,29},{18,28},{19,15},{4,14}... | collective-permute-start | bytes 393224 | tf_op jit(solution)/shard_map/ppermute | solution.py:320
  20.1 1.6 %copy-start.1 = (bf16[16,32,2048]{2,1,0:T(8,128)(2,1)S(1)}, bf16[16,32,2048]{2,1,0:T(8,128)(2,1)}, u32[]{:S(2)}) copy-start(bf16[16,32,2048]{2,1,0:T(8,128)(2,1)} %g_ref) | copy-start | bytes 6291460
  23.7 9.8 %collective-permute-start.8 = (bf16[32,2048]{1,0:T(8,128)(2,1)S(1)}, bf16[32,2048]{1,0:T(8,128)(2,1)S(1)}, u32[]{:S(2)}, u32[]{:S(2)}) collective-permute-start(bf16[32,2048]{1,0:T(8,128)(2,1)S(1)} %collective-permute-done.1.refs_0_), channel_id=1, source_target_pairs={{1,0},{0,1},{3,2},{2,3},{5,4},{4,5},{7,6},{6,7},{9,8},{8,9},{11,10... | collective-permute-start | bytes 393224 | tf_op jit(solution)/shard_map/ppermute | solution.py:306
  26.3 7.7 %collective-permute-start.9 = (bf16[32,2048]{1,0:T(8,128)(2,1)S(1)}, bf16[32,2048]{1,0:T(8,128)(2,1)S(1)}, u32[]{:S(2)}, u32[]{:S(2)}) collective-permute-start(bf16[32,2048]{1,0:T(8,128)(2,1)S(1)} %collective-permute-done.2.refs_1_), channel_id=1, source_target_pairs={{1,0},{0,1},{3,2},{2,3},{5,4},{4,5},{7,6},{6,7},{9,8},{8,9},{11,10... | collective-permute-start | bytes 393224 | tf_op jit(solution)/shard_map/ppermute | solution.py:306
  27.3 6.8 %collective-permute-start.10 = (bf16[32,2048]{1,0:T(8,128)(2,1)S(1)}, bf16[32,2048]{1,0:T(8,128)(2,1)S(1)}, u32[]{:S(2)}, u32[]{:S(2)}) collective-permute-start(bf16[32,2048]{1,0:T(8,128)(2,1)S(1)} %collective-permute-done.3.refs_2_), channel_id=1, source_target_pairs={{1,0},{0,1},{3,2},{2,3},{5,4},{4,5},{7,6},{6,7},{9,8},{8,9},{11,10... | collective-permute-start | bytes 393224 | tf_op jit(solution)/shard_map/ppermute | solution.py:306
  27.9 6.6 %collective-permute-start.11 = (bf16[32,2048]{1,0:T(8,128)(2,1)S(1)}, bf16[32,2048]{1,0:T(8,128)(2,1)S(1)}, u32[]{:S(2)}, u32[]{:S(2)}) collective-permute-start(bf16[32,2048]{1,0:T(8,128)(2,1)S(1)} %collective-permute-done.refs_3_), channel_id=1, source_target_pairs={{1,0},{0,1},{3,2},{2,3},{5,4},{4,5},{7,6},{6,7},{9,8},{8,9},{11,10... | collective-permute-start | bytes 393224 | tf_op jit(solution)/shard_map/ppermute | solution.py:306
  33.5 1.3 %collective-permute-start.12 = (bf16[32,2048]{1,0:T(8,128)(2,1)S(1)}, bf16[32,2048]{1,0:T(8,128)(2,1)S(1)}, u32[]{:S(2)}, u32[]{:S(2)}) collective-permute-start(bf16[32,2048]{1,0:T(8,128)(2,1)S(1)} %collective-permute-done.4.refs_4_), channel_id=1, source_target_pairs={{1,0},{0,1},{3,2},{2,3},{5,4},{4,5},{7,6},{6,7},{9,8},{8,9},{11,10... | collective-permute-start | bytes 393224 | tf_op jit(solution)/shard_map/ppermute | solution.py:306
  33.5 1.5 %collective-permute-start.13 = (bf16[32,2048]{1,0:T(8,128)(2,1)S(1)}, bf16[32,2048]{1,0:T(8,128)(2,1)S(1)}, u32[]{:S(2)}, u32[]{:S(2)}) collective-permute-start(bf16[32,2048]{1,0:T(8,128)(2,1)S(1)} %collective-permute-done.5.refs_5_), channel_id=1, source_target_pairs={{1,0},{0,1},{3,2},{2,3},{5,4},{4,5},{7,6},{6,7},{9,8},{8,9},{11,10... | collective-permute-start | bytes 393224 | tf_op jit(solution)/shard_map/ppermute | solution.py:306
  34.0 1.3 %collective-permute-start.14 = (bf16[32,2048]{1,0:T(8,128)(2,1)S(1)}, bf16[32,2048]{1,0:T(8,128)(2,1)S(1)}, u32[]{:S(2)}, u32[]{:S(2)}) collective-permute-start(bf16[32,2048]{1,0:T(8,128)(2,1)S(1)} %collective-permute-done.6.refs_6_), channel_id=1, source_target_pairs={{1,0},{0,1},{3,2},{2,3},{5,4},{4,5},{7,6},{6,7},{9,8},{8,9},{11,10... | collective-permute-start | bytes 393224 | tf_op jit(solution)/shard_map/ppermute | solution.py:306
  34.1 1.5 %collective-permute-start.15 = (bf16[32,2048]{1,0:T(8,128)(2,1)S(1)}, bf16[32,2048]{1,0:T(8,128)(2,1)S(1)}, u32[]{:S(2)}, u32[]{:S(2)}) collective-permute-start(bf16[32,2048]{1,0:T(8,128)(2,1)S(1)} %collective-permute-done.7.refs_7_), channel_id=1, source_target_pairs={{1,0},{0,1},{3,2},{2,3},{5,4},{4,5},{7,6},{6,7},{9,8},{8,9},{11,10... | collective-permute-start | bytes 393224 | tf_op jit(solution)/shard_map/ppermute | solution.py:306
  49.9 5.9 %collective-permute-start.17 = (bf16[32,2048]{1,0:T(8,128)(2,1)S(1)}, bf16[32,2048]{1,0:T(8,128)(2,1)S(1)}, u32[]{:S(2)}, u32[]{:S(2)}) collective-permute-start(bf16[32,2048]{1,0:T(8,128)(2,1)S(1)} %get-tuple-element.51), channel_id=1, source_target_pairs={{6,0},{23,1},{22,16},{9,17},{8,2},{25,3},{24,18},{11,19},{10,4},{2... | collective-permute-start | bytes 393224 | tf_op jit(solution)/shard_map/ppermute | solution.py:320
  50.0 11.3 %collective-permute-start.18 = (bf16[32,2048]{1,0:T(8,128)(2,1)S(1)}, bf16[32,2048]{1,0:T(8,128)(2,1)S(1)}, u32[]{:S(2)}, u32[]{:S(2)}) collective-permute-start(bf16[32,2048]{1,0:T(8,128)(2,1)S(1)} %get-tuple-element.52), channel_id=1, source_target_pairs={{8,0},{25,1},{24,16},{11,17},{10,2},{27,3},{26,18},{13,19},{12,4},... | collective-permute-start | bytes 393224 | tf_op jit(solution)/shard_map/ppermute | solution.py:320
  52.0 9.3 %collective-permute-start.19 = (bf16[32,2048]{1,0:T(8,128)(2,1)S(1)}, bf16[32,2048]{1,0:T(8,128)(2,1)S(1)}, u32[]{:S(2)}, u32[]{:S(2)}) collective-permute-start(bf16[32,2048]{1,0:T(8,128)(2,1)S(1)} %get-tuple-element.53), channel_id=1, source_target_pairs={{10,0},{27,1},{26,16},{13,17},{12,2},{29,3},{28,18},{15,19},{14,4}... | collective-permute-start | bytes 393224 | tf_op jit(solution)/shard_map/ppermute | solution.py:320
  53.0 10.3 %collective-permute-start.20 = (bf16[32,2048]{1,0:T(8,128)(2,1)S(1)}, bf16[32,2048]{1,0:T(8,128)(2,1)S(1)}, u32[]{:S(2)}, u32[]{:S(2)}) collective-permute-start(bf16[32,2048]{1,0:T(8,128)(2,1)S(1)} %get-tuple-element.54), channel_id=1, source_target_pairs={{0,0},{17,1},{16,16},{3,17},{2,2},{19,3},{18,18},{5,19},{4,4},{21,... | collective-permute-start | bytes 393224 | tf_op jit(solution)/shard_map/ppermute | solution.py:320
  53.7 14.3 %collective-permute-start.21 = (bf16[32,2048]{1,0:T(8,128)(2,1)S(1)}, bf16[32,2048]{1,0:T(8,128)(2,1)S(1)}, u32[]{:S(2)}, u32[]{:S(2)}) collective-permute-start(bf16[32,2048]{1,0:T(8,128)(2,1)S(1)} %get-tuple-element.55), channel_id=1, source_target_pairs={{2,0},{19,1},{18,16},{5,17},{4,2},{21,3},{20,18},{7,19},{6,4},{23,... | collective-permute-start | bytes 393224 | tf_op jit(solution)/shard_map/ppermute | solution.py:320
  55.8 15.9 %collective-permute-start.22 = (bf16[32,2048]{1,0:T(8,128)(2,1)S(1)}, bf16[32,2048]{1,0:T(8,128)(2,1)S(1)}, u32[]{:S(2)}, u32[]{:S(2)}) collective-permute-start(bf16[32,2048]{1,0:T(8,128)(2,1)S(1)} %get-tuple-element.56), channel_id=1, source_target_pairs={{4,0},{21,1},{20,16},{7,17},{6,2},{23,3},{22,18},{9,19},{8,4},{25,... | collective-permute-start | bytes 393224 | tf_op jit(solution)/shard_map/ppermute | solution.py:320
  61.2 13.7 %collective-permute-start.23 = (bf16[32,2048]{1,0:T(8,128)(2,1)S(1)}, bf16[32,2048]{1,0:T(8,128)(2,1)S(1)}, u32[]{:S(2)}, u32[]{:S(2)}) collective-permute-start(bf16[32,2048]{1,0:T(8,128)(2,1)S(1)} %get-tuple-element.58), channel_id=1, source_target_pairs={{14,0},{31,1},{30,16},{1,17},{0,2},{17,3},{16,18},{3,19},{2,4},{19... | collective-permute-start | bytes 393224 | tf_op jit(solution)/shard_map/ppermute | solution.py:320
  61.3 13.7 %collective-permute-start.16 = (bf16[32,2048]{1,0:T(8,128)(2,1)S(1)}, bf16[32,2048]{1,0:T(8,128)(2,1)S(1)}, u32[]{:S(2)}, u32[]{:S(2)}) collective-permute-start(bf16[32,2048]{1,0:T(8,128)(2,1)S(1)} %get-tuple-element.50), channel_id=1, source_target_pairs={{12,0},{29,1},{28,16},{15,17},{14,2},{31,3},{30,18},{1,19},{0,4},{... | collective-permute-start | bytes 393224 | tf_op jit(solution)/shard_map/ppermute | solution.py:320
  63.4 12.2 %collective-permute-start.24 = (bf16[32,2048]{1,0:T(8,128)(2,1)S(1)}, bf16[32,2048]{1,0:T(8,128)(2,1)S(1)}, u32[]{:S(2)}, u32[]{:S(2)}) collective-permute-start(bf16[32,2048]{1,0:T(8,128)(2,1)S(1)} %collective-permute-done.17.refs_1_), channel_id=1, source_target_pairs={{1,0},{0,1},{3,2},{2,3},{5,4},{4,5},{7,6},{6,7},{9,8},{8,9},{11,10... | collective-permute-start | bytes 393224 | tf_op jit(solution)/shard_map/ppermute | solution.py:306
  68.0 7.6 %collective-permute-start.25 = (bf16[32,2048]{1,0:T(8,128)(2,1)S(1)}, bf16[32,2048]{1,0:T(8,128)(2,1)S(1)}, u32[]{:S(2)}, u32[]{:S(2)}) collective-permute-start(bf16[32,2048]{1,0:T(8,128)(2,1)S(1)} %collective-permute-done.18.refs_2_), channel_id=1, source_target_pairs={{1,0},{0,1},{3,2},{2,3},{5,4},{4,5},{7,6},{6,7},{9,8},{8,9},{11,10... | collective-permute-start | bytes 393224 | tf_op jit(solution)/shard_map/ppermute | solution.py:306
  71.7 4.4 %collective-permute-start.26 = (bf16[32,2048]{1,0:T(8,128)(2,1)S(1)}, bf16[32,2048]{1,0:T(8,128)(2,1)S(1)}, u32[]{:S(2)}, u32[]{:S(2)}) collective-permute-start(bf16[32,2048]{1,0:T(8,128)(2,1)S(1)} %collective-permute-done.19.refs_3_), channel_id=1, source_target_pairs={{1,0},{0,1},{3,2},{2,3},{5,4},{4,5},{7,6},{6,7},{9,8},{8,9},{11,10... | collective-permute-start | bytes 393224 | tf_op jit(solution)/shard_map/ppermute | solution.py:306
  75.0 2.1 %collective-permute-start.30 = (bf16[32,2048]{1,0:T(8,128)(2,1)S(1)}, bf16[32,2048]{1,0:T(8,128)(2,1)S(1)}, u32[]{:S(2)}, u32[]{:S(2)}) collective-permute-start(bf16[32,2048]{1,0:T(8,128)(2,1)S(1)} %collective-permute-done.16.refs_2_), channel_id=1, source_target_pairs={{1,0},{0,1},{3,2},{2,3},{5,4},{4,5},{7,6},{6,7},{9,8},{8,9},{11,10... | collective-permute-start | bytes 393224 | tf_op jit(solution)/shard_map/ppermute | solution.py:306
  75.1 1.5 %collective-permute-start.27 = (bf16[32,2048]{1,0:T(8,128)(2,1)S(1)}, bf16[32,2048]{1,0:T(8,128)(2,1)S(1)}, u32[]{:S(2)}, u32[]{:S(2)}) collective-permute-start(bf16[32,2048]{1,0:T(8,128)(2,1)S(1)} %collective-permute-done.20.refs_4_), channel_id=1, source_target_pairs={{1,0},{0,1},{3,2},{2,3},{5,4},{4,5},{7,6},{6,7},{9,8},{8,9},{11,10... | collective-permute-start | bytes 393224 | tf_op jit(solution)/shard_map/ppermute | solution.py:306
  75.6 1.3 %collective-permute-start.28 = (bf16[32,2048]{1,0:T(8,128)(2,1)S(1)}, bf16[32,2048]{1,0:T(8,128)(2,1)S(1)}, u32[]{:S(2)}, u32[]{:S(2)}) collective-permute-start(bf16[32,2048]{1,0:T(8,128)(2,1)S(1)} %collective-permute-done.21.refs_5_), channel_id=1, source_target_pairs={{1,0},{0,1},{3,2},{2,3},{5,4},{4,5},{7,6},{6,7},{9,8},{8,9},{11,10... | collective-permute-start | bytes 393224 | tf_op jit(solution)/shard_map/ppermute | solution.py:306
  75.6 1.5 %collective-permute-start.29 = (bf16[32,2048]{1,0:T(8,128)(2,1)S(1)}, bf16[32,2048]{1,0:T(8,128)(2,1)S(1)}, u32[]{:S(2)}, u32[]{:S(2)}) collective-permute-start(bf16[32,2048]{1,0:T(8,128)(2,1)S(1)} %collective-permute-done.22.refs_6_), channel_id=1, source_target_pairs={{1,0},{0,1},{3,2},{2,3},{5,4},{4,5},{7,6},{6,7},{9,8},{8,9},{11,10... | collective-permute-start | bytes 393224 | tf_op jit(solution)/shard_map/ppermute | solution.py:306
  76.1 1.3 %collective-permute-start.31 = (bf16[32,2048]{1,0:T(8,128)(2,1)S(1)}, bf16[32,2048]{1,0:T(8,128)(2,1)S(1)}, u32[]{:S(2)}, u32[]{:S(2)}) collective-permute-start(bf16[32,2048]{1,0:T(8,128)(2,1)S(1)} %collective-permute-done.23.refs_3_), channel_id=1, source_target_pairs={{1,0},{0,1},{3,2},{2,3},{5,4},{4,5},{7,6},{6,7},{9,8},{8,9},{11,10... | collective-permute-start | bytes 393224 | tf_op jit(solution)/shard_map/ppermute | solution.py:306

commit v13 on v12

--- a/solution.py
+++ b/solution.py
@@ -348,15 +348,9 @@
         update = exchange([update[j] for j in steps], steps, False)
 
         firsts = [lax.rem(place_of + lax.rem(rep + i, n_rep), n_shard)[None] for i in range(n_rep)]
-        whole = place(
-            firsts, [[(0, j)] for j in steps[:early]], update[:early], n_rep, (experts, rows, cols)
-        )
-        update[early:] = [after(x, whole) for x in update[early:]]
-        pieces = {(i, j): x for i, xs in enumerate([update, *others(update)]) for j, x in enumerate(xs)}
-        names = [(i, j) for i, j in pieces if i or j >= early]
-        whole = place(
-            firsts, [[(i, steps[j])] for i, j in names], [pieces[name] for name in names], n_rep, whole
-        )
+        whole = (experts, rows, cols)
+        for i, pieces in enumerate([update, *others(update)]):
+            whole = place(firsts, [[(i, j)] for j in steps], pieces, n_rep, whole)
         return new_momentum, whole
 
     return jax.shard_map(

time: 79.1 us -> 78.7 us (level)
  waiting for transfers between devices: 7.67 us -> 6.42 us
    ppermute x16, waiting for transfers between devices: 2.3 us -> 1.05 us  [others(): return [[lax.ppermute(x, 'rep', pair) for x in pieces] for pair in pairs]]
    ppermute x16, starting transfers between devices: 22.6 us -> 23.8 us  [others(): return [[lax.ppermute(x, 'rep', pair) for x in pieces] for pair in pairs]]
    ppermute x16, starting transfers between devices: 24.9 us -> 23.8 us  [exchange(): moved.append(lax.ppermute(x, ('shard', 'rep'), pairs))]
  transfers between devices with their start and end apart: 32 -> 32, of which waited for: 12 -> 8; matrix products, arithmetic and copies ran while one was open for 0% -> 0% of each run, Pallas kernels for 4% -> 4%
where the time goes in v13:
time: 78.7 us; the launch traced here: 77.6 us
  starting transfers between devices  47.6 us (60%)
  Pallas kernels  21.1 us (27%)
  waiting for transfers between devices  6.42 us (8%)
  local copies, waits for them, and re-layouts  1.6 us (2%)
  between operations  0.93 us (1%)
    ppermute x16, starting transfers between devices, exchange(): moved.append(lax.ppermute(x, ('shard', 'rep'), pairs))  23.8 us
    ppermute x16, starting transfers between devices, others(): return [[lax.ppermute(x, 'rep', pair) for x in pieces] for pair in pairs]  23.8 us
    pallas_call x1, Pallas kernels, orthogonal(): pl.pallas_call(functools.partial(orthogonal_kernel, scale, count), in_spe...  14.3 us
    ppermute x16, waiting for transfers between devices, exchange(): moved.append(lax.ppermute(x, ('shard', 'rep'), pairs))  5.37 us
    pallas_call x1, Pallas kernels, blended_share(): pl.pallas_call(functools.partial(share_kernel, n_rep), in_specs=[pl.Block...  2.65 us
    pallas_call x2, Pallas kernels, place(): pl.pallas_call(functools.partial(place_kernel, which, n_rep), in_specs=[p...  2.06 us
    pallas_call x1, Pallas kernels, new_momentum_of(): pl.pallas_call(momentum_kernel, in_specs=[vmem, vmem], out_specs=vmem, ou...  2 us
    unnamed x4, local copies, waits for them, and re-layouts  1.6 us
  transfers between devices with their start and end apart: 32, of which 8 were waited for; matrix products, arithmetic and copies ran while one was open for 0% of the time, Pallas kernels for 4%

profile of v13, /device:TPU:0, one launch (start us, length us, event | category | flops | bytes accessed | tf_op | source)
XLA Modules:
  0.0 77.6 jit_solution(2369024798450230056)
XLA Ops:
  0.7 2.7 %share.1 = (bf16[32,2048]{1,0:T(8,128)(2,1)}, bf16[32,2048]{1,0:T(8,128)(2,1)}, bf16[32,2048]{1,0:T(8,128)(2,1)}, bf16[32,2048]{1,0:T(8,128)(2,1)}, bf16[32,2048...) custom-call(s32[1]{0:T(128)} %bitcast.at_ref, ...), custom_call_target="tpu_custom_call" | custom-call | tf_op jit(solution)/shard_map/share/pallas_call | solution.py:58
  3.3 3.9 %collective-permute-start = (bf16[32,2048]{1,0:T(8,128)(2,1)}, bf16[32,2048]{1,0:T(8,128)(2,1)S(1)}, u32[]{:S(2)}, u32[]{:S(2)}) collective-permute-start(bf16[32,2048]{1,0:T(8,128)(2,1)} %get-tuple-element.29), channel_id=1, source_target_pairs={{0,6},{1,23},{16,22},{17,9},{2,8},{3,25},{18,24},{19,11},{4,10},{5... | collective-permute-start | bytes 393224 | tf_op jit(solution)/shard_map/ppermute | solution.py:320
  7.3 0.6 collective-permute-start.2
  7.9 1.5 %collective-permute-start.3 = (bf16[32,2048]{1,0:T(8,128)(2,1)}, bf16[32,2048]{1,0:T(8,128)(2,1)S(1)}, u32[]{:S(2)}, u32[]{:S(2)}) collective-permute-start(bf16[32,2048]{1,0:T(8,128)(2,1)} %get-tuple-element.36), channel_id=1, source_target_pairs={{0,4},{1,21},{16,20},{17,7},{2,6},{3,23},{18,22},{19,9},{4,8},{5,2... | collective-permute-start | bytes 393224 | tf_op jit(solution)/shard_map/ppermute | solution.py:320
  9.4 1.6 %collective-permute-start.1 = (bf16[32,2048]{1,0:T(8,128)(2,1)}, bf16[32,2048]{1,0:T(8,128)(2,1)S(1)}, u32[]{:S(2)}, u32[]{:S(2)}) collective-permute-start(bf16[32,2048]{1,0:T(8,128)(2,1)} %get-tuple-element.32), channel_id=1, source_target_pairs={{0,0},{1,17},{16,16},{17,3},{2,2},{3,19},{18,18},{19,5},{4,4},{5,2... | collective-permute-start | bytes 393224 | tf_op jit(solution)/shard_map/ppermute | solution.py:320
  10.9 1.4 %collective-permute-start.6 = (bf16[32,2048]{1,0:T(8,128)(2,1)}, bf16[32,2048]{1,0:T(8,128)(2,1)S(1)}, u32[]{:S(2)}, u32[]{:S(2)}) collective-permute-start(bf16[32,2048]{1,0:T(8,128)(2,1)} %get-tuple-element.44), channel_id=1, source_target_pairs={{0,12},{1,29},{16,28},{17,15},{2,14},{3,31},{18,30},{19,1},{4,0},{... | collective-permute-start | bytes 393224 | tf_op jit(solution)/shard_map/ppermute | solution.py:320
  12.3 2.3 %collective-permute-start.7 = (bf16[32,2048]{1,0:T(8,128)(2,1)}, bf16[32,2048]{1,0:T(8,128)(2,1)S(1)}, u32[]{:S(2)}, u32[]{:S(2)}) collective-permute-start(bf16[32,2048]{1,0:T(8,128)(2,1)} %get-tuple-element.46), channel_id=1, source_target_pairs={{0,14},{1,31},{16,30},{17,1},{2,0},{3,17},{18,16},{19,3},{4,2},{5,... | collective-permute-start | bytes 393224 | tf_op jit(solution)/shard_map/ppermute | solution.py:320
  14.7 1.7 %collective-permute-done.2.refs_1_ = bf16[32,2048]{1,0:T(8,128)(2,1)S(1)} collective-permute-done((bf16[32,2048]{1,0:T(8,128)(2,1)}, bf16[32,2048]{1,0:T(8,128)(2,1)S(1)}, u32[]{:S(2)}, u32[]{:S(2)}) %collective-permute-start.2) | collective-permute-done | bytes 131104 | tf_op jit(solution)/shard_map/ppermute | solution.py:320
  16.3 2.0 %collective-permute-start.4 = (bf16[32,2048]{1,0:T(8,128)(2,1)}, bf16[32,2048]{1,0:T(8,128)(2,1)S(1)}, u32[]{:S(2)}, u32[]{:S(2)}) collective-permute-start(bf16[32,2048]{1,0:T(8,128)(2,1)} %get-tuple-element.40), channel_id=1, source_target_pairs={{0,8},{1,25},{16,24},{17,11},{2,10},{3,27},{18,26},{19,13},{4,12},... | collective-permute-start | bytes 393224 | tf_op jit(solution)/shard_map/ppermute | solution.py:320
  18.4 0.5 collective-permute-done.3.refs_2_
  18.9 1.2 %collective-permute-start.5 = (bf16[32,2048]{1,0:T(8,128)(2,1)}, bf16[32,2048]{1,0:T(8,128)(2,1)S(1)}, u32[]{:S(2)}, u32[]{:S(2)}) collective-permute-start(bf16[32,2048]{1,0:T(8,128)(2,1)} %get-tuple-element.42), channel_id=1, source_target_pairs={{0,10},{1,27},{16,26},{17,13},{2,12},{3,29},{18,28},{19,15},{4,14}... | collective-permute-start | bytes 393224 | tf_op jit(solution)/shard_map/ppermute | solution.py:320
  20.1 1.6 %copy-done.1 = bf16[16,32,2048]{2,1,0:T(8,128)(2,1)S(1)} copy-done((bf16[16,32,2048]{2,1,0:T(8,128)(2,1)S(1)}, bf16[16,32,2048]{2,1,0:T(8,128)(2,1)}, u32[]{:S(2)}) %copy-start.1) | copy-done | bytes 2097176
  21.7 2.0 %new_momentum.1 = bf16[16,32,2048]{2,1,0:T(8,128)(2,1)} custom-call(bf16[16,32,2048]{2,1,0:T(8,128)(2,1)S(1)} %copy-done, bf16[16,32,2048]{2,1,0:T(8,128)(2,1)S(1)} %copy-done.1), custom_call_target="tpu_custom_call" | custom-call | flops 2097152 | bytes 6291456 | tf_op jit(solution)/shard_map/new_momentum/pallas_call | solution.py:80
  23.7 2.6 %collective-permute-start.8 = (bf16[32,2048]{1,0:T(8,128)(2,1)S(1)}, bf16[32,2048]{1,0:T(8,128)(2,1)S(1)}, u32[]{:S(2)}, u32[]{:S(2)}) collective-permute-start(bf16[32,2048]{1,0:T(8,128)(2,1)S(1)} %collective-permute-done.1.refs_0_), channel_id=1, source_target_pairs={{1,0},{0,1},{3,2},{2,3},{5,4},{4,5},{7,6},{6,7},{9,8},{8,9},{11,10... | collective-permute-start | bytes 393224 | tf_op jit(solution)/shard_map/ppermute | solution.py:306
  26.3 0.0 collective-permute-done.6.refs_6_
  26.3 1.0 %collective-permute-start.9 = (bf16[32,2048]{1,0:T(8,128)(2,1)S(1)}, bf16[32,2048]{1,0:T(8,128)(2,1)S(1)}, u32[]{:S(2)}, u32[]{:S(2)}) collective-permute-start(bf16[32,2048]{1,0:T(8,128)(2,1)S(1)} %collective-permute-done.2.refs_1_), channel_id=1, source_target_pairs={{1,0},{0,1},{3,2},{2,3},{5,4},{4,5},{7,6},{6,7},{9,8},{8,9},{11,10... | collective-permute-start | bytes 393224 | tf_op jit(solution)/shard_map/ppermute | solution.py:306
  27.3 0.6 collective-permute-start.10
  27.9 5.5 %collective-permute-start.11 = (bf16[32,2048]{1,0:T(8,128)(2,1)S(1)}, bf16[32,2048]{1,0:T(8,128)(2,1)S(1)}, u32[]{:S(2)}, u32[]{:S(2)}) collective-permute-start(bf16[32,2048]{1,0:T(8,128)(2,1)S(1)} %collective-permute-done.refs_3_), channel_id=1, source_target_pairs={{1,0},{0,1},{3,2},{2,3},{5,4},{4,5},{7,6},{6,7},{9,8},{8,9},{11,10... | collective-permute-start | bytes 393224 | tf_op jit(solution)/shard_map/ppermute | solution.py:306
  33.5 0.0 collective-permute-start.12
  33.5 0.5 collective-permute-start.13
  34.0 0.0 collective-permute-done.9.refs_9_
  34.0 0.1 collective-permute-start.14
  34.1 0.4 collective-permute-start.15
  34.5 0.0 collective-permute-done.11.refs_11_
  34.5 0.3 collective-permute-done.12.refs_12_
  34.8 0.2 collective-permute-done.13.refs_13_
  35.0 0.3 collective-permute-done.14.refs_14_
  35.4 0.2 collective-permute-done.15.refs_15_
  35.5 14.3 %orthogonal.1 = (bf16[32,2048]{1,0:T(8,128)(2,1)S(1)}, bf16[32,2048]{1,0:T(8,128)(2,1)S(1)}, bf16[32,2048]{1,0:T(8,128)(2,1)S(1)}, bf16[32,2048]{1,0:T(8,128)(2,...) custom-call(bf16[32,2048]{1,0:T(8,128)(2,1)S(1)} %collective-permute, ...), custom_call_target="tpu_custom_call" | custom-call | tf_op jit(solution)/shard_map/orthogonal/pallas_call | solution.py:237
  49.9 0.1 collective-permute-start.16
  50.0 2.0 %collective-permute-start.18 = (bf16[32,2048]{1,0:T(8,128)(2,1)S(1)}, bf16[32,2048]{1,0:T(8,128)(2,1)S(1)}, u32[]{:S(2)}, u32[]{:S(2)}) collective-permute-start(bf16[32,2048]{1,0:T(8,128)(2,1)S(1)} %get-tuple-element.49), channel_id=1, source_target_pairs={{8,0},{25,1},{24,16},{11,17},{10,2},{27,3},{26,18},{13,19},{12,4},... | collective-permute-start | bytes 393224 | tf_op jit(solution)/shard_map/ppermute | solution.py:320
  52.0 1.1 %collective-permute-start.20 = (bf16[32,2048]{1,0:T(8,128)(2,1)S(1)}, bf16[32,2048]{1,0:T(8,128)(2,1)S(1)}, u32[]{:S(2)}, u32[]{:S(2)}) collective-permute-start(bf16[32,2048]{1,0:T(8,128)(2,1)S(1)} %get-tuple-element.50), channel_id=1, source_target_pairs={{10,0},{27,1},{26,16},{13,17},{12,2},{29,3},{28,18},{15,19},{14,4}... | collective-permute-start | bytes 393224 | tf_op jit(solution)/shard_map/ppermute | solution.py:320
  53.0 0.7 collective-permute-start.22
  53.7 1.3 %collective-permute-start.24 = (bf16[32,2048]{1,0:T(8,128)(2,1)S(1)}, bf16[32,2048]{1,0:T(8,128)(2,1)S(1)}, u32[]{:S(2)}, u32[]{:S(2)}) collective-permute-start(bf16[32,2048]{1,0:T(8,128)(2,1)S(1)} %get-tuple-element.52), channel_id=1, source_target_pairs={{2,0},{19,1},{18,16},{5,17},{4,2},{21,3},{20,18},{7,19},{6,4},{23,... | collective-permute-start | bytes 393224 | tf_op jit(solution)/shard_map/ppermute | solution.py:320
  55.0 0.8 %collective-permute-done.16.refs_1_ = bf16[32,2048]{1,0:T(8,128)(2,1)S(1)} collective-permute-done((bf16[32,2048]{1,0:T(8,128)(2,1)S(1)}, bf16[32,2048]{1,0:T(8,128)(2,1)S(1)}, u32[]{:S(2)}, u32[]{:S(2)}) %collective-permute-start.16) | collective-permute-done | bytes 131104 | tf_op jit(solution)/shard_map/ppermute | solution.py:320
  55.8 3.1 %collective-permute-start.26 = (bf16[32,2048]{1,0:T(8,128)(2,1)S(1)}, bf16[32,2048]{1,0:T(8,128)(2,1)S(1)}, u32[]{:S(2)}, u32[]{:S(2)}) collective-permute-start(bf16[32,2048]{1,0:T(8,128)(2,1)S(1)} %get-tuple-element.53), channel_id=1, source_target_pairs={{4,0},{21,1},{20,16},{7,17},{6,2},{23,3},{22,18},{9,19},{8,4},{25,... | collective-permute-start | bytes 393224 | tf_op jit(solution)/shard_map/ppermute | solution.py:320
  58.9 2.3 %collective-permute-done.18.refs_2_ = bf16[32,2048]{1,0:T(8,128)(2,1)S(1)} collective-permute-done((bf16[32,2048]{1,0:T(8,128)(2,1)S(1)}, bf16[32,2048]{1,0:T(8,128)(2,1)S(1)}, u32[]{:S(2)}, u32[]{:S(2)}) %collective-permute-start.18) | collective-permute-done | bytes 131104 | tf_op jit(solution)/shard_map/ppermute | solution.py:320
  61.3 1.1 %collective-permute-start.30 = (bf16[32,2048]{1,0:T(8,128)(2,1)S(1)}, bf16[32,2048]{1,0:T(8,128)(2,1)S(1)}, u32[]{:S(2)}, u32[]{:S(2)}) collective-permute-start(bf16[32,2048]{1,0:T(8,128)(2,1)S(1)} %get-tuple-element.55), channel_id=1, source_target_pairs={{14,0},{31,1},{30,16},{1,17},{0,2},{17,3},{16,18},{3,19},{2,4},{19... | collective-permute-start | bytes 393224 | tf_op jit(solution)/shard_map/ppermute | solution.py:320
  62.3 4.8 %collective-permute-start.17 = (bf16[32,2048]{1,0:T(8,128)(2,1)S(1)}, bf16[32,2048]{1,0:T(8,128)(2,1)S(1)}, u32[]{:S(2)}, u32[]{:S(2)}) collective-permute-start(bf16[32,2048]{1,0:T(8,128)(2,1)S(1)} %collective-permute-done.16.refs_1_), channel_id=1, source_target_pairs={{1,0},{0,1},{3,2},{2,3},{5,4},{4,5},{7,6},{6,7},{9,8},{8,9},{11,10... | collective-permute-start | bytes 393224 | tf_op jit(solution)/shard_map/ppermute | solution.py:306
  67.1 4.6 %collective-permute-start.19 = (bf16[32,2048]{1,0:T(8,128)(2,1)S(1)}, bf16[32,2048]{1,0:T(8,128)(2,1)S(1)}, u32[]{:S(2)}, u32[]{:S(2)}) collective-permute-start(bf16[32,2048]{1,0:T(8,128)(2,1)S(1)} %collective-permute-done.18.refs_2_), channel_id=1, source_target_pairs={{1,0},{0,1},{3,2},{2,3},{5,4},{4,5},{7,6},{6,7},{9,8},{8,9},{11,10... | collective-permute-start | bytes 393224 | tf_op jit(solution)/shard_map/ppermute | solution.py:306
  71.7 2.3 %collective-permute-start.21 = (bf16[32,2048]{1,0:T(8,128)(2,1)S(1)}, bf16[32,2048]{1,0:T(8,128)(2,1)S(1)}, u32[]{:S(2)}, u32[]{:S(2)}) collective-permute-start(bf16[32,2048]{1,0:T(8,128)(2,1)S(1)} %collective-permute-done.20.refs_3_), channel_id=1, source_target_pairs={{1,0},{0,1},{3,2},{2,3},{5,4},{4,5},{7,6},{6,7},{9,8},{8,9},{11,10... | collective-permute-start | bytes 393224 | tf_op jit(solution)/shard_map/ppermute | solution.py:306
  74.0 0.0 collective-permute-start.23
  74.0 0.5 collective-permute-start.25
  74.5 0.1 collective-permute-start.27
  74.6 0.4 collective-permute-start.29
  75.1 0.3 collective-permute-start.31
  75.4 1.0 %place.2.refs_9_ = bf16[16,32,2048]{2,1,0:T(8,128)(2,1)} custom-call(s32[1]{0:T(128)} %bitcast.2.refs_0_, bf16[32,2048]{1,0:T(8,128)(2,1)S(1)} %collective-permute-done.16.refs_1_, bf16[32,2048]{1,0:T(8,128)(2,1)S(1)} %collective-permute-done.18.refs_2_, bf16[32,2048]{1,0:T(8,128)(2,1)S(1)} %collective-permute-done.20.refs_3_, ...), custom_call_target="tpu_custom_call" | custom-call | bytes 2097152 | tf_op jit(solution)/shard_map/place/pallas_call | solution.py:280
  76.5 1.0 %place.3 = bf16[16,32,2048]{2,1,0:T(8,128)(2,1)} custom-call(s32[1]{0:T(128)} %bitcast.1.refs_0_, bf16[32,2048]{1,0:T(8,128)(2,1)S(1)} %collective-permute-done.17.refs_1_, bf16[32,2048]{1,0:T(8,128)(2,1)S(1)} %collective-permute-done.19.refs_2_, bf16[32,2048]{1,0:T(8,128)(2,1)S(1)} %collective-permute-done.21.refs_3_, ...), custom_call_target="tpu_custom_call", output_to_operand_aliasing={{}: (9, {})} | custom-call | bytes 2097152 | tf_op jit(solution)/shard_map/place/pallas_call | solution.py:280
  (25 shorter events, 0.1 us)
Async XLA Ops:
  0.7 19.5 %copy-start = (bf16[16,32,2048]{2,1,0:T(8,128)(2,1)S(1)}, bf16[16,32,2048]{2,1,0:T(8,128)(2,1)}, u32[]{:S(2)}) copy-start(bf16[16,32,2048]{2,1,0:T(8,128)(2,1)} %m_ref) | copy-start | bytes 6291460
  3.3 9.0 %collective-permute-start = (bf16[32,2048]{1,0:T(8,128)(2,1)}, bf16[32,2048]{1,0:T(8,128)(2,1)S(1)}, u32[]{:S(2)}, u32[]{:S(2)}) collective-permute-start(bf16[32,2048]{1,0:T(8,128)(2,1)} %get-tuple-element.29), channel_id=1, source_target_pairs={{0,6},{1,23},{16,22},{17,9},{2,8},{3,25},{18,24},{19,11},{4,10},{5... | collective-permute-start | bytes 393224 | tf_op jit(solution)/shard_map/ppermute | solution.py:320
  7.3 9.1 %collective-permute-start.2 = (bf16[32,2048]{1,0:T(8,128)(2,1)}, bf16[32,2048]{1,0:T(8,128)(2,1)S(1)}, u32[]{:S(2)}, u32[]{:S(2)}) collective-permute-start(bf16[32,2048]{1,0:T(8,128)(2,1)} %get-tuple-element.34), channel_id=1, source_target_pairs={{0,2},{1,19},{16,18},{17,5},{2,4},{3,21},{18,20},{19,7},{4,6},{5,2... | collective-permute-start | bytes 393224 | tf_op jit(solution)/shard_map/ppermute | solution.py:320
  7.9 11.0 %collective-permute-start.3 = (bf16[32,2048]{1,0:T(8,128)(2,1)}, bf16[32,2048]{1,0:T(8,128)(2,1)S(1)}, u32[]{:S(2)}, u32[]{:S(2)}) collective-permute-start(bf16[32,2048]{1,0:T(8,128)(2,1)} %get-tuple-element.36), channel_id=1, source_target_pairs={{0,4},{1,21},{16,20},{17,7},{2,6},{3,23},{18,22},{19,9},{4,8},{5,2... | collective-permute-start | bytes 393224 | tf_op jit(solution)/shard_map/ppermute | solution.py:320
  9.4 14.3 %collective-permute-start.1 = (bf16[32,2048]{1,0:T(8,128)(2,1)}, bf16[32,2048]{1,0:T(8,128)(2,1)S(1)}, u32[]{:S(2)}, u32[]{:S(2)}) collective-permute-start(bf16[32,2048]{1,0:T(8,128)(2,1)} %get-tuple-element.32), channel_id=1, source_target_pairs={{0,0},{1,17},{16,16},{17,3},{2,2},{3,19},{18,18},{19,5},{4,4},{5,2... | collective-permute-start | bytes 393224 | tf_op jit(solution)/shard_map/ppermute | solution.py:320
  10.9 15.4 %collective-permute-start.6 = (bf16[32,2048]{1,0:T(8,128)(2,1)}, bf16[32,2048]{1,0:T(8,128)(2,1)S(1)}, u32[]{:S(2)}, u32[]{:S(2)}) collective-permute-start(bf16[32,2048]{1,0:T(8,128)(2,1)} %get-tuple-element.44), channel_id=1, source_target_pairs={{0,12},{1,29},{16,28},{17,15},{2,14},{3,31},{18,30},{19,1},{4,0},{... | collective-permute-start | bytes 393224 | tf_op jit(solution)/shard_map/ppermute | solution.py:320
  12.3 15.0 %collective-permute-start.7 = (bf16[32,2048]{1,0:T(8,128)(2,1)}, bf16[32,2048]{1,0:T(8,128)(2,1)S(1)}, u32[]{:S(2)}, u32[]{:S(2)}) collective-permute-start(bf16[32,2048]{1,0:T(8,128)(2,1)} %get-tuple-element.46), channel_id=1, source_target_pairs={{0,14},{1,31},{16,30},{17,1},{2,0},{3,17},{18,16},{19,3},{4,2},{5,... | collective-permute-start | bytes 393224 | tf_op jit(solution)/shard_map/ppermute | solution.py:320
  16.3 11.6 %collective-permute-start.4 = (bf16[32,2048]{1,0:T(8,128)(2,1)}, bf16[32,2048]{1,0:T(8,128)(2,1)S(1)}, u32[]{:S(2)}, u32[]{:S(2)}) collective-permute-start(bf16[32,2048]{1,0:T(8,128)(2,1)} %get-tuple-element.40), channel_id=1, source_target_pairs={{0,8},{1,25},{16,24},{17,11},{2,10},{3,27},{18,26},{19,13},{4,12},... | collective-permute-start | bytes 393224 | tf_op jit(solution)/shard_map/ppermute | solution.py:320
  18.9 9.0 %collective-permute-start.5 = (bf16[32,2048]{1,0:T(8,128)(2,1)}, bf16[32,2048]{1,0:T(8,128)(2,1)S(1)}, u32[]{:S(2)}, u32[]{:S(2)}) collective-permute-start(bf16[32,2048]{1,0:T(8,128)(2,1)} %get-tuple-element.42), channel_id=1, source_target_pairs={{0,10},{1,27},{16,26},{17,13},{2,12},{3,29},{18,28},{19,15},{4,14}... | collective-permute-start | bytes 393224 | tf_op jit(solution)/shard_map/ppermute | solution.py:320
  20.1 1.6 %copy-start.1 = (bf16[16,32,2048]{2,1,0:T(8,128)(2,1)S(1)}, bf16[16,32,2048]{2,1,0:T(8,128)(2,1)}, u32[]{:S(2)}) copy-start(bf16[16,32,2048]{2,1,0:T(8,128)(2,1)} %g_ref) | copy-start | bytes 6291460
  23.7 9.8 %collective-permute-start.8 = (bf16[32,2048]{1,0:T(8,128)(2,1)S(1)}, bf16[32,2048]{1,0:T(8,128)(2,1)S(1)}, u32[]{:S(2)}, u32[]{:S(2)}) collective-permute-start(bf16[32,2048]{1,0:T(8,128)(2,1)S(1)} %collective-permute-done.1.refs_0_), channel_id=1, source_target_pairs={{1,0},{0,1},{3,2},{2,3},{5,4},{4,5},{7,6},{6,7},{9,8},{8,9},{11,10... | collective-permute-start | bytes 393224 | tf_op jit(solution)/shard_map/ppermute | solution.py:306
  26.3 7.7 %collective-permute-start.9 = (bf16[32,2048]{1,0:T(8,128)(2,1)S(1)}, bf16[32,2048]{1,0:T(8,128)(2,1)S(1)}, u32[]{:S(2)}, u32[]{:S(2)}) collective-permute-start(bf16[32,2048]{1,0:T(8,128)(2,1)S(1)} %collective-permute-done.2.refs_1_), channel_id=1, source_target_pairs={{1,0},{0,1},{3,2},{2,3},{5,4},{4,5},{7,6},{6,7},{9,8},{8,9},{11,10... | collective-permute-start | bytes 393224 | tf_op jit(solution)/shard_map/ppermute | solution.py:306
  27.3 6.8 %collective-permute-start.10 = (bf16[32,2048]{1,0:T(8,128)(2,1)S(1)}, bf16[32,2048]{1,0:T(8,128)(2,1)S(1)}, u32[]{:S(2)}, u32[]{:S(2)}) collective-permute-start(bf16[32,2048]{1,0:T(8,128)(2,1)S(1)} %collective-permute-done.3.refs_2_), channel_id=1, source_target_pairs={{1,0},{0,1},{3,2},{2,3},{5,4},{4,5},{7,6},{6,7},{9,8},{8,9},{11,10... | collective-permute-start | bytes 393224 | tf_op jit(solution)/shard_map/ppermute | solution.py:306
  27.9 6.6 %collective-permute-start.11 = (bf16[32,2048]{1,0:T(8,128)(2,1)S(1)}, bf16[32,2048]{1,0:T(8,128)(2,1)S(1)}, u32[]{:S(2)}, u32[]{:S(2)}) collective-permute-start(bf16[32,2048]{1,0:T(8,128)(2,1)S(1)} %collective-permute-done.refs_3_), channel_id=1, source_target_pairs={{1,0},{0,1},{3,2},{2,3},{5,4},{4,5},{7,6},{6,7},{9,8},{8,9},{11,10... | collective-permute-start | bytes 393224 | tf_op jit(solution)/shard_map/ppermute | solution.py:306
  33.5 1.3 %collective-permute-start.12 = (bf16[32,2048]{1,0:T(8,128)(2,1)S(1)}, bf16[32,2048]{1,0:T(8,128)(2,1)S(1)}, u32[]{:S(2)}, u32[]{:S(2)}) collective-permute-start(bf16[32,2048]{1,0:T(8,128)(2,1)S(1)} %collective-permute-done.4.refs_4_), channel_id=1, source_target_pairs={{1,0},{0,1},{3,2},{2,3},{5,4},{4,5},{7,6},{6,7},{9,8},{8,9},{11,10... | collective-permute-start | bytes 393224 | tf_op jit(solution)/shard_map/ppermute | solution.py:306
  33.5 1.5 %collective-permute-start.13 = (bf16[32,2048]{1,0:T(8,128)(2,1)S(1)}, bf16[32,2048]{1,0:T(8,128)(2,1)S(1)}, u32[]{:S(2)}, u32[]{:S(2)}) collective-permute-start(bf16[32,2048]{1,0:T(8,128)(2,1)S(1)} %collective-permute-done.5.refs_5_), channel_id=1, source_target_pairs={{1,0},{0,1},{3,2},{2,3},{5,4},{4,5},{7,6},{6,7},{9,8},{8,9},{11,10... | collective-permute-start | bytes 393224 | tf_op jit(solution)/shard_map/ppermute | solution.py:306
  34.0 1.3 %collective-permute-start.14 = (bf16[32,2048]{1,0:T(8,128)(2,1)S(1)}, bf16[32,2048]{1,0:T(8,128)(2,1)S(1)}, u32[]{:S(2)}, u32[]{:S(2)}) collective-permute-start(bf16[32,2048]{1,0:T(8,128)(2,1)S(1)} %collective-permute-done.6.refs_6_), channel_id=1, source_target_pairs={{1,0},{0,1},{3,2},{2,3},{5,4},{4,5},{7,6},{6,7},{9,8},{8,9},{11,10... | collective-permute-start | bytes 393224 | tf_op jit(solution)/shard_map/ppermute | solution.py:306
  34.1 1.5 %collective-permute-start.15 = (bf16[32,2048]{1,0:T(8,128)(2,1)S(1)}, bf16[32,2048]{1,0:T(8,128)(2,1)S(1)}, u32[]{:S(2)}, u32[]{:S(2)}) collective-permute-start(bf16[32,2048]{1,0:T(8,128)(2,1)S(1)} %collective-permute-done.7.refs_7_), channel_id=1, source_target_pairs={{1,0},{0,1},{3,2},{2,3},{5,4},{4,5},{7,6},{6,7},{9,8},{8,9},{11,10... | collective-permute-start | bytes 393224 | tf_op jit(solution)/shard_map/ppermute | solution.py:306
  49.9 5.9 %collective-permute-start.16 = (bf16[32,2048]{1,0:T(8,128)(2,1)S(1)}, bf16[32,2048]{1,0:T(8,128)(2,1)S(1)}, u32[]{:S(2)}, u32[]{:S(2)}) collective-permute-start(bf16[32,2048]{1,0:T(8,128)(2,1)S(1)} %get-tuple-element.48), channel_id=1, source_target_pairs={{6,0},{23,1},{22,16},{9,17},{8,2},{25,3},{24,18},{11,19},{10,4},{2... | collective-permute-start | bytes 393224 | tf_op jit(solution)/shard_map/ppermute | solution.py:320
  50.0 11.3 %collective-permute-start.18 = (bf16[32,2048]{1,0:T(8,128)(2,1)S(1)}, bf16[32,2048]{1,0:T(8,128)(2,1)S(1)}, u32[]{:S(2)}, u32[]{:S(2)}) collective-permute-start(bf16[32,2048]{1,0:T(8,128)(2,1)S(1)} %get-tuple-element.49), channel_id=1, source_target_pairs={{8,0},{25,1},{24,16},{11,17},{10,2},{27,3},{26,18},{13,19},{12,4},... | collective-permute-start | bytes 393224 | tf_op jit(solution)/shard_map/ppermute | solution.py:320
  52.0 9.3 %collective-permute-start.20 = (bf16[32,2048]{1,0:T(8,128)(2,1)S(1)}, bf16[32,2048]{1,0:T(8,128)(2,1)S(1)}, u32[]{:S(2)}, u32[]{:S(2)}) collective-permute-start(bf16[32,2048]{1,0:T(8,128)(2,1)S(1)} %get-tuple-element.50), channel_id=1, source_target_pairs={{10,0},{27,1},{26,16},{13,17},{12,2},{29,3},{28,18},{15,19},{14,4}... | collective-permute-start | bytes 393224 | tf_op jit(solution)/shard_map/ppermute | solution.py:320
  53.0 9.3 %collective-permute-start.22 = (bf16[32,2048]{1,0:T(8,128)(2,1)S(1)}, bf16[32,2048]{1,0:T(8,128)(2,1)S(1)}, u32[]{:S(2)}, u32[]{:S(2)}) collective-permute-start(bf16[32,2048]{1,0:T(8,128)(2,1)S(1)} %get-tuple-element.51), channel_id=1, source_target_pairs={{0,0},{17,1},{16,16},{3,17},{2,2},{19,3},{18,18},{5,19},{4,4},{21,... | collective-permute-start | bytes 393224 | tf_op jit(solution)/shard_map/ppermute | solution.py:320
  53.7 13.4 %collective-permute-start.24 = (bf16[32,2048]{1,0:T(8,128)(2,1)S(1)}, bf16[32,2048]{1,0:T(8,128)(2,1)S(1)}, u32[]{:S(2)}, u32[]{:S(2)}) collective-permute-start(bf16[32,2048]{1,0:T(8,128)(2,1)S(1)} %get-tuple-element.52), channel_id=1, source_target_pairs={{2,0},{19,1},{18,16},{5,17},{4,2},{21,3},{20,18},{7,19},{6,4},{23,... | collective-permute-start | bytes 393224 | tf_op jit(solution)/shard_map/ppermute | solution.py:320
  55.8 15.9 %collective-permute-start.26 = (bf16[32,2048]{1,0:T(8,128)(2,1)S(1)}, bf16[32,2048]{1,0:T(8,128)(2,1)S(1)}, u32[]{:S(2)}, u32[]{:S(2)}) collective-permute-start(bf16[32,2048]{1,0:T(8,128)(2,1)S(1)} %get-tuple-element.53), channel_id=1, source_target_pairs={{4,0},{21,1},{20,16},{7,17},{6,2},{23,3},{22,18},{9,19},{8,4},{25,... | collective-permute-start | bytes 393224 | tf_op jit(solution)/shard_map/ppermute | solution.py:320
  61.2 12.8 %collective-permute-start.28 = (bf16[32,2048]{1,0:T(8,128)(2,1)S(1)}, bf16[32,2048]{1,0:T(8,128)(2,1)S(1)}, u32[]{:S(2)}, u32[]{:S(2)}) collective-permute-start(bf16[32,2048]{1,0:T(8,128)(2,1)S(1)} %get-tuple-element.54), channel_id=1, source_target_pairs={{12,0},{29,1},{28,16},{15,17},{14,2},{31,3},{30,18},{1,19},{0,4},{... | collective-permute-start | bytes 393224 | tf_op jit(solution)/shard_map/ppermute | solution.py:320
  61.3 12.8 %collective-permute-start.30 = (bf16[32,2048]{1,0:T(8,128)(2,1)S(1)}, bf16[32,2048]{1,0:T(8,128)(2,1)S(1)}, u32[]{:S(2)}, u32[]{:S(2)}) collective-permute-start(bf16[32,2048]{1,0:T(8,128)(2,1)S(1)} %get-tuple-element.55), channel_id=1, source_target_pairs={{14,0},{31,1},{30,16},{1,17},{0,2},{17,3},{16,18},{3,19},{2,4},{19... | collective-permute-start | bytes 393224 | tf_op jit(solution)/shard_map/ppermute | solution.py:320
  62.3 12.2 %collective-permute-start.17 = (bf16[32,2048]{1,0:T(8,128)(2,1)S(1)}, bf16[32,2048]{1,0:T(8,128)(2,1)S(1)}, u32[]{:S(2)}, u32[]{:S(2)}) collective-permute-start(bf16[32,2048]{1,0:T(8,128)(2,1)S(1)} %collective-permute-done.16.refs_1_), channel_id=1, source_target_pairs={{1,0},{0,1},{3,2},{2,3},{5,4},{4,5},{7,6},{6,7},{9,8},{8,9},{11,10... | collective-permute-start | bytes 393224 | tf_op jit(solution)/shard_map/ppermute | solution.py:306
  67.1 7.5 %collective-permute-start.19 = (bf16[32,2048]{1,0:T(8,128)(2,1)S(1)}, bf16[32,2048]{1,0:T(8,128)(2,1)S(1)}, u32[]{:S(2)}, u32[]{:S(2)}) collective-permute-start(bf16[32,2048]{1,0:T(8,128)(2,1)S(1)} %collective-permute-done.18.refs_2_), channel_id=1, source_target_pairs={{1,0},{0,1},{3,2},{2,3},{5,4},{4,5},{7,6},{6,7},{9,8},{8,9},{11,10... | collective-permute-start | bytes 393224 | tf_op jit(solution)/shard_map/ppermute | solution.py:306
  71.7 3.3 %collective-permute-start.21 = (bf16[32,2048]{1,0:T(8,128)(2,1)S(1)}, bf16[32,2048]{1,0:T(8,128)(2,1)S(1)}, u32[]{:S(2)}, u32[]{:S(2)}) collective-permute-start(bf16[32,2048]{1,0:T(8,128)(2,1)S(1)} %collective-permute-done.20.refs_3_), channel_id=1, source_target_pairs={{1,0},{0,1},{3,2},{2,3},{5,4},{4,5},{7,6},{6,7},{9,8},{8,9},{11,10... | collective-permute-start | bytes 393224 | tf_op jit(solution)/shard_map/ppermute | solution.py:306
  74.0 2.4 %collective-permute-start.23 = (bf16[32,2048]{1,0:T(8,128)(2,1)S(1)}, bf16[32,2048]{1,0:T(8,128)(2,1)S(1)}, u32[]{:S(2)}, u32[]{:S(2)}) collective-permute-start(bf16[32,2048]{1,0:T(8,128)(2,1)S(1)} %collective-permute-done.22.refs_4_), channel_id=1, source_target_pairs={{1,0},{0,1},{3,2},{2,3},{5,4},{4,5},{7,6},{6,7},{9,8},{8,9},{11,10... | collective-permute-start | bytes 393224 | tf_op jit(solution)/shard_map/ppermute | solution.py:306
  74.0 2.4 %collective-permute-start.25 = (bf16[32,2048]{1,0:T(8,128)(2,1)S(1)}, bf16[32,2048]{1,0:T(8,128)(2,1)S(1)}, u32[]{:S(2)}, u32[]{:S(2)}) collective-permute-start(bf16[32,2048]{1,0:T(8,128)(2,1)S(1)} %collective-permute-done.24.refs_5_), channel_id=1, source_target_pairs={{1,0},{0,1},{3,2},{2,3},{5,4},{4,5},{7,6},{6,7},{9,8},{8,9},{11,10... | collective-permute-start | bytes 393224 | tf_op jit(solution)/shard_map/ppermute | solution.py:306
  74.5 1.9 %collective-permute-start.27 = (bf16[32,2048]{1,0:T(8,128)(2,1)S(1)}, bf16[32,2048]{1,0:T(8,128)(2,1)S(1)}, u32[]{:S(2)}, u32[]{:S(2)}) collective-permute-start(bf16[32,2048]{1,0:T(8,128)(2,1)S(1)} %collective-permute-done.26.refs_6_), channel_id=1, source_target_pairs={{1,0},{0,1},{3,2},{2,3},{5,4},{4,5},{7,6},{6,7},{9,8},{8,9},{11,10... | collective-permute-start | bytes 393224 | tf_op jit(solution)/shard_map/ppermute | solution.py:306
  74.6 1.8 %collective-permute-start.29 = (bf16[32,2048]{1,0:T(8,128)(2,1)S(1)}, bf16[32,2048]{1,0:T(8,128)(2,1)S(1)}, u32[]{:S(2)}, u32[]{:S(2)}) collective-permute-start(bf16[32,2048]{1,0:T(8,128)(2,1)S(1)} %collective-permute-done.28.refs_7_), channel_id=1, source_target_pairs={{1,0},{0,1},{3,2},{2,3},{5,4},{4,5},{7,6},{6,7},{9,8},{8,9},{11,10... | collective-permute-start | bytes 393224 | tf_op jit(solution)/shard_map/ppermute | solution.py:306
  75.1 1.4 %collective-permute-start.31 = (bf16[32,2048]{1,0:T(8,128)(2,1)S(1)}, bf16[32,2048]{1,0:T(8,128)(2,1)S(1)}, u32[]{:S(2)}, u32[]{:S(2)}) collective-permute-start(bf16[32,2048]{1,0:T(8,128)(2,1)S(1)} %collective-permute-done.30.refs_8_), channel_id=1, source_target_pairs={{1,0},{0,1},{3,2},{2,3},{5,4},{4,5},{7,6},{6,7},{9,8},{8,9},{11,10... | collective-permute-start | bytes 393224 | tf_op jit(solution)/shard_map/ppermute | solution.py:306

commit v14 on v13

--- a/solution.py
+++ b/solution.py
@@ -62,7 +62,7 @@
         out_shape=[jax.ShapeDtypeStruct((rows, cols), BF)] * count,
         scratch_shapes=[pltpu.VMEM((count, rows, cols), BF)] * 3
         + [pltpu.SemaphoreType.DMA((3, count))],
-        compiler_params=pltpu.CompilerParams(vmem_limit_bytes=60 * 2**20),
+        compiler_params=pltpu.CompilerParams(vmem_limit_bytes=62 * 2**20),
         name="share",
     )(first[None], momentum, gradient)
 
@@ -348,9 +348,10 @@
         update = exchange([update[j] for j in steps], steps, False)
 
         firsts = [lax.rem(place_of + lax.rem(rep + i, n_rep), n_shard)[None] for i in range(n_rep)]
-        whole = (experts, rows, cols)
-        for i, pieces in enumerate([update, *others(update)]):
-            whole = place(firsts, [[(i, j)] for j in steps], pieces, n_rep, whole)
+        groups = [update, *others(update)]
+        names = [[(i, j)] for i in range(n_rep) for j in steps]
+        pieces = [x for xs in groups for x in xs]
+        whole = place(firsts, names, pieces, n_rep, (experts, rows, cols))
         return new_momentum, whole
 
     return jax.shard_map(

time: 78.7 us -> 79 us (level)
  local copies, waits for them, and re-layouts: 1.6 us -> 3.18 us
  starting transfers between devices: 47.6 us -> 46.1 us
  waiting for transfers between devices: 6.42 us -> 7.44 us
  Pallas kernels: 21.1 us -> 20.3 us
    ppermute x16, starting transfers between devices: 23.8 us -> 22.2 us  [others(): return [[lax.ppermute(x, 'rep', pair) for x in pieces] for pair in pairs]]
    unnamed x4, local copies, waits for them, and re-layouts: 1.6 us -> 3.18 us
    ppermute x16, waiting for transfers between devices: 1.05 us -> 2.07 us  [others(): return [[lax.ppermute(x, 'rep', pair) for x in pieces] for pair in pairs]]
    pallas_call x2 -> x1, Pallas kernels: 2.06 us -> 1.44 us  [place(): pl.pallas_call(functools.partial(place_kernel, which, n_rep), in_specs=[p...]
  transfers between devices with their start and end apart: 32 -> 32, of which waited for: 8 -> 12; matrix products, arithmetic and copies ran while one was open for 0% -> 0% of each run, Pallas kernels for 4% -> 3%
where the time goes in v14:
time: 79 us; the launch traced here: 77.9 us
  starting transfers between devices  46.1 us (58%)
  Pallas kernels  20.3 us (26%)
  waiting for transfers between devices  7.44 us (9%)
  local copies, waits for them, and re-layouts  3.18 us (4%)
  between operations  0.88 us (1%)
    ppermute x16, starting transfers between devices, exchange(): moved.append(lax.ppermute(x, ('shard', 'rep'), pairs))  23.9 us
    ppermute x16, starting transfers between devices, others(): return [[lax.ppermute(x, 'rep', pair) for x in pieces] for pair in pairs]  22.2 us
    pallas_call x1, Pallas kernels, orthogonal(): pl.pallas_call(functools.partial(orthogonal_kernel, scale, count), in_spe...  14.3 us
    ppermute x16, waiting for transfers between devices, exchange(): moved.append(lax.ppermute(x, ('shard', 'rep'), pairs))  5.36 us
    unnamed x4, local copies, waits for them, and re-layouts  3.18 us
    pallas_call x1, Pallas kernels, blended_share(): pl.pallas_call(functools.partial(share_kernel, n_rep), in_specs=[pl.Block...  2.52 us
    ppermute x16, waiting for transfers between devices, others(): return [[lax.ppermute(x, 'rep', pair) for x in pieces] for pair in pairs]  2.07 us
    pallas_call x1, Pallas kernels, new_momentum_of(): pl.pallas_call(momentum_kernel, in_specs=[vmem, vmem], out_specs=vmem, ou...  2 us
  transfers between devices with their start and end apart: 32, of which 12 were waited for; matrix products, arithmetic and copies ran while one was open for 0% of the time, Pallas kernels for 3%

profile of v14, /device:TPU:0, one launch (start us, length us, event | category | flops | bytes accessed | tf_op | source)
XLA Modules:
  0.0 77.9 jit_solution(8139012237741542478)
XLA Ops:
  0.7 2.5 %share.1 = (bf16[32,2048]{1,0:T(8,128)(2,1)}, bf16[32,2048]{1,0:T(8,128)(2,1)}, bf16[32,2048]{1,0:T(8,128)(2,1)}, bf16[32,2048]{1,0:T(8,128)(2,1)}, bf16[32,2048...) custom-call(s32[1]{0:T(128)} %bitcast.at_ref, ...), custom_call_target="tpu_custom_call" | custom-call | tf_op jit(solution)/shard_map/share/pallas_call | solution.py:58
  3.2 3.9 %collective-permute-start = (bf16[32,2048]{1,0:T(8,128)(2,1)}, bf16[32,2048]{1,0:T(8,128)(2,1)S(1)}, u32[]{:S(2)}, u32[]{:S(2)}) collective-permute-start(bf16[32,2048]{1,0:T(8,128)(2,1)} %get-tuple-element.29), channel_id=1, source_target_pairs={{0,6},{1,23},{16,22},{17,9},{2,8},{3,25},{18,24},{19,11},{4,10},{5... | collective-permute-start | bytes 393224 | tf_op jit(solution)/shard_map/ppermute | solution.py:320
  7.1 0.6 collective-permute-start.2
  7.7 1.5 %collective-permute-start.3 = (bf16[32,2048]{1,0:T(8,128)(2,1)}, bf16[32,2048]{1,0:T(8,128)(2,1)S(1)}, u32[]{:S(2)}, u32[]{:S(2)}) collective-permute-start(bf16[32,2048]{1,0:T(8,128)(2,1)} %get-tuple-element.36), channel_id=1, source_target_pairs={{0,4},{1,21},{16,20},{17,7},{2,6},{3,23},{18,22},{19,9},{4,8},{5,2... | collective-permute-start | bytes 393224 | tf_op jit(solution)/shard_map/ppermute | solution.py:320
  9.2 1.6 %collective-permute-start.1 = (bf16[32,2048]{1,0:T(8,128)(2,1)}, bf16[32,2048]{1,0:T(8,128)(2,1)S(1)}, u32[]{:S(2)}, u32[]{:S(2)}) collective-permute-start(bf16[32,2048]{1,0:T(8,128)(2,1)} %get-tuple-element.32), channel_id=1, source_target_pairs={{0,0},{1,17},{16,16},{17,3},{2,2},{3,19},{18,18},{19,5},{4,4},{5,2... | collective-permute-start | bytes 393224 | tf_op jit(solution)/shard_map/ppermute | solution.py:320
  10.8 1.4 %collective-permute-start.6 = (bf16[32,2048]{1,0:T(8,128)(2,1)}, bf16[32,2048]{1,0:T(8,128)(2,1)S(1)}, u32[]{:S(2)}, u32[]{:S(2)}) collective-permute-start(bf16[32,2048]{1,0:T(8,128)(2,1)} %get-tuple-element.44), channel_id=1, source_target_pairs={{0,12},{1,29},{16,28},{17,15},{2,14},{3,31},{18,30},{19,1},{4,0},{... | collective-permute-start | bytes 393224 | tf_op jit(solution)/shard_map/ppermute | solution.py:320
  12.2 2.3 %collective-permute-start.7 = (bf16[32,2048]{1,0:T(8,128)(2,1)}, bf16[32,2048]{1,0:T(8,128)(2,1)S(1)}, u32[]{:S(2)}, u32[]{:S(2)}) collective-permute-start(bf16[32,2048]{1,0:T(8,128)(2,1)} %get-tuple-element.46), channel_id=1, source_target_pairs={{0,14},{1,31},{16,30},{17,1},{2,0},{3,17},{18,16},{19,3},{4,2},{5,... | collective-permute-start | bytes 393224 | tf_op jit(solution)/shard_map/ppermute | solution.py:320
  14.5 1.7 %collective-permute-done.2.refs_1_ = bf16[32,2048]{1,0:T(8,128)(2,1)S(1)} collective-permute-done((bf16[32,2048]{1,0:T(8,128)(2,1)}, bf16[32,2048]{1,0:T(8,128)(2,1)S(1)}, u32[]{:S(2)}, u32[]{:S(2)}) %collective-permute-start.2) | collective-permute-done | bytes 131104 | tf_op jit(solution)/shard_map/ppermute | solution.py:320
  16.2 2.0 %collective-permute-start.4 = (bf16[32,2048]{1,0:T(8,128)(2,1)}, bf16[32,2048]{1,0:T(8,128)(2,1)S(1)}, u32[]{:S(2)}, u32[]{:S(2)}) collective-permute-start(bf16[32,2048]{1,0:T(8,128)(2,1)} %get-tuple-element.40), channel_id=1, source_target_pairs={{0,8},{1,25},{16,24},{17,11},{2,10},{3,27},{18,26},{19,13},{4,12},... | collective-permute-start | bytes 393224 | tf_op jit(solution)/shard_map/ppermute | solution.py:320
  18.2 0.5 collective-permute-done.3.refs_2_
  18.8 1.2 %collective-permute-start.5 = (bf16[32,2048]{1,0:T(8,128)(2,1)}, bf16[32,2048]{1,0:T(8,128)(2,1)S(1)}, u32[]{:S(2)}, u32[]{:S(2)}) collective-permute-start(bf16[32,2048]{1,0:T(8,128)(2,1)} %get-tuple-element.42), channel_id=1, source_target_pairs={{0,10},{1,27},{16,26},{17,13},{2,12},{3,29},{18,28},{19,15},{4,14}... | collective-permute-start | bytes 393224 | tf_op jit(solution)/shard_map/ppermute | solution.py:320
  20.0 1.6 %copy-done = bf16[16,32,2048]{2,1,0:T(8,128)(2,1)S(1)} copy-done((bf16[16,32,2048]{2,1,0:T(8,128)(2,1)S(1)}, bf16[16,32,2048]{2,1,0:T(8,128)(2,1)}, u32[]{:S(2)}) %copy-start) | copy-done | bytes 2097176
  21.6 1.6 %copy-done.1 = bf16[16,32,2048]{2,1,0:T(8,128)(2,1)S(1)} copy-done((bf16[16,32,2048]{2,1,0:T(8,128)(2,1)S(1)}, bf16[16,32,2048]{2,1,0:T(8,128)(2,1)}, u32[]{:S(2)}) %copy-start.1) | copy-done | bytes 2097176
  23.2 2.0 %new_momentum.1 = bf16[16,32,2048]{2,1,0:T(8,128)(2,1)} custom-call(bf16[16,32,2048]{2,1,0:T(8,128)(2,1)S(1)} %copy-done, bf16[16,32,2048]{2,1,0:T(8,128)(2,1)S(1)} %copy-done.1), custom_call_target="tpu_custom_call" | custom-call | flops 2097152 | bytes 6291456 | tf_op jit(solution)/shard_map/new_momentum/pallas_call | solution.py:80
  25.2 2.6 %collective-permute-start.8 = (bf16[32,2048]{1,0:T(8,128)(2,1)S(1)}, bf16[32,2048]{1,0:T(8,128)(2,1)S(1)}, u32[]{:S(2)}, u32[]{:S(2)}) collective-permute-start(bf16[32,2048]{1,0:T(8,128)(2,1)S(1)} %collective-permute-done.1.refs_0_), channel_id=1, source_target_pairs={{1,0},{0,1},{3,2},{2,3},{5,4},{4,5},{7,6},{6,7},{9,8},{8,9},{11,10... | collective-permute-start | bytes 393224 | tf_op jit(solution)/shard_map/ppermute | solution.py:306
  27.8 0.1 collective-permute-start.9
  27.8 0.4 collective-permute-start.10
  28.3 5.1 %collective-permute-start.11 = (bf16[32,2048]{1,0:T(8,128)(2,1)S(1)}, bf16[32,2048]{1,0:T(8,128)(2,1)S(1)}, u32[]{:S(2)}, u32[]{:S(2)}) collective-permute-start(bf16[32,2048]{1,0:T(8,128)(2,1)S(1)} %collective-permute-done.refs_3_), channel_id=1, source_target_pairs={{1,0},{0,1},{3,2},{2,3},{5,4},{4,5},{7,6},{6,7},{9,8},{8,9},{11,10... | collective-permute-start | bytes 393224 | tf_op jit(solution)/shard_map/ppermute | solution.py:306
  33.3 0.5 collective-permute-start.13
  33.9 0.1 collective-permute-start.14
  33.9 0.4 collective-permute-start.15
  34.4 0.3 collective-permute-done.12.refs_12_
  34.7 0.2 collective-permute-done.13.refs_13_
  34.9 0.3 collective-permute-done.14.refs_14_
  35.2 0.2 collective-permute-done.15.refs_15_
  35.4 14.3 %orthogonal.1 = (bf16[32,2048]{1,0:T(8,128)(2,1)S(1)}, bf16[32,2048]{1,0:T(8,128)(2,1)S(1)}, bf16[32,2048]{1,0:T(8,128)(2,1)S(1)}, bf16[32,2048]{1,0:T(8,128)(2,...) custom-call(bf16[32,2048]{1,0:T(8,128)(2,1)S(1)} %collective-permute, ...), custom_call_target="tpu_custom_call" | custom-call | tf_op jit(solution)/shard_map/orthogonal/pallas_call | solution.py:237
  49.7 0.1 collective-permute-start.16
  49.8 2.0 %collective-permute-start.17 = (bf16[32,2048]{1,0:T(8,128)(2,1)S(1)}, bf16[32,2048]{1,0:T(8,128)(2,1)S(1)}, u32[]{:S(2)}, u32[]{:S(2)}) collective-permute-start(bf16[32,2048]{1,0:T(8,128)(2,1)S(1)} %get-tuple-element.49), channel_id=1, source_target_pairs={{8,0},{25,1},{24,16},{11,17},{10,2},{27,3},{26,18},{13,19},{12,4},... | collective-permute-start | bytes 393224 | tf_op jit(solution)/shard_map/ppermute | solution.py:320
  51.8 1.1 %collective-permute-start.18 = (bf16[32,2048]{1,0:T(8,128)(2,1)S(1)}, bf16[32,2048]{1,0:T(8,128)(2,1)S(1)}, u32[]{:S(2)}, u32[]{:S(2)}) collective-permute-start(bf16[32,2048]{1,0:T(8,128)(2,1)S(1)} %get-tuple-element.50), channel_id=1, source_target_pairs={{10,0},{27,1},{26,16},{13,17},{12,2},{29,3},{28,18},{15,19},{14,4}... | collective-permute-start | bytes 393224 | tf_op jit(solution)/shard_map/ppermute | solution.py:320
  52.9 0.7 collective-permute-start.19
  53.6 1.3 %collective-permute-start.20 = (bf16[32,2048]{1,0:T(8,128)(2,1)S(1)}, bf16[32,2048]{1,0:T(8,128)(2,1)S(1)}, u32[]{:S(2)}, u32[]{:S(2)}) collective-permute-start(bf16[32,2048]{1,0:T(8,128)(2,1)S(1)} %get-tuple-element.52), channel_id=1, source_target_pairs={{2,0},{19,1},{18,16},{5,17},{4,2},{21,3},{20,18},{7,19},{6,4},{23,... | collective-permute-start | bytes 393224 | tf_op jit(solution)/shard_map/ppermute | solution.py:320
  54.9 0.8 %collective-permute-done.16.refs_2_ = bf16[32,2048]{1,0:T(8,128)(2,1)S(1)} collective-permute-done((bf16[32,2048]{1,0:T(8,128)(2,1)S(1)}, bf16[32,2048]{1,0:T(8,128)(2,1)S(1)}, u32[]{:S(2)}, u32[]{:S(2)}) %collective-permute-start.16) | collective-permute-done | bytes 131104 | tf_op jit(solution)/shard_map/ppermute | solution.py:320
  55.7 3.1 %collective-permute-start.21 = (bf16[32,2048]{1,0:T(8,128)(2,1)S(1)}, bf16[32,2048]{1,0:T(8,128)(2,1)S(1)}, u32[]{:S(2)}, u32[]{:S(2)}) collective-permute-start(bf16[32,2048]{1,0:T(8,128)(2,1)S(1)} %get-tuple-element.53), channel_id=1, source_target_pairs={{4,0},{21,1},{20,16},{7,17},{6,2},{23,3},{22,18},{9,19},{8,4},{25,... | collective-permute-start | bytes 393224 | tf_op jit(solution)/shard_map/ppermute | solution.py:320
  58.8 2.3 %collective-permute-done.17.refs_3_ = bf16[32,2048]{1,0:T(8,128)(2,1)S(1)} collective-permute-done((bf16[32,2048]{1,0:T(8,128)(2,1)S(1)}, bf16[32,2048]{1,0:T(8,128)(2,1)S(1)}, u32[]{:S(2)}, u32[]{:S(2)}) %collective-permute-start.17) | collective-permute-done | bytes 131104 | tf_op jit(solution)/shard_map/ppermute | solution.py:320
  61.1 1.1 %collective-permute-start.23 = (bf16[32,2048]{1,0:T(8,128)(2,1)S(1)}, bf16[32,2048]{1,0:T(8,128)(2,1)S(1)}, u32[]{:S(2)}, u32[]{:S(2)}) collective-permute-start(bf16[32,2048]{1,0:T(8,128)(2,1)S(1)} %get-tuple-element.55), channel_id=1, source_target_pairs={{14,0},{31,1},{30,16},{1,17},{0,2},{17,3},{16,18},{3,19},{2,4},{19... | collective-permute-start | bytes 393224 | tf_op jit(solution)/shard_map/ppermute | solution.py:320
  62.2 4.8 %collective-permute-start.24 = (bf16[32,2048]{1,0:T(8,128)(2,1)S(1)}, bf16[32,2048]{1,0:T(8,128)(2,1)S(1)}, u32[]{:S(2)}, u32[]{:S(2)}) collective-permute-start(bf16[32,2048]{1,0:T(8,128)(2,1)S(1)} %collective-permute-done.16.refs_2_), channel_id=1, source_target_pairs={{1,0},{0,1},{3,2},{2,3},{5,4},{4,5},{7,6},{6,7},{9,8},{8,9},{11,10... | collective-permute-start | bytes 393224 | tf_op jit(solution)/shard_map/ppermute | solution.py:306
  67.0 4.6 %collective-permute-start.25 = (bf16[32,2048]{1,0:T(8,128)(2,1)S(1)}, bf16[32,2048]{1,0:T(8,128)(2,1)S(1)}, u32[]{:S(2)}, u32[]{:S(2)}) collective-permute-start(bf16[32,2048]{1,0:T(8,128)(2,1)S(1)} %collective-permute-done.17.refs_3_), channel_id=1, source_target_pairs={{1,0},{0,1},{3,2},{2,3},{5,4},{4,5},{7,6},{6,7},{9,8},{8,9},{11,10... | collective-permute-start | bytes 393224 | tf_op jit(solution)/shard_map/ppermute | solution.py:306
  71.6 2.3 %collective-permute-start.26 = (bf16[32,2048]{1,0:T(8,128)(2,1)S(1)}, bf16[32,2048]{1,0:T(8,128)(2,1)S(1)}, u32[]{:S(2)}, u32[]{:S(2)}) collective-permute-start(bf16[32,2048]{1,0:T(8,128)(2,1)S(1)} %collective-permute-done.18.refs_4_), channel_id=1, source_target_pairs={{1,0},{0,1},{3,2},{2,3},{5,4},{4,5},{7,6},{6,7},{9,8},{8,9},{11,10... | collective-permute-start | bytes 393224 | tf_op jit(solution)/shard_map/ppermute | solution.py:306
  73.9 0.0 collective-permute-start.27
  73.9 0.5 collective-permute-start.28
  74.4 0.1 collective-permute-start.29
  74.5 0.4 collective-permute-start.30
  74.9 0.3 collective-permute-start.31
  75.2 0.2 collective-permute-done.28.refs_14_
  75.4 0.3 collective-permute-done.29.refs_15_
  75.7 0.2 collective-permute-done.30.refs_16_
  75.9 0.3 collective-permute-done.31.refs_17_
  76.3 1.4 %place.1 = bf16[16,32,2048]{2,1,0:T(8,128)(2,1)} custom-call(s32[1]{0:T(128)} %bitcast.1.refs_0_, s32[1]{0:T(128)} %bitcast.2.refs_1_, bf16[32,2048]{1,0:T(8,128)(2,1)S(1)} %collective-permute-done.16.refs_2_, bf16[32,2048]{1,0:T(8,128)(2,1)S(1)} %collective-permute-done.17.refs_3_, bf16[32,2048]{1,0:T(8,128)(2,1)S(1)} %collective-permute-done.18.refs_4_, ...), custom_call_target="tpu_custom_call" | custom-call | bytes 4194304 | tf_op jit(solution)/shard_map/place/pallas_call | solution.py:280
  (24 shorter events, 0.1 us)
Async XLA Ops:
  3.2 9.0 %collective-permute-start = (bf16[32,2048]{1,0:T(8,128)(2,1)}, bf16[32,2048]{1,0:T(8,128)(2,1)S(1)}, u32[]{:S(2)}, u32[]{:S(2)}) collective-permute-start(bf16[32,2048]{1,0:T(8,128)(2,1)} %get-tuple-element.29), channel_id=1, source_target_pairs={{0,6},{1,23},{16,22},{17,9},{2,8},{3,25},{18,24},{19,11},{4,10},{5... | collective-permute-start | bytes 393224 | tf_op jit(solution)/shard_map/ppermute | solution.py:320
  7.1 9.1 %collective-permute-start.2 = (bf16[32,2048]{1,0:T(8,128)(2,1)}, bf16[32,2048]{1,0:T(8,128)(2,1)S(1)}, u32[]{:S(2)}, u32[]{:S(2)}) collective-permute-start(bf16[32,2048]{1,0:T(8,128)(2,1)} %get-tuple-element.34), channel_id=1, source_target_pairs={{0,2},{1,19},{16,18},{17,5},{2,4},{3,21},{18,20},{19,7},{4,6},{5,2... | collective-permute-start | bytes 393224 | tf_op jit(solution)/shard_map/ppermute | solution.py:320
  7.7 11.0 %collective-permute-start.3 = (bf16[32,2048]{1,0:T(8,128)(2,1)}, bf16[32,2048]{1,0:T(8,128)(2,1)S(1)}, u32[]{:S(2)}, u32[]{:S(2)}) collective-permute-start(bf16[32,2048]{1,0:T(8,128)(2,1)} %get-tuple-element.36), channel_id=1, source_target_pairs={{0,4},{1,21},{16,20},{17,7},{2,6},{3,23},{18,22},{19,9},{4,8},{5,2... | collective-permute-start | bytes 393224 | tf_op jit(solution)/shard_map/ppermute | solution.py:320
  9.2 15.9 %collective-permute-start.1 = (bf16[32,2048]{1,0:T(8,128)(2,1)}, bf16[32,2048]{1,0:T(8,128)(2,1)S(1)}, u32[]{:S(2)}, u32[]{:S(2)}) collective-permute-start(bf16[32,2048]{1,0:T(8,128)(2,1)} %get-tuple-element.32), channel_id=1, source_target_pairs={{0,0},{1,17},{16,16},{17,3},{2,2},{3,19},{18,18},{19,5},{4,4},{5,2... | collective-permute-start | bytes 393224 | tf_op jit(solution)/shard_map/ppermute | solution.py:320
  10.8 17.0 %collective-permute-start.6 = (bf16[32,2048]{1,0:T(8,128)(2,1)}, bf16[32,2048]{1,0:T(8,128)(2,1)S(1)}, u32[]{:S(2)}, u32[]{:S(2)}) collective-permute-start(bf16[32,2048]{1,0:T(8,128)(2,1)} %get-tuple-element.44), channel_id=1, source_target_pairs={{0,12},{1,29},{16,28},{17,15},{2,14},{3,31},{18,30},{19,1},{4,0},{... | collective-permute-start | bytes 393224 | tf_op jit(solution)/shard_map/ppermute | solution.py:320
  12.2 15.6 %collective-permute-start.7 = (bf16[32,2048]{1,0:T(8,128)(2,1)}, bf16[32,2048]{1,0:T(8,128)(2,1)S(1)}, u32[]{:S(2)}, u32[]{:S(2)}) collective-permute-start(bf16[32,2048]{1,0:T(8,128)(2,1)} %get-tuple-element.46), channel_id=1, source_target_pairs={{0,14},{1,31},{16,30},{17,1},{2,0},{3,17},{18,16},{19,3},{4,2},{5,... | collective-permute-start | bytes 393224 | tf_op jit(solution)/shard_map/ppermute | solution.py:320
  16.2 12.1 %collective-permute-start.4 = (bf16[32,2048]{1,0:T(8,128)(2,1)}, bf16[32,2048]{1,0:T(8,128)(2,1)S(1)}, u32[]{:S(2)}, u32[]{:S(2)}) collective-permute-start(bf16[32,2048]{1,0:T(8,128)(2,1)} %get-tuple-element.40), channel_id=1, source_target_pairs={{0,8},{1,25},{16,24},{17,11},{2,10},{3,27},{18,26},{19,13},{4,12},... | collective-permute-start | bytes 393224 | tf_op jit(solution)/shard_map/ppermute | solution.py:320
  18.8 9.5 %collective-permute-start.5 = (bf16[32,2048]{1,0:T(8,128)(2,1)}, bf16[32,2048]{1,0:T(8,128)(2,1)S(1)}, u32[]{:S(2)}, u32[]{:S(2)}) collective-permute-start(bf16[32,2048]{1,0:T(8,128)(2,1)} %get-tuple-element.42), channel_id=1, source_target_pairs={{0,10},{1,27},{16,26},{17,13},{2,12},{3,29},{18,28},{19,15},{4,14}... | collective-permute-start | bytes 393224 | tf_op jit(solution)/shard_map/ppermute | solution.py:320
  20.0 1.6 %copy-start = (bf16[16,32,2048]{2,1,0:T(8,128)(2,1)S(1)}, bf16[16,32,2048]{2,1,0:T(8,128)(2,1)}, u32[]{:S(2)}) copy-start(bf16[16,32,2048]{2,1,0:T(8,128)(2,1)} %m_ref) | copy-start | bytes 6291460
  21.6 1.6 %copy-start.1 = (bf16[16,32,2048]{2,1,0:T(8,128)(2,1)S(1)}, bf16[16,32,2048]{2,1,0:T(8,128)(2,1)}, u32[]{:S(2)}) copy-start(bf16[16,32,2048]{2,1,0:T(8,128)(2,1)} %g_ref) | copy-start | bytes 6291460
  25.2 8.2 %collective-permute-start.8 = (bf16[32,2048]{1,0:T(8,128)(2,1)S(1)}, bf16[32,2048]{1,0:T(8,128)(2,1)S(1)}, u32[]{:S(2)}, u32[]{:S(2)}) collective-permute-start(bf16[32,2048]{1,0:T(8,128)(2,1)S(1)} %collective-permute-done.1.refs_0_), channel_id=1, source_target_pairs={{1,0},{0,1},{3,2},{2,3},{5,4},{4,5},{7,6},{6,7},{9,8},{8,9},{11,10... | collective-permute-start | bytes 393224 | tf_op jit(solution)/shard_map/ppermute | solution.py:306
  27.8 6.1 %collective-permute-start.9 = (bf16[32,2048]{1,0:T(8,128)(2,1)S(1)}, bf16[32,2048]{1,0:T(8,128)(2,1)S(1)}, u32[]{:S(2)}, u32[]{:S(2)}) collective-permute-start(bf16[32,2048]{1,0:T(8,128)(2,1)S(1)} %collective-permute-done.2.refs_1_), channel_id=1, source_target_pairs={{1,0},{0,1},{3,2},{2,3},{5,4},{4,5},{7,6},{6,7},{9,8},{8,9},{11,10... | collective-permute-start | bytes 393224 | tf_op jit(solution)/shard_map/ppermute | solution.py:306
  27.8 6.1 %collective-permute-start.10 = (bf16[32,2048]{1,0:T(8,128)(2,1)S(1)}, bf16[32,2048]{1,0:T(8,128)(2,1)S(1)}, u32[]{:S(2)}, u32[]{:S(2)}) collective-permute-start(bf16[32,2048]{1,0:T(8,128)(2,1)S(1)} %collective-permute-done.3.refs_2_), channel_id=1, source_target_pairs={{1,0},{0,1},{3,2},{2,3},{5,4},{4,5},{7,6},{6,7},{9,8},{8,9},{11,10... | collective-permute-start | bytes 393224 | tf_op jit(solution)/shard_map/ppermute | solution.py:306
  28.3 6.1 %collective-permute-start.11 = (bf16[32,2048]{1,0:T(8,128)(2,1)S(1)}, bf16[32,2048]{1,0:T(8,128)(2,1)S(1)}, u32[]{:S(2)}, u32[]{:S(2)}) collective-permute-start(bf16[32,2048]{1,0:T(8,128)(2,1)S(1)} %collective-permute-done.refs_3_), channel_id=1, source_target_pairs={{1,0},{0,1},{3,2},{2,3},{5,4},{4,5},{7,6},{6,7},{9,8},{8,9},{11,10... | collective-permute-start | bytes 393224 | tf_op jit(solution)/shard_map/ppermute | solution.py:306
  33.3 1.3 %collective-permute-start.12 = (bf16[32,2048]{1,0:T(8,128)(2,1)S(1)}, bf16[32,2048]{1,0:T(8,128)(2,1)S(1)}, u32[]{:S(2)}, u32[]{:S(2)}) collective-permute-start(bf16[32,2048]{1,0:T(8,128)(2,1)S(1)} %collective-permute-done.4.refs_4_), channel_id=1, source_target_pairs={{1,0},{0,1},{3,2},{2,3},{5,4},{4,5},{7,6},{6,7},{9,8},{8,9},{11,10... | collective-permute-start | bytes 393224 | tf_op jit(solution)/shard_map/ppermute | solution.py:306
  33.3 1.5 %collective-permute-start.13 = (bf16[32,2048]{1,0:T(8,128)(2,1)S(1)}, bf16[32,2048]{1,0:T(8,128)(2,1)S(1)}, u32[]{:S(2)}, u32[]{:S(2)}) collective-permute-start(bf16[32,2048]{1,0:T(8,128)(2,1)S(1)} %collective-permute-done.5.refs_5_), channel_id=1, source_target_pairs={{1,0},{0,1},{3,2},{2,3},{5,4},{4,5},{7,6},{6,7},{9,8},{8,9},{11,10... | collective-permute-start | bytes 393224 | tf_op jit(solution)/shard_map/ppermute | solution.py:306
  33.9 1.3 %collective-permute-start.14 = (bf16[32,2048]{1,0:T(8,128)(2,1)S(1)}, bf16[32,2048]{1,0:T(8,128)(2,1)S(1)}, u32[]{:S(2)}, u32[]{:S(2)}) collective-permute-start(bf16[32,2048]{1,0:T(8,128)(2,1)S(1)} %collective-permute-done.6.refs_6_), channel_id=1, source_target_pairs={{1,0},{0,1},{3,2},{2,3},{5,4},{4,5},{7,6},{6,7},{9,8},{8,9},{11,10... | collective-permute-start | bytes 393224 | tf_op jit(solution)/shard_map/ppermute | solution.py:306
  33.9 1.5 %collective-permute-start.15 = (bf16[32,2048]{1,0:T(8,128)(2,1)S(1)}, bf16[32,2048]{1,0:T(8,128)(2,1)S(1)}, u32[]{:S(2)}, u32[]{:S(2)}) collective-permute-start(bf16[32,2048]{1,0:T(8,128)(2,1)S(1)} %collective-permute-done.7.refs_7_), channel_id=1, source_target_pairs={{1,0},{0,1},{3,2},{2,3},{5,4},{4,5},{7,6},{6,7},{9,8},{8,9},{11,10... | collective-permute-start | bytes 393224 | tf_op jit(solution)/shard_map/ppermute | solution.py:306
  49.7 5.9 %collective-permute-start.16 = (bf16[32,2048]{1,0:T(8,128)(2,1)S(1)}, bf16[32,2048]{1,0:T(8,128)(2,1)S(1)}, u32[]{:S(2)}, u32[]{:S(2)}) collective-permute-start(bf16[32,2048]{1,0:T(8,128)(2,1)S(1)} %get-tuple-element.48), channel_id=1, source_target_pairs={{6,0},{23,1},{22,16},{9,17},{8,2},{25,3},{24,18},{11,19},{10,4},{2... | collective-permute-start | bytes 393224 | tf_op jit(solution)/shard_map/ppermute | solution.py:320
  49.8 11.3 %collective-permute-start.17 = (bf16[32,2048]{1,0:T(8,128)(2,1)S(1)}, bf16[32,2048]{1,0:T(8,128)(2,1)S(1)}, u32[]{:S(2)}, u32[]{:S(2)}) collective-permute-start(bf16[32,2048]{1,0:T(8,128)(2,1)S(1)} %get-tuple-element.49), channel_id=1, source_target_pairs={{8,0},{25,1},{24,16},{11,17},{10,2},{27,3},{26,18},{13,19},{12,4},... | collective-permute-start | bytes 393224 | tf_op jit(solution)/shard_map/ppermute | solution.py:320
  51.8 9.3 %collective-permute-start.18 = (bf16[32,2048]{1,0:T(8,128)(2,1)S(1)}, bf16[32,2048]{1,0:T(8,128)(2,1)S(1)}, u32[]{:S(2)}, u32[]{:S(2)}) collective-permute-start(bf16[32,2048]{1,0:T(8,128)(2,1)S(1)} %get-tuple-element.50), channel_id=1, source_target_pairs={{10,0},{27,1},{26,16},{13,17},{12,2},{29,3},{28,18},{15,19},{14,4}... | collective-permute-start | bytes 393224 | tf_op jit(solution)/shard_map/ppermute | solution.py:320
  52.9 9.3 %collective-permute-start.19 = (bf16[32,2048]{1,0:T(8,128)(2,1)S(1)}, bf16[32,2048]{1,0:T(8,128)(2,1)S(1)}, u32[]{:S(2)}, u32[]{:S(2)}) collective-permute-start(bf16[32,2048]{1,0:T(8,128)(2,1)S(1)} %get-tuple-element.51), channel_id=1, source_target_pairs={{0,0},{17,1},{16,16},{3,17},{2,2},{19,3},{18,18},{5,19},{4,4},{21,... | collective-permute-start | bytes 393224 | tf_op jit(solution)/shard_map/ppermute | solution.py:320
  53.6 13.4 %collective-permute-start.20 = (bf16[32,2048]{1,0:T(8,128)(2,1)S(1)}, bf16[32,2048]{1,0:T(8,128)(2,1)S(1)}, u32[]{:S(2)}, u32[]{:S(2)}) collective-permute-start(bf16[32,2048]{1,0:T(8,128)(2,1)S(1)} %get-tuple-element.52), channel_id=1, source_target_pairs={{2,0},{19,1},{18,16},{5,17},{4,2},{21,3},{20,18},{7,19},{6,4},{23,... | collective-permute-start | bytes 393224 | tf_op jit(solution)/shard_map/ppermute | solution.py:320
  55.7 15.9 %collective-permute-start.21 = (bf16[32,2048]{1,0:T(8,128)(2,1)S(1)}, bf16[32,2048]{1,0:T(8,128)(2,1)S(1)}, u32[]{:S(2)}, u32[]{:S(2)}) collective-permute-start(bf16[32,2048]{1,0:T(8,128)(2,1)S(1)} %get-tuple-element.53), channel_id=1, source_target_pairs={{4,0},{21,1},{20,16},{7,17},{6,2},{23,3},{22,18},{9,19},{8,4},{25,... | collective-permute-start | bytes 393224 | tf_op jit(solution)/shard_map/ppermute | solution.py:320
  61.1 12.8 %collective-permute-start.22 = (bf16[32,2048]{1,0:T(8,128)(2,1)S(1)}, bf16[32,2048]{1,0:T(8,128)(2,1)S(1)}, u32[]{:S(2)}, u32[]{:S(2)}) collective-permute-start(bf16[32,2048]{1,0:T(8,128)(2,1)S(1)} %get-tuple-element.54), channel_id=1, source_target_pairs={{12,0},{29,1},{28,16},{15,17},{14,2},{31,3},{30,18},{1,19},{0,4},{... | collective-permute-start | bytes 393224 | tf_op jit(solution)/shard_map/ppermute | solution.py:320
  61.1 12.8 %collective-permute-start.23 = (bf16[32,2048]{1,0:T(8,128)(2,1)S(1)}, bf16[32,2048]{1,0:T(8,128)(2,1)S(1)}, u32[]{:S(2)}, u32[]{:S(2)}) collective-permute-start(bf16[32,2048]{1,0:T(8,128)(2,1)S(1)} %get-tuple-element.55), channel_id=1, source_target_pairs={{14,0},{31,1},{30,16},{1,17},{0,2},{17,3},{16,18},{3,19},{2,4},{19... | collective-permute-start | bytes 393224 | tf_op jit(solution)/shard_map/ppermute | solution.py:320
  62.2 12.2 %collective-permute-start.24 = (bf16[32,2048]{1,0:T(8,128)(2,1)S(1)}, bf16[32,2048]{1,0:T(8,128)(2,1)S(1)}, u32[]{:S(2)}, u32[]{:S(2)}) collective-permute-start(bf16[32,2048]{1,0:T(8,128)(2,1)S(1)} %collective-permute-done.16.refs_2_), channel_id=1, source_target_pairs={{1,0},{0,1},{3,2},{2,3},{5,4},{4,5},{7,6},{6,7},{9,8},{8,9},{11,10... | collective-permute-start | bytes 393224 | tf_op jit(solution)/shard_map/ppermute | solution.py:306
  67.0 7.5 %collective-permute-start.25 = (bf16[32,2048]{1,0:T(8,128)(2,1)S(1)}, bf16[32,2048]{1,0:T(8,128)(2,1)S(1)}, u32[]{:S(2)}, u32[]{:S(2)}) collective-permute-start(bf16[32,2048]{1,0:T(8,128)(2,1)S(1)} %collective-permute-done.17.refs_3_), channel_id=1, source_target_pairs={{1,0},{0,1},{3,2},{2,3},{5,4},{4,5},{7,6},{6,7},{9,8},{8,9},{11,10... | collective-permute-start | bytes 393224 | tf_op jit(solution)/shard_map/ppermute | solution.py:306
  71.6 3.3 %collective-permute-start.26 = (bf16[32,2048]{1,0:T(8,128)(2,1)S(1)}, bf16[32,2048]{1,0:T(8,128)(2,1)S(1)}, u32[]{:S(2)}, u32[]{:S(2)}) collective-permute-start(bf16[32,2048]{1,0:T(8,128)(2,1)S(1)} %collective-permute-done.18.refs_4_), channel_id=1, source_target_pairs={{1,0},{0,1},{3,2},{2,3},{5,4},{4,5},{7,6},{6,7},{9,8},{8,9},{11,10... | collective-permute-start | bytes 393224 | tf_op jit(solution)/shard_map/ppermute | solution.py:306
  73.9 1.3 %collective-permute-start.27 = (bf16[32,2048]{1,0:T(8,128)(2,1)S(1)}, bf16[32,2048]{1,0:T(8,128)(2,1)S(1)}, u32[]{:S(2)}, u32[]{:S(2)}) collective-permute-start(bf16[32,2048]{1,0:T(8,128)(2,1)S(1)} %collective-permute-done.19.refs_5_), channel_id=1, source_target_pairs={{1,0},{0,1},{3,2},{2,3},{5,4},{4,5},{7,6},{6,7},{9,8},{8,9},{11,10... | collective-permute-start | bytes 393224 | tf_op jit(solution)/shard_map/ppermute | solution.py:306
  73.9 1.5 %collective-permute-start.28 = (bf16[32,2048]{1,0:T(8,128)(2,1)S(1)}, bf16[32,2048]{1,0:T(8,128)(2,1)S(1)}, u32[]{:S(2)}, u32[]{:S(2)}) collective-permute-start(bf16[32,2048]{1,0:T(8,128)(2,1)S(1)} %collective-permute-done.20.refs_6_), channel_id=1, source_target_pairs={{1,0},{0,1},{3,2},{2,3},{5,4},{4,5},{7,6},{6,7},{9,8},{8,9},{11,10... | collective-permute-start | bytes 393224 | tf_op jit(solution)/shard_map/ppermute | solution.py:306
  74.4 1.3 %collective-permute-start.29 = (bf16[32,2048]{1,0:T(8,128)(2,1)S(1)}, bf16[32,2048]{1,0:T(8,128)(2,1)S(1)}, u32[]{:S(2)}, u32[]{:S(2)}) collective-permute-start(bf16[32,2048]{1,0:T(8,128)(2,1)S(1)} %collective-permute-done.21.refs_7_), channel_id=1, source_target_pairs={{1,0},{0,1},{3,2},{2,3},{5,4},{4,5},{7,6},{6,7},{9,8},{8,9},{11,10... | collective-permute-start | bytes 393224 | tf_op jit(solution)/shard_map/ppermute | solution.py:306
  74.5 1.5 %collective-permute-start.30 = (bf16[32,2048]{1,0:T(8,128)(2,1)S(1)}, bf16[32,2048]{1,0:T(8,128)(2,1)S(1)}, u32[]{:S(2)}, u32[]{:S(2)}) collective-permute-start(bf16[32,2048]{1,0:T(8,128)(2,1)S(1)} %collective-permute-done.22.refs_8_), channel_id=1, source_target_pairs={{1,0},{0,1},{3,2},{2,3},{5,4},{4,5},{7,6},{6,7},{9,8},{8,9},{11,10... | collective-permute-start | bytes 393224 | tf_op jit(solution)/shard_map/ppermute | solution.py:306
  74.9 1.3 %collective-permute-start.31 = (bf16[32,2048]{1,0:T(8,128)(2,1)S(1)}, bf16[32,2048]{1,0:T(8,128)(2,1)S(1)}, u32[]{:S(2)}, u32[]{:S(2)}) collective-permute-start(bf16[32,2048]{1,0:T(8,128)(2,1)S(1)} %collective-permute-done.23.refs_9_), channel_id=1, source_target_pairs={{1,0},{0,1},{3,2},{2,3},{5,4},{4,5},{7,6},{6,7},{9,8},{8,9},{11,10... | collective-permute-start | bytes 393224 | tf_op jit(solution)/shard_map/ppermute | solution.py:306

commit v15 on v14

--- a/solution.py
+++ b/solution.py
@@ -329,9 +329,10 @@
         place_of = 2 * lax.rem(shard, middle) + shard // middle
         first = lax.rem(place_of + rep, n_shard)
         few = count // 4
-        own = exchange(
-            blended_share(first, momentum, gradient, count, n_rep), range(count), True
-        )
+        early = count - few
+        steps = [(j + early // 2) % early if j < early else j for j in range(count)]
+        sent = blended_share(first, momentum, gradient, count, n_rep)
+        own = exchange([sent[j] for j in steps], steps, True)
 
         middle_piece = (count - 1) // 2
         momentum, gradient, own[middle_piece] = lax.optimization_barrier(
@@ -342,10 +343,7 @@
 
         scale = float(max(experts * rows, cols)) ** 0.5
         parts = own + [x for xs in others(own) for x in xs]
-        update = orthogonal(parts, count, scale)
-        early = count - few
-        steps = [(j + early // 2) % early if j < early else j for j in range(count)]
-        update = exchange([update[j] for j in steps], steps, False)
+        update = exchange(orthogonal(parts, count, scale), steps, False)
 
         firsts = [lax.rem(place_of + lax.rem(rep + i, n_rep), n_shard)[None] for i in range(n_rep)]
         groups = [update, *others(update)]

time: 79 us -> 80.2 us (1.015)
  waiting for transfers between devices: 7.44 us -> 8.25 us
    ppermute x16, starting transfers between devices: 23.9 us -> 29.8 us  [exchange(): moved.append(lax.ppermute(x, ('shard', 'rep'), pairs))]
    ppermute x16, starting transfers between devices: 22.2 us -> 17.1 us  [others(): return [[lax.ppermute(x, 'rep', pair) for x in pieces] for pair in pairs]]
    ppermute x16, waiting for transfers between devices: 5.36 us -> 6.17 us  [exchange(): moved.append(lax.ppermute(x, ('shard', 'rep'), pairs))]
  transfers between devices with their start and end apart: 32 -> 32, of which waited for: 12 -> 11; matrix products, arithmetic and copies ran while one was open for 0% -> 0% of each run, Pallas kernels for 3% -> 3%
where the time goes in v15:
time: 80.2 us; the launch traced here: 79.5 us
  starting transfers between devices  46.9 us (58%)
  Pallas kernels  20.3 us (25%)
  waiting for transfers between devices  8.25 us (10%)
  local copies, waits for them, and re-layouts  3.18 us (4%)
  between operations  0.88 us (1%)
    ppermute x16, starting transfers between devices, exchange(): moved.append(lax.ppermute(x, ('shard', 'rep'), pairs))  29.8 us
    ppermute x16, starting transfers between devices, others(): return [[lax.ppermute(x, 'rep', pair) for x in pieces] for pair in pairs]  17.1 us
    pallas_call x1, Pallas kernels, orthogonal(): pl.pallas_call(functools.partial(orthogonal_kernel, scale, count), in_spe...  14.3 us
    ppermute x16, waiting for transfers between devices, exchange(): moved.append(lax.ppermute(x, ('shard', 'rep'), pairs))  6.17 us
    unnamed x4, local copies, waits for them, and re-layouts  3.18 us
    pallas_call x1, Pallas kernels, blended_share(): pl.pallas_call(functools.partial(share_kernel, n_rep), in_specs=[pl.Block...  2.52 us
    ppermute x16, waiting for transfers between devices, others(): return [[lax.ppermute(x, 'rep', pair) for x in pieces] for pair in pairs]  2.07 us
    pallas_call x1, Pallas kernels, new_momentum_of(): pl.pallas_call(momentum_kernel, in_specs=[vmem, vmem], out_specs=vmem, ou...  2 us
  transfers between devices with their start and end apart: 32, of which 11 were waited for; matrix products, arithmetic and copies ran while one was open for 0% of the time, Pallas kernels for 3%

profile of v15, /device:TPU:0, one launch (start us, length us, event | category | flops | bytes accessed | tf_op | source)
XLA Modules:
  0.0 79.5 jit_solution(9533149096736880547)
XLA Ops:
  0.7 2.5 %share.1 = (bf16[32,2048]{1,0:T(8,128)(2,1)}, bf16[32,2048]{1,0:T(8,128)(2,1)}, bf16[32,2048]{1,0:T(8,128)(2,1)}, bf16[32,2048]{1,0:T(8,128)(2,1)}, bf16[32,2048...) custom-call(s32[1]{0:T(128)} %bitcast.at_ref, ...), custom_call_target="tpu_custom_call" | custom-call | tf_op jit(solution)/shard_map/share/pallas_call | solution.py:58
  3.2 1.6 %collective-permute-start = (bf16[32,2048]{1,0:T(8,128)(2,1)}, bf16[32,2048]{1,0:T(8,128)(2,1)S(1)}, u32[]{:S(2)}, u32[]{:S(2)}) collective-permute-start(bf16[32,2048]{1,0:T(8,128)(2,1)} %get-tuple-element.29), channel_id=1, source_target_pairs={{0,0},{1,17},{16,16},{17,3},{2,2},{3,19},{18,18},{19,5},{4,4},{5,2... | collective-permute-start | bytes 393224 | tf_op jit(solution)/shard_map/ppermute | solution.py:320
  4.7 3.0 %collective-permute-start.2 = (bf16[32,2048]{1,0:T(8,128)(2,1)}, bf16[32,2048]{1,0:T(8,128)(2,1)S(1)}, u32[]{:S(2)}, u32[]{:S(2)}) collective-permute-start(bf16[32,2048]{1,0:T(8,128)(2,1)} %get-tuple-element.34), channel_id=1, source_target_pairs={{0,8},{1,25},{16,24},{17,11},{2,10},{3,27},{18,26},{19,13},{4,12},... | collective-permute-start | bytes 393224 | tf_op jit(solution)/shard_map/ppermute | solution.py:320
  7.8 1.4 %collective-permute-start.3 = (bf16[32,2048]{1,0:T(8,128)(2,1)}, bf16[32,2048]{1,0:T(8,128)(2,1)S(1)}, u32[]{:S(2)}, u32[]{:S(2)}) collective-permute-start(bf16[32,2048]{1,0:T(8,128)(2,1)} %get-tuple-element.36), channel_id=1, source_target_pairs={{0,10},{1,27},{16,26},{17,13},{2,12},{3,29},{18,28},{19,15},{4,14}... | collective-permute-start | bytes 393224 | tf_op jit(solution)/shard_map/ppermute | solution.py:320
  9.1 1.5 %collective-permute-start.1 = (bf16[32,2048]{1,0:T(8,128)(2,1)}, bf16[32,2048]{1,0:T(8,128)(2,1)S(1)}, u32[]{:S(2)}, u32[]{:S(2)}) collective-permute-start(bf16[32,2048]{1,0:T(8,128)(2,1)} %get-tuple-element.32), channel_id=1, source_target_pairs={{0,6},{1,23},{16,22},{17,9},{2,8},{3,25},{18,24},{19,11},{4,10},{5... | collective-permute-start | bytes 393224 | tf_op jit(solution)/shard_map/ppermute | solution.py:320
  10.7 2.3 %collective-permute-start.6 = (bf16[32,2048]{1,0:T(8,128)(2,1)}, bf16[32,2048]{1,0:T(8,128)(2,1)S(1)}, u32[]{:S(2)}, u32[]{:S(2)}) collective-permute-start(bf16[32,2048]{1,0:T(8,128)(2,1)} %get-tuple-element.44), channel_id=1, source_target_pairs={{0,12},{1,29},{16,28},{17,15},{2,14},{3,31},{18,30},{19,1},{4,0},{... | collective-permute-start | bytes 393224 | tf_op jit(solution)/shard_map/ppermute | solution.py:320
  13.0 0.5 collective-permute-start.7
  13.5 0.0 collective-permute-done.2.refs_1_
  13.5 1.5 %collective-permute-start.4 = (bf16[32,2048]{1,0:T(8,128)(2,1)}, bf16[32,2048]{1,0:T(8,128)(2,1)S(1)}, u32[]{:S(2)}, u32[]{:S(2)}) collective-permute-start(bf16[32,2048]{1,0:T(8,128)(2,1)} %get-tuple-element.40), channel_id=1, source_target_pairs={{0,2},{1,19},{16,18},{17,5},{2,4},{3,21},{18,20},{19,7},{4,6},{5,2... | collective-permute-start | bytes 393224 | tf_op jit(solution)/shard_map/ppermute | solution.py:320
  15.0 3.3 %collective-permute-done.3.refs_2_ = bf16[32,2048]{1,0:T(8,128)(2,1)S(1)} collective-permute-done((bf16[32,2048]{1,0:T(8,128)(2,1)}, bf16[32,2048]{1,0:T(8,128)(2,1)S(1)}, u32[]{:S(2)}, u32[]{:S(2)}) %collective-permute-start.3) | collective-permute-done | bytes 131104 | tf_op jit(solution)/shard_map/ppermute | solution.py:320
  18.4 0.0 collective-permute-start.5
  18.4 1.6 %copy-done = bf16[16,32,2048]{2,1,0:T(8,128)(2,1)S(1)} copy-done((bf16[16,32,2048]{2,1,0:T(8,128)(2,1)S(1)}, bf16[16,32,2048]{2,1,0:T(8,128)(2,1)}, u32[]{:S(2)}) %copy-start) | copy-done | bytes 2097176
  20.0 1.6 %copy-done.1 = bf16[16,32,2048]{2,1,0:T(8,128)(2,1)S(1)} copy-done((bf16[16,32,2048]{2,1,0:T(8,128)(2,1)S(1)}, bf16[16,32,2048]{2,1,0:T(8,128)(2,1)}, u32[]{:S(2)}) %copy-start.1) | copy-done | bytes 2097176
  21.6 2.0 %new_momentum.1 = bf16[16,32,2048]{2,1,0:T(8,128)(2,1)} custom-call(bf16[16,32,2048]{2,1,0:T(8,128)(2,1)S(1)} %copy-done, bf16[16,32,2048]{2,1,0:T(8,128)(2,1)S(1)} %copy-done.1), custom_call_target="tpu_custom_call" | custom-call | flops 2097152 | bytes 6291456 | tf_op jit(solution)/shard_map/new_momentum/pallas_call | solution.py:80
  23.6 4.2 %collective-permute-start.8 = (bf16[32,2048]{1,0:T(8,128)(2,1)S(1)}, bf16[32,2048]{1,0:T(8,128)(2,1)S(1)}, u32[]{:S(2)}, u32[]{:S(2)}) collective-permute-start(bf16[32,2048]{1,0:T(8,128)(2,1)S(1)} %collective-permute-done.1.refs_0_), channel_id=1, source_target_pairs={{1,0},{0,1},{3,2},{2,3},{5,4},{4,5},{7,6},{6,7},{9,8},{8,9},{11,10... | collective-permute-start | bytes 393224 | tf_op jit(solution)/shard_map/ppermute | solution.py:306
  27.8 2.7 %collective-permute-start.9 = (bf16[32,2048]{1,0:T(8,128)(2,1)S(1)}, bf16[32,2048]{1,0:T(8,128)(2,1)S(1)}, u32[]{:S(2)}, u32[]{:S(2)}) collective-permute-start(bf16[32,2048]{1,0:T(8,128)(2,1)S(1)} %collective-permute-done.2.refs_1_), channel_id=1, source_target_pairs={{1,0},{0,1},{3,2},{2,3},{5,4},{4,5},{7,6},{6,7},{9,8},{8,9},{11,10... | collective-permute-start | bytes 393224 | tf_op jit(solution)/shard_map/ppermute | solution.py:306
  30.4 0.5 collective-permute-start.10
  31.0 0.1 collective-permute-start.11
  31.0 0.4 collective-permute-start.12
  31.5 0.1 collective-permute-start.13
  31.6 0.4 collective-permute-start.14
  32.0 0.3 collective-permute-start.15
  32.3 0.0 collective-permute-done.11.refs_11_
  32.3 0.2 collective-permute-done.12.refs_12_
  32.5 0.3 collective-permute-done.13.refs_13_
  32.8 0.2 collective-permute-done.14.refs_14_
  33.0 0.3 collective-permute-done.15.refs_15_
  33.4 14.3 %orthogonal.1 = (bf16[32,2048]{1,0:T(8,128)(2,1)S(1)}, bf16[32,2048]{1,0:T(8,128)(2,1)S(1)}, bf16[32,2048]{1,0:T(8,128)(2,1)S(1)}, bf16[32,2048]{1,0:T(8,128)(2,...) custom-call(bf16[32,2048]{1,0:T(8,128)(2,1)S(1)} %collective-permute, ...), custom_call_target="tpu_custom_call" | custom-call | tf_op jit(solution)/shard_map/orthogonal/pallas_call | solution.py:237
  47.7 4.9 %collective-permute-start.16 = (bf16[32,2048]{1,0:T(8,128)(2,1)S(1)}, bf16[32,2048]{1,0:T(8,128)(2,1)S(1)}, u32[]{:S(2)}, u32[]{:S(2)}) collective-permute-start(bf16[32,2048]{1,0:T(8,128)(2,1)S(1)} %get-tuple-element.48), channel_id=1, source_target_pairs={{6,0},{23,1},{22,16},{9,17},{8,2},{25,3},{24,18},{11,19},{10,4},{2... | collective-permute-start | bytes 393224 | tf_op jit(solution)/shard_map/ppermute | solution.py:320
  52.6 2.0 %collective-permute-start.18 = (bf16[32,2048]{1,0:T(8,128)(2,1)S(1)}, bf16[32,2048]{1,0:T(8,128)(2,1)S(1)}, u32[]{:S(2)}, u32[]{:S(2)}) collective-permute-start(bf16[32,2048]{1,0:T(8,128)(2,1)S(1)} %get-tuple-element.50), channel_id=1, source_target_pairs={{10,0},{27,1},{26,16},{13,17},{12,2},{29,3},{28,18},{15,19},{14,4}... | collective-permute-start | bytes 393224 | tf_op jit(solution)/shard_map/ppermute | solution.py:320
  54.6 0.7 collective-permute-start.19
  55.3 2.4 %collective-permute-start.20 = (bf16[32,2048]{1,0:T(8,128)(2,1)S(1)}, bf16[32,2048]{1,0:T(8,128)(2,1)S(1)}, u32[]{:S(2)}, u32[]{:S(2)}) collective-permute-start(bf16[32,2048]{1,0:T(8,128)(2,1)S(1)} %get-tuple-element.52), channel_id=1, source_target_pairs={{2,0},{19,1},{18,16},{5,17},{4,2},{21,3},{20,18},{7,19},{6,4},{23,... | collective-permute-start | bytes 393224 | tf_op jit(solution)/shard_map/ppermute | solution.py:320
  57.7 2.7 %collective-permute-start.21 = (bf16[32,2048]{1,0:T(8,128)(2,1)S(1)}, bf16[32,2048]{1,0:T(8,128)(2,1)S(1)}, u32[]{:S(2)}, u32[]{:S(2)}) collective-permute-start(bf16[32,2048]{1,0:T(8,128)(2,1)S(1)} %get-tuple-element.53), channel_id=1, source_target_pairs={{4,0},{21,1},{20,16},{7,17},{6,2},{23,3},{22,18},{9,19},{8,4},{25,... | collective-permute-start | bytes 393224 | tf_op jit(solution)/shard_map/ppermute | solution.py:320
  60.4 0.5 collective-permute-start.22
  60.8 2.2 %collective-permute-done.18.refs_4_ = bf16[32,2048]{1,0:T(8,128)(2,1)S(1)} collective-permute-done((bf16[32,2048]{1,0:T(8,128)(2,1)S(1)}, bf16[32,2048]{1,0:T(8,128)(2,1)S(1)}, u32[]{:S(2)}, u32[]{:S(2)}) %collective-permute-start.18) | collective-permute-done | bytes 131104 | tf_op jit(solution)/shard_map/ppermute | solution.py:320
  63.1 4.8 %collective-permute-start.23 = (bf16[32,2048]{1,0:T(8,128)(2,1)S(1)}, bf16[32,2048]{1,0:T(8,128)(2,1)S(1)}, u32[]{:S(2)}, u32[]{:S(2)}) collective-permute-start(bf16[32,2048]{1,0:T(8,128)(2,1)S(1)} %get-tuple-element.55), channel_id=1, source_target_pairs={{14,0},{31,1},{30,16},{1,17},{0,2},{17,3},{16,18},{3,19},{2,4},{19... | collective-permute-start | bytes 393224 | tf_op jit(solution)/shard_map/ppermute | solution.py:320
  67.9 5.9 %collective-permute-start.25 = (bf16[32,2048]{1,0:T(8,128)(2,1)S(1)}, bf16[32,2048]{1,0:T(8,128)(2,1)S(1)}, u32[]{:S(2)}, u32[]{:S(2)}) collective-permute-start(bf16[32,2048]{1,0:T(8,128)(2,1)S(1)} %collective-permute-done.17.refs_3_), channel_id=1, source_target_pairs={{1,0},{0,1},{3,2},{2,3},{5,4},{4,5},{7,6},{6,7},{9,8},{8,9},{11,10... | collective-permute-start | bytes 393224 | tf_op jit(solution)/shard_map/ppermute | solution.py:306
  73.7 1.5 %collective-permute-start.26 = (bf16[32,2048]{1,0:T(8,128)(2,1)S(1)}, bf16[32,2048]{1,0:T(8,128)(2,1)S(1)}, u32[]{:S(2)}, u32[]{:S(2)}) collective-permute-start(bf16[32,2048]{1,0:T(8,128)(2,1)S(1)} %collective-permute-done.18.refs_4_), channel_id=1, source_target_pairs={{1,0},{0,1},{3,2},{2,3},{5,4},{4,5},{7,6},{6,7},{9,8},{8,9},{11,10... | collective-permute-start | bytes 393224 | tf_op jit(solution)/shard_map/ppermute | solution.py:306
  75.3 0.0 collective-permute-start.27
  75.3 0.6 collective-permute-done.23.refs_9_
  75.8 0.5 collective-permute-start.29
  76.3 0.1 collective-permute-start.30
  76.4 0.4 collective-permute-start.31
  76.9 0.3 collective-permute-done.28.refs_14_
  77.2 0.2 collective-permute-done.29.refs_15_
  77.4 0.3 collective-permute-done.30.refs_16_
  77.7 0.2 collective-permute-done.31.refs_17_
  77.9 1.4 %place.1 = bf16[16,32,2048]{2,1,0:T(8,128)(2,1)} custom-call(s32[1]{0:T(128)} %bitcast.1.refs_0_, s32[1]{0:T(128)} %bitcast.2.refs_1_, bf16[32,2048]{1,0:T(8,128)(2,1)S(1)} %collective-permute-done.16.refs_2_, bf16[32,2048]{1,0:T(8,128)(2,1)S(1)} %collective-permute-done.17.refs_3_, bf16[32,2048]{1,0:T(8,128)(2,1)S(1)} %collective-permute-done.18.refs_4_, ...), custom_call_target="tpu_custom_call" | custom-call | bytes 4194304 | tf_op jit(solution)/shard_map/place/pallas_call | solution.py:280
  (24 shorter events, 0.1 us)
Async XLA Ops:
  3.2 9.8 %collective-permute-start = (bf16[32,2048]{1,0:T(8,128)(2,1)}, bf16[32,2048]{1,0:T(8,128)(2,1)S(1)}, u32[]{:S(2)}, u32[]{:S(2)}) collective-permute-start(bf16[32,2048]{1,0:T(8,128)(2,1)} %get-tuple-element.29), channel_id=1, source_target_pairs={{0,0},{1,17},{16,16},{17,3},{2,2},{3,19},{18,18},{19,5},{4,4},{5,2... | collective-permute-start | bytes 393224 | tf_op jit(solution)/shard_map/ppermute | solution.py:320
  4.7 8.8 %collective-permute-start.2 = (bf16[32,2048]{1,0:T(8,128)(2,1)}, bf16[32,2048]{1,0:T(8,128)(2,1)S(1)}, u32[]{:S(2)}, u32[]{:S(2)}) collective-permute-start(bf16[32,2048]{1,0:T(8,128)(2,1)} %get-tuple-element.34), channel_id=1, source_target_pairs={{0,8},{1,25},{16,24},{17,11},{2,10},{3,27},{18,26},{19,13},{4,12},... | collective-permute-start | bytes 393224 | tf_op jit(solution)/shard_map/ppermute | solution.py:320
  7.8 10.6 %collective-permute-start.3 = (bf16[32,2048]{1,0:T(8,128)(2,1)}, bf16[32,2048]{1,0:T(8,128)(2,1)S(1)}, u32[]{:S(2)}, u32[]{:S(2)}) collective-permute-start(bf16[32,2048]{1,0:T(8,128)(2,1)} %get-tuple-element.36), channel_id=1, source_target_pairs={{0,10},{1,27},{16,26},{17,13},{2,12},{3,29},{18,28},{19,15},{4,14}... | collective-permute-start | bytes 393224 | tf_op jit(solution)/shard_map/ppermute | solution.py:320
  9.1 14.4 %collective-permute-start.1 = (bf16[32,2048]{1,0:T(8,128)(2,1)}, bf16[32,2048]{1,0:T(8,128)(2,1)S(1)}, u32[]{:S(2)}, u32[]{:S(2)}) collective-permute-start(bf16[32,2048]{1,0:T(8,128)(2,1)} %get-tuple-element.32), channel_id=1, source_target_pairs={{0,6},{1,23},{16,22},{17,9},{2,8},{3,25},{18,24},{19,11},{4,10},{5... | collective-permute-start | bytes 393224 | tf_op jit(solution)/shard_map/ppermute | solution.py:320
  10.7 17.1 %collective-permute-start.6 = (bf16[32,2048]{1,0:T(8,128)(2,1)}, bf16[32,2048]{1,0:T(8,128)(2,1)S(1)}, u32[]{:S(2)}, u32[]{:S(2)}) collective-permute-start(bf16[32,2048]{1,0:T(8,128)(2,1)} %get-tuple-element.44), channel_id=1, source_target_pairs={{0,12},{1,29},{16,28},{17,15},{2,14},{3,31},{18,30},{19,1},{4,0},{... | collective-permute-start | bytes 393224 | tf_op jit(solution)/shard_map/ppermute | solution.py:320
  13.0 17.4 %collective-permute-start.7 = (bf16[32,2048]{1,0:T(8,128)(2,1)}, bf16[32,2048]{1,0:T(8,128)(2,1)S(1)}, u32[]{:S(2)}, u32[]{:S(2)}) collective-permute-start(bf16[32,2048]{1,0:T(8,128)(2,1)} %get-tuple-element.46), channel_id=1, source_target_pairs={{0,14},{1,31},{16,30},{17,1},{2,0},{3,17},{18,16},{19,3},{4,2},{5,... | collective-permute-start | bytes 393224 | tf_op jit(solution)/shard_map/ppermute | solution.py:320
  13.5 17.4 %collective-permute-start.4 = (bf16[32,2048]{1,0:T(8,128)(2,1)}, bf16[32,2048]{1,0:T(8,128)(2,1)S(1)}, u32[]{:S(2)}, u32[]{:S(2)}) collective-permute-start(bf16[32,2048]{1,0:T(8,128)(2,1)} %get-tuple-element.40), channel_id=1, source_target_pairs={{0,2},{1,19},{16,18},{17,5},{2,4},{3,21},{18,20},{19,7},{4,6},{5,2... | collective-permute-start | bytes 393224 | tf_op jit(solution)/shard_map/ppermute | solution.py:320
  18.4 12.6 %collective-permute-start.5 = (bf16[32,2048]{1,0:T(8,128)(2,1)}, bf16[32,2048]{1,0:T(8,128)(2,1)S(1)}, u32[]{:S(2)}, u32[]{:S(2)}) collective-permute-start(bf16[32,2048]{1,0:T(8,128)(2,1)} %get-tuple-element.42), channel_id=1, source_target_pairs={{0,4},{1,21},{16,20},{17,7},{2,6},{3,23},{18,22},{19,9},{4,8},{5,2... | collective-permute-start | bytes 393224 | tf_op jit(solution)/shard_map/ppermute | solution.py:320
  18.4 1.6 %copy-start = (bf16[16,32,2048]{2,1,0:T(8,128)(2,1)S(1)}, bf16[16,32,2048]{2,1,0:T(8,128)(2,1)}, u32[]{:S(2)}) copy-start(bf16[16,32,2048]{2,1,0:T(8,128)(2,1)} %m_ref) | copy-start | bytes 6291460
  20.0 1.6 %copy-start.1 = (bf16[16,32,2048]{2,1,0:T(8,128)(2,1)S(1)}, bf16[16,32,2048]{2,1,0:T(8,128)(2,1)}, u32[]{:S(2)}) copy-start(bf16[16,32,2048]{2,1,0:T(8,128)(2,1)} %g_ref) | copy-start | bytes 6291460
  23.6 7.9 %collective-permute-start.8 = (bf16[32,2048]{1,0:T(8,128)(2,1)S(1)}, bf16[32,2048]{1,0:T(8,128)(2,1)S(1)}, u32[]{:S(2)}, u32[]{:S(2)}) collective-permute-start(bf16[32,2048]{1,0:T(8,128)(2,1)S(1)} %collective-permute-done.1.refs_0_), channel_id=1, source_target_pairs={{1,0},{0,1},{3,2},{2,3},{5,4},{4,5},{7,6},{6,7},{9,8},{8,9},{11,10... | collective-permute-start | bytes 393224 | tf_op jit(solution)/shard_map/ppermute | solution.py:306
  27.8 3.8 %collective-permute-start.9 = (bf16[32,2048]{1,0:T(8,128)(2,1)S(1)}, bf16[32,2048]{1,0:T(8,128)(2,1)S(1)}, u32[]{:S(2)}, u32[]{:S(2)}) collective-permute-start(bf16[32,2048]{1,0:T(8,128)(2,1)S(1)} %collective-permute-done.2.refs_1_), channel_id=1, source_target_pairs={{1,0},{0,1},{3,2},{2,3},{5,4},{4,5},{7,6},{6,7},{9,8},{8,9},{11,10... | collective-permute-start | bytes 393224 | tf_op jit(solution)/shard_map/ppermute | solution.py:306
  30.4 1.6 %collective-permute-start.10 = (bf16[32,2048]{1,0:T(8,128)(2,1)S(1)}, bf16[32,2048]{1,0:T(8,128)(2,1)S(1)}, u32[]{:S(2)}, u32[]{:S(2)}) collective-permute-start(bf16[32,2048]{1,0:T(8,128)(2,1)S(1)} %collective-permute-done.3.refs_2_), channel_id=1, source_target_pairs={{1,0},{0,1},{3,2},{2,3},{5,4},{4,5},{7,6},{6,7},{9,8},{8,9},{11,10... | collective-permute-start | bytes 393224 | tf_op jit(solution)/shard_map/ppermute | solution.py:306
  31.0 1.4 %collective-permute-start.11 = (bf16[32,2048]{1,0:T(8,128)(2,1)S(1)}, bf16[32,2048]{1,0:T(8,128)(2,1)S(1)}, u32[]{:S(2)}, u32[]{:S(2)}) collective-permute-start(bf16[32,2048]{1,0:T(8,128)(2,1)S(1)} %collective-permute-done.refs_3_), channel_id=1, source_target_pairs={{1,0},{0,1},{3,2},{2,3},{5,4},{4,5},{7,6},{6,7},{9,8},{8,9},{11,10... | collective-permute-start | bytes 393224 | tf_op jit(solution)/shard_map/ppermute | solution.py:306
  31.0 1.5 %collective-permute-start.12 = (bf16[32,2048]{1,0:T(8,128)(2,1)S(1)}, bf16[32,2048]{1,0:T(8,128)(2,1)S(1)}, u32[]{:S(2)}, u32[]{:S(2)}) collective-permute-start(bf16[32,2048]{1,0:T(8,128)(2,1)S(1)} %collective-permute-done.4.refs_4_), channel_id=1, source_target_pairs={{1,0},{0,1},{3,2},{2,3},{5,4},{4,5},{7,6},{6,7},{9,8},{8,9},{11,10... | collective-permute-start | bytes 393224 | tf_op jit(solution)/shard_map/ppermute | solution.py:306
  31.5 1.3 %collective-permute-start.13 = (bf16[32,2048]{1,0:T(8,128)(2,1)S(1)}, bf16[32,2048]{1,0:T(8,128)(2,1)S(1)}, u32[]{:S(2)}, u32[]{:S(2)}) collective-permute-start(bf16[32,2048]{1,0:T(8,128)(2,1)S(1)} %collective-permute-done.5.refs_5_), channel_id=1, source_target_pairs={{1,0},{0,1},{3,2},{2,3},{5,4},{4,5},{7,6},{6,7},{9,8},{8,9},{11,10... | collective-permute-start | bytes 393224 | tf_op jit(solution)/shard_map/ppermute | solution.py:306
  31.6 1.5 %collective-permute-start.14 = (bf16[32,2048]{1,0:T(8,128)(2,1)S(1)}, bf16[32,2048]{1,0:T(8,128)(2,1)S(1)}, u32[]{:S(2)}, u32[]{:S(2)}) collective-permute-start(bf16[32,2048]{1,0:T(8,128)(2,1)S(1)} %collective-permute-done.6.refs_6_), channel_id=1, source_target_pairs={{1,0},{0,1},{3,2},{2,3},{5,4},{4,5},{7,6},{6,7},{9,8},{8,9},{11,10... | collective-permute-start | bytes 393224 | tf_op jit(solution)/shard_map/ppermute | solution.py:306
  32.0 1.3 %collective-permute-start.15 = (bf16[32,2048]{1,0:T(8,128)(2,1)S(1)}, bf16[32,2048]{1,0:T(8,128)(2,1)S(1)}, u32[]{:S(2)}, u32[]{:S(2)}) collective-permute-start(bf16[32,2048]{1,0:T(8,128)(2,1)S(1)} %collective-permute-done.7.refs_7_), channel_id=1, source_target_pairs={{1,0},{0,1},{3,2},{2,3},{5,4},{4,5},{7,6},{6,7},{9,8},{8,9},{11,10... | collective-permute-start | bytes 393224 | tf_op jit(solution)/shard_map/ppermute | solution.py:306
  47.7 10.0 %collective-permute-start.16 = (bf16[32,2048]{1,0:T(8,128)(2,1)S(1)}, bf16[32,2048]{1,0:T(8,128)(2,1)S(1)}, u32[]{:S(2)}, u32[]{:S(2)}) collective-permute-start(bf16[32,2048]{1,0:T(8,128)(2,1)S(1)} %get-tuple-element.48), channel_id=1, source_target_pairs={{6,0},{23,1},{22,16},{9,17},{8,2},{25,3},{24,18},{11,19},{10,4},{2... | collective-permute-start | bytes 393224 | tf_op jit(solution)/shard_map/ppermute | solution.py:320
  52.6 7.8 %collective-permute-start.17 = (bf16[32,2048]{1,0:T(8,128)(2,1)S(1)}, bf16[32,2048]{1,0:T(8,128)(2,1)S(1)}, u32[]{:S(2)}, u32[]{:S(2)}) collective-permute-start(bf16[32,2048]{1,0:T(8,128)(2,1)S(1)} %get-tuple-element.49), channel_id=1, source_target_pairs={{8,0},{25,1},{24,16},{11,17},{10,2},{27,3},{26,18},{13,19},{12,4},... | collective-permute-start | bytes 393224 | tf_op jit(solution)/shard_map/ppermute | solution.py:320
  52.6 10.5 %collective-permute-start.18 = (bf16[32,2048]{1,0:T(8,128)(2,1)S(1)}, bf16[32,2048]{1,0:T(8,128)(2,1)S(1)}, u32[]{:S(2)}, u32[]{:S(2)}) collective-permute-start(bf16[32,2048]{1,0:T(8,128)(2,1)S(1)} %get-tuple-element.50), channel_id=1, source_target_pairs={{10,0},{27,1},{26,16},{13,17},{12,2},{29,3},{28,18},{15,19},{14,4}... | collective-permute-start | bytes 393224 | tf_op jit(solution)/shard_map/ppermute | solution.py:320
  54.6 13.3 %collective-permute-start.19 = (bf16[32,2048]{1,0:T(8,128)(2,1)S(1)}, bf16[32,2048]{1,0:T(8,128)(2,1)S(1)}, u32[]{:S(2)}, u32[]{:S(2)}) collective-permute-start(bf16[32,2048]{1,0:T(8,128)(2,1)S(1)} %get-tuple-element.51), channel_id=1, source_target_pairs={{0,0},{17,1},{16,16},{3,17},{2,2},{19,3},{18,18},{5,19},{4,4},{21,... | collective-permute-start | bytes 393224 | tf_op jit(solution)/shard_map/ppermute | solution.py:320
  55.3 12.6 %collective-permute-start.20 = (bf16[32,2048]{1,0:T(8,128)(2,1)S(1)}, bf16[32,2048]{1,0:T(8,128)(2,1)S(1)}, u32[]{:S(2)}, u32[]{:S(2)}) collective-permute-start(bf16[32,2048]{1,0:T(8,128)(2,1)S(1)} %get-tuple-element.52), channel_id=1, source_target_pairs={{2,0},{19,1},{18,16},{5,17},{4,2},{21,3},{20,18},{7,19},{6,4},{23,... | collective-permute-start | bytes 393224 | tf_op jit(solution)/shard_map/ppermute | solution.py:320
  57.7 16.0 %collective-permute-start.21 = (bf16[32,2048]{1,0:T(8,128)(2,1)S(1)}, bf16[32,2048]{1,0:T(8,128)(2,1)S(1)}, u32[]{:S(2)}, u32[]{:S(2)}) collective-permute-start(bf16[32,2048]{1,0:T(8,128)(2,1)S(1)} %get-tuple-element.53), channel_id=1, source_target_pairs={{4,0},{21,1},{20,16},{7,17},{6,2},{23,3},{22,18},{9,19},{8,4},{25,... | collective-permute-start | bytes 393224 | tf_op jit(solution)/shard_map/ppermute | solution.py:320
  60.4 14.9 %collective-permute-start.22 = (bf16[32,2048]{1,0:T(8,128)(2,1)S(1)}, bf16[32,2048]{1,0:T(8,128)(2,1)S(1)}, u32[]{:S(2)}, u32[]{:S(2)}) collective-permute-start(bf16[32,2048]{1,0:T(8,128)(2,1)S(1)} %get-tuple-element.54), channel_id=1, source_target_pairs={{12,0},{29,1},{28,16},{15,17},{14,2},{31,3},{30,18},{1,19},{0,4},{... | collective-permute-start | bytes 393224 | tf_op jit(solution)/shard_map/ppermute | solution.py:320
  63.1 12.8 %collective-permute-start.23 = (bf16[32,2048]{1,0:T(8,128)(2,1)S(1)}, bf16[32,2048]{1,0:T(8,128)(2,1)S(1)}, u32[]{:S(2)}, u32[]{:S(2)}) collective-permute-start(bf16[32,2048]{1,0:T(8,128)(2,1)S(1)} %get-tuple-element.55), channel_id=1, source_target_pairs={{14,0},{31,1},{30,16},{1,17},{0,2},{17,3},{16,18},{3,19},{2,4},{19... | collective-permute-start | bytes 393224 | tf_op jit(solution)/shard_map/ppermute | solution.py:320
  67.9 8.0 %collective-permute-start.24 = (bf16[32,2048]{1,0:T(8,128)(2,1)S(1)}, bf16[32,2048]{1,0:T(8,128)(2,1)S(1)}, u32[]{:S(2)}, u32[]{:S(2)}) collective-permute-start(bf16[32,2048]{1,0:T(8,128)(2,1)S(1)} %collective-permute-done.16.refs_2_), channel_id=1, source_target_pairs={{1,0},{0,1},{3,2},{2,3},{5,4},{4,5},{7,6},{6,7},{9,8},{8,9},{11,10... | collective-permute-start | bytes 393224 | tf_op jit(solution)/shard_map/ppermute | solution.py:306
  67.9 8.5 %collective-permute-start.25 = (bf16[32,2048]{1,0:T(8,128)(2,1)S(1)}, bf16[32,2048]{1,0:T(8,128)(2,1)S(1)}, u32[]{:S(2)}, u32[]{:S(2)}) collective-permute-start(bf16[32,2048]{1,0:T(8,128)(2,1)S(1)} %collective-permute-done.17.refs_3_), channel_id=1, source_target_pairs={{1,0},{0,1},{3,2},{2,3},{5,4},{4,5},{7,6},{6,7},{9,8},{8,9},{11,10... | collective-permute-start | bytes 393224 | tf_op jit(solution)/shard_map/ppermute | solution.py:306
  73.7 2.7 %collective-permute-start.26 = (bf16[32,2048]{1,0:T(8,128)(2,1)S(1)}, bf16[32,2048]{1,0:T(8,128)(2,1)S(1)}, u32[]{:S(2)}, u32[]{:S(2)}) collective-permute-start(bf16[32,2048]{1,0:T(8,128)(2,1)S(1)} %collective-permute-done.18.refs_4_), channel_id=1, source_target_pairs={{1,0},{0,1},{3,2},{2,3},{5,4},{4,5},{7,6},{6,7},{9,8},{8,9},{11,10... | collective-permute-start | bytes 393224 | tf_op jit(solution)/shard_map/ppermute | solution.py:306
  75.3 1.6 %collective-permute-start.27 = (bf16[32,2048]{1,0:T(8,128)(2,1)S(1)}, bf16[32,2048]{1,0:T(8,128)(2,1)S(1)}, u32[]{:S(2)}, u32[]{:S(2)}) collective-permute-start(bf16[32,2048]{1,0:T(8,128)(2,1)S(1)} %collective-permute-done.19.refs_5_), channel_id=1, source_target_pairs={{1,0},{0,1},{3,2},{2,3},{5,4},{4,5},{7,6},{6,7},{9,8},{8,9},{11,10... | collective-permute-start | bytes 393224 | tf_op jit(solution)/shard_map/ppermute | solution.py:306
  75.8 1.3 %collective-permute-start.28 = (bf16[32,2048]{1,0:T(8,128)(2,1)S(1)}, bf16[32,2048]{1,0:T(8,128)(2,1)S(1)}, u32[]{:S(2)}, u32[]{:S(2)}) collective-permute-start(bf16[32,2048]{1,0:T(8,128)(2,1)S(1)} %collective-permute-done.20.refs_6_), channel_id=1, source_target_pairs={{1,0},{0,1},{3,2},{2,3},{5,4},{4,5},{7,6},{6,7},{9,8},{8,9},{11,10... | collective-permute-start | bytes 393224 | tf_op jit(solution)/shard_map/ppermute | solution.py:306
  75.8 1.5 %collective-permute-start.29 = (bf16[32,2048]{1,0:T(8,128)(2,1)S(1)}, bf16[32,2048]{1,0:T(8,128)(2,1)S(1)}, u32[]{:S(2)}, u32[]{:S(2)}) collective-permute-start(bf16[32,2048]{1,0:T(8,128)(2,1)S(1)} %collective-permute-done.21.refs_7_), channel_id=1, source_target_pairs={{1,0},{0,1},{3,2},{2,3},{5,4},{4,5},{7,6},{6,7},{9,8},{8,9},{11,10... | collective-permute-start | bytes 393224 | tf_op jit(solution)/shard_map/ppermute | solution.py:306
  76.3 1.3 %collective-permute-start.30 = (bf16[32,2048]{1,0:T(8,128)(2,1)S(1)}, bf16[32,2048]{1,0:T(8,128)(2,1)S(1)}, u32[]{:S(2)}, u32[]{:S(2)}) collective-permute-start(bf16[32,2048]{1,0:T(8,128)(2,1)S(1)} %collective-permute-done.22.refs_8_), channel_id=1, source_target_pairs={{1,0},{0,1},{3,2},{2,3},{5,4},{4,5},{7,6},{6,7},{9,8},{8,9},{11,10... | collective-permute-start | bytes 393224 | tf_op jit(solution)/shard_map/ppermute | solution.py:306
  76.4 1.5 %collective-permute-start.31 = (bf16[32,2048]{1,0:T(8,128)(2,1)S(1)}, bf16[32,2048]{1,0:T(8,128)(2,1)S(1)}, u32[]{:S(2)}, u32[]{:S(2)}) collective-permute-start(bf16[32,2048]{1,0:T(8,128)(2,1)S(1)} %collective-permute-done.23.refs_9_), channel_id=1, source_target_pairs={{1,0},{0,1},{3,2},{2,3},{5,4},{4,5},{7,6},{6,7},{9,8},{8,9},{11,10... | collective-permute-start | bytes 393224 | tf_op jit(solution)/shard_map/ppermute | solution.py:306
